TPU v7x, 32 devices: a whole 2x2x4 slice. The times are simulated.
32 devices in a mesh: rep: 16 (over z, y, core), shard: 2 (over x).
Axes of the slice: x: 2, y: 2, z: 4, core: 2. Of those that a mesh axis runs over, the one named last changes fastest.
Arguments:
- latents: bfloat16 [32, 256, 384], P(('rep', 'shard')), may hold values from -6 to 6
- timestep_embed: float32 [32, 384], P(('rep', 'shard')), may hold values from -3 to 3
- labels: int32 [32], P(('rep', 'shard')), may hold values from 0 to 1000
- counts: int32 [32], P(('rep', 'shard')), may hold values from 0 to 1, as said below
- class_table: bfloat16 [1001, 384], P(None, 'shard'), may hold values from -3 to 3
- ada_weight: bfloat16 [2, 384, 2304], P(None, 'shard'), may hold values from -0.3125 to 0.3125
- ada_bias: bfloat16 [2, 2304], P(None, 'shard'), may hold values from -2 to 2
- qkv_weight: bfloat16 [2, 384, 1152], P(None, 'shard'), may hold values from -0.3125 to 0.3125
- qv_bias: bfloat16 [2, 768], P(None, 'shard'), may hold values from -3 to 3
- out_weight: bfloat16 [2, 384, 384], P(None, 'shard'), may hold values from -0.625 to 0.625
- out_bias: bfloat16 [2, 384], P(None, 'shard'), may hold values from -3 to 3
- up_weight: bfloat16 [2, 384, 1536], P(None, 'shard'), may hold values from -0.3125 to 0.3125
- up_bias: bfloat16 [2, 1536], P(None, 'shard'), may hold values from -3 to 3
- down_weight: bfloat16 [2, 1536, 384], P(None, 'shard'), may hold values from -0.15625 to 0.15625
- down_bias: bfloat16 [2, 384], P(None, 'shard'), may hold values from -3 to 3
- cotangent: bfloat16 [32, 256, 384], P(('rep', 'shard')), may hold values from -6 to 6
Outputs:
- activations: bfloat16 [32, 256, 384], P(('rep', 'shard'))
- latents_grad: float32 [32, 256, 384], P(('rep', 'shard'))
- cond_grad: float32 [32, 384], P(('rep', 'shard'))
- table_grad: float32 [1001, 384], P(None, 'shard')
- ada_weight_grad: float32 [2, 384, 2304], P(None, 'shard')
- ada_bias_grad: float32 [2, 2304], P(None, 'shard')
- qkv_weight_grad: float32 [2, 384, 1152], P(None, 'shard')
- qv_bias_grad: float32 [2, 768], P(None, 'shard')
- out_weight_grad: float32 [2, 384, 384], P(None, 'shard')
- out_bias_grad: float32 [2, 384], P(None, 'shard')
- up_weight_grad: float32 [2, 384, 1536], P(None, 'shard')
- up_bias_grad: float32 [2, 1536], P(None, 'shard')
- down_weight_grad: float32 [2, 1536, 384], P(None, 'shard')
- down_bias_grad: float32 [2, 384], P(None, 'shard')
Inputs may be any that keep to these rules, and one draw needn't show every extreme that they name: `counts`: whether a device's single slot holds a live latent (1) or not (0); some device holds 1 and some holds 0.
All inputs are finite; a program needn't handle non-finite values.
Results may differ from a plain program's by a relative error of at most 0.012.
Values may be sent and summed in bfloat16 or wider, within the bound.
No kernel may reach another device: no remote copies, remote signals or barrier semaphores. Data moves between devices by JAX's collectives and lax.ppermute only.
A program may use at most 128 MiB of HBM per device.

v0:
```python
import math

import jax
import jax.numpy as jnp
from jax import lax
from jax.sharding import PartitionSpec as P

HEAD_DIM = 64
LAYERS = 2


norm_eps = 1e-06
gelu_coeff = math.sqrt(2.0 / math.pi)
gelu_cubic = 0.044715


def batched(formula, operand_a, operand_b):
    return jnp.einsum(formula, operand_a, operand_b, preferred_element_type=jnp.float32)


def norm_rows(values):
    centered = values - jnp.mean(values, axis=-1, keepdims=True)
    inv_dev = lax.rsqrt(jnp.mean(centered * centered, axis=-1, keepdims=True) + norm_eps)
    return (centered * inv_dev, inv_dev)


def norm_back(grad_normed, normed, inv_dev):
    return (
        grad_normed
        - jnp.mean(grad_normed, axis=-1, keepdims=True)
        - normed * jnp.mean(grad_normed * normed, axis=-1, keepdims=True)
    ) * inv_dev


def gelu_parts(pre_act):
    inner_arg = gelu_coeff * (pre_act + gelu_cubic * pre_act * pre_act * pre_act)
    tanh_val = jnp.tanh(inner_arg)
    value_out = 0.5 * pre_act * (1.0 + tanh_val)
    slope_out = 0.5 * (1.0 + tanh_val) + 0.5 * pre_act * (
        1.0 - tanh_val * tanh_val
    ) * gelu_coeff * (1.0 + 3.0 * gelu_cubic * pre_act * pre_act)
    return (value_out, slope_out)


def layer_forward(stream, cond_act, layer_weights):
    w_ada, b_ada, w_qkv, b_qv, w_out, b_out, w_up, b_up, w_down, b_down = layer_weights
    slot_count, token_count, model_width = stream.shape
    head_count = model_width // HEAD_DIM
    row_count = slot_count * token_count
    shape_heads = (slot_count, token_count, head_count, HEAD_DIM)
    modul = jnp.dot(cond_act, w_ada, preferred_element_type=jnp.float32) + b_ada.astype(jnp.float32)
    shifts = tuple(
        (modul[:, None, member * model_width : (member + 1) * model_width] for member in range(6))
    )
    normed, inv_one = norm_rows(stream)
    modulated = (
        (normed * (1.0 + shifts[1]) + shifts[0])
        .astype(jnp.bfloat16)
        .reshape(row_count, model_width)
    )
    projected = jnp.dot(modulated, w_qkv, preferred_element_type=jnp.float32)
    bias_full = b_qv.astype(jnp.float32)
    query_heads = (
        (projected[:, :model_width] + bias_full[:model_width])
        .astype(jnp.bfloat16)
        .reshape(shape_heads)
    )
    key_heads = (
        projected[:, model_width : 2 * model_width].astype(jnp.bfloat16).reshape(shape_heads)
    )
    value_heads = (
        (projected[:, 2 * model_width :] + bias_full[model_width:])
        .astype(jnp.bfloat16)
        .reshape(shape_heads)
    )
    scores = batched("sqhe,skhe->shqk", query_heads, key_heads) * HEAD_DIM ** (-0.5)
    row_top = jnp.max(scores, axis=-1, keepdims=True)
    log_total = row_top + jnp.log(jnp.sum(jnp.exp(scores - row_top), axis=-1, keepdims=True))
    prob_bf = jnp.exp(scores - log_total).astype(jnp.bfloat16)
    attended = (
        batched("shqk,skhe->sqhe", prob_bf, value_heads)
        .astype(jnp.bfloat16)
        .reshape(row_count, model_width)
    )
    branch_attn = (
        jnp.dot(attended, w_out, preferred_element_type=jnp.float32) + b_out.astype(jnp.float32)
    ).reshape(stream.shape)
    middle = stream + shifts[2] * branch_attn
    normed_two, inv_two = norm_rows(middle)
    mod_two = (
        (normed_two * (1.0 + shifts[4]) + shifts[3])
        .astype(jnp.bfloat16)
        .reshape(row_count, model_width)
    )
    pre_act = jnp.dot(mod_two, w_up, preferred_element_type=jnp.float32) + b_up.astype(jnp.float32)
    act_value, act_slope = gelu_parts(pre_act)
    act_bf = act_value.astype(jnp.bfloat16)
    branch_mlp = (
        jnp.dot(act_bf, w_down, preferred_element_type=jnp.float32) + b_down.astype(jnp.float32)
    ).reshape(stream.shape)
    output = middle + shifts[5] * branch_mlp
    kept_values = (
        shifts,
        normed,
        inv_one,
        modulated,
        query_heads,
        key_heads,
        value_heads,
        log_total,
        attended,
        branch_attn,
        normed_two,
        inv_two,
        mod_two,
        act_slope,
        act_bf,
        branch_mlp,
    )
    return (output, kept_values)


def layer_backward(grad_out, cond_act, layer_weights, kept_values):
    w_ada, b_ada, w_qkv, b_qv, w_out, b_out, w_up, b_up, w_down, b_down = layer_weights
    (
        shifts,
        normed,
        inv_one,
        modulated,
        query_heads,
        key_heads,
        value_heads,
        log_total,
        attended,
        branch_attn,
        normed_two,
        inv_two,
        mod_two,
        act_slope,
        act_bf,
        branch_mlp,
    ) = kept_values
    slot_count, token_count, model_width = grad_out.shape
    row_count = slot_count * token_count
    grad_gate_mlp = jnp.sum(grad_out * branch_mlp, axis=1)
    grad_branch = (grad_out * shifts[5]).reshape(row_count, model_width)
    branch_bf = grad_branch.astype(jnp.bfloat16)
    grad_w_down = jnp.dot(act_bf.T, branch_bf, preferred_element_type=jnp.float32)
    grad_b_down = jnp.sum(grad_branch, axis=0)
    grad_pre = jnp.dot(branch_bf, w_down.T, preferred_element_type=jnp.float32) * act_slope
    pre_bf = grad_pre.astype(jnp.bfloat16)
    grad_w_up = jnp.dot(mod_two.T, pre_bf, preferred_element_type=jnp.float32)
    grad_b_up = jnp.sum(grad_pre, axis=0)
    grad_mod_two = jnp.dot(pre_bf, w_up.T, preferred_element_type=jnp.float32).reshape(
        grad_out.shape
    )
    grad_shift_mlp = jnp.sum(grad_mod_two, axis=1)
    grad_scale_mlp = jnp.sum(grad_mod_two * normed_two, axis=1)
    grad_middle = grad_out + norm_back(grad_mod_two * (1.0 + shifts[4]), normed_two, inv_two)
    grad_gate_attn = jnp.sum(grad_middle * branch_attn, axis=1)
    grad_battn = (grad_middle * shifts[2]).reshape(row_count, model_width)
    battn_bf = grad_battn.astype(jnp.bfloat16)
    grad_w_out = jnp.dot(attended.T, battn_bf, preferred_element_type=jnp.float32)
    grad_b_out = jnp.sum(grad_battn, axis=0)
    grad_att = (
        jnp.dot(battn_bf, w_out.T, preferred_element_type=jnp.float32)
        .astype(jnp.bfloat16)
        .reshape(query_heads.shape)
    )
    scores = batched("sqhe,skhe->shqk", query_heads, key_heads) * HEAD_DIM ** (-0.5)
    prob_full = jnp.exp(scores - log_total)
    prob_bf = prob_full.astype(jnp.bfloat16)
    grad_prob = batched("sqhe,skhe->shqk", grad_att, value_heads)
    grad_values = batched("shqk,sqhe->skhe", prob_bf, grad_att).reshape(row_count, model_width)
    row_dot = jnp.sum(prob_full * grad_prob, axis=-1, keepdims=True)
    grad_scores = (prob_full * (grad_prob - row_dot) * HEAD_DIM ** (-0.5)).astype(jnp.bfloat16)
    grad_queries = batched("shqk,skhe->sqhe", grad_scores, key_heads).reshape(
        row_count, model_width
    )
    grad_keys = batched("shqk,sqhe->skhe", grad_scores, query_heads).reshape(row_count, model_width)
    grad_proj = jnp.concatenate([grad_queries, grad_keys, grad_values], axis=1)
    proj_bf = grad_proj.astype(jnp.bfloat16)
    grad_b_qv = jnp.concatenate([jnp.sum(grad_queries, axis=0), jnp.sum(grad_values, axis=0)])
    grad_w_qkv = jnp.dot(modulated.T, proj_bf, preferred_element_type=jnp.float32)
    grad_modul = jnp.dot(proj_bf, w_qkv.T, preferred_element_type=jnp.float32).reshape(
        grad_out.shape
    )
    grad_shift_attn = jnp.sum(grad_modul, axis=1)
    grad_scale_attn = jnp.sum(grad_modul * normed, axis=1)
    grad_stream = grad_middle + norm_back(grad_modul * (1.0 + shifts[1]), normed, inv_one)
    grad_vector = jnp.concatenate(
        [
            grad_shift_attn,
            grad_scale_attn,
            grad_gate_attn,
            grad_shift_mlp,
            grad_scale_mlp,
            grad_gate_mlp,
        ],
        axis=1,
    )
    vector_bf = grad_vector.astype(jnp.bfloat16)
    grad_w_ada = jnp.dot(cond_act.T, vector_bf, preferred_element_type=jnp.float32)
    grad_b_ada = jnp.sum(grad_vector, axis=0)
    grad_cond = jnp.dot(vector_bf, w_ada.T, preferred_element_type=jnp.float32)
    return (
        grad_stream,
        grad_cond,
        (
            grad_w_ada,
            grad_b_ada,
            grad_w_qkv,
            grad_b_qv,
            grad_w_out,
            grad_b_out,
            grad_w_up,
            grad_b_up,
            grad_w_down,
            grad_b_down,
        ),
    )


def reduce_both(table_term, lower, upper):
    shared = (
        lax.psum_scatter(table_term, "shard", scatter_dimension=1, tiled=True),
        lax.psum_scatter(lower[0][None], "shard", scatter_dimension=1, tiled=True),
        lax.psum_scatter(upper[0][None], "shard", scatter_dimension=1, tiled=True),
        lax.psum_scatter(lower[1][None], "shard", scatter_dimension=1, tiled=True),
        lax.psum_scatter(upper[1][None], "shard", scatter_dimension=1, tiled=True),
        lax.psum_scatter(lower[2][None], "shard", scatter_dimension=1, tiled=True),
        lax.psum_scatter(upper[2][None], "shard", scatter_dimension=1, tiled=True),
        lax.psum_scatter(lower[3][None], "shard", scatter_dimension=1, tiled=True),
        lax.psum_scatter(upper[3][None], "shard", scatter_dimension=1, tiled=True),
        lax.psum_scatter(lower[4][None], "shard", scatter_dimension=1, tiled=True),
        lax.psum_scatter(upper[4][None], "shard", scatter_dimension=1, tiled=True),
        lax.psum_scatter(lower[5][None], "shard", scatter_dimension=1, tiled=True),
        lax.psum_scatter(upper[5][None], "shard", scatter_dimension=1, tiled=True),
        lax.psum_scatter(lower[6][None], "shard", scatter_dimension=1, tiled=True),
        lax.psum_scatter(upper[6][None], "shard", scatter_dimension=1, tiled=True),
        lax.psum_scatter(lower[7][None], "shard", scatter_dimension=1, tiled=True),
        lax.psum_scatter(upper[7][None], "shard", scatter_dimension=1, tiled=True),
        lax.psum_scatter(lower[8][None], "shard", scatter_dimension=1, tiled=True),
        lax.psum_scatter(upper[8][None], "shard", scatter_dimension=1, tiled=True),
        lax.psum_scatter(lower[9][None], "shard", scatter_dimension=1, tiled=True),
        lax.psum_scatter(upper[9][None], "shard", scatter_dimension=1, tiled=True),
    )
    return lax.psum(
        (
            shared[0],
            shared[1],
            shared[2],
            shared[3],
            shared[4],
            shared[5],
            shared[6],
            shared[7],
            shared[8],
            shared[9],
            shared[10],
            shared[11],
            shared[12],
            shared[13],
            shared[14],
            shared[15],
            shared[16],
            shared[17],
            shared[18],
            shared[19],
            shared[20],
        ),
        "rep",
    )


def on_device(
    latents,
    timestep_embed,
    labels,
    counts,
    class_table,
    ada_weight,
    ada_bias,
    qkv_weight,
    qv_bias,
    out_weight,
    out_bias,
    up_weight,
    up_bias,
    down_weight,
    down_bias,
    cotangent,
):
    gathered = (
        lax.all_gather(class_table, "shard", axis=1, tiled=True),
        lax.all_gather(ada_weight, "shard", axis=1, tiled=True),
        lax.all_gather(ada_bias, "shard", axis=1, tiled=True),
        lax.all_gather(qkv_weight, "shard", axis=1, tiled=True),
        lax.all_gather(qv_bias, "shard", axis=1, tiled=True),
        lax.all_gather(out_weight, "shard", axis=1, tiled=True),
        lax.all_gather(out_bias, "shard", axis=1, tiled=True),
        lax.all_gather(up_weight, "shard", axis=1, tiled=True),
        lax.all_gather(up_bias, "shard", axis=1, tiled=True),
        lax.all_gather(down_weight, "shard", axis=1, tiled=True),
        lax.all_gather(down_bias, "shard", axis=1, tiled=True),
    )
    table_full = gathered[0]
    stacks = gathered[1:]
    slot_count = latents.shape[0]
    live_mask = (jnp.arange(slot_count) < counts[0]).astype(jnp.float32)
    one_hot = (labels[:, None] == jnp.arange(class_table.shape[0])[None, :]).astype(jnp.bfloat16)
    condition = timestep_embed + jnp.dot(one_hot, table_full, preferred_element_type=jnp.float32)
    cond_sigmoid = jax.nn.sigmoid(condition)
    cond_act = (condition * cond_sigmoid).astype(jnp.bfloat16)
    stream = latents.astype(jnp.float32)
    kept_layers = []
    for layer_index in range(LAYERS):
        stream, kept_values = layer_forward(
            stream, cond_act, tuple((member[layer_index] for member in stacks))
        )
        kept_layers.append(kept_values)
    activations = (stream * live_mask[:, None, None]).astype(jnp.bfloat16)
    back_stacks = (
        lax.all_gather(ada_weight, "shard", axis=1, tiled=True),
        lax.all_gather(ada_bias, "shard", axis=1, tiled=True),
        lax.all_gather(qkv_weight, "shard", axis=1, tiled=True),
        lax.all_gather(qv_bias, "shard", axis=1, tiled=True),
        lax.all_gather(out_weight, "shard", axis=1, tiled=True),
        lax.all_gather(out_bias, "shard", axis=1, tiled=True),
        lax.all_gather(up_weight, "shard", axis=1, tiled=True),
        lax.all_gather(up_bias, "shard", axis=1, tiled=True),
        lax.all_gather(down_weight, "shard", axis=1, tiled=True),
        lax.all_gather(down_bias, "shard", axis=1, tiled=True),
    )
    grad_stream = cotangent.astype(jnp.float32) * live_mask[:, None, None]
    grad_cond_total = jnp.zeros(condition.shape, jnp.float32)
    grads_by_layer = [None] * LAYERS
    for layer_index in reversed(range(LAYERS)):
        grad_stream, grad_cond, layer_grads = layer_backward(
            grad_stream,
            cond_act,
            tuple((member[layer_index] for member in back_stacks)),
            kept_layers[layer_index],
        )
        grad_cond_total = grad_cond_total + grad_cond
        grads_by_layer[layer_index] = layer_grads
    cond_grad = grad_cond_total * cond_sigmoid * (1.0 + condition * (1.0 - cond_sigmoid))
    table_term = jnp.dot(one_hot.astype(jnp.float32).T, cond_grad, precision=lax.Precision.HIGHEST)
    summed = reduce_both(table_term, grads_by_layer[0], grads_by_layer[1])
    table_grad = summed[0]
    weight_grads = tuple(
        (
            jnp.concatenate([summed[1 + 2 * member], summed[2 + 2 * member]], axis=0)
            for member in range(10)
        )
    )
    return (activations, grad_stream, cond_grad, table_grad) + weight_grads


def solution(mesh):
    in_specs = (
        P(("rep", "shard"), None, None),
        P(("rep", "shard"), None),
        P(("rep", "shard")),
        P(("rep", "shard")),
        P(None, "shard"),
        P(None, "shard", None),
        P(None, "shard"),
        P(None, "shard", None),
        P(None, "shard"),
        P(None, "shard", None),
        P(None, "shard"),
        P(None, "shard", None),
        P(None, "shard"),
        P(None, "shard", None),
        P(None, "shard"),
        P(("rep", "shard"), None, None),
    )
    out_specs = (
        P(("rep", "shard"), None, None),
        P(("rep", "shard"), None, None),
        P(("rep", "shard"), None),
        P(None, "shard"),
        P(None, "shard", None),
        P(None, "shard"),
        P(None, "shard", None),
        P(None, "shard"),
        P(None, "shard", None),
        P(None, "shard"),
        P(None, "shard", None),
        P(None, "shard"),
        P(None, "shard", None),
        P(None, "shard"),
    )
    return jax.shard_map(
        on_device, mesh=mesh, in_specs=in_specs, out_specs=out_specs, check_vma=False
    )
```

profile of v0, /device:TPU:0, one launch (start us, length us, event | category | flops | bytes accessed | tf_op | source)
XLA Modules:
  0.0 1022.7 jit_solution(5916118858010499602)
XLA Ops:
  10.8 14.5 %all_gather.38 = bf16[1001,384]{0,1:T(8,128)(2,1)S(1)} all-gather(bf16[1001,192]{0,1:T(8,128)(2,1)S(1)} %copy-done.53), channel_id=1, replica_groups=mesh['rep'=16,'shard'=2] {'shard'}, dimensions={1}, use_global_device_ids=true | all-gather | bytes 1153152 | tf_op jit(solution)/shard_map/all_gather | solution.py:295
  25.3 4.8 all_gather.40
  30.6 4.3 all_gather.42
  35.0 15.0 %all_gather.43 = bf16[2,384,384]{2,1,0:T(8,128)(2,1)S(1)} all-gather(bf16[2,192,384]{2,1,0:T(8,128)(2,1)S(1)} %copy-done.55), channel_id=1, replica_groups=mesh['rep'=16,'shard'=2] {'shard'}, dimensions={1}, use_global_device_ids=true | all-gather | bytes 884736 | tf_op jit(solution)/shard_map/all_gather | solution.py:300
  50.0 4.2 all-gather
  54.9 4.4 all_gather.46
  59.9 4.2 all-gather.1
  68.3 1.8 fusion.47
  70.2 30.5 %all-gather.9.cloned.1.call-done = bf16[2,384,1152]{2,1,0:T(8,128)(2,1)} async-done(((bf16[2,192,1152]{2,1,0:T(8,128)(2,1)}), bf16[2,384,1152]{2,1,0:T(8,128)(2,1)}) %all-gather.9.cloned.1.call-update) | async-done | bytes 1769488 | tf_op jit(solution)/shard_map/all_gather | solution.py:298
  100.8 1.7 fusion.67
  105.5 32.9 %all-gather.11.cloned.1.call-done = bf16[2,384,1536]{2,1,0:T(8,128)(2,1)} async-done(((bf16[2,192,1536]{2,1,0:T(8,128)(2,1)}), bf16[2,384,1536]{2,1,0:T(8,128)(2,1)}) %all-gather.11.cloned.1.call-update) | async-done | bytes 2359312 | tf_op jit(solution)/shard_map/all_gather | solution.py:302
  138.4 3.0 convolution_add_fusion.1
  141.5 34.5 %all-gather.13.cloned.1.call-done = bf16[2,1536,384]{2,1,0:T(8,128)(2,1)} async-done(((bf16[2,768,384]{2,1,0:T(8,128)(2,1)}), bf16[2,1536,384]{2,1,0:T(8,128)(2,1)}) %all-gather.13.cloned.1.call-update) | async-done | bytes 2359312 | tf_op jit(solution)/shard_map/all_gather | solution.py:304
  175.9 3.3 fusion.180
  183.9 1.4 fusion.187
  185.6 1.7 copy.78
  187.4 1.4 convolution_convert_fusion.2
  192.1 1.9 fusion.192
  195.9 2.2 fusion.111
  199.8 1.7 copy.82
  201.5 2.6 fusion.194
  204.1 3.9 fusion.184
  208.1 3.5 fusion.43
  211.6 2.7 fusion.185
  215.5 2.8 fusion.94
  219.8 1.9 fusion.193
  225.6 2.0 multiply_reduce_fusion.5
  229.2 1.6 fusion.195
  230.8 4.1 fusion.182
  234.9 3.3 fusion.40
  238.2 1.6 fusion.183
  240.1 2.9 fusion.82
  257.0 1.4 dynamic-update-slice.16
  270.4 1.9 convolution_bitcast_fusion.5
  272.4 1.8 convolution_bitcast_fusion.4
  275.5 2.0 convolution_bitcast_fusion.3
  278.8 2.0 convolution_bitcast_fusion.2
  282.3 2.2 convolution_bitcast_fusion.1
  285.9 2.2 convolution_bitcast_fusion
  288.8 3.4 multiply_bitcast_fusion.1
  305.7 1.4 copy.98
  308.8 18.2 %reduce-scatter.48.cloned.1.call-done = f32[1,192,1152]{2,1,0:T(8,128)} async-done(((f32[1,384,1152]{2,1,0:T(8,128)}), f32[1,192,1152]{2,1,0:T(8,128)}) %reduce-scatter.48.cloned.1.call-update) | async-done | bytes 884752 | tf_op jit(solution)/shard_map/reduce_scatter | solution.py:231
  327.0 31.1 %reduce-scatter.50.cloned.1.call-done = f32[1,192,1152]{2,1,0:T(8,128)} async-done(((f32[1,384,1152]{2,1,0:T(8,128)}), f32[1,192,1152]{2,1,0:T(8,128)}) %reduce-scatter.50.cloned.1.call-update) | async-done | bytes 884752 | tf_op jit(solution)/shard_map/reduce_scatter | solution.py:232
  358.1 37.5 %reduce-scatter.56.cloned.1.call-done = f32[1,192,1536]{2,1,0:T(8,128)} async-done(((f32[1,384,1536]{2,1,0:T(8,128)}), f32[1,192,1536]{2,1,0:T(8,128)}) %reduce-scatter.56.cloned.1.call-update) | async-done | bytes 1179664 | tf_op jit(solution)/shard_map/reduce_scatter | solution.py:239
  395.6 37.6 %reduce-scatter.58.cloned.1.call-done = f32[1,192,1536]{2,1,0:T(8,128)} async-done(((f32[1,384,1536]{2,1,0:T(8,128)}), f32[1,192,1536]{2,1,0:T(8,128)}) %reduce-scatter.58.cloned.1.call-update) | async-done | bytes 1179664 | tf_op jit(solution)/shard_map/reduce_scatter | solution.py:240
  433.2 36.9 %reduce-scatter.60.cloned.1.call-done = f32[1,768,384]{2,1,0:T(8,128)} async-done(((f32[1,1536,384]{2,1,0:T(8,128)}), f32[1,768,384]{2,1,0:T(8,128)}) %reduce-scatter.60.cloned.1.call-update) | async-done | bytes 1179664 | tf_op jit(solution)/shard_map/reduce_scatter | solution.py:243
  470.1 37.0 %reduce-scatter.62.cloned.1.call-done = f32[1,768,384]{2,1,0:T(8,128)} async-done(((f32[1,1536,384]{2,1,0:T(8,128)}), f32[1,768,384]{2,1,0:T(8,128)}) %reduce-scatter.62.cloned.1.call-update) | async-done | bytes 1179664 | tf_op jit(solution)/shard_map/reduce_scatter | solution.py:244
  507.1 50.5 %reduce-scatter.44.cloned.1.call-done = f32[1,192,2304]{2,1,0:T(8,128)} async-done(((f32[1,384,2304]{2,1,0:T(8,128)}), f32[1,192,2304]{2,1,0:T(8,128)}) %reduce-scatter.44.cloned.1.call-update) | async-done | bytes 1769488 | tf_op jit(solution)/shard_map/reduce_scatter | solution.py:227
  557.6 49.8 %reduce-scatter.46.cloned.1.call-done = f32[1,192,2304]{2,1,0:T(8,128)} async-done(((f32[1,384,2304]{2,1,0:T(8,128)}), f32[1,192,2304]{2,1,0:T(8,128)}) %reduce-scatter.46.cloned.1.call-update) | async-done | bytes 1769488 | tf_op jit(solution)/shard_map/reduce_scatter | solution.py:228
  609.5 11.1 %reduce-scatter.72.cloned.1.call-done = f32[192,1]{1,0:T(8,128)} async-done(((f32[384,1]{1,0:T(8,128)}), f32[192,1]{1,0:T(8,128)}) %reduce-scatter.72.cloned.1.call-update) | async-done | bytes 784
  621.5 12.2 %reduce-scatter.80.cloned.1.call-done = f32[192,1]{1,0:T(8,128)} async-done(((f32[384,1]{1,0:T(8,128)}), f32[192,1]{1,0:T(8,128)}) %reduce-scatter.80.cloned.1.call-update) | async-done | bytes 784
  634.7 12.2 %reduce-scatter.74.cloned.1.call-done = f32[192,1]{1,0:T(8,128)} async-done(((f32[384,1]{1,0:T(8,128)}), f32[192,1]{1,0:T(8,128)}) %reduce-scatter.74.cloned.1.call-update) | async-done | bytes 784
  647.8 12.3 %reduce-scatter.82.cloned.1.call-done = f32[192,1]{1,0:T(8,128)} async-done(((f32[384,1]{1,0:T(8,128)}), f32[192,1]{1,0:T(8,128)}) %reduce-scatter.82.cloned.1.call-update) | async-done | bytes 784
  661.1 14.4 %reduce-scatter.68.cloned.1.call-done = f32[384,1]{1,0:T(8,128)} async-done(((f32[768,1]{1,0:T(8,128)}), f32[384,1]{1,0:T(8,128)}) %reduce-scatter.68.cloned.1.call-update) | async-done | bytes 1552
  676.5 14.4 %reduce-scatter.70.cloned.1.call-done = f32[384,1]{1,0:T(8,128)} async-done(((f32[768,1]{1,0:T(8,128)}), f32[384,1]{1,0:T(8,128)}) %reduce-scatter.70.cloned.1.call-update) | async-done | bytes 1552
  691.9 18.8 %reduce-scatter.76.cloned.1.call-done = f32[768,1]{1,0:T(8,128)} async-done(((f32[1536,1]{1,0:T(8,128)}), f32[768,1]{1,0:T(8,128)}) %reduce-scatter.76.cloned.1.call-update) | async-done | bytes 3088
  711.8 19.2 %reduce-scatter.78.cloned.1.call-done = f32[768,1]{1,0:T(8,128)} async-done(((f32[1536,1]{1,0:T(8,128)}), f32[768,1]{1,0:T(8,128)}) %reduce-scatter.78.cloned.1.call-update) | async-done | bytes 3088
  732.1 22.8 %reduce-scatter.64.cloned.1.call-done = f32[1152,1]{1,0:T(8,128)} async-done(((f32[2304,1]{1,0:T(8,128)}), f32[1152,1]{1,0:T(8,128)}) %reduce-scatter.64.cloned.1.call-update) | async-done | bytes 4624
  756.2 22.8 %reduce-scatter.66.cloned.1.call-done = f32[1152,1]{1,0:T(8,128)} async-done(((f32[2304,1]{1,0:T(8,128)}), f32[1152,1]{1,0:T(8,128)}) %reduce-scatter.66.cloned.1.call-update) | async-done | bytes 4624
  780.2 64.3 %all-reduce = (f32[1,1152]{1,0:T(1,128)S(1)}, f32[1,1152]{1,0:T(1,128)S(1)}, f32[1,384]{1,0:T(1,128)S(1)}, f32[1,384]{1,0:T(1,128)S(1)}, f32[1,192]{1,0:T(1,128)...) all-reduce(f32[1,1152]{1,0:T(1,128)S(1)} %copy.101, ...), channel_id=1, replica_groups=mesh['rep'=16,'shard'=2] {'rep'}, use_global_device_ids=true, to_apply=%region_43.0 | all-reduce | flops 5376 | bytes 43008 | tf_op jit(solution)/shard_map/psum | solution.py:248
  847.5 156.8 %all-reduce.4.cloned.1.call-done = (f32[1001,192]{0,1:T(8,128)}, f32[1,192,2304]{2,1,0:T(8,128)}, f32[1,192,2304]{2,1,0:T(8,128)}, f32[1,192,1152]{2,1,0:T(8,128...) async-done(((f32[1001,192]{0,1:T(8,128)}, ...) | async-done | bytes 11385616 | tf_op jit(solution)/shard_map/psum | solution.py:248
  1004.3 3.3 pad_maximum_fusion.2
  1007.6 1.6 pad_maximum_fusion.1
  1013.3 2.0 pad_maximum_fusion
  (540 shorter events, 97.7 us)
Async XLA Ops:
  7.2 61.1 %all-gather.7.cloned.1.call-start = ((), (), s32[]{:S(2)}) async-start(), calls=%async_computation.21 | async-start | bytes 5308416 | tf_op jit(solution)/shard_map/all_gather | solution.py:296
  7.9 92.8 %all-gather.9.cloned.1.call-start = ((), (), s32[]{:S(2)}) async-start(), calls=%async_computation.22 | async-start | bytes 2654208 | tf_op jit(solution)/shard_map/all_gather | solution.py:298
  8.7 16.6 %copy-start.145 = (bf16[2,1152]{1,0:T(2,128)(2,1)S(1)}, bf16[2,1152]{1,0:T(2,128)(2,1)}, u32[]{:S(2)}) copy-start(bf16[2,1152]{1,0:T(2,128)(2,1)} %param.22) | copy-start | bytes 13828
  8.7 21.5 %copy-start.7 = (bf16[1,256,384]{2,1,0:T(8,128)(2,1)S(1)}, bf16[1,256,384]{2,1,0:T(8,128)(2,1)}, u32[]{:S(2)}) copy-start(bf16[1,256,384]{2,1,0:T(8,128)(2,1)} %param.16) | copy-start | bytes 589828
  8.7 129.7 %all-gather.11.cloned.1.call-start = ((), (), s32[]{:S(2)}) async-start(), calls=%async_computation.23 | async-start | bytes 3538944 | tf_op jit(solution)/shard_map/all_gather | solution.py:302
  9.4 21.1 %copy-start.156 = (bf16[2,384]{1,0:T(2,128)(2,1)S(1)}, bf16[2,384]{1,0:T(2,128)(2,1)}, u32[]{:S(2)}) copy-start(bf16[2,384]{1,0:T(2,128)(2,1)} %param.24) | copy-start | bytes 4612
  9.4 25.5 %copy-start.55 = (bf16[2,192,384]{2,1,0:T(8,128)(2,1)S(1)}, bf16[2,192,384]{2,1,0:T(8,128)(2,1)}, u32[]{:S(2)}) copy-start(bf16[2,192,384]{2,1,0:T(8,128)(2,1)} %param.25) | copy-start | bytes 884740
  9.5 166.5 %all-gather.13.cloned.1.call-start = ((), (), s32[]{:S(2)}) async-start(), calls=%async_computation.24 | async-start | bytes 3538944 | tf_op jit(solution)/shard_map/all_gather | solution.py:304
  10.0 40.0 %copy-start.158 = (bf16[2,192]{1,0:T(2,128)(2,1)S(1)}, bf16[2,192]{1,0:T(2,128)(2,1)}, u32[]{:S(2)}) copy-start(bf16[2,192]{1,0:T(2,128)(2,1)} %param.26) | copy-start | bytes 2308
  10.0 44.9 %copy-start.150 = (bf16[2,768]{1,0:T(2,128)(2,1)S(1)}, bf16[2,768]{1,0:T(2,128)(2,1)}, u32[]{:S(2)}) copy-start(bf16[2,768]{1,0:T(2,128)(2,1)} %param.28) | copy-start | bytes 9220
  10.0 49.9 %copy-start.159 = (bf16[2,192]{1,0:T(2,128)(2,1)S(1)}, bf16[2,192]{1,0:T(2,128)(2,1)}, u32[]{:S(2)}) copy-start(bf16[2,192]{1,0:T(2,128)(2,1)} %param.30) | copy-start | bytes 2308
  10.1 56.1 %copy-start.157 = (f32[1,384]{1,0:T(1,128)S(1)}, f32[1,384]{1,0:T(1,128)}, u32[]{:S(2)}) copy-start(f32[1,384]{1,0:T(1,128)} %param.17) | copy-start | bytes 4612
  10.1 298.7 %reduce-scatter.54.cloned.1.call-start = ((), (), s32[]{:S(2)}) async-start(), calls=%async_computation.31 | async-start | bytes 884736 | tf_op jit(solution)/shard_map/reduce_scatter | solution.py:236
  30.3 70.4 %copy-start.76 = (f32[256]{0:T(256)}, f32[256]{0:T(256)S(1)}, u32[]{:S(2)}) copy-start(f32[256]{0:T(256)S(1)} %broadcast_multiply_fusion.12) | copy-start | bytes 3076
  30.6 70.2 %copy-start.110 = (f32[256]{0:T(256)}, f32[256]{0:T(256)S(1)}, u32[]{:S(2)}) copy-start(f32[256]{0:T(256)S(1)} %add_rsqrt_fusion.3) | copy-start | bytes 3076
  50.0 54.2 %copy-start.13 = (bf16[2,384,384]{2,1,0:T(8,128)(2,1)}, bf16[2,384,384]{2,1,0:T(8,128)(2,1)S(1)}, u32[]{:S(2)}) copy-start(bf16[2,384,384]{2,1,0:T(8,128)(2,1)S(1)} %all_gather.43) | copy-start | bytes 1769476
  67.1 112.4 %copy-start.86 = (f32[1,384]{1,0:T(1,128)}, f32[1,384]{1,0:T(1,128)S(1)}, u32[]{:S(2)}) copy-start(f32[1,384]{1,0:T(1,128)S(1)} %get-tuple-element.84) | copy-start | bytes 4612
  67.1 112.4 %copy-start.88 = (f32[1,384]{1,0:T(1,128)}, f32[1,384]{1,0:T(1,128)S(1)}, u32[]{:S(2)}) copy-start(f32[1,384]{1,0:T(1,128)S(1)} %get-tuple-element.116) | copy-start | bytes 4612
  70.2 32.4 %copy-start.62 = (f32[384]{0:T(512)}, f32[384]{0:T(512)S(1)}, u32[]{:S(2)}) copy-start(f32[384]{0:T(512)S(1)} %get-tuple-element.50) | copy-start | bytes 4612
  70.2 32.4 %copy-start.100 = (f32[384]{0:T(512)}, f32[384]{0:T(512)S(1)}, u32[]{:S(2)}) copy-start(f32[384]{0:T(512)S(1)} %get-tuple-element.49) | copy-start | bytes 4612
  70.2 34.0 %copy-start.64 = (f32[384]{0:T(512)}, f32[384]{0:T(512)S(1)}, u32[]{:S(2)}) copy-start(f32[384]{0:T(512)S(1)} %get-tuple-element.51) | copy-start | bytes 4612
  70.2 68.2 %copy-start.66 = (f32[384]{0:T(512)}, f32[384]{0:T(512)S(1)}, u32[]{:S(2)}) copy-start(f32[384]{0:T(512)S(1)} %get-tuple-element.48) | copy-start | bytes 4612
  70.2 68.2 %copy-start.98 = (f32[384]{0:T(512)}, f32[384]{0:T(512)S(1)}, u32[]{:S(2)}) copy-start(f32[384]{0:T(512)S(1)} %get-tuple-element.47) | copy-start | bytes 4612
  70.2 105.7 %copy-start.142 = (f32[384]{0:T(512)}, f32[384]{0:T(512)S(1)}, u32[]{:S(2)}) copy-start(f32[384]{0:T(512)S(1)} %get-tuple-element.46) | copy-start | bytes 4612
  105.3 70.7 %copy-start.4 = (f32[1,256,384]{2,1,0:T(8,128)}, f32[1,256,384]{2,1,0:T(8,128)S(1)}, u32[]{:S(2)}) copy-start(f32[1,256,384]{2,1,0:T(8,128)S(1)} %get-tuple-element.95) | copy-start | bytes 1179652
  105.3 36.2 %copy-start.81 = (f32[256]{0:T(256)}, f32[256]{0:T(256)S(1)}, u32[]{:S(2)}) copy-start(f32[256]{0:T(256)S(1)} %broadcast_multiply_fusion.11) | copy-start | bytes 3076
  105.5 36.0 %copy-start.118 = (f32[256]{0:T(256)}, f32[256]{0:T(256)S(1)}, u32[]{:S(2)}) copy-start(f32[256]{0:T(256)S(1)} %add_rsqrt_fusion.2) | copy-start | bytes 3076
  179.3 39.6 %copy-start.2 = (f32[1,256,384]{2,1,0:T(8,128)}, f32[1,256,384]{2,1,0:T(8,128)S(1)}, u32[]{:S(2)}) copy-start(f32[1,256,384]{2,1,0:T(8,128)S(1)} %get-tuple-element.93) | copy-start | bytes 1179652
  225.6 83.2 %reduce-scatter.52.cloned.1.call-start = ((), (), s32[]{:S(2)}) async-start(), calls=%async_computation.30 | async-start | bytes 884736 | tf_op jit(solution)/shard_map/reduce_scatter | solution.py:235
  239.9 68.9 %reduce-scatter.42.cloned.1.call-start = ((), (), s32[]{:S(2)}) async-start(), calls=%async_computation.25 | async-start | bytes 2359296 | tf_op jit(solution)/shard_map/reduce_scatter | solution.py:226
  240.0 6.8 copy-start.136
  240.0 7.3 copy-start.106
  240.0 7.9 copy-start.94
  240.0 8.5 copy-start.134
  240.0 9.0 copy-start.132
  240.0 9.6 copy-start.90
  240.0 10.2 copy-start.128
  240.0 10.8 %copy-start.130 = (f32[384]{0:T(512)S(1)}, f32[384]{0:T(512)}, u32[]{:S(2)}) copy-start(f32[384]{0:T(512)} %get-tuple-element.37) | copy-start | bytes 4612
  240.0 21.1 %copy-start.84 = (bf16[2304]{0:T(1024)(128)(2,1)S(1)}, bf16[2304]{0:T(1024)(128)(2,1)}, u32[]{:S(2)}) copy-start(bf16[2304]{0:T(1024)(128)(2,1)} %custom-call.3) | copy-start | bytes 13828
  240.0 26.2 %copy-start.1 = (bf16[2,384,2304]{2,1,0:T(8,128)(2,1)S(1)}, bf16[2,384,2304]{2,1,0:T(8,128)(2,1)}, u32[]{:S(2)}) copy-start(bf16[2,384,2304]{2,1,0:T(8,128)(2,1)} %all-gather.7.cloned.1.call-done) | copy-start | bytes 10616836
  242.9 7.9 copy-start.138
  270.2 56.8 %reduce-scatter.48.cloned.1.call-start = ((), (), s32[]{:S(2)}) async-start(), calls=%async_computation.28 | async-start | bytes 2654208 | tf_op jit(solution)/shard_map/reduce_scatter | solution.py:231
  272.3 85.9 %reduce-scatter.50.cloned.1.call-start = ((), (), s32[]{:S(2)}) async-start(), calls=%async_computation.29 | async-start | bytes 2654208 | tf_op jit(solution)/shard_map/reduce_scatter | solution.py:232
  274.3 121.4 %reduce-scatter.56.cloned.1.call-start = ((), (), s32[]{:S(2)}) async-start(), calls=%async_computation.32 | async-start | bytes 3538944 | tf_op jit(solution)/shard_map/reduce_scatter | solution.py:239
  277.6 155.7 %reduce-scatter.58.cloned.1.call-start = ((), (), s32[]{:S(2)}) async-start(), calls=%async_computation.33 | async-start | bytes 3538944 | tf_op jit(solution)/shard_map/reduce_scatter | solution.py:240
  280.8 189.3 %reduce-scatter.60.cloned.1.call-start = ((), (), s32[]{:S(2)}) async-start(), calls=%async_computation.34 | async-start | bytes 3538944 | tf_op jit(solution)/shard_map/reduce_scatter | solution.py:243
  284.5 222.6 %reduce-scatter.62.cloned.1.call-start = ((), (), s32[]{:S(2)}) async-start(), calls=%async_computation.35 | async-start | bytes 3538944 | tf_op jit(solution)/shard_map/reduce_scatter | solution.py:244
  288.1 269.5 %reduce-scatter.44.cloned.1.call-start = ((), (), s32[]{:S(2)}) async-start(), calls=%async_computation.26 | async-start | bytes 5308416 | tf_op jit(solution)/shard_map/reduce_scatter | solution.py:227
  292.3 315.1 %reduce-scatter.46.cloned.1.call-start = ((), (), s32[]{:S(2)}) async-start(), calls=%async_computation.27 | async-start | bytes 5308416 | tf_op jit(solution)/shard_map/reduce_scatter | solution.py:228
  292.9 6.8 copy-start.125
  292.9 327.7 %reduce-scatter.72.cloned.1.call-start = ((), (), s32[]{:S(2)}) async-start(), calls=%async_computation.40 | async-start | bytes 294912
  294.2 6.7 copy-start.109
  295.0 6.5 copy-start.93
  295.8 6.3 copy-start.137
  300.9 332.8 %reduce-scatter.80.cloned.1.call-start = ((), (), s32[]{:S(2)}) async-start(), calls=%async_computation.44 | async-start | bytes 294912
  301.4 345.4 %reduce-scatter.74.cloned.1.call-start = ((), (), s32[]{:S(2)}) async-start(), calls=%async_computation.41 | async-start | bytes 294912
  302.0 358.1 %reduce-scatter.82.cloned.1.call-start = ((), (), s32[]{:S(2)}) async-start(), calls=%async_computation.45 | async-start | bytes 294912
  302.8 372.7 %reduce-scatter.68.cloned.1.call-start = ((), (), s32[]{:S(2)}) async-start(), calls=%async_computation.38 | async-start | bytes 589824
  303.4 387.5 %reduce-scatter.70.cloned.1.call-start = ((), (), s32[]{:S(2)}) async-start(), calls=%async_computation.39 | async-start | bytes 589824
  304.1 406.6 %reduce-scatter.76.cloned.1.call-start = ((), (), s32[]{:S(2)}) async-start(), calls=%async_computation.42 | async-start | bytes 1179648
  304.9 426.1 %reduce-scatter.78.cloned.1.call-start = ((), (), s32[]{:S(2)}) async-start(), calls=%async_computation.43 | async-start | bytes 1179648
  305.6 449.3 %reduce-scatter.64.cloned.1.call-start = ((), (), s32[]{:S(2)}) async-start(), calls=%async_computation.36 | async-start | bytes 1769472
  307.1 471.8 %reduce-scatter.66.cloned.1.call-start = ((), (), s32[]{:S(2)}) async-start(), calls=%async_computation.37 | async-start | bytes 1769472
  308.7 695.6 %all-reduce.4.cloned.1.call-start = ((), (), s32[]{:S(2)}) async-start(), calls=%async_computation.46 | async-start | bytes 22806528 | tf_op jit(solution)/shard_map/psum | solution.py:248
  (127 other events, 291.4 us)
Sparse Core Ops, SparseCore 0:
  9.6 58.6 all-gather.6
  69.8 30.9 all-gather.8
  102.3 36.0 all-gather.10
  139.8 36.0 all-gather.12
  225.7 15.2 reduce-scatter.53
  243.8 15.2 reduce-scatter.51
  270.3 26.0 reduce-scatter.41
  298.7 28.2 reduce-scatter.47
  329.9 28.2 reduce-scatter.49
  360.9 34.6 reduce-scatter.55
  398.5 34.7 reduce-scatter.57
  435.4 34.6 reduce-scatter.59
  472.4 34.7 reduce-scatter.61
  509.9 47.6 reduce-scatter.43
  559.7 47.6 reduce-scatter.45
  609.5 10.9 reduce-scatter.71
  622.7 10.9 reduce-scatter.79
  635.9 10.9 reduce-scatter.73
  649.2 10.9 reduce-scatter.81
  662.3 13.1 reduce-scatter.67
  677.7 13.1 reduce-scatter.69
  693.2 17.4 reduce-scatter.75
  713.5 17.4 reduce-scatter.77
  733.2 21.7 reduce-scatter.63
  757.2 21.7 reduce-scatter.65
  784.7 219.4 all-reduce.3
where the time goes:
time: 1020 us
  waiting for transfers between devices  722 us (71%)
  blocking collectives  116 us (11%)
  matrix products  72.4 us (7%)
  local copies, waits for them, and re-layouts  56.8 us (6%)
  other arithmetic  37.2 us (4%)
  between operations  17.2 us (2%)
    unnamed x36, waiting for transfers between devices  167 us
    psum x1, waiting for transfers between devices, reduce_both(): lax.psum((shared[0], shared[1], shared[2], shared[3], shared[4], shared[5...  157 us
    psum x1, blocking collectives, reduce_both(): lax.psum((shared[0], shared[1], shared[2], shared[3], shared[4], shared[5...  64.3 us
    reduce_scatter x1, waiting for transfers between devices, reduce_both(): lax.psum_scatter(lower[0][None], 'shard', scatter_dimension=1, tiled=True)  50.5 us
    reduce_scatter x1, waiting for transfers between devices, reduce_both(): lax.psum_scatter(upper[0][None], 'shard', scatter_dimension=1, tiled=True)  49.8 us
    unnamed x373, local copies, waits for them, and re-layouts  47 us
    reduce_scatter x1, waiting for transfers between devices, reduce_both(): lax.psum_scatter(upper[6][None], 'shard', scatter_dimension=1, tiled=True)  37.6 us
    reduce_scatter x1, waiting for transfers between devices, reduce_both(): lax.psum_scatter(lower[6][None], 'shard', scatter_dimension=1, tiled=True)  37.5 us
  transfers between devices with their start and end apart: 26, of which 23 were waited for; matrix products, arithmetic and copies ran while one was open for 10% of the time, Pallas kernels for 0%

commit v1 on v0

v1 whole, which is shorter than its diff:
```python
import functools
import math

import jax
import jax.numpy as jnp
from jax import lax
from jax.experimental import pallas as pl
from jax.experimental.pallas import tpu as pltpu
from jax.sharding import PartitionSpec as P

D = 384
HEAD_DIM = 64
LAYERS = 2
F32 = jnp.float32
BF16 = jnp.bfloat16

norm_eps = 1e-06
gelu_coeff = math.sqrt(2.0 / math.pi)
gelu_cubic = 0.044715

VMEM = pl.BlockSpec(memory_space=pltpu.VMEM)
SMEM = pl.BlockSpec(memory_space=pltpu.SMEM)
HBM = pl.BlockSpec(memory_space=pl.ANY)
LIMIT = 48 * 1024 * 1024


def sds(shape, dtype):
    return jax.ShapeDtypeStruct(shape, dtype)


def norm_rows(values):
    centered = values - jnp.mean(values, axis=-1, keepdims=True)
    inv_dev = lax.rsqrt(jnp.mean(centered * centered, axis=-1, keepdims=True) + norm_eps)
    return (centered * inv_dev, inv_dev)


def norm_back(grad_normed, normed, inv_dev):
    return (
        grad_normed
        - jnp.mean(grad_normed, axis=-1, keepdims=True)
        - normed * jnp.mean(grad_normed * normed, axis=-1, keepdims=True)
    ) * inv_dev


def gelu_parts(pre_act):
    square = pre_act * pre_act
    inner_arg = gelu_coeff * pre_act * (1.0 + gelu_cubic * square)
    tanh_val = jnp.tanh(inner_arg)
    half_up = 0.5 * (1.0 + tanh_val)
    value_out = pre_act * half_up
    slope_out = half_up + 0.5 * pre_act * (1.0 - tanh_val * tanh_val) * (
        gelu_coeff + (3.0 * gelu_cubic * gelu_coeff) * square
    )
    return (value_out, slope_out)


def dot(a, b):
    return jnp.dot(a, b, preferred_element_type=F32)


def dot_nt(a, b):
    return lax.dot_general(a, b, (((1,), (1,)), ((), ())), preferred_element_type=F32)


def dot_tn(a, b):
    return lax.dot_general(a, b, (((0,), (0,)), ((), ())), preferred_element_type=F32)


def head_masks():
    lane = lax.broadcasted_iota(jnp.int32, (1, 2 * HEAD_DIM), 1)
    first = lane < HEAD_DIM
    return first, jnp.logical_not(first)


def keep_lanes(values, mask):
    return jnp.where(mask, values, jnp.zeros_like(values))


def rows_of(start, size):
    return pl.ds(pl.multiple_of(start, 16), size)


def attn_weight_copies(meta, layer, qkv_hbm, out_hbm, pieces, offsets, w_qkv, w_out, sems):
    half = qkv_hbm.shape[1]
    x = meta[0]
    copies = [
        (qkv_hbm.at[layer], w_qkv.at[rows_of(x * half, half), :]),
        (out_hbm.at[layer], w_out.at[rows_of(x * half, half), :]),
    ]
    for piece, offset in zip(pieces, offsets):
        size = piece.shape[0]
        start = (1 - x) * half + offset * size
        copies.append((piece.at[:, pl.ds(0, 3 * D)], w_qkv.at[rows_of(start, size), :]))
        copies.append((piece.at[:, pl.ds(3 * D, D)], w_out.at[rows_of(start, size), :]))
    return [pltpu.make_async_copy(s, d, sems.at[i]) for i, (s, d) in enumerate(copies)]


def mlp_weight_copies(meta, layer, up_hbm, down_hbm, pieces, offsets, w_up, w_down, sems):
    half = up_hbm.shape[1]
    tall = down_hbm.shape[1]
    blocks = tall // half
    x = meta[0]
    copies = [
        (up_hbm.at[layer], w_up.at[rows_of(x * half, half), :]),
        (down_hbm.at[layer], w_down.at[rows_of(x * tall, tall), :]),
    ]
    for piece, offset in zip(pieces, offsets):
        size = piece.shape[0] // 2
        start = (1 - x) * half + offset * size
        copies.append((piece.at[pl.ds(0, size), :], w_up.at[rows_of(start, size), :]))
        for b in range(blocks):
            start = (1 - x) * tall + offset * (blocks * size) + b * size
            copies.append(
                (
                    piece.at[pl.ds(size, size), pl.ds(b * D, D)],
                    w_down.at[rows_of(start, size), :],
                )
            )
    return [pltpu.make_async_copy(s, d, sems.at[i]) for i, (s, d) in enumerate(copies)]


def piece_offsets(meta, count, far):
    core, y, z = meta[1], meta[2], meta[3]
    if count == 2:
        return [core, 1 - core]
    near = z % 2 if far else y
    return [
        near * 2 + core,
        (1 - near) * 2 + core,
        near * 2 + (1 - core),
        (1 - near) * 2 + (1 - core),
    ]


def pack_attn_kernel(layer, far, parts, meta, qkv, out, send, sems):
    size = qkv.shape[1] // parts
    offset = piece_offsets(meta, parts, far)[0]
    rows = rows_of(offset * size, size)
    copies = [
        pltpu.make_async_copy(qkv.at[layer, rows, :], send.at[:, pl.ds(0, 3 * D)], sems.at[0]),
        pltpu.make_async_copy(out.at[layer, rows, :], send.at[:, pl.ds(3 * D, D)], sems.at[1]),
    ]
    for copy in copies:
        copy.start()
    for copy in copies:
        copy.wait()


def pack_attn(layer, far, parts, meta, qkv, out):
    size = qkv.shape[1] // parts
    return pl.pallas_call(
        functools.partial(pack_attn_kernel, layer, far, parts),
        out_shape=sds((size, 4 * D), BF16),
        in_specs=[SMEM, HBM, HBM],
        out_specs=HBM,
        scratch_shapes=[pltpu.SemaphoreType.DMA((2,))],
        name="pack_attn",
    )(meta, qkv, out)


def pack_mlp_kernel(layer, far, parts, meta, up, down, send, sems):
    size = up.shape[1] // parts
    blocks = down.shape[1] // up.shape[1]
    offset = piece_offsets(meta, parts, far)[0]
    copies = [
        pltpu.make_async_copy(
            up.at[layer, rows_of(offset * size, size), :], send.at[pl.ds(0, size), :], sems.at[0]
        )
    ]
    for b in range(blocks):
        rows = rows_of(offset * (blocks * size) + b * size, size)
        copies.append(
            pltpu.make_async_copy(
                down.at[layer, rows, :],
                send.at[pl.ds(size, size), pl.ds(b * D, D)],
                sems.at[1 + b],
            )
        )
    for copy in copies:
        copy.start()
    for copy in copies:
        copy.wait()


def pack_mlp(layer, far, parts, meta, up, down):
    size = up.shape[1] // parts
    return pl.pallas_call(
        functools.partial(pack_mlp_kernel, layer, far, parts),
        out_shape=sds((2 * size, 4 * D), BF16),
        in_specs=[SMEM, HBM, HBM],
        out_specs=HBM,
        scratch_shapes=[pltpu.SemaphoreType.DMA((8,))],
        name="pack_mlp",
    )(meta, up, down)


def attn_fwd_kernel(layer, far, count, *refs):
    meta, x_ref, vecs, qkv_hbm, out_hbm = refs[:5]
    pieces = refs[5 : 5 + count]
    modulated_out, qkv_out, prob_out, att_out, branch_out, middle_out = refs[5 + count : 11 + count]
    w_qkv, w_out, sems = refs[11 + count :]
    copies = attn_weight_copies(
        meta, layer, qkv_hbm, out_hbm, pieces, piece_offsets(meta, count, far), w_qkv, w_out, sems
    )
    for copy in copies:
        copy.start()
    stream = x_ref[...].astype(F32)
    normed, _ = norm_rows(stream)
    modulated = (normed * (1.0 + vecs[1:2, :]) + vecs[0:1, :]).astype(BF16)
    modulated_out[...] = modulated
    for copy in copies:
        copy.wait()
    for part in range(3):
        cols = slice(part * D, (part + 1) * D)
        value = dot(modulated, w_qkv[:, cols])
        if part == 0:
            value = value + vecs[6:7, :]
        if part == 2:
            value = value + vecs[7:8, :]
        qkv_out[:, cols] = value.astype(BF16)
    masks = head_masks()
    tokens = stream.shape[0]
    for pair in range(D // (2 * HEAD_DIM)):
        lanes = slice(pair * 2 * HEAD_DIM, (pair + 1) * 2 * HEAD_DIM)
        query = qkv_out[:, lanes]
        key = qkv_out[:, pair * 128 + D : (pair + 1) * 128 + D]
        value = qkv_out[:, pair * 128 + 2 * D : (pair + 1) * 128 + 2 * D]
        attended = None
        for member in range(2):
            head = 2 * pair + member
            scores = dot_nt(query, keep_lanes(key, masks[member])) * HEAD_DIM ** (-0.5)
            top = jnp.max(scores, axis=-1, keepdims=True)
            expo = jnp.exp(scores - top)
            prob = (expo * (1.0 / jnp.sum(expo, axis=-1, keepdims=True))).astype(BF16)
            prob_out[head * tokens : (head + 1) * tokens, :] = prob
            part = dot(prob, keep_lanes(value, masks[member]))
            attended = part if attended is None else attended + part
        att_out[:, lanes] = attended.astype(BF16)
    branch = dot(att_out[...], w_out[...]) + vecs[8:9, :]
    branch_out[...] = branch
    middle_out[...] = stream + vecs[2:3, :] * branch


def attn_fwd(layer, far, meta, x, vecs, qkv, out, pieces):
    tokens = x.shape[0]
    count = len(pieces)
    heads = D // HEAD_DIM
    return pl.pallas_call(
        functools.partial(attn_fwd_kernel, layer, far, count),
        out_shape=(
            sds((tokens, D), BF16),
            sds((tokens, 3 * D), BF16),
            sds((heads * tokens, tokens), BF16),
            sds((tokens, D), BF16),
            sds((tokens, D), F32),
            sds((tokens, D), F32),
        ),
        in_specs=[SMEM, VMEM, VMEM] + [HBM] * (2 + count),
        out_specs=(VMEM,) * 6,
        scratch_shapes=[
            pltpu.VMEM((D, 3 * D), BF16),
            pltpu.VMEM((D, D), BF16),
            pltpu.SemaphoreType.DMA((2 + 2 * count,)),
        ],
        compiler_params=pltpu.CompilerParams(vmem_limit_bytes=LIMIT),
        cost_estimate=pl.CostEstimate(flops=6 * 10**8, bytes_accessed=8 * 10**6, transcendentals=4 * 10**5),
        name="attn_fwd",
    )(meta, x, vecs, qkv, out, *pieces)


def mlp_fwd_kernel(layer, far, count, last, *refs):
    meta, middle_ref, vecs, up_hbm, down_hbm = refs[:5]
    pieces = refs[5 : 5 + count]
    x_out, mod_out, act_out, slope_out, branch_out = refs[5 + count : 10 + count]
    w_up, w_down, sems = refs[10 + count :]
    copies = mlp_weight_copies(
        meta, layer, up_hbm, down_hbm, pieces, piece_offsets(meta, count, far), w_up, w_down, sems
    )
    for copy in copies:
        copy.start()
    middle = middle_ref[...]
    normed, _ = norm_rows(middle)
    mod_two = (normed * (1.0 + vecs[4:5, :]) + vecs[3:4, :]).astype(BF16)
    mod_out[...] = mod_two
    for copy in copies:
        copy.wait()
    branch = None
    for part in range(4):
        cols = slice(part * D, (part + 1) * D)
        pre_act = dot(mod_two, w_up[:, cols]) + vecs[10 + part : 11 + part, :]
        value, slope = gelu_parts(pre_act)
        value = value.astype(BF16)
        act_out[:, cols] = value
        slope_out[:, cols] = slope.astype(BF16)
        term = dot(value, w_down[cols, :])
        branch = term if branch is None else branch + term
    branch = branch + vecs[9:10, :]
    branch_out[...] = branch
    result = middle + vecs[5:6, :] * branch
    if last:
        live = meta[4].astype(F32)
        result = result * live
    x_out[...] = result.astype(x_out.dtype)


def mlp_fwd(layer, far, last, meta, middle, vecs, up, down, pieces):
    tokens = middle.shape[0]
    count = len(pieces)
    return pl.pallas_call(
        functools.partial(mlp_fwd_kernel, layer, far, count, last),
        out_shape=(
            sds((tokens, D), BF16 if last else F32),
            sds((tokens, D), BF16),
            sds((tokens, 4 * D), BF16),
            sds((tokens, 4 * D), BF16),
            sds((tokens, D), F32),
        ),
        in_specs=[SMEM, VMEM, VMEM] + [HBM] * (2 + count),
        out_specs=(VMEM,) * 5,
        scratch_shapes=[
            pltpu.VMEM((D, 4 * D), BF16),
            pltpu.VMEM((4 * D, D), BF16),
            pltpu.SemaphoreType.DMA((2 + 5 * count,)),
        ],
        compiler_params=pltpu.CompilerParams(vmem_limit_bytes=LIMIT),
        cost_estimate=pl.CostEstimate(flops=6 * 10**8, bytes_accessed=8 * 10**6, transcendentals=4 * 10**5),
        name="mlp_fwd",
    )(meta, middle, vecs, up, down, *pieces)


def split_store(core, value, half, keep, send, rows):
    @pl.when(core == half)
    def _():
        keep[rows, :] = value

    @pl.when(core != half)
    def _():
        send[rows, :] = value


def mlp_bwd_kernel(layer, far, count, masked, extra, *refs):
    meta, grad_ref, vecs, middle_ref, branch_ref, act_ref, slope_ref, mod_ref = refs[:8]
    refs = refs[8:]
    if extra:
        ride, refs = refs[0], refs[1:]
    up_hbm, down_hbm = refs[:2]
    pieces = refs[2 : 2 + count]
    keep, send, grad_out, sums_out = refs[2 + count : 6 + count]
    w_up, w_down, pre_bf, sems = refs[6 + count :]
    copies = mlp_weight_copies(
        meta, layer, up_hbm, down_hbm, pieces, piece_offsets(meta, count, far), w_up, w_down, sems
    )
    for copy in copies:
        copy.start()
    core = meta[1]
    grad = grad_ref[...].astype(F32)
    if masked:
        grad = grad * meta[4].astype(F32)
    sums_out[...] = jnp.zeros_like(sums_out)
    sums_out[5:6, :] = jnp.sum(grad * branch_ref[...], axis=0, keepdims=True)
    grad_branch = grad * vecs[5:6, :]
    sums_out[9:10, :] = jnp.sum(grad_branch, axis=0, keepdims=True)
    branch_bf = grad_branch.astype(BF16)
    half = D // 2
    for part in range(4):
        value = dot_tn(act_ref[:, part * D : (part + 1) * D], branch_bf).astype(BF16)
        base = (part // 2) * 4 * half + 2 * half
        split_store(core, value, part % 2, keep, send, slice(base, base + D))
    for copy in copies:
        copy.wait()
    mod_two = mod_ref[...]
    grad_mod = None
    for part in range(4):
        cols = slice(part * D, (part + 1) * D)
        grad_pre = dot_nt(branch_bf, w_down[cols, :]) * slope_ref[:, cols].astype(F32)
        sums_out[10 + part : 11 + part, :] = jnp.sum(grad_pre, axis=0, keepdims=True)
        pre = grad_pre.astype(BF16)
        value = dot_tn(mod_two, pre).astype(BF16)
        for side in range(2):
            base = side * 4 * half + (part % 2) * half
            split_store(
                core,
                value[side * half : (side + 1) * half, :],
                part // 2,
                keep,
                send,
                slice(base, base + half),
            )
        term = dot_nt(pre, w_up[:, cols])
        grad_mod = term if grad_mod is None else grad_mod + term
    normed, inv_dev = norm_rows(middle_ref[...])
    sums_out[3:4, :] = jnp.sum(grad_mod, axis=0, keepdims=True)
    sums_out[4:5, :] = jnp.sum(grad_mod * normed, axis=0, keepdims=True)
    grad_out[...] = grad + norm_back(grad_mod * (1.0 + vecs[4:5, :]), normed, inv_dev)
    if extra:
        send[8 * half : 8 * half + 16, :] = ride[...]


def mlp_bwd(layer, far, masked, meta, grad, vecs, kept, up, down, pieces, ride=None):
    middle, mod_two, act, slope, branch = kept
    tokens = middle.shape[0]
    count = len(pieces)
    extra = 0 if ride is None else ride.shape[0]
    rides = () if ride is None else (ride,)
    return pl.pallas_call(
        functools.partial(mlp_bwd_kernel, layer, far, count, masked, extra),
        out_shape=(
            sds((4 * D, D), BF16),
            sds((4 * D + extra, D), BF16),
            sds((tokens, D), F32),
            sds((16, D), F32),
        ),
        in_specs=[SMEM] + [VMEM] * (7 + len(rides)) + [HBM] * (2 + count),
        out_specs=(VMEM,) * 4,
        scratch_shapes=[
            pltpu.VMEM((D, 4 * D), BF16),
            pltpu.VMEM((4 * D, D), BF16),
            pltpu.VMEM((16, D), BF16),
            pltpu.SemaphoreType.DMA((2 + 5 * count,)),
        ],
        compiler_params=pltpu.CompilerParams(vmem_limit_bytes=LIMIT),
        cost_estimate=pl.CostEstimate(flops=12 * 10**8, bytes_accessed=14 * 10**6, transcendentals=10**4),
        name="mlp_bwd",
    )(meta, grad, vecs, middle, branch, act, slope, mod_two, *rides, up, down, *pieces)


def attn_bwd_kernel(layer, far, count, extra, *refs):
    meta, grad_ref, vecs, x_ref, modulated_ref, qkv_ref, prob_ref, att_ref, branch_ref, part_sums = refs[:10]
    qkv_hbm, out_hbm = refs[10:12]
    pieces = refs[12 : 12 + count]
    keep, send, grad_out, sums_out = refs[12 + count : 16 + count]
    w_qkv, w_out, ga_ref, proj_ref, sems = refs[16 + count :]
    copies = attn_weight_copies(
        meta, layer, qkv_hbm, out_hbm, pieces, piece_offsets(meta, count, far), w_qkv, w_out, sems
    )
    for copy in copies:
        copy.start()
    core = meta[1]
    half = D // 2
    tokens = grad_ref.shape[0]
    sums = {}
    grad = grad_ref[...]
    sums[2] = jnp.sum(grad * branch_ref[...], axis=0, keepdims=True)
    grad_battn = grad * vecs[2:3, :]
    sums[8] = jnp.sum(grad_battn, axis=0, keepdims=True)
    battn_bf = grad_battn.astype(BF16)

    def store(value, block):
        for side in range(2):
            base = side * 2 * half + (block % 2) * half
            split_store(
                core,
                value[side * half : (side + 1) * half, :],
                block // 2,
                keep,
                send,
                slice(base, base + half),
            )

    store(dot_tn(att_ref[...], battn_bf).astype(BF16), 3)
    for copy in copies:
        copy.wait()
    ga_ref[...] = dot_nt(battn_bf, w_out[...]).astype(BF16)
    masks = head_masks()
    grad_q_sums, grad_v_sums = [], []
    for pair in range(D // (2 * HEAD_DIM)):
        lanes = slice(pair * 128, (pair + 1) * 128)
        query = qkv_ref[:, lanes]
        key = qkv_ref[:, pair * 128 + D : (pair + 1) * 128 + D]
        value = qkv_ref[:, pair * 128 + 2 * D : (pair + 1) * 128 + 2 * D]
        grad_att = ga_ref[:, lanes]
        grad_q = grad_k = grad_v = None
        for member in range(2):
            head = 2 * pair + member
            mask = masks[member]
            prob_bf = prob_ref[head * tokens : (head + 1) * tokens, :]
            prob = prob_bf.astype(F32)
            grad_prob = dot_nt(grad_att, keep_lanes(value, mask))
            term_v = dot_tn(prob_bf, keep_lanes(grad_att, mask))
            weighted = prob * grad_prob
            row_dot = jnp.sum(weighted, axis=-1, keepdims=True)
            grad_scores = ((weighted - prob * row_dot) * HEAD_DIM ** (-0.5)).astype(BF16)
            term_q = dot(grad_scores, keep_lanes(key, mask))
            term_k = dot_tn(grad_scores, keep_lanes(query, mask))
            grad_q = term_q if grad_q is None else grad_q + term_q
            grad_k = term_k if grad_k is None else grad_k + term_k
            grad_v = term_v if grad_v is None else grad_v + term_v
        grad_q_sums.append(jnp.sum(grad_q, axis=0, keepdims=True))
        grad_v_sums.append(jnp.sum(grad_v, axis=0, keepdims=True))
        proj_ref[:, lanes] = grad_q.astype(BF16)
        proj_ref[:, pair * 128 + D : (pair + 1) * 128 + D] = grad_k.astype(BF16)
        proj_ref[:, pair * 128 + 2 * D : (pair + 1) * 128 + 2 * D] = grad_v.astype(BF16)
    sums[6] = jnp.concatenate(grad_q_sums, axis=1)
    sums[7] = jnp.concatenate(grad_v_sums, axis=1)
    modulated = modulated_ref[...]
    for block in range(3):
        store(dot_tn(modulated, proj_ref[:, block * D : (block + 1) * D]).astype(BF16), block)
    grad_mod = dot_nt(proj_ref[...], w_qkv[...])
    normed, inv_dev = norm_rows(x_ref[...].astype(F32))
    sums[0] = jnp.sum(grad_mod, axis=0, keepdims=True)
    sums[1] = jnp.sum(grad_mod * normed, axis=0, keepdims=True)
    grad_out[...] = grad + norm_back(grad_mod * (1.0 + vecs[1:2, :]), normed, inv_dev)
    row = lax.broadcasted_iota(jnp.int32, (16, 1), 0)
    total = part_sums[...]
    for index, value in sums.items():
        total = jnp.where(row == index, value, total)
    total = total.astype(BF16)
    sums_out[...] = total
    if extra:
        send[4 * half : 4 * half + 16, :] = total


def attn_bwd(layer, far, extra, meta, grad, vecs, x, kept, part_sums, qkv, out, pieces):
    modulated, qkv_val, prob, att, branch = kept
    tokens = x.shape[0]
    count = len(pieces)
    return pl.pallas_call(
        functools.partial(attn_bwd_kernel, layer, far, count, extra),
        out_shape=(
            sds((2 * D, D), BF16),
            sds((2 * D + extra, D), BF16),
            sds((tokens, D), F32),
            sds((16, D), BF16),
        ),
        in_specs=[SMEM] + [VMEM] * 9 + [HBM] * (2 + count),
        out_specs=(VMEM,) * 4,
        scratch_shapes=[
            pltpu.VMEM((D, 3 * D), BF16),
            pltpu.VMEM((D, D), BF16),
            pltpu.VMEM((tokens, D), BF16),
            pltpu.VMEM((tokens, 3 * D), BF16),
            pltpu.SemaphoreType.DMA((2 + 2 * count,)),
        ],
        compiler_params=pltpu.CompilerParams(vmem_limit_bytes=LIMIT),
        cost_estimate=pl.CostEstimate(flops=14 * 10**8, bytes_accessed=14 * 10**6, transcendentals=10**4),
        name="attn_bwd",
    )(meta, grad, vecs, x, modulated, qkv_val, prob, att, branch, part_sums, qkv, out, *pieces)


def add_split_kernel(axis, extra, *refs):
    meta, keep, got = refs[:3]
    mine_out, send_out = refs[-2:]
    half = keep.shape[0] // 2
    place = meta[axis]
    mine, other = rows_of(place * half, half), rows_of((1 - place) * half, half)
    mine_out[0:half, :] = (keep[mine, :].astype(F32) + got[mine, :].astype(F32)).astype(BF16)
    send_out[0:half, :] = (keep[other, :].astype(F32) + got[other, :].astype(F32)).astype(BF16)
    if extra:
        rides = refs[3]
        send_out[half : half + extra, :] = rides[...]
        send_out[half + extra : half + 2 * extra, :] = got[2 * half : 2 * half + extra, :]


def add_split(axis, meta, keep, got, ride=None):
    half = keep.shape[0] // 2
    extra = 0 if ride is None else ride.shape[0]
    rides = () if ride is None else (ride,)
    return pl.pallas_call(
        functools.partial(add_split_kernel, axis, extra),
        out_shape=(sds((half, D), BF16), sds((half + 2 * extra, D), BF16)),
        in_specs=[SMEM] + [VMEM] * (2 + len(rides)),
        out_specs=(VMEM, VMEM),
        compiler_params=pltpu.CompilerParams(vmem_limit_bytes=LIMIT),
        cost_estimate=pl.CostEstimate(flops=10**6, bytes_accessed=2 * 10**6, transcendentals=0),
        name="add_split",
    )(meta, keep, got, *rides)


def add_spread_kernel(extra, *refs):
    meta, keep, got = refs[:3]
    mine_out = refs[-4]
    quarter = keep.shape[0] // 4
    z = meta[3]
    for step in range(4):
        rows = rows_of((z ^ step) * quarter, quarter)
        out = refs[step - 4]
        out[0:quarter, :] = (keep[rows, :].astype(F32) + got[rows, :].astype(F32)).astype(BF16)
        if extra:
            out[quarter : quarter + extra, :] = refs[3][...]
            out[quarter + extra : quarter + 2 * extra, :] = got[4 * quarter : 4 * quarter + extra, :]


def add_spread(meta, keep, got, ride=None):
    quarter = keep.shape[0] // 4
    extra = 0 if ride is None else ride.shape[0]
    rides = () if ride is None else (ride,)
    return pl.pallas_call(
        functools.partial(add_spread_kernel, extra),
        out_shape=(sds((quarter + 2 * extra, D), BF16),) * 4,
        in_specs=[SMEM] + [VMEM] * (2 + len(rides)),
        out_specs=(VMEM,) * 4,
        compiler_params=pltpu.CompilerParams(vmem_limit_bytes=LIMIT),
        cost_estimate=pl.CostEstimate(flops=10**6, bytes_accessed=2 * 10**6, transcendentals=0),
        name="add_spread",
    )(meta, keep, got, *rides)


def add_all_kernel(rows, extra, *refs):
    out = refs[4]
    total = refs[0][0:rows, :].astype(F32)
    for ref in refs[1:4]:
        total = total + ref[0:rows, :].astype(F32)
    out[...] = total.astype(BF16)
    if extra:
        for index in range(4):
            refs[5][index * extra : (index + 1) * extra, :] = refs[index][rows : rows + extra, :]


def add_all(parts, rows):
    extra = parts[0].shape[0] - rows
    shapes = (sds((rows, D), BF16),)
    if extra:
        shapes = shapes + (sds((4 * extra, D), BF16),)
    return pl.pallas_call(
        functools.partial(add_all_kernel, rows, extra),
        out_shape=shapes,
        in_specs=[VMEM] * 4,
        out_specs=(VMEM,) * len(shapes),
        compiler_params=pltpu.CompilerParams(vmem_limit_bytes=LIMIT),
        cost_estimate=pl.CostEstimate(flops=10**6, bytes_accessed=10**6, transcendentals=0),
        name="add_all",
    )(*parts)


def join_kernel(meta, *refs):
    out = refs[4]
    rows = refs[0].shape[0]
    z = meta[3]
    for step in range(4):
        out[rows_of((z ^ step) * rows, rows), :] = refs[step][...]


def join(meta, parts):
    return pl.pallas_call(
        join_kernel,
        out_shape=sds((4 * parts[0].shape[0], D), BF16),
        in_specs=[SMEM] + [VMEM] * 4,
        out_specs=VMEM,
        compiler_params=pltpu.CompilerParams(vmem_limit_bytes=LIMIT),
        cost_estimate=pl.CostEstimate(flops=10**6, bytes_accessed=10**6, transcendentals=0),
        name="join",
    )(meta, *parts)


def gather_rows(meta, refs, scratch):
    core, y = meta[1], meta[2]
    rows = refs[0].shape[0]
    for index, (c, v) in enumerate(((core, y), (core, 1 - y), (1 - core, y), (1 - core, 1 - y))):
        scratch[c, rows_of(v * rows, rows), :] = refs[index][...]


def attn_result_kernel(meta, *refs):
    qkv_out, out_out, scratch = refs[8:]
    half = D // 2
    for layer in range(LAYERS):
        gather_rows(meta, refs[4 * layer : 4 * layer + 4], scratch)
        for block in range(4):
            value = scratch[block // 2, (block % 2) * half : (block % 2 + 1) * half, :].astype(F32)
            if block < 3:
                qkv_out[layer, :, block * D : (block + 1) * D] = value
            else:
                out_out[layer, :, :] = value


def attn_result(meta, lower, upper):
    half = D // 2
    return pl.pallas_call(
        attn_result_kernel,
        out_shape=(sds((LAYERS, half, 3 * D), F32), sds((LAYERS, half, D), F32)),
        in_specs=[SMEM] + [VMEM] * 8,
        out_specs=(VMEM, VMEM),
        scratch_shapes=[pltpu.VMEM((2, 2 * half, D), BF16)],
        compiler_params=pltpu.CompilerParams(vmem_limit_bytes=LIMIT),
        cost_estimate=pl.CostEstimate(flops=10**6, bytes_accessed=4 * 10**6, transcendentals=0),
        name="attn_result",
    )(meta, *lower, *upper)


def mlp_result_kernel(meta, *refs):
    up_out, down_out, scratch = refs[8:]
    half = D // 2
    for layer in range(LAYERS):
        gather_rows(meta, refs[4 * layer : 4 * layer + 4], scratch)
        for block in range(4):
            value = scratch[block // 2, (block % 2) * half : (block % 2 + 1) * half, :].astype(F32)
            up_out[layer, :, block * D : (block + 1) * D] = value
        for core in range(2):
            down_out[layer, core * D : (core + 1) * D, :] = scratch[core, D : 2 * D, :].astype(F32)


def mlp_result(meta, lower, upper):
    half = D // 2
    return pl.pallas_call(
        mlp_result_kernel,
        out_shape=(sds((LAYERS, half, 4 * D), F32), sds((LAYERS, 2 * D, D), F32)),
        in_specs=[SMEM] + [VMEM] * 8,
        out_specs=(VMEM, VMEM),
        scratch_shapes=[pltpu.VMEM((2, 2 * D, D), BF16)],
        compiler_params=pltpu.CompilerParams(vmem_limit_bytes=LIMIT),
        cost_estimate=pl.CostEstimate(flops=10**6, bytes_accessed=8 * 10**6, transcendentals=0),
        name="mlp_result",
    )(meta, *lower, *upper)


def on_device(reps, *arguments):
    (
        latents,
        timestep_embed,
        labels,
        counts,
        class_table,
        ada_weight,
        ada_bias,
        qkv_weight,
        qv_bias,
        out_weight,
        out_bias,
        up_weight,
        up_bias,
        down_weight,
        down_bias,
        cotangent,
    ) = arguments
    half = D // 2
    rep = lax.axis_index("rep")
    x = lax.axis_index("shard")
    core, y, z = rep & 1, (rep >> 1) & 1, (rep >> 2) & 3
    meta = jnp.stack([x, core, y, z, jnp.minimum(counts[0], 1)]).astype(jnp.int32)

    def over_x(value):
        return lax.ppermute(value, "shard", [(0, 1), (1, 0)])

    def over_rep(value, distance):
        return lax.ppermute(value, "rep", [(r, r ^ distance) for r in range(reps)])

    CORE, Y, Z = 1, 2, 4

    bias_parts = (ada_bias, qv_bias, out_bias, up_bias, down_bias)
    own_bias = [member.astype(F32) for member in bias_parts]
    timestep_mine = lax.dynamic_slice(timestep_embed, (0, x * half), (1, half))
    timestep_other = lax.dynamic_slice(timestep_embed, (0, (1 - x) * half), (1, half))
    first = jnp.concatenate(
        [timestep_other[0], labels.astype(F32)] + [member.reshape(-1) for member in own_bias]
    )[None]
    got_first = over_x(first)[0]
    send_a0 = pack_attn(0, False, 2, meta, qkv_weight, out_weight)
    send_m0 = pack_mlp(0, False, 4, meta, up_weight, down_weight)
    send_a1 = pack_attn(1, False, 4, meta, qkv_weight, out_weight)
    send_m1 = pack_mlp(1, True, 4, meta, up_weight, down_weight)

    def fetch(send, distance):
        got = over_x(send)
        if distance is None:
            return [got, over_rep(got, CORE)]
        next_got = over_rep(got, distance)
        return [got, next_got, over_rep(got, CORE), over_rep(next_got, CORE)]

    pieces_a0 = fetch(send_a0, None)
    pieces_m0 = fetch(send_m0, Y)
    pieces_a1 = fetch(send_a1, Y)
    pieces_m1 = fetch(send_m1, Z)

    timestep_pair = jnp.concatenate([timestep_mine, got_first[None, :half]], axis=0)
    label_pair = jnp.stack([labels[0], got_first[half].astype(jnp.int32)])
    classes = class_table.shape[0]
    one_hot_pair = (label_pair[:, None] == jnp.arange(classes)[None, :]).astype(BF16)
    condition_pair = timestep_pair + dot(one_hot_pair, class_table)
    act_pair = (condition_pair * jax.nn.sigmoid(condition_pair)).astype(BF16)
    partial = jnp.einsum("nk,lkm->nlm", act_pair, ada_weight, preferred_element_type=F32)
    modul = partial[0] + over_x(partial[1])

    offset = half + 1
    full_bias = []
    for member in own_bias:
        size = member.size
        other = got_first[offset : offset + size].reshape(member.shape)
        offset += size
        full_bias.append(
            jnp.where(
                x == 0,
                jnp.concatenate([member, other], axis=1),
                jnp.concatenate([other, member], axis=1),
            )
        )
    vecs_all = jnp.concatenate(
        [
            (modul + full_bias[0]).reshape(LAYERS, 6, D),
            full_bias[1].reshape(LAYERS, 2, D),
            full_bias[2].reshape(LAYERS, 1, D),
            full_bias[4].reshape(LAYERS, 1, D),
            full_bias[3].reshape(LAYERS, 4, D),
            jnp.zeros((LAYERS, 2, D), F32),
        ],
        axis=1,
    )
    vecs = [vecs_all[layer] for layer in range(LAYERS)]

    def spread(value, axis_steps):
        parts = [value[None]]
        for step in axis_steps:
            parts.append(over_rep(value, step)[None])
        return jnp.concatenate(parts, axis=0)

    info = jnp.concatenate(
        [condition_pair, label_pair.astype(F32)[:, None], jnp.zeros((2, 63), F32)], axis=1
    )
    info = spread(info, [CORE])
    info = spread(info, [Y])
    info = spread(info, [Z, 2 * Z, 3 * Z])
    outer = reps // 16
    if outer > 1:
        info = spread(info, [16 * step for step in range(1, outer)])
    info = info.reshape(2 * reps, half + 64)

    stream = latents[0]
    attn_weights = (qkv_weight, out_weight)
    mlp_weights = (up_weight, down_weight)
    *kept_a0, middle0 = attn_fwd(0, False, meta, stream, vecs[0], *attn_weights, pieces_a0)
    stream1, *kept_m0 = mlp_fwd(0, False, False, meta, middle0, vecs[0], *mlp_weights, pieces_m0)
    *kept_a1, middle1 = attn_fwd(1, False, meta, stream1, vecs[1], *attn_weights, pieces_a1)
    activations, *kept_m1 = mlp_fwd(1, True, True, meta, middle1, vecs[1], *mlp_weights, pieces_m1)

    def reduce_chunk(keep, sent, ride=None):
        got = over_rep(sent, CORE)
        mine, send = add_split(0, meta, keep, got, ride)
        if ride is not None:
            ride = send[mine.shape[0] :]
        got = over_x(send)
        mine, send = add_split(2, meta, mine, got, ride)
        if ride is not None:
            ride = send[mine.shape[0] :]
        got = over_rep(send, Y)
        mine, *sends = add_spread(meta, mine, got, ride)
        rows = keep.shape[0] // 16
        parts = [mine] + [over_rep(send, Z * (1 + step)) for step, send in enumerate(sends)]
        mine, *rides = add_all(parts, rows)
        if outer > 1:
            total = mine.astype(F32)
            for step in range(1, outer):
                total = total + over_rep(mine, 16 * step).astype(F32)
            mine = total.astype(BF16)
        parts = [mine] + [over_rep(mine, Z * step) for step in range(1, 4)]
        mine = join(meta, parts)
        next_mine = over_rep(mine, Y)
        result = (mine, next_mine, over_rep(mine, CORE), over_rep(next_mine, CORE))
        if not rides:
            return result, None
        rides = rides[0]
        if outer > 1:
            rides = spread(rides, [16 * step for step in range(1, outer)])
        return result, rides

    keep, sent, grad, part_sums = mlp_bwd(
        1, True, True, meta, cotangent[0], vecs[1], (middle1, *kept_m1), *mlp_weights, pieces_m1
    )
    result_m1, _ = reduce_chunk(keep, sent)
    keep, sent, grad, sums1 = attn_bwd(
        1, False, 0, meta, grad, vecs[1], stream1, kept_a1, part_sums, *attn_weights, pieces_a1
    )
    result_a1, _ = reduce_chunk(keep, sent)
    keep, sent, grad, part_sums = mlp_bwd(
        0, False, False, meta, grad, vecs[0], (middle0, *kept_m0), *mlp_weights, pieces_m0, sums1
    )
    result_m0, rides1 = reduce_chunk(keep, sent, sums1)
    keep, sent, grad_stream, sums0 = attn_bwd(
        0, False, 16, meta, grad, vecs[0], stream, kept_a0, part_sums, *attn_weights, pieces_a0
    )
    result_a0, rides0 = reduce_chunk(keep, sent, sums0)

    up_grad, down_grad = mlp_result(meta, result_m0, result_m1)
    qkv_grad, out_grad = attn_result(meta, result_a0, result_a1)

    condition = info[:, :half]
    label_all = info[:, half].astype(jnp.int32)
    sigmoid = jax.nn.sigmoid(condition)
    act_all = (condition * sigmoid).astype(BF16)
    grad_cond = jnp.zeros_like(condition)
    ada_grads, sum_rows = [], []
    for layer, rides in enumerate((rides0, rides1)):
        rides = rides.reshape(outer * 8, 2, 2, 16, D).swapaxes(1, 2).reshape(2 * reps, 16, D)
        vectors = rides[:, :6].reshape(2 * reps, 6 * D)
        ada_grads.append(dot_tn(act_all, vectors))
        grad_cond = grad_cond + dot_nt(vectors, ada_weight[layer])
        sum_rows.append(jnp.sum(rides.astype(F32), axis=0))
    ada_grad = jnp.stack(ada_grads)
    cond_grads = grad_cond * sigmoid * (1.0 + condition * (1.0 - sigmoid))
    one_hot = (label_all[:, None] == jnp.arange(classes)[None, :]).astype(F32)
    table_grad = lax.dot_general(
        one_hot, cond_grads, (((0,), (0,)), ((), ())), precision=lax.Precision.HIGHEST
    )
    other_cond = over_x(cond_grads[1:2])
    cond_grad = jnp.where(
        x == 0,
        jnp.concatenate([cond_grads[0:1], other_cond], axis=1),
        jnp.concatenate([other_cond, cond_grads[0:1]], axis=1),
    )
    sums_all = jnp.stack(sum_rows)

    def bias_grad(low, high):
        whole = sums_all[:, low:high].reshape(LAYERS, (high - low) * D)
        return lax.dynamic_slice(whole, (0, x * (whole.shape[1] // 2)), (LAYERS, whole.shape[1] // 2))

    return (
        activations[None],
        grad_stream[None],
        cond_grad,
        table_grad,
        ada_grad,
        bias_grad(0, 6),
        qkv_grad,
        bias_grad(6, 8),
        out_grad,
        bias_grad(8, 9),
        up_grad,
        bias_grad(10, 14),
        down_grad,
        bias_grad(9, 10),
    )


def solution(mesh):
    reps = mesh.shape["rep"]
    both = ("rep", "shard")
    in_specs = (
        P(both, None, None),
        P(both, None),
        P(both),
        P(both),
        P(None, "shard"),
    ) + (P(None, "shard", None), P(None, "shard")) * 5 + (P(both, None, None),)
    out_specs = (
        P(both, None, None),
        P(both, None, None),
        P(both, None),
        P(None, "shard"),
    ) + (P(None, "shard", None), P(None, "shard")) * 5
    return jax.shard_map(
        functools.partial(on_device, reps),
        mesh=mesh,
        in_specs=in_specs,
        out_specs=out_specs,
        check_vma=False,
    )
```

time: 1020 us -> 264 us (0.26)
  waiting for transfers between devices: 722 us -> 46.9 us
  blocking collectives: 116 us -> 0 us
  Pallas kernels: 0 us -> 98.4 us
  starting transfers between devices: 1.28 us -> 72.5 us
  matrix products: 72.4 us -> 4.99 us
  local copies, waits for them, and re-layouts: 56.8 us -> 26.4 us
  other arithmetic: 37.2 us -> 9.8 us
  between operations: 17.2 us -> 3.55 us
    reduce_scatter x11 -> x0, waiting for transfers between devices: 299 us -> none  [the longest x1 50.5 us: reduce_both(): lax.psum_scatter(lower[0][None], 'shard', scatter_dimension=1, tiled=True)]
    unnamed x36 -> x0, waiting for transfers between devices: 167 us -> none
    psum x1 -> x0, waiting for transfers between devices: 157 us -> none  [reduce_both(): lax.psum((shared[0], shared[1], shared[2], shared[3], shared[4], shared[5...]
    all_gather x4 -> x0, waiting for transfers between devices: 99.1 us -> none  [the longest x1 34.5 us: on_device(): lax.all_gather(down_weight, 'shard', axis=1, tiled=True)]
    pallas_call x0 -> x34, Pallas kernels: none -> 98.4 us  [the longest x2 21.6 us: pack_mlp(): pl.pallas_call(functools.partial(pack_mlp_kernel, layer, far, parts), out...]
    ppermute x0 -> x70, starting transfers between devices: none -> 72.5 us  [the longest x59 59.2 us: over_rep(): return lax.ppermute(value, 'rep', [(r, r ^ distance) for r in range(reps)])]
    dot_general x41 -> x7, matrix products: 72.4 us -> 4.99 us  [the longest x1 1.81 us: on_device(): jnp.einsum('nk,lkm->nlm', act_pair, ada_weight, preferred_element_type=F32)]
    psum x1 -> x0, blocking collectives: 64.3 us -> none  [reduce_both(): lax.psum((shared[0], shared[1], shared[2], shared[3], shared[4], shared[5...]
  transfers between devices with their start and end apart: 26 -> 70, of which waited for: 23 -> 15; matrix products, arithmetic and copies ran while one was open for 10% -> 13% of each run, Pallas kernels for 0% -> 32%
where the time goes in v1:
time: 264 us; the launch traced here: 262 us
  Pallas kernels  98.4 us (37%)
  starting transfers between devices  72.5 us (27%)
  waiting for transfers between devices  46.9 us (18%)
  local copies, waits for them, and re-layouts  26.4 us (10%)
  other arithmetic  9.8 us (4%)
  matrix products  4.99 us (2%)
  between operations  3.55 us (1%)
    ppermute x59, starting transfers between devices, over_rep(): return lax.ppermute(value, 'rep', [(r, r ^ distance) for r in range(reps)])  59.2 us
    ppermute x59, waiting for transfers between devices, over_rep(): return lax.ppermute(value, 'rep', [(r, r ^ distance) for r in range(reps)])  38 us
    pallas_call x2, Pallas kernels, pack_mlp(): pl.pallas_call(functools.partial(pack_mlp_kernel, layer, far, parts), out...  21.6 us
    pallas_call x2, Pallas kernels, pack_attn(): pl.pallas_call(functools.partial(pack_attn_kernel, layer, far, parts), ou...  17 us
    pallas_call x2, Pallas kernels, mlp_bwd(): pl.pallas_call(functools.partial(mlp_bwd_kernel, layer, far, count, maske...  13.4 us
    ppermute x11, starting transfers between devices, over_x(): return lax.ppermute(value, 'shard', [(0, 1), (1, 0)])  13.3 us
    pallas_call x2, Pallas kernels, attn_bwd(): pl.pallas_call(functools.partial(attn_bwd_kernel, layer, far, count, extr...  11.6 us
    pallas_call x2, Pallas kernels, mlp_fwd(): pl.pallas_call(functools.partial(mlp_fwd_kernel, layer, far, count, last)...  9.05 us
  transfers between devices with their start and end apart: 70, of which 15 were waited for; matrix products, arithmetic and copies ran while one was open for 13% of the time, Pallas kernels for 32%

profile of v1, /device:TPU:0, one launch (start us, length us, event | category | flops | bytes accessed | tf_op | source)
XLA Modules:
  0.0 262.5 jit_solution(4794174722750006117)
XLA Ops:
  5.9 3.0 %collective-permute-start = (f32[1,5569]{1,0:T(1,128)S(1)}, f32[1,5569]{1,0:T(1,128)S(1)}, u32[]{:S(2)}, u32[]{:S(2)}) collective-permute-start(f32[1,5569]{1,0:T(1,128)S(1)} %broadcast_in_dim.45), channel_id=1, source_target_pairs={{0,1},{1,0},{2,3},{3,2},{4,5},{5,4},{6,7},{7,6},{8,9},{9,8},{10,11... | collective-permute-start | bytes 66836 | tf_op jit(solution)/shard_map/ppermute | solution.py:731
  10.2 10.7 %pack_attn.2 = bf16[96,1536]{1,0:T(8,128)(2,1)} custom-call(s32[5]{0:T(128)} %stack.48.meta.refs_0_, bf16[2,192,1152]{2,1,0:T(8,128)(2,1)} %refs_10_.5, bf16[2,192,384]{2,1,0:T(8,128)(2,1)} %refs_11_.3), custom_call_target="tpu_custom_call" | custom-call | tf_op jit(solution)/shard_map/pack_attn/pallas_call | solution.py:151
  21.0 10.8 %pack_mlp.2 = bf16[96,1536]{1,0:T(8,128)(2,1)} custom-call(s32[5]{0:T(128)} %stack.48.meta.refs_0_, bf16[2,192,1536]{2,1,0:T(8,128)(2,1)} %refs_9_.3, bf16[2,768,384]{2,1,0:T(8,128)(2,1)} %refs_10_.4), custom_call_target="tpu_custom_call" | custom-call | tf_op jit(solution)/shard_map/pack_mlp/pallas_call | solution.py:187
  31.9 2.1 collective-permute-start.4
  34.0 6.3 %pack_attn.3 = bf16[48,1536]{1,0:T(8,128)(2,1)} custom-call(s32[5]{0:T(128)} %stack.48.meta.refs_0_, bf16[2,192,1152]{2,1,0:T(8,128)(2,1)} %refs_10_.5, bf16[2,192,384]{2,1,0:T(8,128)(2,1)} %refs_11_.3), custom_call_target="tpu_custom_call" | custom-call | tf_op jit(solution)/shard_map/pack_attn/pallas_call | solution.py:151
  40.3 10.8 %pack_mlp.3 = bf16[96,1536]{1,0:T(8,128)(2,1)} custom-call(s32[5]{0:T(128)} %stack.48.meta.refs_0_, bf16[2,192,1536]{2,1,0:T(8,128)(2,1)} %refs_9_.3, bf16[2,768,384]{2,1,0:T(8,128)(2,1)} %refs_10_.4), custom_call_target="tpu_custom_call" | custom-call | tf_op jit(solution)/shard_map/pack_mlp/pallas_call | solution.py:187
  51.1 2.1 collective-permute-start.12
  57.7 1.8 fusion.25
  63.1 2.0 collective-permute-start.5
  65.1 1.4 maximum_select_fusion.2
  66.5 1.4 broadcast_select_fusion.1
  67.9 1.3 concatenate.141
  69.2 1.4 broadcast_select_fusion
  70.6 1.3 reshape.325
  72.5 2.0 collective-permute-start.13
  74.6 1.4 fusion.11
  76.0 1.3 reshape.326
  78.0 2.7 %concatenate.148 = f32[2,16,384]{2,1,0:T(8,128)} concatenate(f32[2,6,384]{2,1,0:T(8,128)} %reshape.326, f32[2,2,384]{2,1,0:T(2,128)} %maximum_select_fusion.2, f32[2,1,384]{2,1,0:T(1,128)} %broadcast_select_fusion.1, f32[2,1,384]{2,1,0:T(1,128)} %broadcast_select_fusion, f32[2,4,384]{2,1,0:T(4,128)S(1)} %maximum_select_fusion.1, f32[2,2,384]{2,1,0:T(2,128)} %broadcast_in_dim.46), dimensions={1} | concatenate | bytes 98304 | tf_op jit(solution)/shard_map/concatenate | solution.py:785
  83.7 4.2 %attn_fwd.2 = (bf16[256,384]{1,0:T(8,128)(2,1)S(1)}, bf16[256,1152]{1,0:T(8,128)(2,1)S(1)}, bf16[1536,256]{1,0:T(8,128)(2,1)S(1)}, bf16[256,384]{1,0:T(8,128)(2,...) custom-call(s32[5]{0:T(128)S(1)} %copy-done.7, bf16[256,384]{1,0:T(8,128)(2,1)S(1)} %bitcast.93, ...), custom_call_target="tpu_custom_call" | custom-call | flops 600000000 | bytes 8000000 | tf_op jit(solution)/shard_map/attn_fwd/pallas_call | solution.py:248
  88.7 4.3 %mlp_fwd.2 = (f32[256,384]{1,0:T(8,128)S(1)}, bf16[256,384]{1,0:T(8,128)(2,1)S(1)}, bf16[256,1536]{1,0:T(8,128)(2,1)S(1)}, bf16[256,1536]{1,0:T(8,128)(2,1)S(1)}, f32[256,384]{1,0:T(8,128)S(1)}) custom-call(s32[5]{0:T(128)S(1)} %copy-done.7, f32[256,384]{1,0:T(8,128)S(1)} %get-tuple-element.92.refs_1_.refs_3_, f32[16,384]{1,0:T(8,128)S(1)} %get-tuple-element.173.refs_2_, ...), custom_call_target="tpu_custom_call" | custom-call | flops 600000000 | bytes 8000000 | tf_op jit(solution)/shard_map/mlp_fwd/pallas_call | solution.py:309
  93.1 4.0 %attn_fwd.3 = (bf16[256,384]{1,0:T(8,128)(2,1)S(1)}, bf16[256,1152]{1,0:T(8,128)(2,1)S(1)}, bf16[1536,256]{1,0:T(8,128)(2,1)S(1)}, bf16[256,384]{1,0:T(8,128)(2,...) custom-call(s32[5]{0:T(128)S(1)} %copy-done.7, f32[256,384]{1,0:T(8,128)S(1)} %get-tuple-element.93.refs_1_.refs_3_, ...), custom_call_target="tpu_custom_call" | custom-call | flops 600000000 | bytes 8000000 | tf_op jit(solution)/shard_map/attn_fwd/pallas_call | solution.py:248
  98.0 4.7 %mlp_fwd.3 = (bf16[256,384]{1,0:T(8,128)(2,1)}, bf16[256,384]{1,0:T(8,128)(2,1)S(1)}, bf16[256,1536]{1,0:T(8,128)(2,1)S(1)}, bf16[256,1536]{1,0:T(8,128)(2,1)S(1)}, f32[256,384]{1,0:T(8,128)S(1)}) custom-call(s32[5]{0:T(128)S(1)} %copy-done.7, f32[256,384]{1,0:T(8,128)S(1)} %get-tuple-element.94.refs_1_.refs_3_, f32[16,384]{1,0:T(8,128)S(1)} %get-tuple-element.172.refs_2_, ...), custom_call_target="tpu_custom_call" | custom-call | flops 600000000 | bytes 8000000 | tf_op jit(solution)/shard_map/mlp_fwd/pallas_call | solution.py:309
  102.7 6.7 %mlp_bwd.2 = (bf16[1536,384]{1,0:T(8,128)(2,1)S(1)}, bf16[1536,384]{1,0:T(8,128)(2,1)}, f32[256,384]{1,0:T(8,128)S(1)}, f32[16,384]{1,0:T(8,128)S(1)}) custom-call(s32[5]{0:T(128)S(1)} %copy-done.7, bf16[256,384]{1,0:T(8,128)(2,1)S(1)} %bitcast.92, f32[16,384]{1,0:T(8,128)S(1)} %get-tuple-element.172.refs_2_, ...), custom_call_target="tpu_custom_call" | custom-call | flops 1200000000 | bytes 14000000 | tf_op jit(solution)/shard_map/mlp_bwd/pallas_call | solution.py:405
  110.0 5.1 %attn_bwd.2 = (bf16[768,384]{1,0:T(8,128)(2,1)S(1)}, bf16[768,384]{1,0:T(8,128)(2,1)S(1)}, f32[256,384]{1,0:T(8,128)S(1)}, bf16[16,384]{1,0:T(8,128)(2,1)S(1)}) custom-call(s32[5]{0:T(128)S(1)} %copy-done.7, f32[256,384]{1,0:T(8,128)S(1)} %get-tuple-element.100.refs_1_, f32[16,384]{1,0:T(8,128)S(1)} %get-tuple-element.172.refs_2_, ...), custom_call_target="tpu_custom_call" | custom-call | flops 1400000000 | bytes 14000000 | tf_op jit(solution)/shard_map/attn_bwd/pallas_call | solution.py:517
  115.2 6.6 %mlp_bwd.3 = (bf16[1536,384]{1,0:T(8,128)(2,1)S(1)}, bf16[1552,384]{1,0:T(8,128)(2,1)}, f32[256,384]{1,0:T(8,128)S(1)}, f32[16,384]{1,0:T(8,128)S(1)}) custom-call(s32[5]{0:T(128)S(1)} %copy-done.7, f32[256,384]{1,0:T(8,128)S(1)} %get-tuple-element.107.refs_1_, f32[16,384]{1,0:T(8,128)S(1)} %get-tuple-element.173.refs_2_, ...), custom_call_target="tpu_custom_call" | custom-call | flops 1200000000 | bytes 14000000 | tf_op jit(solution)/shard_map/mlp_bwd/pallas_call | solution.py:405
  122.1 6.5 %attn_bwd.3 = (bf16[768,384]{1,0:T(8,128)(2,1)S(1)}, bf16[784,384]{1,0:T(8,128)(2,1)S(1)}, f32[256,384]{1,0:T(8,128)}, bf16[16,384]{1,0:T(8,128)(2,1)S(1)}) custom-call(s32[5]{0:T(128)S(1)} %copy-done.7, f32[256,384]{1,0:T(8,128)S(1)} %get-tuple-element.113.refs_1_, f32[16,384]{1,0:T(8,128)S(1)} %get-tuple-element.173.refs_2_, ...), custom_call_target="tpu_custom_call" | custom-call | flops 1400000000 | bytes 14000000 | tf_op jit(solution)/shard_map/attn_bwd/pallas_call | solution.py:517
  129.2 2.3 collective-permute-done.40.refs_2_
  132.3 1.7 collective-permute-start.41
  136.0 1.7 collective-permute-start.59
  137.8 4.4 %collective-permute-done.41.refs_2_ = bf16[384,384]{1,0:T(8,128)(2,1)S(1)} collective-permute-done((bf16[384,384]{1,0:T(8,128)(2,1)S(1)}, bf16[384,384]{1,0:T(8,128)(2,1)S(1)}, u32[]{:S(2)}, u32[]{:S(2)}) %collective-permute-start.41) | collective-permute-done | bytes 294944 | tf_op jit(solution)/shard_map/ppermute | solution.py:731
  142.8 1.7 collective-permute-start.42
  144.5 4.5 %collective-permute-done.17.refs_2_ = bf16[416,384]{1,0:T(8,128)(2,1)S(1)} collective-permute-done((bf16[416,384]{1,0:T(8,128)(2,1)S(1)}, bf16[416,384]{1,0:T(8,128)(2,1)S(1)}, u32[]{:S(2)}, u32[]{:S(2)}) %collective-permute-start.17) | collective-permute-done | bytes 319520 | tf_op jit(solution)/shard_map/ppermute | solution.py:731
  149.6 1.7 collective-permute-start.18
  152.1 1.6 collective-permute-start.43
  153.7 2.6 collective-permute-start.44
  156.3 1.5 add_split.10
  157.8 1.5 collective-permute-start.23
  160.5 2.5 collective-permute-done.29
  163.8 3.6 %collective-permute-start.21 = (bf16[176,384]{1,0:T(8,128)(2,1)S(1)}, bf16[176,384]{1,0:T(8,128)(2,1)S(1)}, u32[]{:S(2)}, u32[]{:S(2)}) collective-permute-start(bf16[176,384]{1,0:T(8,128)(2,1)S(1)} %get-tuple-element.131), channel_id=1, source_target_pairs={{0,24},{2,26},{4,28},{6,30},{8,16},{10,18},{12,20},{14,22},{16,8},... | collective-permute-start | bytes 405512 | tf_op jit(solution)/shard_map/ppermute | solution.py:734
  167.6 1.3 add_split.15
  169.0 4.2 %collective-permute-done.45.refs_3_ = bf16[48,384]{1,0:T(8,128)(2,1)S(1)} collective-permute-done((bf16[48,384]{1,0:T(8,128)(2,1)S(1)}, bf16[48,384]{1,0:T(8,128)(2,1)S(1)}, u32[]{:S(2)}, u32[]{:S(2)}) %collective-permute-start.45) | collective-permute-done | bytes 36896 | tf_op jit(solution)/shard_map/ppermute | solution.py:734
  173.7 4.4 %collective-permute-start.46 = (bf16[48,384]{1,0:T(8,128)(2,1)S(1)}, bf16[48,384]{1,0:T(8,128)(2,1)S(1)}, u32[]{:S(2)}, u32[]{:S(2)}) collective-permute-start(bf16[48,384]{1,0:T(8,128)(2,1)S(1)} %add_all.6.refs_0_), channel_id=1, source_target_pairs={{0,8},{2,10},{4,12},{6,14},{8,0},{10,2},{12,4},{14,6},{16,24},{18,... | collective-permute-start | bytes 110600 | tf_op jit(solution)/shard_map/ppermute | solution.py:734
  178.1 2.4 collective-permute-start.48
  180.6 1.7 collective-permute-start.34
  183.9 2.5 collective-permute-start.36
  186.4 1.4 collective-permute-start.32
  189.7 1.2 collective-permute-start.30
  192.1 1.6 collective-permute-start.49
  195.7 2.1 collective-permute-start.62
  201.3 3.0 %collective-permute-start.63 = (bf16[96,384]{1,0:T(8,128)(2,1)S(1)}, bf16[96,384]{1,0:T(8,128)(2,1)S(1)}, u32[]{:S(2)}, u32[]{:S(2)}) collective-permute-start(bf16[96,384]{1,0:T(8,128)(2,1)S(1)} %get-tuple-element.167), channel_id=1, source_target_pairs={{0,24},{2,26},{4,28},{6,30},{8,16},{10,18},{12,20},{14,22},{16,8},... | collective-permute-start | bytes 221192 | tf_op jit(solution)/shard_map/ppermute | solution.py:734
  204.7 2.8 %collective-permute-done.63.refs_3_ = bf16[96,384]{1,0:T(8,128)(2,1)S(1)} collective-permute-done((bf16[96,384]{1,0:T(8,128)(2,1)S(1)}, bf16[96,384]{1,0:T(8,128)(2,1)S(1)}, u32[]{:S(2)}, u32[]{:S(2)}) %collective-permute-start.63) | collective-permute-done | bytes 73760 | tf_op jit(solution)/shard_map/ppermute | solution.py:734
  207.6 3.1 %collective-permute-done.24.refs_2_ = bf16[448,384]{1,0:T(8,128)(2,1)S(1)} collective-permute-done((bf16[448,384]{1,0:T(8,128)(2,1)S(1)}, bf16[448,384]{1,0:T(8,128)(2,1)S(1)}, u32[]{:S(2)}, u32[]{:S(2)}) %collective-permute-start.24) | collective-permute-done | bytes 344096 | tf_op jit(solution)/shard_map/ppermute | solution.py:734
  214.3 2.6 collective-permute-start.27
  217.8 2.1 collective-permute-start.66
  219.8 2.6 attn_result.1
  222.4 14.0 %collective-permute-done.65.refs_2_ = bf16[96,384]{1,0:T(8,128)(2,1)S(1)} collective-permute-done((bf16[96,384]{1,0:T(8,128)(2,1)S(1)}, bf16[96,384]{1,0:T(8,128)(2,1)S(1)}, u32[]{:S(2)}, u32[]{:S(2)}) %collective-permute-start.65) | collective-permute-done | bytes 73760 | tf_op jit(solution)/shard_map/ppermute | solution.py:734
  238.2 1.4 collective-permute-start.52
  239.6 1.3 collective-permute-start.53
  240.9 1.8 collective-permute-start.54
  243.6 2.2 pad_maximum_fusion
  247.0 1.7 collective-permute-done.53.refs_2_
  250.8 1.4 fusion.7
  252.8 4.0 %collective-permute-done.55.refs_1_ = bf16[384,384]{1,0:T(8,128)(2,1)S(1)} collective-permute-done((bf16[384,384]{1,0:T(8,128)(2,1)S(1)}, bf16[384,384]{1,0:T(8,128)(2,1)S(1)}, u32[]{:S(2)}, u32[]{:S(2)}) %collective-permute-start.55) | collective-permute-done | bytes 294944 | tf_op jit(solution)/shard_map/ppermute | solution.py:734
  259.3 3.2 %mlp_result.1 = (f32[2,192,1536]{2,1,0:T(8,128)}, f32[2,768,384]{2,1,0:T(8,128)}) custom-call(s32[5]{0:T(128)S(1)} %copy-done.7, bf16[384,384]{1,0:T(8,128)(2,1)S(1)} %join.6.refs_0_, bf16[384,384]{1,0:T(8,128)(2,1)S(1)} %collective-permute-done.55.refs_1_, bf16[384,384]{1,0:T(8,128)(2,1)S(1)} %collective-permute-done.56.refs_2_, ...), custom_call_target="tpu_custom_call" | custom-call | flops 1000000 | bytes 8000000 | tf_op jit(solution)/shard_map/mlp_result/pallas_call | solution.py:693
  (252 shorter events, 51.4 us)
Async XLA Ops:
  5.9 49.7 %collective-permute-start = (f32[1,5569]{1,0:T(1,128)S(1)}, f32[1,5569]{1,0:T(1,128)S(1)}, u32[]{:S(2)}, u32[]{:S(2)}) collective-permute-start(f32[1,5569]{1,0:T(1,128)S(1)} %broadcast_in_dim.45), channel_id=1, source_target_pairs={{0,1},{1,0},{2,3},{3,2},{4,5},{5,4},{6,7},{7,6},{8,9},{9,8},{10,11... | collective-permute-start | bytes 66836 | tf_op jit(solution)/shard_map/ppermute | solution.py:731
  21.0 51.1 %collective-permute-start.2 = (bf16[96,1536]{1,0:T(8,128)(2,1)}, bf16[96,1536]{1,0:T(8,128)(2,1)}, u32[]{:S(2)}, u32[]{:S(2)}) collective-permute-start(bf16[96,1536]{1,0:T(8,128)(2,1)} %pack_attn.2), channel_id=1, source_target_pairs={{0,1},{1,0},{2,3},{3,2},{4,5},{5,4},{6,7},{7,6},{8,9},{9,8},{10,11... | collective-permute-start | bytes 884744 | tf_op jit(solution)/shard_map/ppermute | solution.py:731
  31.9 31.2 %collective-permute-start.4 = (bf16[96,1536]{1,0:T(8,128)(2,1)}, bf16[96,1536]{1,0:T(8,128)(2,1)S(1)}, u32[]{:S(2)}, u32[]{:S(2)}) collective-permute-start(bf16[96,1536]{1,0:T(8,128)(2,1)} %pack_mlp.2), channel_id=1, source_target_pairs={{0,1},{1,0},{2,3},{3,2},{4,5},{5,4},{6,7},{7,6},{8,9},{9,8},{10,11... | collective-permute-start | bytes 884744 | tf_op jit(solution)/shard_map/ppermute | solution.py:731
  40.2 31.7 %collective-permute-start.8 = (bf16[48,1536]{1,0:T(8,128)(2,1)}, bf16[48,1536]{1,0:T(8,128)(2,1)}, u32[]{:S(2)}, u32[]{:S(2)}) collective-permute-start(bf16[48,1536]{1,0:T(8,128)(2,1)} %pack_attn.3), channel_id=1, source_target_pairs={{0,1},{1,0},{2,3},{3,2},{4,5},{5,4},{6,7},{7,6},{8,9},{9,8},{10,11... | collective-permute-start | bytes 442376 | tf_op jit(solution)/shard_map/ppermute | solution.py:731
  51.1 21.4 %collective-permute-start.12 = (bf16[96,1536]{1,0:T(8,128)(2,1)}, bf16[96,1536]{1,0:T(8,128)(2,1)S(1)}, u32[]{:S(2)}, u32[]{:S(2)}) collective-permute-start(bf16[96,1536]{1,0:T(8,128)(2,1)} %pack_mlp.3), channel_id=1, source_target_pairs={{0,1},{1,0},{2,3},{3,2},{4,5},{5,4},{6,7},{7,6},{8,9},{9,8},{10,11... | collective-permute-start | bytes 884744 | tf_op jit(solution)/shard_map/ppermute | solution.py:731
  60.8 11.1 %collective-permute-start.1 = (f32[2,2304]{1,0:T(2,128)}, f32[2,2304]{1,0:T(2,128)}, u32[]{:S(2)}, u32[]{:S(2)}) collective-permute-start(f32[2,2304]{1,0:T(2,128)} %bitcast.84), channel_id=1, source_target_pairs={{0,1},{1,0},{2,3},{3,2},{4,5},{5,4},{6,7},{7,6},{8,9},{9,8},{10,11... | collective-permute-start | bytes 55304 | tf_op jit(solution)/shard_map/ppermute | solution.py:731
  63.1 11.5 %collective-permute-start.5 = (bf16[96,1536]{1,0:T(8,128)(2,1)S(1)}, bf16[96,1536]{1,0:T(8,128)(2,1)S(1)}, u32[]{:S(2)}, u32[]{:S(2)}) collective-permute-start(bf16[96,1536]{1,0:T(8,128)(2,1)S(1)} %collective-permute-done.4.refs_5_.refs_11_), channel_id=1, source_target_pairs={{0,4},{2,6},{4,0},{6,2},{8,12},{10,14},{12,8},{14,10},{16,20},{18,... | collective-permute-start | bytes 884744 | tf_op jit(solution)/shard_map/ppermute | solution.py:734
  72.0 8.7 %collective-permute-start.9 = (bf16[48,1536]{1,0:T(8,128)(2,1)}, bf16[48,1536]{1,0:T(8,128)(2,1)}, u32[]{:S(2)}, u32[]{:S(2)}) collective-permute-start(bf16[48,1536]{1,0:T(8,128)(2,1)} %collective-permute-done.8.refs_5_.refs_12_), channel_id=1, source_target_pairs={{0,4},{2,6},{4,0},{6,2},{8,12},{10,14},{12,8},{14,10},{16,20},{18,... | collective-permute-start | bytes 442376 | tf_op jit(solution)/shard_map/ppermute | solution.py:734
  72.0 9.3 %collective-permute-start.6 = (bf16[96,1536]{1,0:T(8,128)(2,1)S(1)}, bf16[96,1536]{1,0:T(8,128)(2,1)}, u32[]{:S(2)}, u32[]{:S(2)}) collective-permute-start(bf16[96,1536]{1,0:T(8,128)(2,1)S(1)} %collective-permute-done.4.refs_5_.refs_11_), channel_id=1, source_target_pairs={{0,2},{2,0},{4,6},{6,4},{8,10},{10,8},{12,14},{14,12},{16,18},{18,... | collective-permute-start | bytes 884744 | tf_op jit(solution)/shard_map/ppermute | solution.py:734
  72.1 9.1 %collective-permute-start.3 = (bf16[96,1536]{1,0:T(8,128)(2,1)}, bf16[96,1536]{1,0:T(8,128)(2,1)}, u32[]{:S(2)}, u32[]{:S(2)}) collective-permute-start(bf16[96,1536]{1,0:T(8,128)(2,1)} %collective-permute-done.2.refs_5_.refs_12_), channel_id=1, source_target_pairs={{0,2},{2,0},{4,6},{6,4},{8,10},{10,8},{12,14},{14,12},{16,18},{18,... | collective-permute-start | bytes 884744 | tf_op jit(solution)/shard_map/ppermute | solution.py:734
  72.5 9.4 %collective-permute-start.13 = (bf16[96,1536]{1,0:T(8,128)(2,1)S(1)}, bf16[96,1536]{1,0:T(8,128)(2,1)}, u32[]{:S(2)}, u32[]{:S(2)}) collective-permute-start(bf16[96,1536]{1,0:T(8,128)(2,1)S(1)} %collective-permute-done.12.refs_5_.refs_10_), channel_id=1, source_target_pairs={{0,8},{2,10},{4,12},{6,14},{8,0},{10,2},{12,4},{14,6},{16,24},{18,... | collective-permute-start | bytes 884744 | tf_op jit(solution)/shard_map/ppermute | solution.py:734
  74.6 14.1 %collective-permute-start.7 = (bf16[96,1536]{1,0:T(8,128)(2,1)S(1)}, bf16[96,1536]{1,0:T(8,128)(2,1)}, u32[]{:S(2)}, u32[]{:S(2)}) collective-permute-start(bf16[96,1536]{1,0:T(8,128)(2,1)S(1)} %collective-permute-done.5.refs_6_.refs_12_), channel_id=1, source_target_pairs={{0,2},{2,0},{4,6},{6,4},{8,10},{10,8},{12,14},{14,12},{16,18},{18,... | collective-permute-start | bytes 884744 | tf_op jit(solution)/shard_map/ppermute | solution.py:734
  80.7 12.4 %collective-permute-start.10 = (bf16[48,1536]{1,0:T(8,128)(2,1)}, bf16[48,1536]{1,0:T(8,128)(2,1)S(1)}, u32[]{:S(2)}, u32[]{:S(2)}) collective-permute-start(bf16[48,1536]{1,0:T(8,128)(2,1)} %collective-permute-done.8.refs_5_.refs_12_), channel_id=1, source_target_pairs={{0,2},{2,0},{4,6},{6,4},{8,10},{10,8},{12,14},{14,12},{16,18},{18,... | collective-permute-start | bytes 442376 | tf_op jit(solution)/shard_map/ppermute | solution.py:734
  81.2 16.8 %collective-permute-start.14 = (bf16[96,1536]{1,0:T(8,128)(2,1)S(1)}, bf16[96,1536]{1,0:T(8,128)(2,1)S(1)}, u32[]{:S(2)}, u32[]{:S(2)}) collective-permute-start(bf16[96,1536]{1,0:T(8,128)(2,1)S(1)} %collective-permute-done.12.refs_5_.refs_10_), channel_id=1, source_target_pairs={{0,2},{2,0},{4,6},{6,4},{8,10},{10,8},{12,14},{14,12},{16,18},{18,... | collective-permute-start | bytes 884744 | tf_op jit(solution)/shard_map/ppermute | solution.py:734
  81.2 11.8 %collective-permute-start.11 = (bf16[48,1536]{1,0:T(8,128)(2,1)}, bf16[48,1536]{1,0:T(8,128)(2,1)S(1)}, u32[]{:S(2)}, u32[]{:S(2)}) collective-permute-start(bf16[48,1536]{1,0:T(8,128)(2,1)} %collective-permute-done.9.refs_6_.refs_13_), channel_id=1, source_target_pairs={{0,2},{2,0},{4,6},{6,4},{8,10},{10,8},{12,14},{14,12},{16,18},{18,... | collective-permute-start | bytes 442376 | tf_op jit(solution)/shard_map/ppermute | solution.py:734
  81.9 16.0 %collective-permute-start.15 = (bf16[96,1536]{1,0:T(8,128)(2,1)}, bf16[96,1536]{1,0:T(8,128)(2,1)S(1)}, u32[]{:S(2)}, u32[]{:S(2)}) collective-permute-start(bf16[96,1536]{1,0:T(8,128)(2,1)} %collective-permute-done.13.refs_6_.refs_11_), channel_id=1, source_target_pairs={{0,2},{2,0},{4,6},{6,4},{8,10},{10,8},{12,14},{14,12},{16,18},{18,... | collective-permute-start | bytes 884744 | tf_op jit(solution)/shard_map/ppermute | solution.py:734
  109.5 25.7 %collective-permute-start.58 = (bf16[1536,384]{1,0:T(8,128)(2,1)}, bf16[1536,384]{1,0:T(8,128)(2,1)S(1)}, u32[]{:S(2)}, u32[]{:S(2)}) collective-permute-start(bf16[1536,384]{1,0:T(8,128)(2,1)} %get-tuple-element.159), channel_id=1, source_target_pairs={{0,2},{2,0},{4,6},{6,4},{8,10},{10,8},{12,14},{14,12},{16,18},{18,... | collective-permute-start | bytes 3538952 | tf_op jit(solution)/shard_map/ppermute | solution.py:734
  121.9 31.8 %collective-permute-start.22 = (bf16[1552,384]{1,0:T(8,128)(2,1)}, bf16[1552,384]{1,0:T(8,128)(2,1)S(1)}, u32[]{:S(2)}, u32[]{:S(2)}) collective-permute-start(bf16[1552,384]{1,0:T(8,128)(2,1)} %get-tuple-element.134), channel_id=1, source_target_pairs={{0,2},{2,0},{4,6},{6,4},{8,10},{10,8},{12,14},{14,12},{16,18},{18,... | collective-permute-start | bytes 3575816 | tf_op jit(solution)/shard_map/ppermute | solution.py:734
  128.6 5.4 %collective-permute-start.16 = (bf16[784,384]{1,0:T(8,128)(2,1)S(1)}, bf16[784,384]{1,0:T(8,128)(2,1)S(1)}, u32[]{:S(2)}, u32[]{:S(2)}) collective-permute-start(bf16[784,384]{1,0:T(8,128)(2,1)S(1)} %get-tuple-element.122), channel_id=1, source_target_pairs={{0,2},{2,0},{4,6},{6,4},{8,10},{10,8},{12,14},{14,12},{16,18},{18,... | collective-permute-start | bytes 1806344 | tf_op jit(solution)/shard_map/ppermute | solution.py:734
  132.3 9.9 %collective-permute-start.41 = (bf16[384,384]{1,0:T(8,128)(2,1)S(1)}, bf16[384,384]{1,0:T(8,128)(2,1)S(1)}, u32[]{:S(2)}, u32[]{:S(2)}) collective-permute-start(bf16[384,384]{1,0:T(8,128)(2,1)S(1)} %get-tuple-element.148), channel_id=1, source_target_pairs={{0,1},{1,0},{2,3},{3,2},{4,5},{5,4},{6,7},{7,6},{8,9},{9,8},{10,11... | collective-permute-start | bytes 884744 | tf_op jit(solution)/shard_map/ppermute | solution.py:731
  134.7 14.3 %collective-permute-start.17 = (bf16[416,384]{1,0:T(8,128)(2,1)S(1)}, bf16[416,384]{1,0:T(8,128)(2,1)S(1)}, u32[]{:S(2)}, u32[]{:S(2)}) collective-permute-start(bf16[416,384]{1,0:T(8,128)(2,1)S(1)} %get-tuple-element.125), channel_id=1, source_target_pairs={{0,1},{1,0},{2,3},{3,2},{4,5},{5,4},{6,7},{7,6},{8,9},{9,8},{10,11... | collective-permute-start | bytes 958472 | tf_op jit(solution)/shard_map/ppermute | solution.py:731
  136.0 31.4 %collective-permute-start.59 = (bf16[768,384]{1,0:T(8,128)(2,1)S(1)}, bf16[768,384]{1,0:T(8,128)(2,1)S(1)}, u32[]{:S(2)}, u32[]{:S(2)}) collective-permute-start(bf16[768,384]{1,0:T(8,128)(2,1)S(1)} %get-tuple-element.161), channel_id=1, source_target_pairs={{0,1},{1,0},{2,3},{3,2},{4,5},{5,4},{6,7},{7,6},{8,9},{9,8},{10,11... | collective-permute-start | bytes 1769480 | tf_op jit(solution)/shard_map/ppermute | solution.py:731
  137.8 20.0 %collective-permute-start.28 = (f32[2,256]{1,0:T(2,128)S(1)}, f32[2,256]{1,0:T(2,128)S(1)}, u32[]{:S(2)}, u32[]{:S(2)}) collective-permute-start(f32[2,256]{1,0:T(2,128)S(1)} %maximum_maximum_fusion), channel_id=1, source_target_pairs={{0,2},{2,0},{4,6},{6,4},{8,10},{10,8},{12,14},{14,12},{16,18},{18,... | collective-permute-start | bytes 6152 | tf_op jit(solution)/shard_map/ppermute | solution.py:734
  142.8 8.7 %collective-permute-start.42 = (bf16[192,384]{1,0:T(8,128)(2,1)S(1)}, bf16[192,384]{1,0:T(8,128)(2,1)S(1)}, u32[]{:S(2)}, u32[]{:S(2)}) collective-permute-start(bf16[192,384]{1,0:T(8,128)(2,1)S(1)} %get-tuple-element.150), channel_id=1, source_target_pairs={{0,4},{2,6},{4,0},{6,2},{8,12},{10,14},{12,8},{14,10},{16,20},{18,... | collective-permute-start | bytes 442376 | tf_op jit(solution)/shard_map/ppermute | solution.py:734
  149.6 9.7 %collective-permute-start.18 = (bf16[256,384]{1,0:T(8,128)(2,1)S(1)}, bf16[256,384]{1,0:T(8,128)(2,1)S(1)}, u32[]{:S(2)}, u32[]{:S(2)}) collective-permute-start(bf16[256,384]{1,0:T(8,128)(2,1)S(1)} %get-tuple-element.127), channel_id=1, source_target_pairs={{0,4},{2,6},{4,0},{6,2},{8,12},{10,14},{12,8},{14,10},{16,20},{18,... | collective-permute-start | bytes 589832 | tf_op jit(solution)/shard_map/ppermute | solution.py:734
  152.1 11.4 %collective-permute-start.43 = (bf16[48,384]{1,0:T(8,128)(2,1)S(1)}, bf16[48,384]{1,0:T(8,128)(2,1)S(1)}, u32[]{:S(2)}, u32[]{:S(2)}) collective-permute-start(bf16[48,384]{1,0:T(8,128)(2,1)S(1)} %get-tuple-element.152), channel_id=1, source_target_pairs={{0,8},{2,10},{4,12},{6,14},{8,0},{10,2},{12,4},{14,6},{16,24},{18,... | collective-permute-start | bytes 110600 | tf_op jit(solution)/shard_map/ppermute | solution.py:734
  153.7 10.1 %collective-permute-start.44 = (bf16[48,384]{1,0:T(8,128)(2,1)S(1)}, bf16[48,384]{1,0:T(8,128)(2,1)S(1)}, u32[]{:S(2)}, u32[]{:S(2)}) collective-permute-start(bf16[48,384]{1,0:T(8,128)(2,1)S(1)} %get-tuple-element.153), channel_id=1, source_target_pairs={{0,16},{2,18},{4,20},{6,22},{8,24},{10,26},{12,28},{14,30},{16,0},... | collective-permute-start | bytes 110600 | tf_op jit(solution)/shard_map/ppermute | solution.py:734
  157.8 41.2 %collective-permute-start.23 = (bf16[800,384]{1,0:T(8,128)(2,1)}, bf16[800,384]{1,0:T(8,128)(2,1)S(1)}, u32[]{:S(2)}, u32[]{:S(2)}) collective-permute-start(bf16[800,384]{1,0:T(8,128)(2,1)} %get-tuple-element.136), channel_id=1, source_target_pairs={{0,1},{1,0},{2,3},{3,2},{4,5},{5,4},{6,7},{7,6},{8,9},{9,8},{10,11... | collective-permute-start | bytes 1843208 | tf_op jit(solution)/shard_map/ppermute | solution.py:731
  163.0 10.7 %collective-permute-start.19 = (bf16[176,384]{1,0:T(8,128)(2,1)S(1)}, bf16[176,384]{1,0:T(8,128)(2,1)S(1)}, u32[]{:S(2)}, u32[]{:S(2)}) collective-permute-start(bf16[176,384]{1,0:T(8,128)(2,1)S(1)} %get-tuple-element.129), channel_id=1, source_target_pairs={{0,8},{2,10},{4,12},{6,14},{8,0},{10,2},{12,4},{14,6},{16,24},{18,... | collective-permute-start | bytes 405512 | tf_op jit(solution)/shard_map/ppermute | solution.py:734
  163.4 14.6 %collective-permute-start.20 = (bf16[176,384]{1,0:T(8,128)(2,1)S(1)}, bf16[176,384]{1,0:T(8,128)(2,1)S(1)}, u32[]{:S(2)}, u32[]{:S(2)}) collective-permute-start(bf16[176,384]{1,0:T(8,128)(2,1)S(1)} %get-tuple-element.130), channel_id=1, source_target_pairs={{0,16},{2,18},{4,20},{6,22},{8,24},{10,26},{12,28},{14,30},{16,0},... | collective-permute-start | bytes 405512 | tf_op jit(solution)/shard_map/ppermute | solution.py:734
  163.8 14.3 %collective-permute-start.21 = (bf16[176,384]{1,0:T(8,128)(2,1)S(1)}, bf16[176,384]{1,0:T(8,128)(2,1)S(1)}, u32[]{:S(2)}, u32[]{:S(2)}) collective-permute-start(bf16[176,384]{1,0:T(8,128)(2,1)S(1)} %get-tuple-element.131), channel_id=1, source_target_pairs={{0,24},{2,26},{4,28},{6,30},{8,16},{10,18},{12,20},{14,22},{16,8},... | collective-permute-start | bytes 405512 | tf_op jit(solution)/shard_map/ppermute | solution.py:734
  167.4 5.8 %collective-permute-start.45 = (bf16[48,384]{1,0:T(8,128)(2,1)S(1)}, bf16[48,384]{1,0:T(8,128)(2,1)S(1)}, u32[]{:S(2)}, u32[]{:S(2)}) collective-permute-start(bf16[48,384]{1,0:T(8,128)(2,1)S(1)} %get-tuple-element.154), channel_id=1, source_target_pairs={{0,24},{2,26},{4,28},{6,30},{8,16},{10,18},{12,20},{14,22},{16,8},... | collective-permute-start | bytes 110600 | tf_op jit(solution)/shard_map/ppermute | solution.py:734
  173.2 21.4 %collective-permute-start.60 = (bf16[384,384]{1,0:T(8,128)(2,1)}, bf16[384,384]{1,0:T(8,128)(2,1)S(1)}, u32[]{:S(2)}, u32[]{:S(2)}) collective-permute-start(bf16[384,384]{1,0:T(8,128)(2,1)} %get-tuple-element.163), channel_id=1, source_target_pairs={{0,4},{2,6},{4,0},{6,2},{8,12},{10,14},{12,8},{14,10},{16,20},{18,... | collective-permute-start | bytes 884744 | tf_op jit(solution)/shard_map/ppermute | solution.py:734
  173.7 6.9 %collective-permute-start.46 = (bf16[48,384]{1,0:T(8,128)(2,1)S(1)}, bf16[48,384]{1,0:T(8,128)(2,1)S(1)}, u32[]{:S(2)}, u32[]{:S(2)}) collective-permute-start(bf16[48,384]{1,0:T(8,128)(2,1)S(1)} %add_all.6.refs_0_), channel_id=1, source_target_pairs={{0,8},{2,10},{4,12},{6,14},{8,0},{10,2},{12,4},{14,6},{16,24},{18,... | collective-permute-start | bytes 110600 | tf_op jit(solution)/shard_map/ppermute | solution.py:734
  178.1 5.3 %collective-permute-start.47 = (bf16[48,384]{1,0:T(8,128)(2,1)S(1)}, bf16[48,384]{1,0:T(8,128)(2,1)S(1)}, u32[]{:S(2)}, u32[]{:S(2)}) collective-permute-start(bf16[48,384]{1,0:T(8,128)(2,1)S(1)} %add_all.6.refs_0_), channel_id=1, source_target_pairs={{0,16},{2,18},{4,20},{6,22},{8,24},{10,26},{12,28},{14,30},{16,0},... | collective-permute-start | bytes 110600 | tf_op jit(solution)/shard_map/ppermute | solution.py:734
  178.1 5.8 %collective-permute-start.48 = (bf16[48,384]{1,0:T(8,128)(2,1)S(1)}, bf16[48,384]{1,0:T(8,128)(2,1)S(1)}, u32[]{:S(2)}, u32[]{:S(2)}) collective-permute-start(bf16[48,384]{1,0:T(8,128)(2,1)S(1)} %add_all.6.refs_0_), channel_id=1, source_target_pairs={{0,24},{2,26},{4,28},{6,30},{8,16},{10,18},{12,20},{14,22},{16,8},... | collective-permute-start | bytes 110600 | tf_op jit(solution)/shard_map/ppermute | solution.py:734
  180.6 5.9 %collective-permute-start.34 = (bf16[48,384]{1,0:T(8,128)(2,1)S(1)}, bf16[48,384]{1,0:T(8,128)(2,1)S(1)}, u32[]{:S(2)}, u32[]{:S(2)}) collective-permute-start(bf16[48,384]{1,0:T(8,128)(2,1)S(1)} %get-tuple-element.144.refs_0_), channel_id=1, source_target_pairs={{0,8},{2,10},{4,12},{6,14},{8,0},{10,2},{12,4},{14,6},{16,24},{18,... | collective-permute-start | bytes 110600 | tf_op jit(solution)/shard_map/ppermute | solution.py:734
  183.9 5.8 %collective-permute-start.36 = (bf16[48,384]{1,0:T(8,128)(2,1)S(1)}, bf16[48,384]{1,0:T(8,128)(2,1)S(1)}, u32[]{:S(2)}, u32[]{:S(2)}) collective-permute-start(bf16[48,384]{1,0:T(8,128)(2,1)S(1)} %get-tuple-element.144.refs_0_), channel_id=1, source_target_pairs={{0,24},{2,26},{4,28},{6,30},{8,16},{10,18},{12,20},{14,22},{16,8},... | collective-permute-start | bytes 110600 | tf_op jit(solution)/shard_map/ppermute | solution.py:734
  186.4 5.6 %collective-permute-start.32 = (f32[2,2,2,256]{3,2,1,0:T(2,128)S(1)}, f32[2,2,2,256]{3,2,1,0:T(2,128)S(1)}, u32[]{:S(2)}, u32[]{:S(2)}) collective-permute-start(f32[2,2,2,256]{3,2,1,0:T(2,128)S(1)} %get-tuple-element.179), channel_id=1, source_target_pairs={{0,24},{2,26},{4,28},{6,30},{8,16},{10,18},{12,20},{14,22},{16,8},... | collective-permute-start | bytes 24584 | tf_op jit(solution)/shard_map/ppermute | solution.py:734
  188.3 5.4 %collective-permute-start.31 = (f32[2,2,2,256]{3,2,1,0:T(2,128)S(1)}, f32[2,2,2,256]{3,2,1,0:T(2,128)S(1)}, u32[]{:S(2)}, u32[]{:S(2)}) collective-permute-start(f32[2,2,2,256]{3,2,1,0:T(2,128)S(1)} %get-tuple-element.179), channel_id=1, source_target_pairs={{0,16},{2,18},{4,20},{6,22},{8,24},{10,26},{12,28},{14,30},{16,0},... | collective-permute-start | bytes 24584 | tf_op jit(solution)/shard_map/ppermute | solution.py:734
  192.1 6.8 %collective-permute-start.49 = (bf16[192,384]{1,0:T(8,128)(2,1)S(1)}, bf16[192,384]{1,0:T(8,128)(2,1)S(1)}, u32[]{:S(2)}, u32[]{:S(2)}) collective-permute-start(bf16[192,384]{1,0:T(8,128)(2,1)S(1)} %join.5.refs_4_), channel_id=1, source_target_pairs={{0,4},{2,6},{4,0},{6,2},{8,12},{10,14},{12,8},{14,10},{16,20},{18,... | collective-permute-start | bytes 442376 | tf_op jit(solution)/shard_map/ppermute | solution.py:734
  193.6 6.5 %collective-permute-start.37 = (bf16[192,384]{1,0:T(8,128)(2,1)S(1)}, bf16[192,384]{1,0:T(8,128)(2,1)}, u32[]{:S(2)}, u32[]{:S(2)}) collective-permute-start(bf16[192,384]{1,0:T(8,128)(2,1)S(1)} %join.4.refs_0_), channel_id=1, source_target_pairs={{0,4},{2,6},{4,0},{6,2},{8,12},{10,14},{12,8},{14,10},{16,20},{18,... | collective-permute-start | bytes 442376 | tf_op jit(solution)/shard_map/ppermute | solution.py:734
  195.7 5.6 %collective-permute-start.62 = (bf16[96,384]{1,0:T(8,128)(2,1)S(1)}, bf16[96,384]{1,0:T(8,128)(2,1)S(1)}, u32[]{:S(2)}, u32[]{:S(2)}) collective-permute-start(bf16[96,384]{1,0:T(8,128)(2,1)S(1)} %get-tuple-element.166), channel_id=1, source_target_pairs={{0,16},{2,18},{4,20},{6,22},{8,24},{10,26},{12,28},{14,30},{16,0},... | collective-permute-start | bytes 221192 | tf_op jit(solution)/shard_map/ppermute | solution.py:734
  198.9 13.5 %collective-permute-start.50 = (bf16[192,384]{1,0:T(8,128)(2,1)S(1)}, bf16[192,384]{1,0:T(8,128)(2,1)S(1)}, u32[]{:S(2)}, u32[]{:S(2)}) collective-permute-start(bf16[192,384]{1,0:T(8,128)(2,1)S(1)} %join.5.refs_4_), channel_id=1, source_target_pairs={{0,2},{2,0},{4,6},{6,4},{8,10},{10,8},{12,14},{14,12},{16,18},{18,... | collective-permute-start | bytes 442376 | tf_op jit(solution)/shard_map/ppermute | solution.py:734
  199.0 14.5 %collective-permute-start.51 = (bf16[192,384]{1,0:T(8,128)(2,1)S(1)}, bf16[192,384]{1,0:T(8,128)(2,1)S(1)}, u32[]{:S(2)}, u32[]{:S(2)}) collective-permute-start(bf16[192,384]{1,0:T(8,128)(2,1)S(1)} %collective-permute-done.49.refs_5_), channel_id=1, source_target_pairs={{0,2},{2,0},{4,6},{6,4},{8,10},{10,8},{12,14},{14,12},{16,18},{18,... | collective-permute-start | bytes 442376 | tf_op jit(solution)/shard_map/ppermute | solution.py:734
  200.2 14.1 %collective-permute-start.38 = (bf16[192,384]{1,0:T(8,128)(2,1)S(1)}, bf16[192,384]{1,0:T(8,128)(2,1)S(1)}, u32[]{:S(2)}, u32[]{:S(2)}) collective-permute-start(bf16[192,384]{1,0:T(8,128)(2,1)S(1)} %join.4.refs_0_), channel_id=1, source_target_pairs={{0,2},{2,0},{4,6},{6,4},{8,10},{10,8},{12,14},{14,12},{16,18},{18,... | collective-permute-start | bytes 442376 | tf_op jit(solution)/shard_map/ppermute | solution.py:734
  200.3 10.4 %collective-permute-start.24 = (bf16[448,384]{1,0:T(8,128)(2,1)S(1)}, bf16[448,384]{1,0:T(8,128)(2,1)S(1)}, u32[]{:S(2)}, u32[]{:S(2)}) collective-permute-start(bf16[448,384]{1,0:T(8,128)(2,1)S(1)} %get-tuple-element.138), channel_id=1, source_target_pairs={{0,4},{2,6},{4,0},{6,2},{8,12},{10,14},{12,8},{14,10},{16,20},{18,... | collective-permute-start | bytes 1032200 | tf_op jit(solution)/shard_map/ppermute | solution.py:734
  201.3 6.2 %collective-permute-start.63 = (bf16[96,384]{1,0:T(8,128)(2,1)S(1)}, bf16[96,384]{1,0:T(8,128)(2,1)S(1)}, u32[]{:S(2)}, u32[]{:S(2)}) collective-permute-start(bf16[96,384]{1,0:T(8,128)(2,1)S(1)} %get-tuple-element.167), channel_id=1, source_target_pairs={{0,24},{2,26},{4,28},{6,30},{8,16},{10,18},{12,20},{14,22},{16,8},... | collective-permute-start | bytes 221192 | tf_op jit(solution)/shard_map/ppermute | solution.py:734
  207.5 9.8 %collective-permute-start.39 = (bf16[192,384]{1,0:T(8,128)(2,1)}, bf16[192,384]{1,0:T(8,128)(2,1)S(1)}, u32[]{:S(2)}, u32[]{:S(2)}) collective-permute-start(bf16[192,384]{1,0:T(8,128)(2,1)} %collective-permute-done.37.refs_1_), channel_id=1, source_target_pairs={{0,2},{2,0},{4,6},{6,4},{8,10},{10,8},{12,14},{14,12},{16,18},{18,... | collective-permute-start | bytes 442376 | tf_op jit(solution)/shard_map/ppermute | solution.py:734
  210.7 7.0 %collective-permute-start.64 = (bf16[96,384]{1,0:T(8,128)(2,1)S(1)}, bf16[96,384]{1,0:T(8,128)(2,1)S(1)}, u32[]{:S(2)}, u32[]{:S(2)}) collective-permute-start(bf16[96,384]{1,0:T(8,128)(2,1)S(1)} %add_all.7.refs_0_), channel_id=1, source_target_pairs={{0,8},{2,10},{4,12},{6,14},{8,0},{10,2},{12,4},{14,6},{16,24},{18,... | collective-permute-start | bytes 221192 | tf_op jit(solution)/shard_map/ppermute | solution.py:734
  212.4 25.6 %collective-permute-start.25 = (bf16[224,384]{1,0:T(8,128)(2,1)S(1)}, bf16[224,384]{1,0:T(8,128)(2,1)S(1)}, u32[]{:S(2)}, u32[]{:S(2)}) collective-permute-start(bf16[224,384]{1,0:T(8,128)(2,1)S(1)} %get-tuple-element.140), channel_id=1, source_target_pairs={{0,8},{2,10},{4,12},{6,14},{8,0},{10,2},{12,4},{14,6},{16,24},{18,... | collective-permute-start | bytes 516104 | tf_op jit(solution)/shard_map/ppermute | solution.py:734
  213.5 24.5 %collective-permute-start.26 = (bf16[224,384]{1,0:T(8,128)(2,1)S(1)}, bf16[224,384]{1,0:T(8,128)(2,1)S(1)}, u32[]{:S(2)}, u32[]{:S(2)}) collective-permute-start(bf16[224,384]{1,0:T(8,128)(2,1)S(1)} %get-tuple-element.141), channel_id=1, source_target_pairs={{0,16},{2,18},{4,20},{6,22},{8,24},{10,26},{12,28},{14,30},{16,0},... | collective-permute-start | bytes 516104 | tf_op jit(solution)/shard_map/ppermute | solution.py:734
  214.3 23.7 %collective-permute-start.27 = (bf16[224,384]{1,0:T(8,128)(2,1)S(1)}, bf16[224,384]{1,0:T(8,128)(2,1)S(1)}, u32[]{:S(2)}, u32[]{:S(2)}) collective-permute-start(bf16[224,384]{1,0:T(8,128)(2,1)S(1)} %get-tuple-element.142), channel_id=1, source_target_pairs={{0,24},{2,26},{4,28},{6,30},{8,16},{10,18},{12,20},{14,22},{16,8},... | collective-permute-start | bytes 516104 | tf_op jit(solution)/shard_map/ppermute | solution.py:734
  217.3 19.1 %collective-permute-start.65 = (bf16[96,384]{1,0:T(8,128)(2,1)S(1)}, bf16[96,384]{1,0:T(8,128)(2,1)S(1)}, u32[]{:S(2)}, u32[]{:S(2)}) collective-permute-start(bf16[96,384]{1,0:T(8,128)(2,1)S(1)} %add_all.7.refs_0_), channel_id=1, source_target_pairs={{0,16},{2,18},{4,20},{6,22},{8,24},{10,26},{12,28},{14,30},{16,0},... | collective-permute-start | bytes 221192 | tf_op jit(solution)/shard_map/ppermute | solution.py:734
  217.8 18.6 %collective-permute-start.66 = (bf16[96,384]{1,0:T(8,128)(2,1)S(1)}, bf16[96,384]{1,0:T(8,128)(2,1)S(1)}, u32[]{:S(2)}, u32[]{:S(2)}) collective-permute-start(bf16[96,384]{1,0:T(8,128)(2,1)S(1)} %add_all.7.refs_0_), channel_id=1, source_target_pairs={{0,24},{2,26},{4,28},{6,30},{8,16},{10,18},{12,20},{14,22},{16,8},... | collective-permute-start | bytes 221192 | tf_op jit(solution)/shard_map/ppermute | solution.py:734
  237.0 15.3 %collective-permute-start.67 = (bf16[384,384]{1,0:T(8,128)(2,1)S(1)}, bf16[384,384]{1,0:T(8,128)(2,1)S(1)}, u32[]{:S(2)}, u32[]{:S(2)}) collective-permute-start(bf16[384,384]{1,0:T(8,128)(2,1)S(1)} %join.7.refs_4_), channel_id=1, source_target_pairs={{0,4},{2,6},{4,0},{6,2},{8,12},{10,14},{12,8},{14,10},{16,20},{18,... | collective-permute-start | bytes 884744 | tf_op jit(solution)/shard_map/ppermute | solution.py:734
  238.0 21.3 %collective-permute-start.68 = (bf16[384,384]{1,0:T(8,128)(2,1)S(1)}, bf16[384,384]{1,0:T(8,128)(2,1)S(1)}, u32[]{:S(2)}, u32[]{:S(2)}) collective-permute-start(bf16[384,384]{1,0:T(8,128)(2,1)S(1)} %join.7.refs_4_), channel_id=1, source_target_pairs={{0,2},{2,0},{4,6},{6,4},{8,10},{10,8},{12,14},{14,12},{16,18},{18,... | collective-permute-start | bytes 884744 | tf_op jit(solution)/shard_map/ppermute | solution.py:734
  238.2 8.8 %collective-permute-start.52 = (bf16[96,384]{1,0:T(8,128)(2,1)S(1)}, bf16[96,384]{1,0:T(8,128)(2,1)S(1)}, u32[]{:S(2)}, u32[]{:S(2)}) collective-permute-start(bf16[96,384]{1,0:T(8,128)(2,1)S(1)} %get-tuple-element.157.refs_0_), channel_id=1, source_target_pairs={{0,8},{2,10},{4,12},{6,14},{8,0},{10,2},{12,4},{14,6},{16,24},{18,... | collective-permute-start | bytes 221192 | tf_op jit(solution)/shard_map/ppermute | solution.py:734
  239.6 9.1 %collective-permute-start.53 = (bf16[96,384]{1,0:T(8,128)(2,1)S(1)}, bf16[96,384]{1,0:T(8,128)(2,1)S(1)}, u32[]{:S(2)}, u32[]{:S(2)}) collective-permute-start(bf16[96,384]{1,0:T(8,128)(2,1)S(1)} %get-tuple-element.157.refs_0_), channel_id=1, source_target_pairs={{0,16},{2,18},{4,20},{6,22},{8,24},{10,26},{12,28},{14,30},{16,0},... | collective-permute-start | bytes 221192 | tf_op jit(solution)/shard_map/ppermute | solution.py:734
  240.9 7.8 %collective-permute-start.54 = (bf16[96,384]{1,0:T(8,128)(2,1)S(1)}, bf16[96,384]{1,0:T(8,128)(2,1)S(1)}, u32[]{:S(2)}, u32[]{:S(2)}) collective-permute-start(bf16[96,384]{1,0:T(8,128)(2,1)S(1)} %get-tuple-element.157.refs_0_), channel_id=1, source_target_pairs={{0,24},{2,26},{4,28},{6,30},{8,16},{10,18},{12,20},{14,22},{16,8},... | collective-permute-start | bytes 221192 | tf_op jit(solution)/shard_map/ppermute | solution.py:734
  249.3 7.5 %collective-permute-start.55 = (bf16[384,384]{1,0:T(8,128)(2,1)S(1)}, bf16[384,384]{1,0:T(8,128)(2,1)S(1)}, u32[]{:S(2)}, u32[]{:S(2)}) collective-permute-start(bf16[384,384]{1,0:T(8,128)(2,1)S(1)} %join.6.refs_0_), channel_id=1, source_target_pairs={{0,4},{2,6},{4,0},{6,2},{8,12},{10,14},{12,8},{14,10},{16,20},{18,... | collective-permute-start | bytes 884744 | tf_op jit(solution)/shard_map/ppermute | solution.py:734
  250.3 8.3 %collective-permute-start.33 = (f32[1,192]{1,0:T(1,128)S(1)}, f32[1,192]{1,0:T(1,128)S(1)}, u32[]{:S(2)}, u32[]{:S(2)}) collective-permute-start(f32[1,192]{1,0:T(1,128)S(1)} %get-tuple-element.177), channel_id=1, source_target_pairs={{0,1},{1,0},{2,3},{3,2},{4,5},{5,4},{6,7},{7,6},{8,9},{9,8},{10,11... | collective-permute-start | bytes 2312 | tf_op jit(solution)/shard_map/ppermute | solution.py:731
  252.3 7.0 %collective-permute-start.56 = (bf16[384,384]{1,0:T(8,128)(2,1)S(1)}, bf16[384,384]{1,0:T(8,128)(2,1)S(1)}, u32[]{:S(2)}, u32[]{:S(2)}) collective-permute-start(bf16[384,384]{1,0:T(8,128)(2,1)S(1)} %join.6.refs_0_), channel_id=1, source_target_pairs={{0,2},{2,0},{4,6},{6,4},{8,10},{10,8},{12,14},{14,12},{16,18},{18,... | collective-permute-start | bytes 884744 | tf_op jit(solution)/shard_map/ppermute | solution.py:734
  252.3 7.0 %collective-permute-start.69 = (bf16[384,384]{1,0:T(8,128)(2,1)S(1)}, bf16[384,384]{1,0:T(8,128)(2,1)S(1)}, u32[]{:S(2)}, u32[]{:S(2)}) collective-permute-start(bf16[384,384]{1,0:T(8,128)(2,1)S(1)} %collective-permute-done.67.refs_5_), channel_id=1, source_target_pairs={{0,2},{2,0},{4,6},{6,4},{8,10},{10,8},{12,14},{14,12},{16,18},{18,... | collective-permute-start | bytes 884744 | tf_op jit(solution)/shard_map/ppermute | solution.py:734
  (36 other events, 415.8 us)

commit v2 on v1

v2 whole, which is shorter than its diff:
```python
import functools
import math

import jax
import jax.numpy as jnp
from jax import lax
from jax.experimental import pallas as pl
from jax.experimental.pallas import tpu as pltpu
from jax.sharding import PartitionSpec as P

D = 384
HEAD_DIM = 64
LAYERS = 2
F32 = jnp.float32
BF16 = jnp.bfloat16

norm_eps = 1e-06
gelu_coeff = math.sqrt(2.0 / math.pi)
gelu_cubic = 0.044715

VMEM = pl.BlockSpec(memory_space=pltpu.VMEM)
SMEM = pl.BlockSpec(memory_space=pltpu.SMEM)
ANY = pl.BlockSpec(memory_space=pl.ANY)
HBM = pl.BlockSpec(memory_space=pltpu.HBM)
LIMIT = 16 * 1024 * 1024
SMALL = 8 * 1024 * 1024


def sds(shape, dtype):
    return jax.ShapeDtypeStruct(shape, dtype)


def norm_rows(values):
    centered = values - jnp.mean(values, axis=-1, keepdims=True)
    inv_dev = lax.rsqrt(jnp.mean(centered * centered, axis=-1, keepdims=True) + norm_eps)
    return (centered * inv_dev, inv_dev)


def norm_back(grad_normed, normed, inv_dev):
    return (
        grad_normed
        - jnp.mean(grad_normed, axis=-1, keepdims=True)
        - normed * jnp.mean(grad_normed * normed, axis=-1, keepdims=True)
    ) * inv_dev


def gelu_parts(pre_act):
    square = pre_act * pre_act
    inner_arg = gelu_coeff * pre_act * (1.0 + gelu_cubic * square)
    tanh_val = jnp.tanh(inner_arg)
    half_up = 0.5 * (1.0 + tanh_val)
    value_out = pre_act * half_up
    slope_out = half_up + 0.5 * pre_act * (1.0 - tanh_val * tanh_val) * (
        gelu_coeff + (3.0 * gelu_cubic * gelu_coeff) * square
    )
    return (value_out, slope_out)


def dot(a, b):
    return jnp.dot(a, b, preferred_element_type=F32)


def dot_nt(a, b):
    return lax.dot_general(a, b, (((1,), (1,)), ((), ())), preferred_element_type=F32)


def dot_tn(a, b):
    return lax.dot_general(a, b, (((0,), (0,)), ((), ())), preferred_element_type=F32)


def head_masks():
    lane = lax.broadcasted_iota(jnp.int32, (1, 2 * HEAD_DIM), 1)
    first = lane < HEAD_DIM
    return first, jnp.logical_not(first)


def keep_lanes(values, mask):
    return jnp.where(mask, values, jnp.zeros_like(values))


def rows_of(start, size):
    return pl.ds(pl.multiple_of(start, 16), size)


def attn_weight_copies(meta, layer, qkv_hbm, out_hbm, pieces, offsets, w_qkv, w_out, sems):
    half = qkv_hbm.shape[1]
    x = meta[0]
    copies = [
        (qkv_hbm.at[layer], w_qkv.at[rows_of(x * half, half), :]),
        (out_hbm.at[layer], w_out.at[rows_of(x * half, half), :]),
    ]
    for piece, offset in zip(pieces, offsets):
        size = piece.shape[0]
        start = (1 - x) * half + offset * size
        copies.append((piece.at[:, pl.ds(0, 3 * D)], w_qkv.at[rows_of(start, size), :]))
        copies.append((piece.at[:, pl.ds(3 * D, D)], w_out.at[rows_of(start, size), :]))
    return [pltpu.make_async_copy(s, d, sems.at[i]) for i, (s, d) in enumerate(copies)]


def mlp_weight_copies(meta, layer, up_hbm, down_hbm, pieces, offsets, w_up, w_down, sems):
    half = up_hbm.shape[1]
    tall = down_hbm.shape[1]
    blocks = tall // half
    x = meta[0]
    copies = [
        (up_hbm.at[layer], w_up.at[rows_of(x * half, half), :]),
        (down_hbm.at[layer], w_down.at[rows_of(x * tall, tall), :]),
    ]
    for piece, offset in zip(pieces, offsets):
        size = piece.shape[0] // 2
        start = (1 - x) * half + offset * size
        copies.append((piece.at[pl.ds(0, size), :], w_up.at[rows_of(start, size), :]))
        for b in range(blocks):
            start = (1 - x) * tall + offset * (blocks * size) + b * size
            copies.append(
                (
                    piece.at[pl.ds(size, size), pl.ds(b * D, D)],
                    w_down.at[rows_of(start, size), :],
                )
            )
    return [pltpu.make_async_copy(s, d, sems.at[i]) for i, (s, d) in enumerate(copies)]


def piece_offsets(meta, count, far):
    core, y, z = meta[1], meta[2], meta[3]
    if count == 2:
        return [core, 1 - core]
    near = z % 2 if far else y
    return [
        near * 2 + core,
        (1 - near) * 2 + core,
        near * 2 + (1 - core),
        (1 - near) * 2 + (1 - core),
    ]


def call(body, ins, in_specs, out_shape, out_specs, name, scratch=(), deps=(), **more):
    given, late = len(ins), len(deps)

    def kernel(*refs):
        body(*refs[:given], *refs[given + late :])

    return pl.pallas_call(
        kernel,
        out_shape=out_shape,
        in_specs=list(in_specs) + [ANY] * late,
        out_specs=out_specs,
        scratch_shapes=list(scratch),
        compiler_params=pltpu.CompilerParams(vmem_limit_bytes=SMALL),
        cost_estimate=pl.CostEstimate(flops=10**10, bytes_accessed=0, transcendentals=0),
        name=name,
        **more,
    )(*ins, *deps)


def pack_attn_into(send, parts, offset, qkv, out):
    size = qkv.shape[1] // parts
    rows = rows_of(offset * size, size)
    send[:, 0 : 3 * D] = qkv[0, rows, :]
    send[:, 3 * D : 4 * D] = out[0, rows, :]


def pack_mlp_into(send, layer, offset, up, down):
    size = up.shape[1] // 4
    blocks = down.shape[1] // up.shape[1]
    send[0:size, :] = up[layer, rows_of(offset * size, size), :]
    for b in range(blocks):
        rows = rows_of(offset * (blocks * size) + b * size, size)
        send[size : 2 * size, b * D : (b + 1) * D] = down[layer, rows, :]


def pack_first(meta, qkv, out):
    half = qkv.shape[1]

    def body(meta, qkv, out, send):
        pack_attn_into(send, 2, piece_offsets(meta, 2, False)[0], qkv, out)

    return pl.pallas_call(
        body,
        grid=(1,),
        out_shape=sds((half // 2, 4 * D), BF16),
        in_specs=[
            SMEM,
            pl.BlockSpec((1, half, 3 * D), lambda i: (0, 0, 0)),
            pl.BlockSpec((1, half, D), lambda i: (0, 0, 0)),
        ],
        out_specs=pl.BlockSpec((half // 2, 4 * D), lambda i: (0, 0)),
        compiler_params=pltpu.CompilerParams(vmem_limit_bytes=LIMIT),
        name="pack_first",
    )(meta, qkv, out)


def pack_rest(meta, qkv, out, up, down, info, deps):
    half = qkv.shape[1]
    size = half // 4

    def body(meta, qkv, out, up, down, *refs):
        send_m0, send_a1, send_m1, info_out = refs[-4:]
        info_out[...] = refs[0][...]
        pack_mlp_into(send_m0, 0, piece_offsets(meta, 4, False)[0], up, down)
        pack_attn_into(send_a1, 4, piece_offsets(meta, 4, False)[0], qkv, out)
        pack_mlp_into(send_m1, 1, piece_offsets(meta, 4, True)[0], up, down)

    whole = lambda i: (0, 0, 0)
    flat = lambda i: (0, 0)
    return pl.pallas_call(
        body,
        grid=(1,),
        out_shape=(
            sds((2 * size, 4 * D), BF16),
            sds((size, 4 * D), BF16),
            sds((2 * size, 4 * D), BF16),
            sds(info.shape, F32),
        ),
        in_specs=[
            SMEM,
            pl.BlockSpec((1, half, 3 * D), lambda i: (1, 0, 0)),
            pl.BlockSpec((1, half, D), lambda i: (1, 0, 0)),
            pl.BlockSpec(up.shape, whole),
            pl.BlockSpec(down.shape, whole),
            pl.BlockSpec(info.shape, flat),
        ]
        + [ANY] * len(deps),
        out_specs=(
            pl.BlockSpec((2 * size, 4 * D), flat),
            pl.BlockSpec((size, 4 * D), flat),
            pl.BlockSpec((2 * size, 4 * D), flat),
            pl.BlockSpec(info.shape, flat),
        ),
        compiler_params=pltpu.CompilerParams(vmem_limit_bytes=LIMIT),
        name="pack_rest",
    )(meta, qkv, out, up, down, info, *deps)


def first_message(timestep, labels, ada_bias, qv_bias, out_bias, up_bias, down_bias):
    ins = (timestep, ada_bias, qv_bias, out_bias, up_bias, down_bias)

    def body(labels, *refs):
        send, held, sems = refs[6], refs[7:13], refs[13]
        copies = [pltpu.make_async_copy(refs[i], held[i], sems.at[i]) for i in range(6)]
        for copy in copies:
            copy.start()
        send[...] = jnp.zeros_like(send)
        send[4:5, D : D + 128] = jnp.full((1, 128), labels[0], jnp.int32).astype(F32)
        for copy in copies:
            copy.wait()
        time, ada, qv, out, up, down = held
        send[0:2, 0 : 3 * D] = ada[...].astype(F32)
        send[0:2, 3 * D : 4 * D] = qv[...].astype(F32)
        send[2:4, 0 : 2 * D] = up[...].astype(F32)
        send[2:4, 2 * D : 2 * D + D // 2] = out[...].astype(F32)
        send[2:4, 1024 : 1024 + D // 2] = down[...].astype(F32)
        send[4:5, 0:D] = time[...]

    return call(
        body,
        (labels,) + ins,
        [SMEM] + [HBM] * 6,
        sds((8, 4 * D), F32),
        VMEM,
        "first_message",
        scratch=[pltpu.VMEM(member.shape, member.dtype) for member in ins]
        + [pltpu.SemaphoreType.DMA((6,))],
    )


def condition_kernel(meta, own, got, table_ref, ada_ref, info_out, mine_out, send_out, table, ada, sems):
    half = D // 2
    x = meta[0]
    copy = pltpu.make_async_copy(ada_ref, ada, sems.at[0])
    copy.start()
    classes = table_ref.shape[1]
    aligned = classes // 128 * 128
    table[:, aligned:] = jnp.zeros((half, table.shape[1] - aligned), BF16)
    table[:, 0:classes] = table_ref[...]
    row = lax.broadcasted_iota(jnp.int32, (8, 1), 0)
    timestep = jnp.where(row == 0, own[4:5, 0:D], got[4:5, 0:D])
    label = jnp.where(row == 0, own[4:5, D : D + 1], got[4:5, D : D + 1])
    timestep = jnp.where(x == 0, timestep[:, :half], timestep[:, half:])
    classes = lax.broadcasted_iota(jnp.int32, (8, table.shape[1]), 1).astype(F32)
    one_hot = jnp.where(classes == label, 1.0, 0.0).astype(BF16)
    condition = timestep + dot_nt(one_hot, table[...])
    act = (condition * (1.0 / (1.0 + jnp.exp(-condition)))).astype(BF16)
    info_out[:, 0:half] = condition[0:2, :]
    info_out[:, half:256] = jnp.zeros((2, 256 - half), F32)
    info_out[:, 256:384] = jnp.broadcast_to(label[0:2, :], (2, 128))
    copy.wait()
    for layer in range(LAYERS):
        part = dot(act, ada[layer])
        mine_out[layer : layer + 1, :] = part[0:1, :]
        send_out[layer : layer + 1, :] = part[1:2, :]


def condition_step(meta, own, got, table, ada):
    return call(
        condition_kernel,
        (meta, own, got, table.T, ada),
        [SMEM] + [VMEM] * 3 + [HBM],
        (sds((2, D), F32), sds((LAYERS, 6 * D), F32), sds((LAYERS, 6 * D), F32)),
        (VMEM,) * 3,
        "condition",
        scratch=[
            pltpu.VMEM((D // 2, -(-table.shape[0] // 128) * 128), BF16),
            pltpu.VMEM(ada.shape, BF16),
            pltpu.SemaphoreType.DMA((1,)),
        ],
    )


def vectors_kernel(meta, own, got, mine_part, got_part, out):
    x = meta[0]
    low = jnp.where(x == 0, own[...], got[...])
    high = jnp.where(x == 0, got[...], own[...])
    modul = mine_part[...] + got_part[...]
    half = D // 2
    out[...] = jnp.zeros_like(out)
    for layer in range(LAYERS):
        rows = slice(layer, layer + 1)
        for member in range(6):
            side = low if member < 3 else high
            col = (member % 3) * D
            out[layer, member : member + 1, :] = (
                modul[rows, member * D : (member + 1) * D] + side[rows, col : col + D]
            )
        out[layer, 6:7, :] = low[rows, 3 * D : 4 * D]
        out[layer, 7:8, :] = high[rows, 3 * D : 4 * D]
        rows = slice(2 + layer, 3 + layer)
        for index, start in ((8, 2 * D), (9, 1024)):
            out[layer, index : index + 1, :] = jnp.concatenate(
                [low[rows, start : start + half], high[rows, start : start + half]], axis=1
            )
        for index, side, col in ((10, low, 0), (11, low, D), (12, high, 0), (13, high, D)):
            out[layer, index : index + 1, :] = side[rows, col : col + D]


def vectors_step(meta, own, got, mine_part, got_part):
    return call(
        vectors_kernel,
        (meta, own, got, mine_part, got_part),
        [SMEM] + [VMEM] * 4,
        sds((LAYERS, 16, D), F32),
        VMEM,
        "vectors",
    )


def attn_fwd_kernel(layer, far, count, *refs):
    meta, x_ref, vecs, qkv_hbm, out_hbm = refs[:5]
    pieces = refs[5 : 5 + count]
    modulated_out, qkv_out, prob_out, att_out, branch_out, middle_out = refs[5 + count : 11 + count]
    w_qkv, w_out, sems = refs[11 + count :]
    copies = attn_weight_copies(
        meta, layer, qkv_hbm, out_hbm, pieces, piece_offsets(meta, count, far), w_qkv, w_out, sems
    )
    for copy in copies:
        copy.start()
    stream = x_ref[...].astype(F32)
    normed, _ = norm_rows(stream)
    modulated = (normed * (1.0 + vecs[1:2, :]) + vecs[0:1, :]).astype(BF16)
    modulated_out[...] = modulated
    for copy in copies:
        copy.wait()
    for part in range(3):
        cols = slice(part * D, (part + 1) * D)
        value = dot(modulated, w_qkv[:, cols])
        if part == 0:
            value = value + vecs[6:7, :]
        if part == 2:
            value = value + vecs[7:8, :]
        qkv_out[:, cols] = value.astype(BF16)
    masks = head_masks()
    tokens = stream.shape[0]
    for pair in range(D // (2 * HEAD_DIM)):
        lanes = slice(pair * 2 * HEAD_DIM, (pair + 1) * 2 * HEAD_DIM)
        query = qkv_out[:, lanes]
        key = qkv_out[:, pair * 128 + D : (pair + 1) * 128 + D]
        value = qkv_out[:, pair * 128 + 2 * D : (pair + 1) * 128 + 2 * D]
        attended = None
        for member in range(2):
            head = 2 * pair + member
            scores = dot_nt(query, keep_lanes(key, masks[member])) * HEAD_DIM ** (-0.5)
            top = jnp.max(scores, axis=-1, keepdims=True)
            expo = jnp.exp(scores - top)
            prob = (expo * (1.0 / jnp.sum(expo, axis=-1, keepdims=True))).astype(BF16)
            prob_out[head * tokens : (head + 1) * tokens, :] = prob
            part = dot(prob, keep_lanes(value, masks[member]))
            attended = part if attended is None else attended + part
        att_out[:, lanes] = attended.astype(BF16)
    branch = dot(att_out[...], w_out[...]) + vecs[8:9, :]
    branch_out[...] = branch
    middle_out[...] = stream + vecs[2:3, :] * branch


def attn_fwd(layer, far, meta, x, vecs, qkv, out, pieces):
    tokens = x.shape[0]
    count = len(pieces)
    heads = D // HEAD_DIM
    return pl.pallas_call(
        functools.partial(attn_fwd_kernel, layer, far, count),
        out_shape=(
            sds((tokens, D), BF16),
            sds((tokens, 3 * D), BF16),
            sds((heads * tokens, tokens), BF16),
            sds((tokens, D), BF16),
            sds((tokens, D), F32),
            sds((tokens, D), F32),
        ),
        in_specs=[SMEM, VMEM, VMEM] + [HBM] * 2 + [ANY] * count,
        out_specs=(VMEM,) * 6,
        scratch_shapes=[
            pltpu.VMEM((D, 3 * D), BF16),
            pltpu.VMEM((D, D), BF16),
            pltpu.SemaphoreType.DMA((2 + 2 * count,)),
        ],
        compiler_params=pltpu.CompilerParams(vmem_limit_bytes=LIMIT),
        cost_estimate=pl.CostEstimate(flops=10**10, bytes_accessed=0, transcendentals=0),
        name="attn_fwd",
    )(meta, x, vecs, qkv, out, *pieces)


def mlp_fwd_kernel(layer, far, count, last, late, *refs):
    refs = refs[:3] + refs[3 + late :]
    meta, middle_ref, vecs, up_hbm, down_hbm = refs[:5]
    pieces = refs[5 : 5 + count]
    x_out, mod_out, act_out, slope_out, branch_out = refs[5 + count : 10 + count]
    w_up, w_down, sems = refs[10 + count :]
    copies = mlp_weight_copies(
        meta, layer, up_hbm, down_hbm, pieces, piece_offsets(meta, count, far), w_up, w_down, sems
    )
    for copy in copies:
        copy.start()
    middle = middle_ref[...]
    normed, _ = norm_rows(middle)
    mod_two = (normed * (1.0 + vecs[4:5, :]) + vecs[3:4, :]).astype(BF16)
    mod_out[...] = mod_two
    for copy in copies:
        copy.wait()
    branch = None
    for part in range(4):
        cols = slice(part * D, (part + 1) * D)
        pre_act = dot(mod_two, w_up[:, cols]) + vecs[10 + part : 11 + part, :]
        value, slope = gelu_parts(pre_act)
        value = value.astype(BF16)
        act_out[:, cols] = value
        slope_out[:, cols] = slope.astype(BF16)
        term = dot(value, w_down[cols, :])
        branch = term if branch is None else branch + term
    branch = branch + vecs[9:10, :]
    branch_out[...] = branch
    result = middle + vecs[5:6, :] * branch
    if last:
        live = meta[4].astype(F32)
        result = result * live
    x_out[...] = result.astype(x_out.dtype)


def mlp_fwd(layer, far, last, meta, middle, vecs, up, down, pieces, deps=()):
    tokens = middle.shape[0]
    count = len(pieces)
    return pl.pallas_call(
        functools.partial(mlp_fwd_kernel, layer, far, count, last, len(deps)),
        out_shape=(
            sds((tokens, D), BF16 if last else F32),
            sds((tokens, D), BF16),
            sds((tokens, 4 * D), BF16),
            sds((tokens, 4 * D), BF16),
            sds((tokens, D), F32),
        ),
        in_specs=[SMEM, VMEM, VMEM] + [ANY] * len(deps) + [HBM] * 2 + [ANY] * count,
        out_specs=(VMEM,) * 5,
        scratch_shapes=[
            pltpu.VMEM((D, 4 * D), BF16),
            pltpu.VMEM((4 * D, D), BF16),
            pltpu.SemaphoreType.DMA((2 + 5 * count,)),
        ],
        compiler_params=pltpu.CompilerParams(vmem_limit_bytes=LIMIT),
        cost_estimate=pl.CostEstimate(flops=10**10, bytes_accessed=0, transcendentals=0),
        name="mlp_fwd",
    )(meta, middle, vecs, *deps, up, down, *pieces)


def split_store(core, value, half, keep, send, rows):
    @pl.when(core == half)
    def _():
        keep[rows, :] = value

    @pl.when(core != half)
    def _():
        send[rows, :] = value


def mlp_bwd_kernel(layer, far, count, masked, late, *refs):
    meta, grad_ref, vecs, middle_ref, branch_ref, act_ref, slope_ref, mod_ref = refs[:8]
    refs = refs[8 + late :]
    up_hbm, down_hbm = refs[:2]
    pieces = refs[2 : 2 + count]
    keep, send, grad_out, sums_out = refs[2 + count : 6 + count]
    w_up, w_down, pre_bf, sems = refs[6 + count :]
    copies = mlp_weight_copies(
        meta, layer, up_hbm, down_hbm, pieces, piece_offsets(meta, count, far), w_up, w_down, sems
    )
    for copy in copies:
        copy.start()
    core = meta[1]
    grad = grad_ref[...].astype(F32)
    if masked:
        grad = grad * meta[4].astype(F32)
    sums_out[...] = jnp.zeros_like(sums_out)
    sums_out[5:6, :] = jnp.sum(grad * branch_ref[...], axis=0, keepdims=True)
    grad_branch = grad * vecs[5:6, :]
    sums_out[9:10, :] = jnp.sum(grad_branch, axis=0, keepdims=True)
    branch_bf = grad_branch.astype(BF16)
    half = D // 2
    for part in range(4):
        value = dot_tn(act_ref[:, part * D : (part + 1) * D], branch_bf).astype(BF16)
        base = (part // 2) * 4 * half + 2 * half
        split_store(core, value, part % 2, keep, send, slice(base, base + D))
    for copy in copies:
        copy.wait()
    mod_two = mod_ref[...]
    grad_mod = None
    for part in range(4):
        cols = slice(part * D, (part + 1) * D)
        grad_pre = dot_nt(branch_bf, w_down[cols, :]) * slope_ref[:, cols].astype(F32)
        sums_out[10 + part : 11 + part, :] = jnp.sum(grad_pre, axis=0, keepdims=True)
        pre = grad_pre.astype(BF16)
        value = dot_tn(mod_two, pre).astype(BF16)
        for side in range(2):
            base = side * 4 * half + (part % 2) * half
            split_store(
                core,
                value[side * half : (side + 1) * half, :],
                part // 2,
                keep,
                send,
                slice(base, base + half),
            )
        term = dot_nt(pre, w_up[:, cols])
        grad_mod = term if grad_mod is None else grad_mod + term
    normed, inv_dev = norm_rows(middle_ref[...])
    sums_out[3:4, :] = jnp.sum(grad_mod, axis=0, keepdims=True)
    sums_out[4:5, :] = jnp.sum(grad_mod * normed, axis=0, keepdims=True)
    grad_out[...] = grad + norm_back(grad_mod * (1.0 + vecs[4:5, :]), normed, inv_dev)


def mlp_bwd(layer, far, masked, meta, grad, vecs, kept, up, down, pieces, deps=()):
    middle, mod_two, act, slope, branch = kept
    tokens = middle.shape[0]
    count = len(pieces)
    late = len(deps)
    return pl.pallas_call(
        functools.partial(mlp_bwd_kernel, layer, far, count, masked, late),
        out_shape=(
            sds((4 * D, D), BF16),
            sds((4 * D, D), BF16),
            sds((tokens, D), F32),
            sds((16, D), F32),
        ),
        in_specs=[SMEM] + [VMEM] * 7 + [ANY] * late + [HBM] * 2 + [ANY] * count,
        out_specs=(VMEM,) * 4,
        scratch_shapes=[
            pltpu.VMEM((D, 4 * D), BF16),
            pltpu.VMEM((4 * D, D), BF16),
            pltpu.VMEM((16, D), BF16),
            pltpu.SemaphoreType.DMA((2 + 5 * count,)),
        ],
        compiler_params=pltpu.CompilerParams(vmem_limit_bytes=LIMIT),
        cost_estimate=pl.CostEstimate(flops=10**10, bytes_accessed=0, transcendentals=0),
        name="mlp_bwd",
    )(meta, grad, vecs, middle, branch, act, slope, mod_two, *deps, up, down, *pieces)


def attn_bwd_kernel(layer, far, count, extra, late, *refs):
    meta, grad_ref, vecs, x_ref, modulated_ref, qkv_ref, prob_ref, att_ref, branch_ref, part_sums = refs[:10]
    refs = refs[:10] + refs[10 + late :]
    qkv_hbm, out_hbm = refs[10:12]
    pieces = refs[12 : 12 + count]
    keep, send, grad_out, sums_out = refs[12 + count : 16 + count]
    w_qkv, w_out, ga_ref, proj_ref, sems = refs[16 + count :]
    copies = attn_weight_copies(
        meta, layer, qkv_hbm, out_hbm, pieces, piece_offsets(meta, count, far), w_qkv, w_out, sems
    )
    for copy in copies:
        copy.start()
    core = meta[1]
    half = D // 2
    tokens = grad_ref.shape[0]
    sums = {}
    grad = grad_ref[...]
    sums[2] = jnp.sum(grad * branch_ref[...], axis=0, keepdims=True)
    grad_battn = grad * vecs[2:3, :]
    sums[8] = jnp.sum(grad_battn, axis=0, keepdims=True)
    battn_bf = grad_battn.astype(BF16)

    def store(value, block):
        for side in range(2):
            base = side * 2 * half + (block % 2) * half
            split_store(
                core,
                value[side * half : (side + 1) * half, :],
                block // 2,
                keep,
                send,
                slice(base, base + half),
            )

    store(dot_tn(att_ref[...], battn_bf).astype(BF16), 3)
    for copy in copies:
        copy.wait()
    ga_ref[...] = dot_nt(battn_bf, w_out[...]).astype(BF16)
    masks = head_masks()
    grad_q_sums, grad_v_sums = [], []
    for pair in range(D // (2 * HEAD_DIM)):
        lanes = slice(pair * 128, (pair + 1) * 128)
        query = qkv_ref[:, lanes]
        key = qkv_ref[:, pair * 128 + D : (pair + 1) * 128 + D]
        value = qkv_ref[:, pair * 128 + 2 * D : (pair + 1) * 128 + 2 * D]
        grad_att = ga_ref[:, lanes]
        grad_q = grad_k = grad_v = None
        for member in range(2):
            head = 2 * pair + member
            mask = masks[member]
            prob_bf = prob_ref[head * tokens : (head + 1) * tokens, :]
            prob = prob_bf.astype(F32)
            grad_prob = dot_nt(grad_att, keep_lanes(value, mask))
            term_v = dot_tn(prob_bf, keep_lanes(grad_att, mask))
            weighted = prob * grad_prob
            row_dot = jnp.sum(weighted, axis=-1, keepdims=True)
            grad_scores = ((weighted - prob * row_dot) * HEAD_DIM ** (-0.5)).astype(BF16)
            term_q = dot(grad_scores, keep_lanes(key, mask))
            term_k = dot_tn(grad_scores, keep_lanes(query, mask))
            grad_q = term_q if grad_q is None else grad_q + term_q
            grad_k = term_k if grad_k is None else grad_k + term_k
            grad_v = term_v if grad_v is None else grad_v + term_v
        grad_q_sums.append(jnp.sum(grad_q, axis=0, keepdims=True))
        grad_v_sums.append(jnp.sum(grad_v, axis=0, keepdims=True))
        proj_ref[:, lanes] = grad_q.astype(BF16)
        proj_ref[:, pair * 128 + D : (pair + 1) * 128 + D] = grad_k.astype(BF16)
        proj_ref[:, pair * 128 + 2 * D : (pair + 1) * 128 + 2 * D] = grad_v.astype(BF16)
    sums[6] = jnp.concatenate(grad_q_sums, axis=1)
    sums[7] = jnp.concatenate(grad_v_sums, axis=1)
    modulated = modulated_ref[...]
    for block in range(3):
        store(dot_tn(modulated, proj_ref[:, block * D : (block + 1) * D]).astype(BF16), block)
    grad_mod = dot_nt(proj_ref[...], w_qkv[...])
    normed, inv_dev = norm_rows(x_ref[...].astype(F32))
    sums[0] = jnp.sum(grad_mod, axis=0, keepdims=True)
    sums[1] = jnp.sum(grad_mod * normed, axis=0, keepdims=True)
    grad_out[...] = grad + norm_back(grad_mod * (1.0 + vecs[1:2, :]), normed, inv_dev)
    row = lax.broadcasted_iota(jnp.int32, (16, 1), 0)
    total = part_sums[...]
    for index, value in sums.items():
        total = jnp.where(row == index, value, total)
    total = total.astype(BF16)
    sums_out[...] = total
    if extra:
        send[4 * half : 4 * half + 16, :] = total


def attn_bwd(layer, far, extra, meta, grad, vecs, x, kept, part_sums, qkv, out, pieces, deps=()):
    modulated, qkv_val, prob, att, branch = kept
    tokens = x.shape[0]
    count = len(pieces)
    return pl.pallas_call(
        functools.partial(attn_bwd_kernel, layer, far, count, extra, len(deps)),
        out_shape=(
            sds((2 * D, D), BF16),
            sds((2 * D + extra, D), BF16),
            sds((tokens, D), F32),
            sds((16, D), BF16),
        ),
        in_specs=[SMEM] + [VMEM] * 9 + [ANY] * len(deps) + [HBM] * 2 + [ANY] * count,
        out_specs=(VMEM,) * 4,
        scratch_shapes=[
            pltpu.VMEM((D, 3 * D), BF16),
            pltpu.VMEM((D, D), BF16),
            pltpu.VMEM((tokens, D), BF16),
            pltpu.VMEM((tokens, 3 * D), BF16),
            pltpu.SemaphoreType.DMA((2 + 2 * count,)),
        ],
        compiler_params=pltpu.CompilerParams(vmem_limit_bytes=LIMIT),
        cost_estimate=pl.CostEstimate(flops=10**10, bytes_accessed=0, transcendentals=0),
        name="attn_bwd",
    )(meta, grad, vecs, x, modulated, qkv_val, prob, att, branch, part_sums, *deps, qkv, out, *pieces)


def add_rows(a, a_rows, b, b_rows):
    return (a[a_rows, :].astype(F32) + b[b_rows, :].astype(F32)).astype(BF16)


def first_split(meta, keep, got, sums, deps):
    half = keep.shape[0] // 2
    extra = 0 if sums is None else sums.shape[0]

    def body(meta, keep, got, *refs):
        mine_out, send_out = refs[-2:]
        x = meta[0]
        mine, other = rows_of(x * half, half), rows_of((1 - x) * half, half)
        mine_out[...] = add_rows(keep, mine, got, mine)
        send_out[0:half, :] = add_rows(keep, other, got, other)
        if extra:
            own, far = refs[0][...], got[2 * half : 2 * half + extra, :]
            lanes = D // 2
            low = jnp.concatenate([own[:, :lanes], far[:, :lanes]], axis=1)
            high = jnp.concatenate([own[:, lanes:], far[:, lanes:]], axis=1)
            send_out[half : half + extra, :] = jnp.where(meta[1] == 0, low, high)

    rides = () if sums is None else (sums,)
    return call(
        body,
        (meta, keep, got) + rides,
        [SMEM] + [VMEM] * (2 + len(rides)),
        (sds((half, D), BF16), sds((half + extra, D), BF16)),
        (VMEM, VMEM),
        "first_split",
        deps=deps,
    )


def next_split(axis, meta, keep, sent, got, deps):
    whole = keep.shape[0]
    half = whole // 2
    extra = got.shape[0] - whole

    def body(meta, keep, sent, got, mine_out, send_out):
        place = meta[axis]
        mine, other = rows_of(place * half, half), rows_of((1 - place) * half, half)
        mine_out[...] = add_rows(keep, mine, got, mine)
        send_out[0:half, :] = add_rows(keep, other, got, other)
        if extra:
            send_out[half : half + extra, :] = sent[whole : whole + extra, :]
            send_out[half + extra : half + 2 * extra, :] = got[whole : whole + extra, :]

    return call(
        body,
        (meta, keep, sent, got),
        [SMEM] + [VMEM] * 3,
        (sds((half, D), BF16), sds((half + 2 * extra, D), BF16)),
        (VMEM, VMEM),
        "next_split",
        deps=deps,
    )


def add_join(keep, sent, got, rows, last, deps):
    extra = got.shape[0] - rows

    def body(keep, sent, got, *outs):
        everything = slice(0, rows)
        outs[0][0:rows, :] = add_rows(keep, everything, got, everything)
        if extra:
            out, start = (outs[1], 0) if last else (outs[0], rows)
            out[start : start + extra, :] = sent[rows : rows + extra, :]
            out[start + extra : start + 2 * extra, :] = got[rows : rows + extra, :]

    out_shape = (sds((rows + (0 if last else 2 * extra), D), BF16),)
    if last and extra:
        out_shape = out_shape + (sds((2 * extra, D), BF16),)
    return call(
        body,
        (keep, sent, got),
        [VMEM] * 3,
        out_shape,
        (VMEM,) * len(out_shape),
        "add_join",
        deps=deps,
    )


def join(meta, mine, got, deps):
    rows = mine.shape[0]

    def body(meta, mine, got, out):
        low = meta[5]
        out[rows_of(low * rows, rows), :] = mine[...]
        out[rows_of((1 - low) * rows, rows), :] = got[...]

    return call(
        body, (meta, mine, got), [SMEM, VMEM, VMEM], sds((2 * rows, D), BF16), VMEM, "join", deps=deps
    )


def gather_rows(meta, refs, scratch):
    core, y = meta[1], meta[2]
    rows = refs[0].shape[0]
    for index, (c, v) in enumerate(((core, y), (core, 1 - y), (1 - core, y), (1 - core, 1 - y))):
        scratch[c, rows_of(v * rows, rows), :] = refs[index][...]


def attn_result(layer, meta, parts, before, deps):
    half = D // 2

    def body(meta, *refs):
        qkv_out, out_out, scratch = refs[-3:]
        gather_rows(meta, refs[:4], scratch)
        for block in range(4):
            value = scratch[block // 2, (block % 2) * half : (block % 2 + 1) * half, :].astype(F32)
            if block < 3:
                qkv_out[0, :, block * D : (block + 1) * D] = value
            else:
                out_out[0, :, :] = value

    return result_call(
        body,
        (meta, *parts),
        before,
        ((LAYERS, half, 3 * D), (LAYERS, half, D)),
        layer,
        (2, 2 * half, D),
        "attn_result",
        deps,
    )


def mlp_result(layer, meta, parts, before, deps):
    half = D // 2

    def body(meta, *refs):
        up_out, down_out, scratch = refs[-3:]
        gather_rows(meta, refs[:4], scratch)
        for block in range(4):
            value = scratch[block // 2, (block % 2) * half : (block % 2 + 1) * half, :].astype(F32)
            up_out[0, :, block * D : (block + 1) * D] = value
        for core in range(2):
            down_out[0, core * D : (core + 1) * D, :] = scratch[core, D : 2 * D, :].astype(F32)

    return result_call(
        body,
        (meta, *parts),
        before,
        ((LAYERS, half, 4 * D), (LAYERS, 2 * D, D)),
        layer,
        (2, 2 * D, D),
        "mlp_result",
        deps,
    )


def result_call(body, ins, before, shapes, layer, scratch, name, deps):
    given, count = len(ins), len(shapes)

    def kernel(*refs):
        rest = refs[given + len(before) + len(deps) :]
        outs, blocks, held, sems = rest[:count], rest[count : 2 * count], rest[-2], rest[-1]
        body(*refs[:given], *blocks, held)
        copies = [
            pltpu.make_async_copy(blocks[i], outs[i].at[pl.ds(layer, 1)], sems.at[i])
            for i in range(count)
        ]
        for copy in copies:
            copy.start()
        for copy in copies:
            copy.wait()

    return pl.pallas_call(
        kernel,
        out_shape=tuple(sds(shape, F32) for shape in shapes),
        in_specs=[SMEM] + [VMEM] * (given - 1) + [HBM] * len(before) + [ANY] * len(deps),
        out_specs=(HBM,) * count,
        scratch_shapes=[pltpu.VMEM((1,) + shape[1:], F32) for shape in shapes]
        + [pltpu.VMEM(scratch, BF16), pltpu.SemaphoreType.DMA((count,))],
        input_output_aliases={given + index: index for index in range(len(before))},
        compiler_params=pltpu.CompilerParams(vmem_limit_bytes=LIMIT),
        cost_estimate=pl.CostEstimate(flops=10**10, bytes_accessed=0, transcendentals=0),
        name=name,
    )(*ins, *before, *deps)


def silu_bf16(condition):
    return (condition * (1.0 / (1.0 + jnp.exp(-condition)))).astype(BF16)


def ada_result(layer, meta, info, rides, far, ada_weight, before, deps):
    slots = rides.shape[0] // 16
    half = D // 2

    def kernel(meta, info, rides, far, ada_hbm, *refs):
        ada_hbm_out, cond_out, sums_out, own_f32, far_f32, ada, ada_out, sems = refs[-8:]
        load = pltpu.make_async_copy(ada_hbm.at[pl.ds(layer, 1)], ada, sems.at[0])
        load.start()
        for block in range(D // 128):
            lanes = slice(block * 128, (block + 1) * 128)
            own_f32[block, :, :] = rides[:, lanes].astype(F32)
            far_f32[block, :, :] = far[:, lanes].astype(F32)
        act = silu_bf16(info[:, 0:half])
        first = meta[1] == 0
        grad_cond = jnp.zeros((2 * slots, half), F32)
        load.wait()
        sums_out[...] = jnp.zeros_like(sums_out)
        for row in range(14):
            mine, other = (
                jnp.concatenate(
                    [held[block, pl.ds(row, slots, stride=16), :] for block in range(D // 128)], axis=1
                )
                for held in (own_f32, far_f32)
            )
            vectors = []
            for one, two in (
                (mine[:, :half], other[:, half:]),
                (mine[:, half:], other[:, :half]),
            ):
                vectors.append(
                    jnp.concatenate([jnp.where(first, one, two), jnp.where(first, two, one)], axis=1)
                )
            both = jnp.concatenate(vectors, axis=0)
            sums_out[row : row + 1, :] = jnp.sum(both, axis=0, keepdims=True)
            if row < 6:
                cols = slice(row * D, (row + 1) * D)
                both = both.astype(BF16)
                ada_out[0, :, cols] = dot_tn(act, both)
                grad_cond = grad_cond + dot_nt(both, ada[0, :, cols])
        store = pltpu.make_async_copy(ada_out, ada_hbm_out.at[pl.ds(layer, 1)], sems.at[1])
        store.start()
        cond_out[...] = grad_cond
        store.wait()

    shape = ada_weight.shape
    return pl.pallas_call(
        kernel,
        out_shape=(sds(shape, F32), sds((2 * slots, half), F32), sds((16, D), F32)),
        in_specs=[SMEM, VMEM, VMEM, VMEM] + [HBM] * (1 + len(before)) + [ANY] * len(deps),
        out_specs=(HBM, VMEM, VMEM),
        scratch_shapes=[pltpu.VMEM((D // 128, 16 * slots, 128), F32)] * 2
        + [
            pltpu.VMEM((1,) + shape[1:], BF16),
            pltpu.VMEM((1,) + shape[1:], F32),
            pltpu.SemaphoreType.DMA((2,)),
        ],
        input_output_aliases={5: 0} if before else {},
        compiler_params=pltpu.CompilerParams(vmem_limit_bytes=LIMIT),
        cost_estimate=pl.CostEstimate(flops=10**10, bytes_accessed=0, transcendentals=0),
        name="ada_result",
    )(meta, info, rides, far, ada_weight, *before, *deps)


def condition_result(meta, info, conds, sums, classes, deps):
    half = D // 2

    def body(meta, info, cond0, cond1, sums0, sums1, *outs):
        table, mine, send, ada, qv, out, up, down = outs
        condition = info[:, 0:half]
        sigmoid = 1.0 / (1.0 + jnp.exp(-condition))
        grads = (cond0[...] + cond1[...]) * sigmoid * (1.0 + condition * (1.0 - sigmoid))
        mine[...] = grads[0:1, :]
        send[...] = grads[1:2, :]
        labels = info[:, 256:257]
        count = -(-classes // 128) * 128
        numbers = lax.broadcasted_iota(jnp.int32, (info.shape[0], count), 1).astype(F32)
        one_hot = jnp.where(numbers == labels, 1.0, 0.0)
        total = lax.dot_general(
            grads,
            one_hot,
            (((0,), (0,)), ((), ())),
            precision=lax.Precision.HIGHEST,
            preferred_element_type=F32,
        )
        table[...] = total[:, 0:classes]
        low = meta[0] == 0
        for layer, rows in enumerate((sums0, sums1)):
            at = slice(layer, layer + 1)

            def pick(one, two):
                return jnp.where(low, rows[one : one + 1, :], rows[two : two + 1, :])

            for index in range(3):
                ada[at, index * D : (index + 1) * D] = pick(index, index + 3)
            qv[at, :] = pick(6, 7)
            for index in range(2):
                up[at, index * D : (index + 1) * D] = pick(10 + index, 12 + index)
            for ref, row in ((out, 8), (down, 9)):
                value = rows[row : row + 1, :]
                ref[at, :] = jnp.where(low, value[:, :half], value[:, half:])

    shapes = (
        (half, classes),
        (1, half),
        (1, half),
        (LAYERS, 3 * D),
        (LAYERS, D),
        (LAYERS, half),
        (LAYERS, 2 * D),
        (LAYERS, half),
    )
    return call(
        body,
        (meta, info, *conds, *sums),
        [SMEM] + [VMEM] * 5,
        tuple(sds(shape, F32) for shape in shapes),
        (VMEM,) * len(shapes),
        "condition_result",
        deps=deps,
    )


def both_halves(meta, mine, other):
    def body(meta, mine, other, out):
        low = meta[0] == 0
        a, b = mine[...], other[...]
        out[...] = jnp.concatenate([jnp.where(low, a, b), jnp.where(low, b, a)], axis=1)

    return call(
        body, (meta, mine, other), [SMEM, VMEM, VMEM], sds((1, D), F32), VMEM, "both_halves"
    )


def on_device(reps, *arguments):
    (
        latents,
        timestep_embed,
        labels,
        counts,
        class_table,
        ada_weight,
        ada_bias,
        qkv_weight,
        qv_bias,
        out_weight,
        out_bias,
        up_weight,
        up_bias,
        down_weight,
        down_bias,
        cotangent,
    ) = arguments
    half = D // 2
    rep = lax.axis_index("rep")
    x = lax.axis_index("shard")
    core, y, z = rep & 1, (rep >> 1) & 1, (rep >> 2) & 3
    meta = jnp.stack([x, core, y, z, jnp.minimum(counts[0], 1), z & 1]).astype(jnp.int32)

    def over_x(value):
        return lax.ppermute(value, "shard", [(0, 1), (1, 0)])

    def over_rep(value, distance):
        return lax.ppermute(value, "rep", [(r, r ^ distance) for r in range(reps)])

    CORE, Y, Z = 1, 2, 4

    first = first_message(timestep_embed, labels, ada_bias, qv_bias, out_bias, up_bias, down_bias)
    got_first = over_x(first)
    send_a0 = pack_first(meta, qkv_weight, out_weight)
    classes = class_table.shape[0]
    info, mine_part, send_part = condition_step(meta, first, got_first, class_table, ada_weight)
    send_m0, send_a1, send_m1, info = pack_rest(
        meta, qkv_weight, out_weight, up_weight, down_weight, info, (send_part,)
    )

    def fetch(send, distance):
        got = over_x(send)
        if distance is None:
            return [got, over_rep(got, CORE)]
        next_got = over_rep(got, distance)
        return [got, next_got, over_rep(got, CORE), over_rep(next_got, CORE)]

    pieces_a0 = fetch(send_a0, None)
    vecs_all = vectors_step(meta, first, got_first, mine_part, over_x(send_part))
    pieces_m0 = fetch(send_m0, Y)
    pieces_a1 = fetch(send_a1, Y)
    pieces_m1 = fetch(send_m1, Z)
    vecs = [vecs_all[layer] for layer in range(LAYERS)]

    distances = [Z]
    while 2 * distances[-1] < reps:
        distances.append(2 * distances[-1])
    for distance in [Y] + distances + [CORE]:
        info = jnp.concatenate([info, over_rep(info, distance)], axis=0)

    stream = latents[0]
    attn_weights = (qkv_weight, out_weight)
    mlp_weights = (up_weight, down_weight)
    *kept_a0, middle0 = attn_fwd(0, False, meta, stream, vecs[0], *attn_weights, pieces_a0)
    stream1, *kept_m0 = mlp_fwd(
        0, False, False, meta, middle0, vecs[0], *mlp_weights, pieces_m0, (info,)
    )
    *kept_a1, middle1 = attn_fwd(1, False, meta, stream1, vecs[1], *attn_weights, pieces_a1)
    activations, *kept_m1 = mlp_fwd(1, True, True, meta, middle1, vecs[1], *mlp_weights, pieces_m1)

    last = [activations]

    def deps():
        return (last[0],)

    def ran(result):
        last[0] = result[-1] if isinstance(result, (tuple, list)) else result
        return result

    def reduce_chunk(keep, sent, sums):
        got = over_rep(sent, CORE)
        yield
        keep, sent = ran(first_split(meta, keep, got, sums, deps()))
        got = over_x(sent)
        yield
        keep, sent = ran(next_split(2, meta, keep, sent, got, deps()))
        got = over_rep(sent, Y)
        yield
        steps = distances
        if sums is None:
            keep, sent = ran(next_split(5, meta, keep, sent, got, deps()))
            got = over_rep(sent, Z)
            steps = distances[1:]
            yield
        rows = keep.shape[0]
        for distance in steps:
            (sent,) = ran(add_join(keep, sent, got, rows, False, deps()))
            keep = sent
            got = over_rep(sent, distance)
            yield
        mine, *rides = ran(add_join(keep, sent, got, rows, True, deps()))
        if sums is None:
            got = over_rep(mine, Z)
            yield
            mine = ran(join(meta, mine, got, deps()))
        next_mine = over_rep(mine, Y)
        result = (mine, next_mine, over_rep(mine, CORE), over_rep(next_mine, CORE))
        if rides:
            rides = (rides[0], over_rep(rides[0], CORE))
        yield result, rides

    def advance(chunk, times=1):
        result = None
        for _ in range(times):
            result = next(chunk)
        return result

    more = len(distances) - 1

    keep, sent, grad, part_sums = mlp_bwd(
        1, True, True, meta, cotangent[0], vecs[1], (middle1, *kept_m1), *mlp_weights, pieces_m1, deps()
    )
    m1 = reduce_chunk(keep, sent, None)
    advance(m1)
    keep, sent, grad, sums1 = ran(
        attn_bwd(
            1, False, 16, meta, grad, vecs[1], stream1, kept_a1, part_sums, *attn_weights, pieces_a1
        )
    )
    a1 = reduce_chunk(keep, sent, sums1)
    advance(a1)
    advance(m1)
    keep, sent, grad, part_sums = ran(
        mlp_bwd(
            0, False, False, meta, grad, vecs[0], (middle0, *kept_m0), *mlp_weights, pieces_m0, deps()
        )
    )
    m0 = reduce_chunk(keep, sent, None)
    advance(m0)
    advance(a1)
    keep, sent, grad_stream, sums0 = ran(
        attn_bwd(
            0,
            False,
            16,
            meta,
            grad,
            vecs[0],
            stream,
            kept_a0,
            part_sums,
            *attn_weights,
            pieces_a0,
            deps(),
        )
    )
    a0 = reduce_chunk(keep, sent, sums0)
    advance(a0)
    for chunk in (m1, m0, a1, a0, m1, a1):
        advance(chunk)
    advance(m1, more)
    advance(m0)
    advance(a1, more)
    advance(a0)
    advance(m1)
    advance(m0)
    advance(a0)
    result_m1, _ = advance(m1)
    advance(m0, more)
    result_a1, rides1 = advance(a1)
    advance(a0, more)
    ada_grad, cond1, sums1 = ran(ada_result(1, meta, info, *rides1, ada_weight, (), deps()))
    mlp_grads = ran(mlp_result(1, meta, result_m1, (), deps()))
    advance(m0)
    result_m0, _ = advance(m0)
    result_a0, rides0 = advance(a0)
    attn_grads = ran(attn_result(1, meta, result_a1, (), deps()))
    ada_grad, cond0, sums0 = ran(ada_result(0, meta, info, *rides0, ada_weight, (ada_grad,), deps()))
    table_grad, mine_cond, send_cond, *bias_grads = ran(
        condition_result(meta, info, (cond0, cond1), (sums0, sums1), classes, deps())
    )
    other_cond = over_x(send_cond)
    up_grad, down_grad = ran(mlp_result(0, meta, result_m0, mlp_grads, deps()))
    qkv_grad, out_grad = ran(attn_result(0, meta, result_a0, attn_grads, deps()))
    cond_grad = both_halves(meta, mine_cond, other_cond)
    ada_b, qv_b, out_b, up_b, down_b = bias_grads

    return (
        activations[None],
        grad_stream[None],
        cond_grad,
        table_grad.T,
        ada_grad,
        ada_b,
        qkv_grad,
        qv_b,
        out_grad,
        out_b,
        up_grad,
        up_b,
        down_grad,
        down_b,
    )


def solution(mesh):
    reps = mesh.shape["rep"]
    both = ("rep", "shard")
    in_specs = (
        P(both, None, None),
        P(both, None),
        P(both),
        P(both),
        P(None, "shard"),
    ) + (P(None, "shard", None), P(None, "shard")) * 5 + (P(both, None, None),)
    out_specs = (
        P(both, None, None),
        P(both, None, None),
        P(both, None),
        P(None, "shard"),
    ) + (P(None, "shard", None), P(None, "shard")) * 5
    return jax.shard_map(
        functools.partial(on_device, reps),
        mesh=mesh,
        in_specs=in_specs,
        out_specs=out_specs,
        check_vma=False,
    )
```

time: 264 us -> 193 us (0.73)
  Pallas kernels: 98.4 us -> 70.3 us
  starting transfers between devices: 72.5 us -> 49.2 us
  other arithmetic: 9.8 us -> 0.03 us
  local copies, waits for them, and re-layouts: 26.4 us -> 21.4 us
  matrix products: 4.99 us -> 0 us
    pallas_call x28 -> x37, Pallas kernels: 65.2 us -> 38.2 us  [the longest x27 14.3 us: call(): pl.pallas_call(kernel, out_shape=out_shape, in_specs=list(in_specs) + [AN...]
    ppermute x59 -> x46, starting transfers between devices: 59.2 us -> 34.6 us  [over_rep(): return lax.ppermute(value, 'rep', [(r, r ^ distance) for r in range(reps)])]
    unnamed x68, local copies, waits for them, and re-layouts: 5.17 us -> 16.8 us
    reshape x10 -> x0, local copies, waits for them, and re-layouts: 6.37 us -> none  [the longest x5 3.61 us: on_device(): member.reshape(-1)]
    dot_general x7 -> x0, matrix products: 4.99 us -> none  [the longest x1 1.81 us: on_device(): jnp.einsum('nk,lkm->nlm', act_pair, ada_weight, preferred_element_type=F32)]
    select_n x5 -> x0, other arithmetic: 4.85 us -> none  [the longest x4 4.22 us: on_device(): jnp.where(x == 0, jnp.concatenate([member, other], axis=1), jnp.concatena...]
    ppermute x11, waiting for transfers between devices: 8.86 us -> 13.4 us  [over_x(): return lax.ppermute(value, 'shard', [(0, 1), (1, 0)])]
    slice x16 -> x0, local copies, waits for them, and re-layouts: 3.6 us -> none  [the longest x4 1.52 us: on_device(): other = got_first[offset:offset + size].reshape(member.shape)]
  transfers between devices with their start and end apart: 70 -> 57, of which waited for: 15 -> 19; matrix products, arithmetic and copies ran while one was open for 13% -> 2% of each run, Pallas kernels for 32% -> 28%
where the time goes in v2:
time: 193 us; the launch traced here: 192 us
  Pallas kernels  70.3 us (36%)
  starting transfers between devices  49.2 us (25%)
  waiting for transfers between devices  48.2 us (25%)
  local copies, waits for them, and re-layouts  21.4 us (11%)
  between operations  2.71 us (1%)
    ppermute x46, waiting for transfers between devices, over_rep(): return lax.ppermute(value, 'rep', [(r, r ^ distance) for r in range(reps)])  34.8 us
    ppermute x46, starting transfers between devices, over_rep(): return lax.ppermute(value, 'rep', [(r, r ^ distance) for r in range(reps)])  34.6 us
    unnamed x68, local copies, waits for them, and re-layouts  16.8 us
    ppermute x11, starting transfers between devices, over_x(): return lax.ppermute(value, 'shard', [(0, 1), (1, 0)])  14.6 us
    pallas_call x27, Pallas kernels, call(): pl.pallas_call(kernel, out_shape=out_shape, in_specs=list(in_specs) + [AN...  14.3 us
    ppermute x11, waiting for transfers between devices, over_x(): return lax.ppermute(value, 'shard', [(0, 1), (1, 0)])  13.4 us
    pallas_call x2, Pallas kernels, mlp_bwd(): pl.pallas_call(functools.partial(mlp_bwd_kernel, layer, far, count, maske...  12.3 us
    pallas_call x2, Pallas kernels, attn_bwd(): pl.pallas_call(functools.partial(attn_bwd_kernel, layer, far, count, extr...  11.5 us
  transfers between devices with their start and end apart: 57, of which 19 were waited for; matrix products, arithmetic and copies ran while one was open for 2% of the time, Pallas kernels for 28%

profile of v2, /device:TPU:0, one launch (start us, length us, event | category | flops | bytes accessed | tf_op | source)
XLA Modules:
  0.0 191.9 jit_solution(5237688128587552386)
XLA Ops:
  5.5 3.0 %collective-permute-start = (f32[8,1536]{1,0:T(8,128)S(1)}, f32[8,1536]{1,0:T(8,128)S(1)}, u32[]{:S(2)}, u32[]{:S(2)}) collective-permute-start(f32[8,1536]{1,0:T(8,128)S(1)} %first_message.1.refs_1_), channel_id=1, source_target_pairs={{0,1},{1,0},{2,3},{3,2},{4,5},{5,4},{6,7},{7,6},{8,9},{9,8},{10,11... | collective-permute-start | bytes 147464 | tf_op jit(solution)/shard_map/ppermute | solution.py:1032
  11.2 1.5 copy-done.9
  12.7 1.0 copy-done.11
  15.3 1.5 condition.1
  17.2 1.4 pack_rest.1
  18.6 2.0 %collective-permute-start.4 = (f32[2,384]{1,0:T(2,128)S(1)}, f32[2,384]{1,0:T(2,128)S(1)}, u32[]{:S(2)}, u32[]{:S(2)}) collective-permute-start(f32[2,384]{1,0:T(2,128)S(1)} %get-tuple-element.109), channel_id=1, source_target_pairs={{0,4},{2,6},{4,0},{6,2},{8,12},{10,14},{12,8},{14,10},{16,20},{18,... | collective-permute-start | bytes 9224 | tf_op jit(solution)/shard_map/ppermute | solution.py:1035
  20.6 1.6 collective-permute-done.4
  22.2 2.1 %collective-permute-start.5 = (f32[4,384]{1,0:T(4,128)S(1)}, f32[4,384]{1,0:T(4,128)S(1)}, u32[]{:S(2)}, u32[]{:S(2)}) collective-permute-start(f32[4,384]{1,0:T(4,128)S(1)} %pad_maximum_fusion.2), channel_id=1, source_target_pairs={{0,8},{2,10},{4,12},{6,14},{8,0},{10,2},{12,4},{14,6},{16,24},{18,... | collective-permute-start | bytes 18440 | tf_op jit(solution)/shard_map/ppermute | solution.py:1035
  24.9 1.6 collective-permute-start.2
  27.0 1.5 collective-permute-start.8
  29.0 1.5 collective-permute-start.16
  30.5 4.8 %collective-permute-done.1.refs_4_ = f32[2,2304]{1,0:T(2,128)S(1)} collective-permute-done((f32[2,2304]{1,0:T(2,128)S(1)}, f32[2,2304]{1,0:T(2,128)S(1)}, u32[]{:S(2)}, u32[]{:S(2)}) %collective-permute-start.1) | collective-permute-done | bytes 18464 | tf_op jit(solution)/shard_map/ppermute | solution.py:1032
  35.3 2.6 %collective-permute-start.6 = (f32[8,384]{1,0:T(8,128)S(1)}, f32[8,384]{1,0:T(8,128)S(1)}, u32[]{:S(2)}, u32[]{:S(2)}) collective-permute-start(f32[8,384]{1,0:T(8,128)S(1)} %pad_maximum_fusion.1), channel_id=1, source_target_pairs={{0,16},{2,18},{4,20},{6,22},{8,24},{10,26},{12,28},{14,30},{16,0},... | collective-permute-start | bytes 36872 | tf_op jit(solution)/shard_map/ppermute | solution.py:1035
  38.6 3.1 %collective-permute-done.8.refs_6_.refs_11_ = bf16[96,1536]{1,0:T(8,128)(2,1)} collective-permute-done((bf16[96,1536]{1,0:T(8,128)(2,1)S(1)}, bf16[96,1536]{1,0:T(8,128)(2,1)}, u32[]{:S(2)}, u32[]{:S(2)}) %collective-permute-start.8) | collective-permute-done | bytes 294944 | tf_op jit(solution)/shard_map/ppermute | solution.py:1032
  41.7 1.5 collective-permute-start.9
  44.7 3.9 %concatenate.18.refs_3_.info.refs_1_ = f32[32,384]{1,0:T(8,128)} concatenate(f32[2,384]{1,0:T(2,128)S(1)} %get-tuple-element.109, f32[2,384]{1,0:T(2,128)} %copy-done.32, f32[4,384]{1,0:T(4,128)S(1)} %collective-permute-done.5, f32[8,384]{1,0:T(8,128)} %copy-done.33, f32[16,384]{1,0:T(8,128)} %collective-permute-done.7), dimensions={0} | concatenate | bytes 98304 | tf_op jit(solution)/shard_map/concatenate | solution.py:1066
  50.6 0.9 copy-done.13
  51.5 4.2 %attn_fwd.2 = (bf16[256,384]{1,0:T(8,128)(2,1)S(1)}, bf16[256,1152]{1,0:T(8,128)(2,1)S(1)}, bf16[1536,256]{1,0:T(8,128)(2,1)S(1)}, bf16[256,384]{1,0:T(8,128)(2,...) custom-call(s32[6]{0:T(128)S(1)} %stack.24.refs_0_.meta, bf16[256,384]{1,0:T(8,128)(2,1)S(1)} %bitcast.17, ...), custom_call_target="tpu_custom_call" | custom-call | flops 10000000000 | tf_op jit(solution)/shard_map/attn_fwd/pallas_call | solution.py:398
  56.2 2.6 %collective-permute-done.17.refs_6_.refs_12_ = bf16[96,1536]{1,0:T(8,128)(2,1)S(1)} collective-permute-done((bf16[96,1536]{1,0:T(8,128)(2,1)}, bf16[96,1536]{1,0:T(8,128)(2,1)S(1)}, u32[]{:S(2)}, u32[]{:S(2)}) %collective-permute-start.17) | collective-permute-done | bytes 294944 | tf_op jit(solution)/shard_map/ppermute | solution.py:1035
  58.9 4.0 %mlp_fwd.2 = (f32[256,384]{1,0:T(8,128)S(1)}, bf16[256,384]{1,0:T(8,128)(2,1)S(1)}, bf16[256,1536]{1,0:T(8,128)(2,1)S(1)}, bf16[256,1536]{1,0:T(8,128)(2,1)S(1)}, f32[256,384]{1,0:T(8,128)S(1)}) custom-call(s32[6]{0:T(128)S(1)} %stack.24.refs_0_.meta, f32[256,384]{1,0:T(8,128)S(1)} %get-tuple-element.107.refs_1_.refs_3_, f32[16,384]{1,0:T(8,128)S(1)} %copy-done.6, ...), custom_call_target="tpu_custom_call" | custom-call | flops 10000000000 | tf_op jit(solution)/shard_map/mlp_fwd/pallas_call | solution.py:460
  62.9 4.0 %attn_fwd.3 = (bf16[256,384]{1,0:T(8,128)(2,1)S(1)}, bf16[256,1152]{1,0:T(8,128)(2,1)S(1)}, bf16[1536,256]{1,0:T(8,128)(2,1)S(1)}, bf16[256,384]{1,0:T(8,128)(2,...) custom-call(s32[6]{0:T(128)S(1)} %stack.24.refs_0_.meta, f32[256,384]{1,0:T(8,128)S(1)} %get-tuple-element.111.refs_1_.refs_3_, ...), custom_call_target="tpu_custom_call" | custom-call | flops 10000000000 | tf_op jit(solution)/shard_map/attn_fwd/pallas_call | solution.py:398
  66.9 4.5 %mlp_fwd.3 = (bf16[256,384]{1,0:T(8,128)(2,1)}, bf16[256,384]{1,0:T(8,128)(2,1)S(1)}, bf16[256,1536]{1,0:T(8,128)(2,1)S(1)}, bf16[256,1536]{1,0:T(8,128)(2,1)S(1)}, f32[256,384]{1,0:T(8,128)S(1)}) custom-call(s32[6]{0:T(128)S(1)} %stack.24.refs_0_.meta, f32[256,384]{1,0:T(8,128)S(1)} %get-tuple-element.113.refs_1_.refs_3_, f32[16,384]{1,0:T(8,128)S(1)} %copy-done.8, ...), custom_call_target="tpu_custom_call" | custom-call | flops 10000000000 | tf_op jit(solution)/shard_map/mlp_fwd/pallas_call | solution.py:460
  71.5 0.9 copy-done.30
  72.4 6.4 %mlp_bwd.2 = (bf16[1536,384]{1,0:T(8,128)(2,1)S(1)}, bf16[1536,384]{1,0:T(8,128)(2,1)S(1)}, f32[256,384]{1,0:T(8,128)S(1)}, f32[16,384]{1,0:T(8,128)S(1)}) custom-call(s32[6]{0:T(128)S(1)} %stack.24.refs_0_.meta, bf16[256,384]{1,0:T(8,128)(2,1)S(1)} %bitcast.16, f32[16,384]{1,0:T(8,128)S(1)} %copy-done.8, f32[256,384]{1,0:T(8,128)S(1)} %get-tuple-element.113.refs_1_.refs_3_, ...), custom_call_target="tpu_custom_call" | custom-call | flops 10000000000 | tf_op jit(solution)/shard_map/mlp_bwd/pallas_call | solution.py:551
  79.3 5.3 %attn_bwd.2 = (bf16[768,384]{1,0:T(8,128)(2,1)S(1)}, bf16[784,384]{1,0:T(8,128)(2,1)S(1)}, f32[256,384]{1,0:T(8,128)S(1)}, bf16[16,384]{1,0:T(8,128)(2,1)S(1)}) custom-call(s32[6]{0:T(128)S(1)} %stack.24.refs_0_.meta, f32[256,384]{1,0:T(8,128)S(1)} %get-tuple-element.120.refs_1_, f32[16,384]{1,0:T(8,128)S(1)} %copy-done.8, ...), custom_call_target="tpu_custom_call" | custom-call | flops 10000000000 | tf_op jit(solution)/shard_map/attn_bwd/pallas_call | solution.py:664
  84.7 0.8 first_split.4
  85.6 1.5 collective-permute-start.25
  87.1 6.0 %mlp_bwd.3 = (bf16[1536,384]{1,0:T(8,128)(2,1)S(1)}, bf16[1536,384]{1,0:T(8,128)(2,1)S(1)}, f32[256,384]{1,0:T(8,128)S(1)}, f32[16,384]{1,0:T(8,128)S(1)}) custom-call(s32[6]{0:T(128)S(1)} %stack.24.refs_0_.meta, f32[256,384]{1,0:T(8,128)S(1)} %get-tuple-element.127.refs_1_, f32[16,384]{1,0:T(8,128)S(1)} %copy-done.7, ...), custom_call_target="tpu_custom_call" | custom-call | flops 10000000000 | tf_op jit(solution)/shard_map/mlp_bwd/pallas_call | solution.py:551
  94.8 6.3 %attn_bwd.3 = (bf16[768,384]{1,0:T(8,128)(2,1)S(1)}, bf16[784,384]{1,0:T(8,128)(2,1)S(1)}, f32[256,384]{1,0:T(8,128)}, bf16[16,384]{1,0:T(8,128)(2,1)S(1)}) custom-call(s32[6]{0:T(128)S(1)} %stack.24.refs_0_.meta, f32[256,384]{1,0:T(8,128)S(1)} %get-tuple-element.136.refs_1_, f32[16,384]{1,0:T(8,128)S(1)} %copy-done.7, bf16[256,384]{1,0:T(8,128)(2,1)S(1)} %bitcast.18, ...), custom_call_target="tpu_custom_call" | custom-call | flops 10000000000 | tf_op jit(solution)/shard_map/attn_bwd/pallas_call | solution.py:664
  102.4 1.6 collective-permute-start.28
  104.0 0.9 first_split.6
  104.9 1.5 collective-permute-start.30
  106.4 1.9 collective-permute-done.23.refs_3_
  109.0 1.6 collective-permute-start.27
  111.3 1.5 collective-permute-start.26
  114.0 1.0 collective-permute-done.27.refs_2_
  115.7 4.4 %collective-permute-done.31.refs_2_ = bf16[192,384]{1,0:T(8,128)(2,1)S(1)} collective-permute-done((bf16[192,384]{1,0:T(8,128)(2,1)S(1)}, bf16[192,384]{1,0:T(8,128)(2,1)S(1)}, u32[]{:S(2)}, u32[]{:S(2)}) %collective-permute-start.31) | collective-permute-done | bytes 147488 | tf_op jit(solution)/shard_map/ppermute | solution.py:1035
  120.2 2.9 %collective-permute-start.34 = (bf16[192,384]{1,0:T(8,128)(2,1)S(1)}, bf16[192,384]{1,0:T(8,128)(2,1)S(1)}, u32[]{:S(2)}, u32[]{:S(2)}) collective-permute-start(bf16[192,384]{1,0:T(8,128)(2,1)S(1)} %add_join.11.refs_4_.refs_0_.refs_1_), channel_id=1, source_target_pairs={{0,16},{2,18},{4,20},{6,22},{8,24},{10,26},{12,28},{14,30},{16,0},... | collective-permute-start | bytes 442376 | tf_op jit(solution)/shard_map/ppermute | solution.py:1035
  124.0 2.6 %collective-permute-start.36 = (bf16[320,384]{1,0:T(8,128)(2,1)S(1)}, bf16[320,384]{1,0:T(8,128)(2,1)S(1)}, u32[]{:S(2)}, u32[]{:S(2)}) collective-permute-start(bf16[320,384]{1,0:T(8,128)(2,1)S(1)} %add_join.12.refs_4_.refs_0_.refs_1_), channel_id=1, source_target_pairs={{0,16},{2,18},{4,20},{6,22},{8,24},{10,26},{12,28},{14,30},{16,0},... | collective-permute-start | bytes 737288 | tf_op jit(solution)/shard_map/ppermute | solution.py:1035
  127.8 1.6 collective-permute-start.32
  129.3 4.8 %collective-permute-done.34.refs_2_ = bf16[192,384]{1,0:T(8,128)(2,1)S(1)} collective-permute-done((bf16[192,384]{1,0:T(8,128)(2,1)S(1)}, bf16[192,384]{1,0:T(8,128)(2,1)S(1)}, u32[]{:S(2)}, u32[]{:S(2)}) %collective-permute-start.34) | collective-permute-done | bytes 147488 | tf_op jit(solution)/shard_map/ppermute | solution.py:1035
  134.9 2.1 %collective-permute-start.37 = (bf16[192,384]{1,0:T(8,128)(2,1)S(1)}, bf16[192,384]{1,0:T(8,128)(2,1)S(1)}, u32[]{:S(2)}, u32[]{:S(2)}) collective-permute-start(bf16[192,384]{1,0:T(8,128)(2,1)S(1)} %get-tuple-element.168.refs_3_.refs_1_), channel_id=1, source_target_pairs={{0,8},{2,10},{4,12},{6,14},{8,0},{10,2},{12,4},{14,6},{16,24},{18,... | collective-permute-start | bytes 442376 | tf_op jit(solution)/shard_map/ppermute | solution.py:1035
  137.1 4.8 %collective-permute-done.38.refs_2_ = bf16[192,384]{1,0:T(8,128)(2,1)S(1)} collective-permute-done((bf16[192,384]{1,0:T(8,128)(2,1)S(1)}, bf16[192,384]{1,0:T(8,128)(2,1)S(1)}, u32[]{:S(2)}, u32[]{:S(2)}) %collective-permute-start.38) | collective-permute-done | bytes 147488 | tf_op jit(solution)/shard_map/ppermute | solution.py:1035
  142.5 1.4 collective-permute-start.41
  143.9 1.2 collective-permute-done.37.refs_2_
  145.7 2.1 %collective-permute-done.35.refs_2_ = bf16[256,384]{1,0:T(8,128)(2,1)S(1)} collective-permute-done((bf16[256,384]{1,0:T(8,128)(2,1)S(1)}, bf16[256,384]{1,0:T(8,128)(2,1)S(1)}, u32[]{:S(2)}, u32[]{:S(2)}) %collective-permute-start.35) | collective-permute-done | bytes 196640 | tf_op jit(solution)/shard_map/ppermute | solution.py:1035
  148.2 1.3 collective-permute-done.41.refs_2_
  149.6 2.8 %ada_result.2 = (f32[2,192,2304]{2,1,0:T(8,128)}, f32[32,192]{1,0:T(8,128)S(1)}, f32[16,384]{1,0:T(8,128)S(1)}) custom-call(s32[6]{0:T(128)S(1)} %stack.24.refs_0_.meta, f32[32,384]{1,0:T(8,128)S(1)} %copy-done.5, bf16[256,384]{1,0:T(8,128)(2,1)S(1)} %get-tuple-element.170.refs_3_.rides, bf16[256,384]{1,0:T(8,128)(2,1)S(1)} %collective-permute-done.44.far, ...), custom_call_target="tpu_custom_call" | custom-call | flops 10000000000 | tf_op jit(solution)/shard_map/ada_result/pallas_call | solution.py:918
  152.4 2.1 %mlp_result.2 = (f32[2,192,1536]{2,1,0:T(8,128)}, f32[2,768,384]{2,1,0:T(8,128)}) custom-call(s32[6]{0:T(128)S(1)} %stack.24.refs_0_.meta, bf16[384,384]{1,0:T(8,128)(2,1)S(1)} %join.2.refs_3_.refs_1_, bf16[384,384]{1,0:T(8,128)(2,1)S(1)} %collective-permute-done.41.refs_2_, bf16[384,384]{1,0:T(8,128)(2,1)S(1)} %collective-permute-done.42.refs_3_, ...), custom_call_target="tpu_custom_call" | custom-call | flops 10000000000 | tf_op jit(solution)/shard_map/mlp_result/pallas_call | solution.py:855
  154.6 1.7 copy-done.27
  156.9 2.7 %collective-permute-start.39 = (bf16[320,384]{1,0:T(8,128)(2,1)S(1)}, bf16[320,384]{1,0:T(8,128)(2,1)S(1)}, u32[]{:S(2)}, u32[]{:S(2)}) collective-permute-start(bf16[320,384]{1,0:T(8,128)(2,1)S(1)} %add_join.17.refs_0_.refs_1_), channel_id=1, source_target_pairs={{0,16},{2,18},{4,20},{6,22},{8,24},{10,26},{12,28},{14,30},{16,0},... | collective-permute-start | bytes 737288 | tf_op jit(solution)/shard_map/ppermute | solution.py:1035
  159.7 5.6 %collective-permute-done.45.refs_2_ = bf16[192,384]{1,0:T(8,128)(2,1)S(1)} collective-permute-done((bf16[192,384]{1,0:T(8,128)(2,1)S(1)}, bf16[192,384]{1,0:T(8,128)(2,1)S(1)}, u32[]{:S(2)}, u32[]{:S(2)}) %collective-permute-start.45) | collective-permute-done | bytes 147488 | tf_op jit(solution)/shard_map/ppermute | solution.py:1035
  165.8 0.9 collective-permute-start.54
  166.8 4.6 %collective-permute-done.39.refs_2_ = bf16[320,384]{1,0:T(8,128)(2,1)S(1)} collective-permute-done((bf16[320,384]{1,0:T(8,128)(2,1)S(1)}, bf16[320,384]{1,0:T(8,128)(2,1)S(1)}, u32[]{:S(2)}, u32[]{:S(2)}) %collective-permute-start.39) | collective-permute-done | bytes 245792 | tf_op jit(solution)/shard_map/ppermute | solution.py:1035
  171.5 1.9 collective-permute-start.51
  173.4 1.7 attn_result.2
  175.1 1.1 copy-done.29
  176.2 3.0 %ada_result.3 = (f32[2,192,2304]{2,1,0:T(8,128)}, f32[32,192]{1,0:T(8,128)S(1)}, f32[16,384]{1,0:T(8,128)S(1)}) custom-call(s32[6]{0:T(128)S(1)} %stack.24.refs_0_.meta, f32[32,384]{1,0:T(8,128)S(1)} %copy-done.5, bf16[256,384]{1,0:T(8,128)(2,1)S(1)} %get-tuple-element.173.refs_5_.rides, ...), custom_call_target="tpu_custom_call", output_to_operand_aliasing={{0}: (5, {})} | custom-call | flops 10000000000 | tf_op jit(solution)/shard_map/ada_result/pallas_call | solution.py:918
  179.1 2.3 %condition_result.1 = (f32[192,1001]{1,0:T(8,128)}, f32[1,192]{1,0:T(1,128)S(1)}, f32[1,192]{1,0:T(1,128)S(1)}, f32[2,1152]{1,0:T(2,128)}, f32[2,384]{1,0:T(2,12...) custom-call(s32[6]{0:T(128)S(1)} %stack.24.refs_0_.meta, f32[32,384]{1,0:T(8,128)S(1)} %copy-done.5, ...), custom_call_target="tpu_custom_call" | custom-call | flops 10000000000 | tf_op jit(solution)/shard_map/condition_result/pallas_call | solution.py:143
  183.2 1.8 collective-permute-done.50.refs_2_
  185.0 1.2 both_halves.1
  186.2 2.1 %mlp_result.3 = (f32[2,192,1536]{2,1,0:T(8,128)}, f32[2,768,384]{2,1,0:T(8,128)}) custom-call(s32[6]{0:T(128)S(1)} %stack.24.refs_0_.meta, bf16[384,384]{1,0:T(8,128)(2,1)S(1)} %join.3.refs_3_.refs_1_, bf16[384,384]{1,0:T(8,128)(2,1)S(1)} %collective-permute-done.54.refs_2_, ...), custom_call_target="tpu_custom_call", output_to_operand_aliasing={{0}: (5, {}), {1}: (6, {})} | custom-call | flops 10000000000 | tf_op jit(solution)/shard_map/mlp_result/pallas_call | solution.py:855
  188.4 1.7 copy-done.28
  190.0 1.7 attn_result.3
  (167 shorter events, 29.2 us)
Async XLA Ops:
  5.5 5.1 %collective-permute-start = (f32[8,1536]{1,0:T(8,128)S(1)}, f32[8,1536]{1,0:T(8,128)S(1)}, u32[]{:S(2)}, u32[]{:S(2)}) collective-permute-start(f32[8,1536]{1,0:T(8,128)S(1)} %first_message.1.refs_1_), channel_id=1, source_target_pairs={{0,1},{1,0},{2,3},{3,2},{4,5},{5,4},{6,7},{7,6},{8,9},{9,8},{10,11... | collective-permute-start | bytes 147464 | tf_op jit(solution)/shard_map/ppermute | solution.py:1032
  17.2 20.7 %copy-start.17 = (f32[8,1536]{1,0:T(8,128)S(1)}, f32[8,1536]{1,0:T(8,128)}, u32[]{:S(2)}) copy-start(f32[8,1536]{1,0:T(8,128)} %copy-done.15) | copy-start | bytes 147460
  17.2 20.7 %copy-start.20 = (f32[8,1536]{1,0:T(8,128)S(1)}, f32[8,1536]{1,0:T(8,128)}, u32[]{:S(2)}) copy-start(f32[8,1536]{1,0:T(8,128)} %copy-done.18) | copy-start | bytes 147460
  18.6 3.6 %collective-permute-start.4 = (f32[2,384]{1,0:T(2,128)S(1)}, f32[2,384]{1,0:T(2,128)S(1)}, u32[]{:S(2)}, u32[]{:S(2)}) collective-permute-start(f32[2,384]{1,0:T(2,128)S(1)} %get-tuple-element.109), channel_id=1, source_target_pairs={{0,4},{2,6},{4,0},{6,2},{8,12},{10,14},{12,8},{14,10},{16,20},{18,... | collective-permute-start | bytes 9224 | tf_op jit(solution)/shard_map/ppermute | solution.py:1035
  22.2 21.1 %copy-start.32 = (f32[2,384]{1,0:T(2,128)}, f32[2,384]{1,0:T(2,128)S(1)}, u32[]{:S(2)}) copy-start(f32[2,384]{1,0:T(2,128)S(1)} %collective-permute-done.4) | copy-start | bytes 9220
  22.2 6.8 %collective-permute-start.5 = (f32[4,384]{1,0:T(4,128)S(1)}, f32[4,384]{1,0:T(4,128)S(1)}, u32[]{:S(2)}, u32[]{:S(2)}) collective-permute-start(f32[4,384]{1,0:T(4,128)S(1)} %pad_maximum_fusion.2), channel_id=1, source_target_pairs={{0,8},{2,10},{4,12},{6,14},{8,0},{10,2},{12,4},{14,6},{16,24},{18,... | collective-permute-start | bytes 18440 | tf_op jit(solution)/shard_map/ppermute | solution.py:1035
  24.9 13.6 %collective-permute-start.2 = (bf16[96,1536]{1,0:T(8,128)(2,1)S(1)}, bf16[96,1536]{1,0:T(8,128)(2,1)}, u32[]{:S(2)}, u32[]{:S(2)}) collective-permute-start(bf16[96,1536]{1,0:T(8,128)(2,1)S(1)} %pack_first.1), channel_id=1, source_target_pairs={{0,1},{1,0},{2,3},{3,2},{4,5},{5,4},{6,7},{7,6},{8,9},{9,8},{10,11... | collective-permute-start | bytes 884744 | tf_op jit(solution)/shard_map/ppermute | solution.py:1032
  26.5 8.8 %collective-permute-start.1 = (f32[2,2304]{1,0:T(2,128)S(1)}, f32[2,2304]{1,0:T(2,128)S(1)}, u32[]{:S(2)}, u32[]{:S(2)}) collective-permute-start(f32[2,2304]{1,0:T(2,128)S(1)} %get-tuple-element.106.refs_1_), channel_id=1, source_target_pairs={{0,1},{1,0},{2,3},{3,2},{4,5},{5,4},{6,7},{7,6},{8,9},{9,8},{10,11... | collective-permute-start | bytes 55304 | tf_op jit(solution)/shard_map/ppermute | solution.py:1032
  27.0 14.7 %collective-permute-start.8 = (bf16[96,1536]{1,0:T(8,128)(2,1)S(1)}, bf16[96,1536]{1,0:T(8,128)(2,1)}, u32[]{:S(2)}, u32[]{:S(2)}) collective-permute-start(bf16[96,1536]{1,0:T(8,128)(2,1)S(1)} %get-tuple-element.110), channel_id=1, source_target_pairs={{0,1},{1,0},{2,3},{3,2},{4,5},{5,4},{6,7},{7,6},{8,9},{9,8},{10,11... | collective-permute-start | bytes 884744 | tf_op jit(solution)/shard_map/ppermute | solution.py:1032
  28.5 20.1 %collective-permute-start.12 = (bf16[48,1536]{1,0:T(8,128)(2,1)}, bf16[48,1536]{1,0:T(8,128)(2,1)}, u32[]{:S(2)}, u32[]{:S(2)}) collective-permute-start(bf16[48,1536]{1,0:T(8,128)(2,1)} %get-tuple-element.112), channel_id=1, source_target_pairs={{0,1},{1,0},{2,3},{3,2},{4,5},{5,4},{6,7},{7,6},{8,9},{9,8},{10,11... | collective-permute-start | bytes 442376 | tf_op jit(solution)/shard_map/ppermute | solution.py:1032
  29.0 20.1 %collective-permute-start.16 = (bf16[96,1536]{1,0:T(8,128)(2,1)}, bf16[96,1536]{1,0:T(8,128)(2,1)}, u32[]{:S(2)}, u32[]{:S(2)}) collective-permute-start(bf16[96,1536]{1,0:T(8,128)(2,1)} %get-tuple-element.114), channel_id=1, source_target_pairs={{0,1},{1,0},{2,3},{3,2},{4,5},{5,4},{6,7},{7,6},{8,9},{9,8},{10,11... | collective-permute-start | bytes 884744 | tf_op jit(solution)/shard_map/ppermute | solution.py:1032
  35.3 7.9 %collective-permute-start.6 = (f32[8,384]{1,0:T(8,128)S(1)}, f32[8,384]{1,0:T(8,128)S(1)}, u32[]{:S(2)}, u32[]{:S(2)}) collective-permute-start(f32[8,384]{1,0:T(8,128)S(1)} %pad_maximum_fusion.1), channel_id=1, source_target_pairs={{0,16},{2,18},{4,20},{6,22},{8,24},{10,26},{12,28},{14,30},{16,0},... | collective-permute-start | bytes 36872 | tf_op jit(solution)/shard_map/ppermute | solution.py:1035
  38.5 11.1 %collective-permute-start.3 = (bf16[96,1536]{1,0:T(8,128)(2,1)}, bf16[96,1536]{1,0:T(8,128)(2,1)}, u32[]{:S(2)}, u32[]{:S(2)}) collective-permute-start(bf16[96,1536]{1,0:T(8,128)(2,1)} %collective-permute-done.2.refs_5_.refs_13_), channel_id=1, source_target_pairs={{0,2},{2,0},{4,6},{6,4},{8,10},{10,8},{12,14},{14,12},{16,18},{18,... | collective-permute-start | bytes 884744 | tf_op jit(solution)/shard_map/ppermute | solution.py:1035
  41.7 7.9 %collective-permute-start.9 = (bf16[96,1536]{1,0:T(8,128)(2,1)}, bf16[96,1536]{1,0:T(8,128)(2,1)}, u32[]{:S(2)}, u32[]{:S(2)}) collective-permute-start(bf16[96,1536]{1,0:T(8,128)(2,1)} %collective-permute-done.8.refs_6_.refs_11_), channel_id=1, source_target_pairs={{0,4},{2,6},{4,0},{6,2},{8,12},{10,14},{12,8},{14,10},{16,20},{18,... | collective-permute-start | bytes 884744 | tf_op jit(solution)/shard_map/ppermute | solution.py:1035
  43.3 1.4 collective-permute-start.7
  48.6 7.0 %collective-permute-start.13 = (bf16[48,1536]{1,0:T(8,128)(2,1)}, bf16[48,1536]{1,0:T(8,128)(2,1)S(1)}, u32[]{:S(2)}, u32[]{:S(2)}) collective-permute-start(bf16[48,1536]{1,0:T(8,128)(2,1)} %collective-permute-done.12.refs_5_.refs_12_), channel_id=1, source_target_pairs={{0,4},{2,6},{4,0},{6,2},{8,12},{10,14},{12,8},{14,10},{16,20},{18,... | collective-permute-start | bytes 442376 | tf_op jit(solution)/shard_map/ppermute | solution.py:1035
  49.1 13.7 %collective-permute-start.14 = (bf16[48,1536]{1,0:T(8,128)(2,1)}, bf16[48,1536]{1,0:T(8,128)(2,1)S(1)}, u32[]{:S(2)}, u32[]{:S(2)}) collective-permute-start(bf16[48,1536]{1,0:T(8,128)(2,1)} %collective-permute-done.12.refs_5_.refs_12_), channel_id=1, source_target_pairs={{0,2},{2,0},{4,6},{6,4},{8,10},{10,8},{12,14},{14,12},{16,18},{18,... | collective-permute-start | bytes 442376 | tf_op jit(solution)/shard_map/ppermute | solution.py:1035
  49.1 7.0 %collective-permute-start.10 = (bf16[96,1536]{1,0:T(8,128)(2,1)}, bf16[96,1536]{1,0:T(8,128)(2,1)S(1)}, u32[]{:S(2)}, u32[]{:S(2)}) collective-permute-start(bf16[96,1536]{1,0:T(8,128)(2,1)} %collective-permute-done.8.refs_6_.refs_11_), channel_id=1, source_target_pairs={{0,2},{2,0},{4,6},{6,4},{8,10},{10,8},{12,14},{14,12},{16,18},{18,... | collective-permute-start | bytes 884744 | tf_op jit(solution)/shard_map/ppermute | solution.py:1035
  49.7 9.2 %collective-permute-start.17 = (bf16[96,1536]{1,0:T(8,128)(2,1)}, bf16[96,1536]{1,0:T(8,128)(2,1)S(1)}, u32[]{:S(2)}, u32[]{:S(2)}) collective-permute-start(bf16[96,1536]{1,0:T(8,128)(2,1)} %collective-permute-done.16.refs_5_.refs_11_), channel_id=1, source_target_pairs={{0,8},{2,10},{4,12},{6,14},{8,0},{10,2},{12,4},{14,6},{16,24},{18,... | collective-permute-start | bytes 884744 | tf_op jit(solution)/shard_map/ppermute | solution.py:1035
  49.7 9.2 %collective-permute-start.11 = (bf16[96,1536]{1,0:T(8,128)(2,1)}, bf16[96,1536]{1,0:T(8,128)(2,1)S(1)}, u32[]{:S(2)}, u32[]{:S(2)}) collective-permute-start(bf16[96,1536]{1,0:T(8,128)(2,1)} %collective-permute-done.9.refs_7_.refs_12_), channel_id=1, source_target_pairs={{0,2},{2,0},{4,6},{6,4},{8,10},{10,8},{12,14},{14,12},{16,18},{18,... | collective-permute-start | bytes 884744 | tf_op jit(solution)/shard_map/ppermute | solution.py:1035
  51.5 7.4 %copy-start.4 = (f32[32,384]{1,0:T(8,128)S(1)}, f32[32,384]{1,0:T(8,128)}, u32[]{:S(2)}) copy-start(f32[32,384]{1,0:T(8,128)} %concatenate.18.refs_3_.info.refs_1_) | copy-start | bytes 147460
  55.7 11.2 %collective-permute-start.18 = (bf16[96,1536]{1,0:T(8,128)(2,1)}, bf16[96,1536]{1,0:T(8,128)(2,1)S(1)}, u32[]{:S(2)}, u32[]{:S(2)}) collective-permute-start(bf16[96,1536]{1,0:T(8,128)(2,1)} %collective-permute-done.16.refs_5_.refs_11_), channel_id=1, source_target_pairs={{0,2},{2,0},{4,6},{6,4},{8,10},{10,8},{12,14},{14,12},{16,18},{18,... | collective-permute-start | bytes 884744 | tf_op jit(solution)/shard_map/ppermute | solution.py:1035
  56.2 6.7 %collective-permute-start.15 = (bf16[48,1536]{1,0:T(8,128)(2,1)S(1)}, bf16[48,1536]{1,0:T(8,128)(2,1)S(1)}, u32[]{:S(2)}, u32[]{:S(2)}) collective-permute-start(bf16[48,1536]{1,0:T(8,128)(2,1)S(1)} %collective-permute-done.13.refs_6_.refs_13_), channel_id=1, source_target_pairs={{0,2},{2,0},{4,6},{6,4},{8,10},{10,8},{12,14},{14,12},{16,18},{18,... | collective-permute-start | bytes 442376 | tf_op jit(solution)/shard_map/ppermute | solution.py:1035
  58.9 8.0 %collective-permute-start.19 = (bf16[96,1536]{1,0:T(8,128)(2,1)S(1)}, bf16[96,1536]{1,0:T(8,128)(2,1)S(1)}, u32[]{:S(2)}, u32[]{:S(2)}) collective-permute-start(bf16[96,1536]{1,0:T(8,128)(2,1)S(1)} %collective-permute-done.17.refs_6_.refs_12_), channel_id=1, source_target_pairs={{0,2},{2,0},{4,6},{6,4},{8,10},{10,8},{12,14},{14,12},{16,18},{18,... | collective-permute-start | bytes 884744 | tf_op jit(solution)/shard_map/ppermute | solution.py:1035
  58.9 4.0 %copy-start.8 = (f32[16,384]{1,0:T(8,128)S(1)}, f32[16,384]{1,0:T(8,128)}, u32[]{:S(2)}) copy-start(f32[16,384]{1,0:T(8,128)} %get-tuple-element.196.refs_2_) | copy-start | bytes 73732
  66.9 4.6 %copy-start.12 = (bf16[1,256,384]{2,1,0:T(8,128)(2,1)S(1)}, bf16[1,256,384]{2,1,0:T(8,128)(2,1)}, u32[]{:S(2)}) copy-start(bf16[1,256,384]{2,1,0:T(8,128)(2,1)} %param.31) | copy-start | bytes 589828
  78.8 5.9 %collective-permute-start.20 = (bf16[1536,384]{1,0:T(8,128)(2,1)S(1)}, bf16[1536,384]{1,0:T(8,128)(2,1)S(1)}, u32[]{:S(2)}, u32[]{:S(2)}) collective-permute-start(bf16[1536,384]{1,0:T(8,128)(2,1)S(1)} %get-tuple-element.133), channel_id=1, source_target_pairs={{0,2},{2,0},{4,6},{6,4},{8,10},{10,8},{12,14},{14,12},{16,18},{18,... | collective-permute-start | bytes 3538952 | tf_op jit(solution)/shard_map/ppermute | solution.py:1035
  84.6 8.8 %collective-permute-start.21 = (bf16[784,384]{1,0:T(8,128)(2,1)S(1)}, bf16[784,384]{1,0:T(8,128)(2,1)S(1)}, u32[]{:S(2)}, u32[]{:S(2)}) collective-permute-start(bf16[784,384]{1,0:T(8,128)(2,1)S(1)} %get-tuple-element.144), channel_id=1, source_target_pairs={{0,2},{2,0},{4,6},{6,4},{8,10},{10,8},{12,14},{14,12},{16,18},{18,... | collective-permute-start | bytes 1806344 | tf_op jit(solution)/shard_map/ppermute | solution.py:1035
  84.7 2.4 %copy-start.7 = (f32[16,384]{1,0:T(8,128)S(1)}, f32[16,384]{1,0:T(8,128)}, u32[]{:S(2)}) copy-start(f32[16,384]{1,0:T(8,128)} %get-tuple-element.197.refs_2_) | copy-start | bytes 73732
  85.6 16.2 %collective-permute-start.25 = (bf16[768,384]{1,0:T(8,128)(2,1)S(1)}, bf16[768,384]{1,0:T(8,128)(2,1)S(1)}, u32[]{:S(2)}, u32[]{:S(2)}) collective-permute-start(bf16[768,384]{1,0:T(8,128)(2,1)S(1)} %get-tuple-element.135.refs_8_.refs_2_), channel_id=1, source_target_pairs={{0,1},{1,0},{2,3},{3,2},{4,5},{5,4},{6,7},{7,6},{8,9},{9,8},{10,11... | collective-permute-start | bytes 1769480 | tf_op jit(solution)/shard_map/ppermute | solution.py:1032
  93.1 10.9 %collective-permute-start.24 = (bf16[1536,384]{1,0:T(8,128)(2,1)S(1)}, bf16[1536,384]{1,0:T(8,128)(2,1)S(1)}, u32[]{:S(2)}, u32[]{:S(2)}) collective-permute-start(bf16[1536,384]{1,0:T(8,128)(2,1)S(1)} %get-tuple-element.152), channel_id=1, source_target_pairs={{0,2},{2,0},{4,6},{6,4},{8,10},{10,8},{12,14},{14,12},{16,18},{18,... | collective-permute-start | bytes 3538952 | tf_op jit(solution)/shard_map/ppermute | solution.py:1035
  94.2 14.2 %collective-permute-start.23 = (bf16[400,384]{1,0:T(8,128)(2,1)S(1)}, bf16[400,384]{1,0:T(8,128)(2,1)S(1)}, u32[]{:S(2)}, u32[]{:S(2)}) collective-permute-start(bf16[400,384]{1,0:T(8,128)(2,1)S(1)} %get-tuple-element.145.refs_10_.refs_2_), channel_id=1, source_target_pairs={{0,1},{1,0},{2,3},{3,2},{4,5},{5,4},{6,7},{7,6},{8,9},{9,8},{10,11... | collective-permute-start | bytes 921608 | tf_op jit(solution)/shard_map/ppermute | solution.py:1032
  101.1 9.5 %collective-permute-start.22 = (bf16[784,384]{1,0:T(8,128)(2,1)S(1)}, bf16[784,384]{1,0:T(8,128)(2,1)S(1)}, u32[]{:S(2)}, u32[]{:S(2)}) collective-permute-start(bf16[784,384]{1,0:T(8,128)(2,1)S(1)} %get-tuple-element.148), channel_id=1, source_target_pairs={{0,2},{2,0},{4,6},{6,4},{8,10},{10,8},{12,14},{14,12},{16,18},{18,... | collective-permute-start | bytes 1806344 | tf_op jit(solution)/shard_map/ppermute | solution.py:1035
  102.4 10.4 %collective-permute-start.28 = (bf16[384,384]{1,0:T(8,128)(2,1)S(1)}, bf16[384,384]{1,0:T(8,128)(2,1)S(1)}, u32[]{:S(2)}, u32[]{:S(2)}) collective-permute-start(bf16[384,384]{1,0:T(8,128)(2,1)S(1)} %get-tuple-element.154.refs_3_.refs_2_), channel_id=1, source_target_pairs={{0,4},{2,6},{4,0},{6,2},{8,12},{10,14},{12,8},{14,10},{16,20},{18,... | collective-permute-start | bytes 884744 | tf_op jit(solution)/shard_map/ppermute | solution.py:1035
  104.9 18.2 %collective-permute-start.30 = (bf16[768,384]{1,0:T(8,128)(2,1)S(1)}, bf16[768,384]{1,0:T(8,128)(2,1)S(1)}, u32[]{:S(2)}, u32[]{:S(2)}) collective-permute-start(bf16[768,384]{1,0:T(8,128)(2,1)S(1)} %get-tuple-element.155.refs_4_.refs_2_), channel_id=1, source_target_pairs={{0,1},{1,0},{2,3},{3,2},{4,5},{5,4},{6,7},{7,6},{8,9},{9,8},{10,11... | collective-permute-start | bytes 1769480 | tf_op jit(solution)/shard_map/ppermute | solution.py:1032
  109.0 6.0 %collective-permute-start.27 = (bf16[224,384]{1,0:T(8,128)(2,1)S(1)}, bf16[224,384]{1,0:T(8,128)(2,1)S(1)}, u32[]{:S(2)}, u32[]{:S(2)}) collective-permute-start(bf16[224,384]{1,0:T(8,128)(2,1)S(1)} %get-tuple-element.156.refs_4_.refs_1_), channel_id=1, source_target_pairs={{0,4},{2,6},{4,0},{6,2},{8,12},{10,14},{12,8},{14,10},{16,20},{18,... | collective-permute-start | bytes 516104 | tf_op jit(solution)/shard_map/ppermute | solution.py:1035
  111.3 15.8 %collective-permute-start.26 = (bf16[400,384]{1,0:T(8,128)(2,1)S(1)}, bf16[400,384]{1,0:T(8,128)(2,1)S(1)}, u32[]{:S(2)}, u32[]{:S(2)}) collective-permute-start(bf16[400,384]{1,0:T(8,128)(2,1)S(1)} %get-tuple-element.158.refs_4_.refs_2_), channel_id=1, source_target_pairs={{0,1},{1,0},{2,3},{3,2},{4,5},{5,4},{6,7},{7,6},{8,9},{9,8},{10,11... | collective-permute-start | bytes 921608 | tf_op jit(solution)/shard_map/ppermute | solution.py:1032
  113.5 6.6 %collective-permute-start.31 = (bf16[192,384]{1,0:T(8,128)(2,1)S(1)}, bf16[192,384]{1,0:T(8,128)(2,1)S(1)}, u32[]{:S(2)}, u32[]{:S(2)}) collective-permute-start(bf16[192,384]{1,0:T(8,128)(2,1)S(1)} %get-tuple-element.161.refs_3_.refs_1_), channel_id=1, source_target_pairs={{0,8},{2,10},{4,12},{6,14},{8,0},{10,2},{12,4},{14,6},{16,24},{18,... | collective-permute-start | bytes 442376 | tf_op jit(solution)/shard_map/ppermute | solution.py:1035
  115.0 8.9 %collective-permute-start.29 = (bf16[256,384]{1,0:T(8,128)(2,1)S(1)}, bf16[256,384]{1,0:T(8,128)(2,1)S(1)}, u32[]{:S(2)}, u32[]{:S(2)}) collective-permute-start(bf16[256,384]{1,0:T(8,128)(2,1)S(1)} %add_join.10.refs_3_.refs_0_.refs_1_), channel_id=1, source_target_pairs={{0,8},{2,10},{4,12},{6,14},{8,0},{10,2},{12,4},{14,6},{16,24},{18,... | collective-permute-start | bytes 589832 | tf_op jit(solution)/shard_map/ppermute | solution.py:1035
  120.2 13.9 %collective-permute-start.34 = (bf16[192,384]{1,0:T(8,128)(2,1)S(1)}, bf16[192,384]{1,0:T(8,128)(2,1)S(1)}, u32[]{:S(2)}, u32[]{:S(2)}) collective-permute-start(bf16[192,384]{1,0:T(8,128)(2,1)S(1)} %add_join.11.refs_4_.refs_0_.refs_1_), channel_id=1, source_target_pairs={{0,16},{2,18},{4,20},{6,22},{8,24},{10,26},{12,28},{14,30},{16,0},... | collective-permute-start | bytes 442376 | tf_op jit(solution)/shard_map/ppermute | solution.py:1035
  123.8 10.5 %collective-permute-start.33 = (bf16[384,384]{1,0:T(8,128)(2,1)S(1)}, bf16[384,384]{1,0:T(8,128)(2,1)S(1)}, u32[]{:S(2)}, u32[]{:S(2)}) collective-permute-start(bf16[384,384]{1,0:T(8,128)(2,1)S(1)} %get-tuple-element.164.refs_3_.refs_2_), channel_id=1, source_target_pairs={{0,4},{2,6},{4,0},{6,2},{8,12},{10,14},{12,8},{14,10},{16,20},{18,... | collective-permute-start | bytes 884744 | tf_op jit(solution)/shard_map/ppermute | solution.py:1035
  124.0 21.6 %collective-permute-start.36 = (bf16[320,384]{1,0:T(8,128)(2,1)S(1)}, bf16[320,384]{1,0:T(8,128)(2,1)S(1)}, u32[]{:S(2)}, u32[]{:S(2)}) collective-permute-start(bf16[320,384]{1,0:T(8,128)(2,1)S(1)} %add_join.12.refs_4_.refs_0_.refs_1_), channel_id=1, source_target_pairs={{0,16},{2,18},{4,20},{6,22},{8,24},{10,26},{12,28},{14,30},{16,0},... | collective-permute-start | bytes 737288 | tf_op jit(solution)/shard_map/ppermute | solution.py:1035
  127.8 9.2 %collective-permute-start.32 = (bf16[224,384]{1,0:T(8,128)(2,1)S(1)}, bf16[224,384]{1,0:T(8,128)(2,1)S(1)}, u32[]{:S(2)}, u32[]{:S(2)}) collective-permute-start(bf16[224,384]{1,0:T(8,128)(2,1)S(1)} %get-tuple-element.166.refs_3_.refs_1_), channel_id=1, source_target_pairs={{0,4},{2,6},{4,0},{6,2},{8,12},{10,14},{12,8},{14,10},{16,20},{18,... | collective-permute-start | bytes 516104 | tf_op jit(solution)/shard_map/ppermute | solution.py:1035
  134.2 7.8 %collective-permute-start.38 = (bf16[192,384]{1,0:T(8,128)(2,1)S(1)}, bf16[192,384]{1,0:T(8,128)(2,1)S(1)}, u32[]{:S(2)}, u32[]{:S(2)}) collective-permute-start(bf16[192,384]{1,0:T(8,128)(2,1)S(1)} %add_join.13.refs_4_.refs_1_), channel_id=1, source_target_pairs={{0,8},{2,10},{4,12},{6,14},{8,0},{10,2},{12,4},{14,6},{16,24},{18,... | collective-permute-start | bytes 442376 | tf_op jit(solution)/shard_map/ppermute | solution.py:1035
  134.9 10.2 %collective-permute-start.37 = (bf16[192,384]{1,0:T(8,128)(2,1)S(1)}, bf16[192,384]{1,0:T(8,128)(2,1)S(1)}, u32[]{:S(2)}, u32[]{:S(2)}) collective-permute-start(bf16[192,384]{1,0:T(8,128)(2,1)S(1)} %get-tuple-element.168.refs_3_.refs_1_), channel_id=1, source_target_pairs={{0,8},{2,10},{4,12},{6,14},{8,0},{10,2},{12,4},{14,6},{16,24},{18,... | collective-permute-start | bytes 442376 | tf_op jit(solution)/shard_map/ppermute | solution.py:1035
  137.0 10.8 %collective-permute-start.35 = (bf16[256,384]{1,0:T(8,128)(2,1)S(1)}, bf16[256,384]{1,0:T(8,128)(2,1)S(1)}, u32[]{:S(2)}, u32[]{:S(2)}) collective-permute-start(bf16[256,384]{1,0:T(8,128)(2,1)S(1)} %add_join.14.refs_3_.refs_0_.refs_1_), channel_id=1, source_target_pairs={{0,8},{2,10},{4,12},{6,14},{8,0},{10,2},{12,4},{14,6},{16,24},{18,... | collective-permute-start | bytes 589832 | tf_op jit(solution)/shard_map/ppermute | solution.py:1035
  142.5 7.0 %collective-permute-start.41 = (bf16[384,384]{1,0:T(8,128)(2,1)S(1)}, bf16[384,384]{1,0:T(8,128)(2,1)S(1)}, u32[]{:S(2)}, u32[]{:S(2)}) collective-permute-start(bf16[384,384]{1,0:T(8,128)(2,1)S(1)} %join.2.refs_3_.refs_1_), channel_id=1, source_target_pairs={{0,4},{2,6},{4,0},{6,2},{8,12},{10,14},{12,8},{14,10},{16,20},{18,... | collective-permute-start | bytes 884744 | tf_op jit(solution)/shard_map/ppermute | solution.py:1035
  143.9 8.5 %collective-permute-start.42 = (bf16[384,384]{1,0:T(8,128)(2,1)S(1)}, bf16[384,384]{1,0:T(8,128)(2,1)S(1)}, u32[]{:S(2)}, u32[]{:S(2)}) collective-permute-start(bf16[384,384]{1,0:T(8,128)(2,1)S(1)} %join.2.refs_3_.refs_1_), channel_id=1, source_target_pairs={{0,2},{2,0},{4,6},{6,4},{8,10},{10,8},{12,14},{14,12},{16,18},{18,... | collective-permute-start | bytes 884744 | tf_op jit(solution)/shard_map/ppermute | solution.py:1035
  145.1 9.4 %collective-permute-start.40 = (bf16[192,384]{1,0:T(8,128)(2,1)S(1)}, bf16[192,384]{1,0:T(8,128)(2,1)S(1)}, u32[]{:S(2)}, u32[]{:S(2)}) collective-permute-start(bf16[192,384]{1,0:T(8,128)(2,1)S(1)} %add_join.15.refs_3_.refs_0_.refs_1_), channel_id=1, source_target_pairs={{0,16},{2,18},{4,20},{6,22},{8,24},{10,26},{12,28},{14,30},{16,0},... | collective-permute-start | bytes 442376 | tf_op jit(solution)/shard_map/ppermute | solution.py:1035
  145.6 3.9 %collective-permute-start.44 = (bf16[256,384]{1,0:T(8,128)(2,1)S(1)}, bf16[256,384]{1,0:T(8,128)(2,1)S(1)}, u32[]{:S(2)}, u32[]{:S(2)}) collective-permute-start(bf16[256,384]{1,0:T(8,128)(2,1)S(1)} %get-tuple-element.170.refs_3_.rides), channel_id=1, source_target_pairs={{0,2},{2,0},{4,6},{6,4},{8,10},{10,8},{12,14},{14,12},{16,18},{18,... | collective-permute-start | bytes 589832 | tf_op jit(solution)/shard_map/ppermute | solution.py:1035
  147.8 11.9 %collective-permute-start.47 = (bf16[192,384]{1,0:T(8,128)(2,1)S(1)}, bf16[192,384]{1,0:T(8,128)(2,1)S(1)}, u32[]{:S(2)}, u32[]{:S(2)}) collective-permute-start(bf16[192,384]{1,0:T(8,128)(2,1)S(1)} %get-tuple-element.175.refs_1_), channel_id=1, source_target_pairs={{0,4},{2,6},{4,0},{6,2},{8,12},{10,14},{12,8},{14,10},{16,20},{18,... | collective-permute-start | bytes 442376 | tf_op jit(solution)/shard_map/ppermute | solution.py:1035
  149.6 2.9 %collective-permute-start.43 = (bf16[384,384]{1,0:T(8,128)(2,1)S(1)}, bf16[384,384]{1,0:T(8,128)(2,1)S(1)}, u32[]{:S(2)}, u32[]{:S(2)}) collective-permute-start(bf16[384,384]{1,0:T(8,128)(2,1)S(1)} %collective-permute-done.41.refs_2_), channel_id=1, source_target_pairs={{0,2},{2,0},{4,6},{6,4},{8,10},{10,8},{12,14},{14,12},{16,18},{18,... | collective-permute-start | bytes 884744 | tf_op jit(solution)/shard_map/ppermute | solution.py:1035
  156.3 9.0 %collective-permute-start.45 = (bf16[192,384]{1,0:T(8,128)(2,1)S(1)}, bf16[192,384]{1,0:T(8,128)(2,1)S(1)}, u32[]{:S(2)}, u32[]{:S(2)}) collective-permute-start(bf16[192,384]{1,0:T(8,128)(2,1)S(1)} %add_join.18.refs_1_.refs_3_), channel_id=1, source_target_pairs={{0,8},{2,10},{4,12},{6,14},{8,0},{10,2},{12,4},{14,6},{16,24},{18,... | collective-permute-start | bytes 442376 | tf_op jit(solution)/shard_map/ppermute | solution.py:1035
  156.5 16.9 %collective-permute-start.48 = (bf16[192,384]{1,0:T(8,128)(2,1)S(1)}, bf16[192,384]{1,0:T(8,128)(2,1)S(1)}, u32[]{:S(2)}, u32[]{:S(2)}) collective-permute-start(bf16[192,384]{1,0:T(8,128)(2,1)S(1)} %get-tuple-element.175.refs_1_), channel_id=1, source_target_pairs={{0,2},{2,0},{4,6},{6,4},{8,10},{10,8},{12,14},{14,12},{16,18},{18,... | collective-permute-start | bytes 442376 | tf_op jit(solution)/shard_map/ppermute | solution.py:1035
  156.9 14.4 %collective-permute-start.39 = (bf16[320,384]{1,0:T(8,128)(2,1)S(1)}, bf16[320,384]{1,0:T(8,128)(2,1)S(1)}, u32[]{:S(2)}, u32[]{:S(2)}) collective-permute-start(bf16[320,384]{1,0:T(8,128)(2,1)S(1)} %add_join.17.refs_0_.refs_1_), channel_id=1, source_target_pairs={{0,16},{2,18},{4,20},{6,22},{8,24},{10,26},{12,28},{14,30},{16,0},... | collective-permute-start | bytes 737288 | tf_op jit(solution)/shard_map/ppermute | solution.py:1035
  159.7 13.7 %collective-permute-start.49 = (bf16[192,384]{1,0:T(8,128)(2,1)S(1)}, bf16[192,384]{1,0:T(8,128)(2,1)S(1)}, u32[]{:S(2)}, u32[]{:S(2)}) collective-permute-start(bf16[192,384]{1,0:T(8,128)(2,1)S(1)} %collective-permute-done.47.refs_2_), channel_id=1, source_target_pairs={{0,2},{2,0},{4,6},{6,4},{8,10},{10,8},{12,14},{14,12},{16,18},{18,... | collective-permute-start | bytes 442376 | tf_op jit(solution)/shard_map/ppermute | solution.py:1035
  165.8 16.9 %collective-permute-start.54 = (bf16[384,384]{1,0:T(8,128)(2,1)S(1)}, bf16[384,384]{1,0:T(8,128)(2,1)S(1)}, u32[]{:S(2)}, u32[]{:S(2)}) collective-permute-start(bf16[384,384]{1,0:T(8,128)(2,1)S(1)} %join.3.refs_3_.refs_1_), channel_id=1, source_target_pairs={{0,4},{2,6},{4,0},{6,2},{8,12},{10,14},{12,8},{14,10},{16,20},{18,... | collective-permute-start | bytes 884744 | tf_op jit(solution)/shard_map/ppermute | solution.py:1035
  171.4 3.7 %collective-permute-start.46 = (bf16[256,384]{1,0:T(8,128)(2,1)S(1)}, bf16[256,384]{1,0:T(8,128)(2,1)S(1)}, u32[]{:S(2)}, u32[]{:S(2)}) collective-permute-start(bf16[256,384]{1,0:T(8,128)(2,1)S(1)} %get-tuple-element.173.refs_5_.rides), channel_id=1, source_target_pairs={{0,2},{2,0},{4,6},{6,4},{8,10},{10,8},{12,14},{14,12},{16,18},{18,... | collective-permute-start | bytes 589832 | tf_op jit(solution)/shard_map/ppermute | solution.py:1035
  171.5 11.2 %collective-permute-start.51 = (bf16[192,384]{1,0:T(8,128)(2,1)S(1)}, bf16[192,384]{1,0:T(8,128)(2,1)S(1)}, u32[]{:S(2)}, u32[]{:S(2)}) collective-permute-start(bf16[192,384]{1,0:T(8,128)(2,1)S(1)} %get-tuple-element.185.refs_1_), channel_id=1, source_target_pairs={{0,4},{2,6},{4,0},{6,2},{8,12},{10,14},{12,8},{14,10},{16,20},{18,... | collective-permute-start | bytes 442376 | tf_op jit(solution)/shard_map/ppermute | solution.py:1035
  181.4 3.6 %collective-permute-start.50 = (f32[1,192]{1,0:T(1,128)S(1)}, f32[1,192]{1,0:T(1,128)S(1)}, u32[]{:S(2)}, u32[]{:S(2)}) collective-permute-start(f32[1,192]{1,0:T(1,128)S(1)} %get-tuple-element.181), channel_id=1, source_target_pairs={{0,1},{1,0},{2,3},{3,2},{4,5},{5,4},{6,7},{7,6},{8,9},{9,8},{10,11... | collective-permute-start | bytes 2312 | tf_op jit(solution)/shard_map/ppermute | solution.py:1032
  182.2 4.0 %collective-permute-start.55 = (bf16[384,384]{1,0:T(8,128)(2,1)S(1)}, bf16[384,384]{1,0:T(8,128)(2,1)S(1)}, u32[]{:S(2)}, u32[]{:S(2)}) collective-permute-start(bf16[384,384]{1,0:T(8,128)(2,1)S(1)} %join.3.refs_3_.refs_1_), channel_id=1, source_target_pairs={{0,2},{2,0},{4,6},{6,4},{8,10},{10,8},{12,14},{14,12},{16,18},{18,... | collective-permute-start | bytes 884744 | tf_op jit(solution)/shard_map/ppermute | solution.py:1035
  182.2 6.1 %collective-permute-start.52 = (bf16[192,384]{1,0:T(8,128)(2,1)S(1)}, bf16[192,384]{1,0:T(8,128)(2,1)S(1)}, u32[]{:S(2)}, u32[]{:S(2)}) collective-permute-start(bf16[192,384]{1,0:T(8,128)(2,1)S(1)} %get-tuple-element.185.refs_1_), channel_id=1, source_target_pairs={{0,2},{2,0},{4,6},{6,4},{8,10},{10,8},{12,14},{14,12},{16,18},{18,... | collective-permute-start | bytes 442376 | tf_op jit(solution)/shard_map/ppermute | solution.py:1035
  182.7 5.6 %collective-permute-start.53 = (bf16[192,384]{1,0:T(8,128)(2,1)S(1)}, bf16[192,384]{1,0:T(8,128)(2,1)S(1)}, u32[]{:S(2)}, u32[]{:S(2)}) collective-permute-start(bf16[192,384]{1,0:T(8,128)(2,1)S(1)} %collective-permute-done.51.refs_2_), channel_id=1, source_target_pairs={{0,2},{2,0},{4,6},{6,4},{8,10},{10,8},{12,14},{14,12},{16,18},{18,... | collective-permute-start | bytes 442376 | tf_op jit(solution)/shard_map/ppermute | solution.py:1035
  182.7 3.5 %collective-permute-start.56 = (bf16[384,384]{1,0:T(8,128)(2,1)S(1)}, bf16[384,384]{1,0:T(8,128)(2,1)S(1)}, u32[]{:S(2)}, u32[]{:S(2)}) collective-permute-start(bf16[384,384]{1,0:T(8,128)(2,1)S(1)} %collective-permute-done.54.refs_2_), channel_id=1, source_target_pairs={{0,2},{2,0},{4,6},{6,4},{8,10},{10,8},{12,14},{14,12},{16,18},{18,... | collective-permute-start | bytes 884744 | tf_op jit(solution)/shard_map/ppermute | solution.py:1035
  (27 other events, 30.2 us)

commit v3 on v2

--- a/solution.py
+++ b/solution.py
@@ -24,6 +24,7 @@
 HBM = pl.BlockSpec(memory_space=pltpu.HBM)
 LIMIT = 16 * 1024 * 1024
 SMALL = 8 * 1024 * 1024
+WIDE = 56 * 1024 * 1024
 
 
 def sds(shape, dtype):
@@ -134,7 +135,7 @@
     ]
 
 
-def call(body, ins, in_specs, out_shape, out_specs, name, scratch=(), deps=(), **more):
+def call(body, ins, in_specs, out_shape, out_specs, name, scratch=(), deps=(), limit=SMALL, **more):
     given, late = len(ins), len(deps)
 
     def kernel(*refs):
@@ -146,90 +147,56 @@
         in_specs=list(in_specs) + [ANY] * late,
         out_specs=out_specs,
         scratch_shapes=list(scratch),
-        compiler_params=pltpu.CompilerParams(vmem_limit_bytes=SMALL),
-        cost_estimate=pl.CostEstimate(flops=10**10, bytes_accessed=0, transcendentals=0),
+        compiler_params=pltpu.CompilerParams(vmem_limit_bytes=limit),
+        cost_estimate=pl.CostEstimate(flops=10000000000, bytes_accessed=0, transcendentals=0),
         name=name,
         **more,
     )(*ins, *deps)
 
 
-def pack_attn_into(send, parts, offset, qkv, out):
+def pack_attn_copies(send, layer, parts, offset, qkv, out):
     size = qkv.shape[1] // parts
     rows = rows_of(offset * size, size)
-    send[:, 0 : 3 * D] = qkv[0, rows, :]
-    send[:, 3 * D : 4 * D] = out[0, rows, :]
-
-
-def pack_mlp_into(send, layer, offset, up, down):
+    return [
+        (qkv.at[layer, rows, :], send.at[:, pl.ds(0, 3 * D)]),
+        (out.at[layer, rows, :], send.at[:, pl.ds(3 * D, D)]),
+    ]
+
+
+def pack_mlp_copies(send, layer, offset, up, down):
     size = up.shape[1] // 4
     blocks = down.shape[1] // up.shape[1]
-    send[0:size, :] = up[layer, rows_of(offset * size, size), :]
+    copies = [(up.at[layer, rows_of(offset * size, size), :], send.at[pl.ds(0, size), :])]
     for b in range(blocks):
         rows = rows_of(offset * (blocks * size) + b * size, size)
-        send[size : 2 * size, b * D : (b + 1) * D] = down[layer, rows, :]
-
-
-def pack_first(meta, qkv, out):
-    half = qkv.shape[1]
-
-    def body(meta, qkv, out, send):
-        pack_attn_into(send, 2, piece_offsets(meta, 2, False)[0], qkv, out)
-
-    return pl.pallas_call(
-        body,
-        grid=(1,),
-        out_shape=sds((half // 2, 4 * D), BF16),
-        in_specs=[
-            SMEM,
-            pl.BlockSpec((1, half, 3 * D), lambda i: (0, 0, 0)),
-            pl.BlockSpec((1, half, D), lambda i: (0, 0, 0)),
-        ],
-        out_specs=pl.BlockSpec((half // 2, 4 * D), lambda i: (0, 0)),
-        compiler_params=pltpu.CompilerParams(vmem_limit_bytes=LIMIT),
-        name="pack_first",
-    )(meta, qkv, out)
-
-
-def pack_rest(meta, qkv, out, up, down, info, deps):
+        copies.append((down.at[layer, rows, :], send.at[pl.ds(size, size), pl.ds(b * D, D)]))
+    return copies
+
+
+def pack(layer, far, parts, meta, qkv, out, up, down, deps, name):
     half = qkv.shape[1]
     size = half // 4
 
-    def body(meta, qkv, out, up, down, *refs):
-        send_m0, send_a1, send_m1, info_out = refs[-4:]
-        info_out[...] = refs[0][...]
-        pack_mlp_into(send_m0, 0, piece_offsets(meta, 4, False)[0], up, down)
-        pack_attn_into(send_a1, 4, piece_offsets(meta, 4, False)[0], qkv, out)
-        pack_mlp_into(send_m1, 1, piece_offsets(meta, 4, True)[0], up, down)
-
-    whole = lambda i: (0, 0, 0)
-    flat = lambda i: (0, 0)
-    return pl.pallas_call(
+    def body(meta, qkv, out, up, down, send_attn, send_mlp, sems):
+        copies = pack_attn_copies(send_attn, layer, parts, piece_offsets(meta, parts, False)[0], qkv, out)
+        copies += pack_mlp_copies(send_mlp, layer, piece_offsets(meta, 4, far)[0], up, down)
+        copies = [pltpu.make_async_copy(s, d, sems.at[i]) for i, (s, d) in enumerate(copies)]
+        for copy in copies:
+            copy.start()
+        for copy in copies:
+            copy.wait()
+
+    return call(
         body,
-        grid=(1,),
-        out_shape=(
-            sds((2 * size, 4 * D), BF16),
-            sds((size, 4 * D), BF16),
-            sds((2 * size, 4 * D), BF16),
-            sds(info.shape, F32),
-        ),
-        in_specs=[
-            SMEM,
-            pl.BlockSpec((1, half, 3 * D), lambda i: (1, 0, 0)),
-            pl.BlockSpec((1, half, D), lambda i: (1, 0, 0)),
-            pl.BlockSpec(up.shape, whole),
-            pl.BlockSpec(down.shape, whole),
-            pl.BlockSpec(info.shape, flat),
-        ]
-        + [ANY] * len(deps),
-        out_specs=(
-            pl.BlockSpec((2 * size, 4 * D), flat),
-            pl.BlockSpec((size, 4 * D), flat),
-            pl.BlockSpec((2 * size, 4 * D), flat),
-            pl.BlockSpec(info.shape, flat),
-        ),
-        compiler_params=pltpu.CompilerParams(vmem_limit_bytes=LIMIT),
-        name="pack_rest",
-    )(meta, qkv, out, up, down, info, *deps)
+        (meta, qkv, out, up, down),
+        [SMEM] + [HBM] * 4,
+        (sds((half // parts, 4 * D), BF16), sds((2 * size, 4 * D), BF16)),
+        (VMEM, VMEM),
+        name,
+        scratch=[pltpu.SemaphoreType.DMA((8,))],
+        deps=deps,
+        limit=WIDE,
+    )
 
 
 def first_message(timestep, labels, ada_bias, qv_bias, out_bias, up_bias, down_bias):
@@ -261,10 +228,11 @@
         "first_message",
         scratch=[pltpu.VMEM(member.shape, member.dtype) for member in ins]
         + [pltpu.SemaphoreType.DMA((6,))],
-    )
-
-
-def condition_kernel(meta, own, got, table_ref, ada_ref, info_out, mine_out, send_out, table, ada, sems):
+        limit=WIDE,
+    )
+
+
+def condition_kernel(meta, own, got, table_ref, ada_ref, mine_out, send_out, table, ada, sems):
     half = D // 2
     x = meta[0]
     copy = pltpu.make_async_copy(ada_ref, ada, sems.at[0])
@@ -281,9 +249,9 @@
     one_hot = jnp.where(classes == label, 1.0, 0.0).astype(BF16)
     condition = timestep + dot_nt(one_hot, table[...])
     act = (condition * (1.0 / (1.0 + jnp.exp(-condition)))).astype(BF16)
-    info_out[:, 0:half] = condition[0:2, :]
-    info_out[:, half:256] = jnp.zeros((2, 256 - half), F32)
-    info_out[:, 256:384] = jnp.broadcast_to(label[0:2, :], (2, 128))
+    for ref, index in ((mine_out, 0), (send_out, 1)):
+        ref[2:3, 0:half] = condition[index : index + 1, :]
+        ref[2:3, half:] = jnp.zeros((1, 6 * D - half), F32)
     copy.wait()
     for layer in range(LAYERS):
         part = dot(act, ada[layer])
@@ -291,19 +259,21 @@
         send_out[layer : layer + 1, :] = part[1:2, :]
 
 
-def condition_step(meta, own, got, table, ada):
+def condition_step(meta, own, got, table, ada, deps):
     return call(
         condition_kernel,
         (meta, own, got, table.T, ada),
         [SMEM] + [VMEM] * 3 + [HBM],
-        (sds((2, D), F32), sds((LAYERS, 6 * D), F32), sds((LAYERS, 6 * D), F32)),
-        (VMEM,) * 3,
+        (sds((LAYERS + 1, 6 * D), F32),) * 2,
+        (VMEM,) * 2,
         "condition",
         scratch=[
             pltpu.VMEM((D // 2, -(-table.shape[0] // 128) * 128), BF16),
             pltpu.VMEM(ada.shape, BF16),
             pltpu.SemaphoreType.DMA((1,)),
         ],
+        deps=deps,
+        limit=WIDE,
     )
 
 
@@ -313,8 +283,14 @@
     high = jnp.where(x == 0, got[...], own[...])
     modul = mine_part[...] + got_part[...]
     half = D // 2
-    out[...] = jnp.zeros_like(out)
+    mine_cond, got_cond = mine_part[2:3, 0:half], got_part[2:3, 0:half]
+    condition = jnp.concatenate(
+        [jnp.where(x == 0, mine_cond, got_cond), jnp.where(x == 0, got_cond, mine_cond)], axis=1
+    )
+    label = jnp.broadcast_to(own[4:5, D : D + 1], (1, D))
     for layer in range(LAYERS):
+        out[layer, 14:15, :] = condition
+        out[layer, 15:16, :] = label
         rows = slice(layer, layer + 1)
         for member in range(6):
             side = low if member < 3 else high
@@ -413,7 +389,7 @@
             pltpu.SemaphoreType.DMA((2 + 2 * count,)),
         ],
         compiler_params=pltpu.CompilerParams(vmem_limit_bytes=LIMIT),
-        cost_estimate=pl.CostEstimate(flops=10**10, bytes_accessed=0, transcendentals=0),
+        cost_estimate=pl.CostEstimate(flops=10000000000, bytes_accessed=0, transcendentals=0),
         name="attn_fwd",
     )(meta, x, vecs, qkv, out, *pieces)
 
@@ -474,7 +450,7 @@
             pltpu.SemaphoreType.DMA((2 + 5 * count,)),
         ],
         compiler_params=pltpu.CompilerParams(vmem_limit_bytes=LIMIT),
-        cost_estimate=pl.CostEstimate(flops=10**10, bytes_accessed=0, transcendentals=0),
+        cost_estimate=pl.CostEstimate(flops=10000000000, bytes_accessed=0, transcendentals=0),
         name="mlp_fwd",
     )(meta, middle, vecs, *deps, up, down, *pieces)
 
@@ -565,7 +541,7 @@
             pltpu.SemaphoreType.DMA((2 + 5 * count,)),
         ],
         compiler_params=pltpu.CompilerParams(vmem_limit_bytes=LIMIT),
-        cost_estimate=pl.CostEstimate(flops=10**10, bytes_accessed=0, transcendentals=0),
+        cost_estimate=pl.CostEstimate(flops=10000000000, bytes_accessed=0, transcendentals=0),
         name="mlp_bwd",
     )(meta, grad, vecs, middle, branch, act, slope, mod_two, *deps, up, down, *pieces)
 
@@ -647,6 +623,12 @@
     sums[0] = jnp.sum(grad_mod, axis=0, keepdims=True)
     sums[1] = jnp.sum(grad_mod * normed, axis=0, keepdims=True)
     grad_out[...] = grad + norm_back(grad_mod * (1.0 + vecs[1:2, :]), normed, inv_dev)
+    if layer == 1:
+        high = vecs[14:15, :].astype(BF16).astype(F32)
+        sums[14], sums[15] = high, vecs[14:15, :] - high
+    else:
+        high = jnp.floor(vecs[15:16, :] * (1.0 / 32.0))
+        sums[14], sums[15] = high, vecs[15:16, :] - high * 32.0
     row = lax.broadcasted_iota(jnp.int32, (16, 1), 0)
     total = part_sums[...]
     for index, value in sums.items():
@@ -679,7 +661,7 @@
             pltpu.SemaphoreType.DMA((2 + 2 * count,)),
         ],
         compiler_params=pltpu.CompilerParams(vmem_limit_bytes=LIMIT),
-        cost_estimate=pl.CostEstimate(flops=10**10, bytes_accessed=0, transcendentals=0),
+        cost_estimate=pl.CostEstimate(flops=10000000000, bytes_accessed=0, transcendentals=0),
         name="attn_bwd",
     )(meta, grad, vecs, x, modulated, qkv_val, prob, att, branch, part_sums, *deps, qkv, out, *pieces)
 
@@ -841,7 +823,8 @@
 
     def kernel(*refs):
         rest = refs[given + len(before) + len(deps) :]
-        outs, blocks, held, sems = rest[:count], rest[count : 2 * count], rest[-2], rest[-1]
+        outs, blocks, held, sems = rest[:count], rest[count + 1 : 2 * count + 1], rest[-2], rest[-1]
+        rest[count][...] = jnp.zeros((8, 128), F32)
         body(*refs[:given], *blocks, held)
         copies = [
             pltpu.make_async_copy(blocks[i], outs[i].at[pl.ds(layer, 1)], sems.at[i])
@@ -854,14 +837,14 @@
 
     return pl.pallas_call(
         kernel,
-        out_shape=tuple(sds(shape, F32) for shape in shapes),
+        out_shape=tuple(sds(shape, F32) for shape in shapes) + (sds((8, 128), F32),),
         in_specs=[SMEM] + [VMEM] * (given - 1) + [HBM] * len(before) + [ANY] * len(deps),
-        out_specs=(HBM,) * count,
+        out_specs=(HBM,) * count + (VMEM,),
         scratch_shapes=[pltpu.VMEM((1,) + shape[1:], F32) for shape in shapes]
         + [pltpu.VMEM(scratch, BF16), pltpu.SemaphoreType.DMA((count,))],
         input_output_aliases={given + index: index for index in range(len(before))},
         compiler_params=pltpu.CompilerParams(vmem_limit_bytes=LIMIT),
-        cost_estimate=pl.CostEstimate(flops=10**10, bytes_accessed=0, transcendentals=0),
+        cost_estimate=pl.CostEstimate(flops=100000000, bytes_accessed=0, transcendentals=0),
         name=name,
     )(*ins, *before, *deps)
 
@@ -870,24 +853,25 @@
     return (condition * (1.0 / (1.0 + jnp.exp(-condition)))).astype(BF16)
 
 
-def ada_result(layer, meta, info, rides, far, ada_weight, before, deps):
+def ada_result(layer, meta, condition, rides, far, ada_weight, before, deps):
+    given = () if condition is None else (condition,)
     slots = rides.shape[0] // 16
     half = D // 2
 
-    def kernel(meta, info, rides, far, ada_hbm, *refs):
-        ada_hbm_out, cond_out, sums_out, own_f32, far_f32, ada, ada_out, sems = refs[-8:]
+    def kernel(meta, rides, far, ada_hbm, *refs):
+        ada_hbm_out, cond_out, known_out, sums_out, own_f32, far_f32, ada, ada_out, sems = refs[-9:]
         load = pltpu.make_async_copy(ada_hbm.at[pl.ds(layer, 1)], ada, sems.at[0])
         load.start()
         for block in range(D // 128):
             lanes = slice(block * 128, (block + 1) * 128)
             own_f32[block, :, :] = rides[:, lanes].astype(F32)
             far_f32[block, :, :] = far[:, lanes].astype(F32)
-        act = silu_bf16(info[:, 0:half])
         first = meta[1] == 0
         grad_cond = jnp.zeros((2 * slots, half), F32)
         load.wait()
         sums_out[...] = jnp.zeros_like(sums_out)
-        for row in range(14):
+
+        def latents_row(row):
             mine, other = (
                 jnp.concatenate(
                     [held[block, pl.ds(row, slots, stride=16), :] for block in range(D // 128)], axis=1
@@ -902,7 +886,18 @@
                 vectors.append(
                     jnp.concatenate([jnp.where(first, one, two), jnp.where(first, two, one)], axis=1)
                 )
-            both = jnp.concatenate(vectors, axis=0)
+            return jnp.concatenate(vectors, axis=0)
+
+        if layer == 1:
+            known = latents_row(14) + latents_row(15)
+            known = jnp.where(meta[0] == 0, known[:, :half], known[:, half:])
+            act = silu_bf16(known)
+        else:
+            known = (latents_row(14) * 32.0 + latents_row(15))[:, :half]
+            act = silu_bf16(refs[0][...])
+        known_out[...] = known
+        for row in range(14):
+            both = latents_row(row)
             sums_out[row : row + 1, :] = jnp.sum(both, axis=0, keepdims=True)
             if row < 6:
                 cols = slice(row * D, (row + 1) * D)
@@ -917,35 +912,38 @@
     shape = ada_weight.shape
     return pl.pallas_call(
         kernel,
-        out_shape=(sds(shape, F32), sds((2 * slots, half), F32), sds((16, D), F32)),
-        in_specs=[SMEM, VMEM, VMEM, VMEM] + [HBM] * (1 + len(before)) + [ANY] * len(deps),
-        out_specs=(HBM, VMEM, VMEM),
+        out_shape=(sds(shape, F32),) + (sds((2 * slots, half), F32),) * 2 + (sds((16, D), F32),),
+        in_specs=[SMEM, VMEM, VMEM, HBM]
+        + [VMEM] * len(given)
+        + [HBM] * len(before)
+        + [ANY] * len(deps),
+        out_specs=(HBM, VMEM, VMEM, VMEM),
         scratch_shapes=[pltpu.VMEM((D // 128, 16 * slots, 128), F32)] * 2
         + [
             pltpu.VMEM((1,) + shape[1:], BF16),
             pltpu.VMEM((1,) + shape[1:], F32),
             pltpu.SemaphoreType.DMA((2,)),
         ],
-        input_output_aliases={5: 0} if before else {},
+        input_output_aliases={4 + len(given): 0} if before else {},
         compiler_params=pltpu.CompilerParams(vmem_limit_bytes=LIMIT),
-        cost_estimate=pl.CostEstimate(flops=10**10, bytes_accessed=0, transcendentals=0),
+        cost_estimate=pl.CostEstimate(flops=100000000, bytes_accessed=0, transcendentals=0),
         name="ada_result",
-    )(meta, info, rides, far, ada_weight, *before, *deps)
-
-
-def condition_result(meta, info, conds, sums, classes, deps):
+    )(meta, rides, far, ada_weight, *given, *before, *deps)
+
+
+def condition_result(meta, condition, labels, conds, sums, classes, deps):
     half = D // 2
 
-    def body(meta, info, cond0, cond1, sums0, sums1, *outs):
+    def body(meta, condition, labels, cond0, cond1, sums0, sums1, *outs):
         table, mine, send, ada, qv, out, up, down = outs
-        condition = info[:, 0:half]
+        condition = condition[...]
         sigmoid = 1.0 / (1.0 + jnp.exp(-condition))
         grads = (cond0[...] + cond1[...]) * sigmoid * (1.0 + condition * (1.0 - sigmoid))
         mine[...] = grads[0:1, :]
         send[...] = grads[1:2, :]
-        labels = info[:, 256:257]
+        labels = labels[:, 0:1]
         count = -(-classes // 128) * 128
-        numbers = lax.broadcasted_iota(jnp.int32, (info.shape[0], count), 1).astype(F32)
+        numbers = lax.broadcasted_iota(jnp.int32, (condition.shape[0], count), 1).astype(F32)
         one_hot = jnp.where(numbers == labels, 1.0, 0.0)
         total = lax.dot_general(
             grads,
@@ -983,8 +981,8 @@
     )
     return call(
         body,
-        (meta, info, *conds, *sums),
-        [SMEM] + [VMEM] * 5,
+        (meta, condition, labels, *conds, *sums),
+        [SMEM] + [VMEM] * 6,
         tuple(sds(shape, F32) for shape in shapes),
         (VMEM,) * len(shapes),
         "condition_result",
@@ -1038,11 +1036,15 @@
 
     first = first_message(timestep_embed, labels, ada_bias, qv_bias, out_bias, up_bias, down_bias)
     got_first = over_x(first)
-    send_a0 = pack_first(meta, qkv_weight, out_weight)
+    send_a0, send_m0 = pack(
+        0, False, 2, meta, qkv_weight, out_weight, up_weight, down_weight, (), "pack_first"
+    )
     classes = class_table.shape[0]
-    info, mine_part, send_part = condition_step(meta, first, got_first, class_table, ada_weight)
-    send_m0, send_a1, send_m1, info = pack_rest(
-        meta, qkv_weight, out_weight, up_weight, down_weight, info, (send_part,)
+    mine_part, send_part = condition_step(
+        meta, first, got_first, class_table, ada_weight, (send_m0,)
+    )
+    send_a1, send_m1 = pack(
+        1, True, 4, meta, qkv_weight, out_weight, up_weight, down_weight, (send_part,), "pack_rest"
     )
 
     def fetch(send, distance):
@@ -1062,20 +1064,18 @@
     distances = [Z]
     while 2 * distances[-1] < reps:
         distances.append(2 * distances[-1])
-    for distance in [Y] + distances + [CORE]:
-        info = jnp.concatenate([info, over_rep(info, distance)], axis=0)
 
     stream = latents[0]
     attn_weights = (qkv_weight, out_weight)
     mlp_weights = (up_weight, down_weight)
     *kept_a0, middle0 = attn_fwd(0, False, meta, stream, vecs[0], *attn_weights, pieces_a0)
     stream1, *kept_m0 = mlp_fwd(
-        0, False, False, meta, middle0, vecs[0], *mlp_weights, pieces_m0, (info,)
+        0, False, False, meta, middle0, vecs[0], *mlp_weights, pieces_m0
     )
     *kept_a1, middle1 = attn_fwd(1, False, meta, stream1, vecs[1], *attn_weights, pieces_a1)
     activations, *kept_m1 = mlp_fwd(1, True, True, meta, middle1, vecs[1], *mlp_weights, pieces_m1)
 
-    last = [activations]
+    last = [vecs_all]
 
     def deps():
         return (last[0],)
@@ -1176,19 +1176,23 @@
     advance(m0, more)
     result_a1, rides1 = advance(a1)
     advance(a0, more)
-    ada_grad, cond1, sums1 = ran(ada_result(1, meta, info, *rides1, ada_weight, (), deps()))
-    mlp_grads = ran(mlp_result(1, meta, result_m1, (), deps()))
+    ada_grad, cond1, condition, sums1 = ran(ada_result(1, meta, None, *rides1, ada_weight, (), deps()))
     advance(m0)
+    *mlp_grads, _ = ran(mlp_result(1, meta, result_m1, (), deps()))
+    *attn_grads, _ = ran(attn_result(1, meta, result_a1, (), deps()))
+    result_a0, rides0 = advance(a0)
     result_m0, _ = advance(m0)
-    result_a0, rides0 = advance(a0)
-    attn_grads = ran(attn_result(1, meta, result_a1, (), deps()))
-    ada_grad, cond0, sums0 = ran(ada_result(0, meta, info, *rides0, ada_weight, (ada_grad,), deps()))
+    ada_grad, cond0, labels_all, sums0 = ran(
+        ada_result(0, meta, condition, *rides0, ada_weight, (ada_grad,), deps())
+    )
     table_grad, mine_cond, send_cond, *bias_grads = ran(
-        condition_result(meta, info, (cond0, cond1), (sums0, sums1), classes, deps())
+        condition_result(
+            meta, condition, labels_all, (cond0, cond1), (sums0, sums1), classes, deps()
+        )
     )
     other_cond = over_x(send_cond)
-    up_grad, down_grad = ran(mlp_result(0, meta, result_m0, mlp_grads, deps()))
-    qkv_grad, out_grad = ran(attn_result(0, meta, result_a0, attn_grads, deps()))
+    qkv_grad, out_grad, _ = ran(attn_result(0, meta, result_a0, attn_grads, deps()))
+    up_grad, down_grad, _ = ran(mlp_result(0, meta, result_m0, mlp_grads, deps()))
     cond_grad = both_halves(meta, mine_cond, other_cond)
     ada_b, qv_b, out_b, up_b, down_b = bias_grads
 

time: 193 us -> 170 us (0.88)
  local copies, waits for them, and re-layouts: 21.4 us -> 2.63 us
  starting transfers between devices: 49.2 us -> 43.2 us
  Pallas kernels: 70.3 us -> 76.2 us
  waiting for transfers between devices: 48.2 us -> 45.2 us
    unnamed x68 -> x26, local copies, waits for them, and re-layouts: 16.8 us -> 2.03 us
    pallas_call x27 -> x29, Pallas kernels: 14.3 us -> 22.8 us  [call(): pl.pallas_call(kernel, out_shape=out_shape, in_specs=list(in_specs) + [AN...]
    ppermute x46 -> x42, waiting for transfers between devices: 34.8 us -> 30.1 us  [over_rep(): return lax.ppermute(value, 'rep', [(r, r ^ distance) for r in range(reps)])]
    concatenate x1 -> x0, local copies, waits for them, and re-layouts: 3.95 us -> none  [on_device(): info = jnp.concatenate([info, over_rep(info, distance)], axis=0)]
    ppermute x11, starting transfers between devices: 14.6 us -> 10.7 us  [over_x(): return lax.ppermute(value, 'shard', [(0, 1), (1, 0)])]
    ppermute x46 -> x42, starting transfers between devices: 34.6 us -> 32.5 us  [over_rep(): return lax.ppermute(value, 'rep', [(r, r ^ distance) for r in range(reps)])]
    pallas_call x4 -> x2, Pallas kernels: 7.7 us -> 6.04 us  [ada_result(): pl.pallas_call(kernel, out_shape=(sds(shape, F32),) + (sds((2 * slots, ha...]
  transfers between devices with their start and end apart: 57 -> 53, of which waited for: 19 -> 16; matrix products, arithmetic and copies ran while one was open for 2% -> 0% of each run, Pallas kernels for 28% -> 36%
where the time goes in v3:
time: 170 us
  Pallas kernels  76.2 us (45%)
  waiting for transfers between devices  45.2 us (27%)
  starting transfers between devices  43.2 us (25%)
  between operations  2.7 us (2%)
  local copies, waits for them, and re-layouts  2.63 us (2%)
    ppermute x42, starting transfers between devices, over_rep(): return lax.ppermute(value, 'rep', [(r, r ^ distance) for r in range(reps)])  32.5 us
    ppermute x42, waiting for transfers between devices, over_rep(): return lax.ppermute(value, 'rep', [(r, r ^ distance) for r in range(reps)])  30.1 us
    pallas_call x29, Pallas kernels, call(): pl.pallas_call(kernel, out_shape=out_shape, in_specs=list(in_specs) + [AN...  22.8 us
    ppermute x11, waiting for transfers between devices, over_x(): return lax.ppermute(value, 'shard', [(0, 1), (1, 0)])  15.1 us
    pallas_call x2, Pallas kernels, mlp_bwd(): pl.pallas_call(functools.partial(mlp_bwd_kernel, layer, far, count, maske...  13 us
    ppermute x11, starting transfers between devices, over_x(): return lax.ppermute(value, 'shard', [(0, 1), (1, 0)])  10.7 us
    pallas_call x2, Pallas kernels, attn_bwd(): pl.pallas_call(functools.partial(attn_bwd_kernel, layer, far, count, extr...  10.6 us
    pallas_call x2, Pallas kernels, mlp_fwd(): pl.pallas_call(functools.partial(mlp_fwd_kernel, layer, far, count, last,...  8.81 us
  transfers between devices with their start and end apart: 53, of which 16 were waited for; matrix products, arithmetic and copies ran while one was open for 0% of the time, Pallas kernels for 36%

profile of v3, /device:TPU:0, one launch (start us, length us, event | category | flops | bytes accessed | tf_op | source)
XLA Modules:
  0.0 169.9 jit_solution(17823839464178417616)
XLA Ops:
  1.3 1.4 first_message.1.refs_1_
  2.7 3.0 %collective-permute-start = (f32[8,1536]{1,0:T(8,128)}, f32[8,1536]{1,0:T(8,128)S(1)}, u32[]{:S(2)}, u32[]{:S(2)}) collective-permute-start(f32[8,1536]{1,0:T(8,128)} %first_message.1.refs_1_), channel_id=1, source_target_pairs={{0,1},{1,0},{2,3},{3,2},{4,5},{5,4},{6,7},{7,6},{8,9},{9,8},{10,11... | collective-permute-start | bytes 147464 | tf_op jit(solution)/shard_map/ppermute | solution.py:1030
  7.0 2.6 %pack_first.1 = (bf16[96,1536]{1,0:T(8,128)(2,1)}, bf16[96,1536]{1,0:T(8,128)(2,1)}) custom-call(s32[6]{0:T(128)} %stack.24.refs_0_.meta, bf16[2,192,1152]{2,1,0:T(8,128)(2,1)} %refs_11_.3, bf16[2,192,384]{2,1,0:T(8,128)(2,1)} %refs_12_.1, bf16[2,192,1536]{2,1,0:T(8,128)(2,1)} %refs_9_.3, bf16[2,768,384]{2,1,0:T(8,128)(2,1)} %refs_10_.5), custom_call_target="tpu_custom_call" | custom-call | flops 10000000000 | tf_op jit(solution)/shard_map/pack_first/pallas_call | solution.py:144
  9.7 2.0 %collective-permute-start.4 = (bf16[96,1536]{1,0:T(8,128)(2,1)}, bf16[96,1536]{1,0:T(8,128)(2,1)S(1)}, u32[]{:S(2)}, u32[]{:S(2)}) collective-permute-start(bf16[96,1536]{1,0:T(8,128)(2,1)} %get-tuple-element.109.refs_5_), channel_id=1, source_target_pairs={{0,1},{1,0},{2,3},{3,2},{4,5},{5,4},{6,7},{7,6},{8,9},{9,8},{10,11... | collective-permute-start | bytes 884744 | tf_op jit(solution)/shard_map/ppermute | solution.py:1030
  12.3 3.5 %condition.1 = (f32[3,2304]{1,0:T(4,128)}, f32[3,2304]{1,0:T(4,128)}) custom-call(s32[6]{0:T(128)} %stack.24.refs_0_.meta, f32[8,1536]{1,0:T(8,128)} %first_message.1.refs_1_, f32[8,1536]{1,0:T(8,128)} %copy-done.10, bf16[192,1001]{1,0:T(8,128)(2,1)} %bitcast.18, bf16[2,192,2304]{2,1,0:T(8,128)(2,1)} %ada_hbm.3, bf16[96,1536]{1,0:T(8,128)(2,1)} %get-tuple-element.109.refs_5_), custom_call_target="tpu_custom_call" | custom-call | flops 10000000000 | tf_op jit(solution)/shard_map/condition/pallas_call | solution.py:144
  16.1 2.5 %pack_rest.1 = (bf16[48,1536]{1,0:T(8,128)(2,1)}, bf16[96,1536]{1,0:T(8,128)(2,1)}) custom-call(s32[6]{0:T(128)} %stack.24.refs_0_.meta, bf16[2,192,1152]{2,1,0:T(8,128)(2,1)} %refs_11_.3, bf16[2,192,384]{2,1,0:T(8,128)(2,1)} %refs_12_.1, bf16[2,192,1536]{2,1,0:T(8,128)(2,1)} %refs_9_.3, bf16[2,768,384]{2,1,0:T(8,128)(2,1)} %refs_10_.5, ...), custom_call_target="tpu_custom_call" | custom-call | flops 10000000000 | tf_op jit(solution)/shard_map/pack_rest/pallas_call | solution.py:144
  18.6 2.0 %collective-permute-start.8 = (bf16[48,1536]{1,0:T(8,128)(2,1)}, bf16[48,1536]{1,0:T(8,128)(2,1)S(1)}, u32[]{:S(2)}, u32[]{:S(2)}) collective-permute-start(bf16[48,1536]{1,0:T(8,128)(2,1)} %get-tuple-element.115), channel_id=1, source_target_pairs={{0,1},{1,0},{2,3},{3,2},{4,5},{5,4},{6,7},{7,6},{8,9},{9,8},{10,11... | collective-permute-start | bytes 442376 | tf_op jit(solution)/shard_map/ppermute | solution.py:1030
  20.7 5.5 %collective-permute-done.4.refs_5_.refs_11_ = bf16[96,1536]{1,0:T(8,128)(2,1)S(1)} collective-permute-done((bf16[96,1536]{1,0:T(8,128)(2,1)}, bf16[96,1536]{1,0:T(8,128)(2,1)S(1)}, u32[]{:S(2)}, u32[]{:S(2)}) %collective-permute-start.4) | collective-permute-done | bytes 294944 | tf_op jit(solution)/shard_map/ppermute | solution.py:1030
  26.1 1.5 collective-permute-start.5
  27.7 0.6 vectors.1.refs_8_
  28.4 1.7 %collective-permute-done.8.refs_5_.refs_12_ = bf16[48,1536]{1,0:T(8,128)(2,1)S(1)} collective-permute-done((bf16[48,1536]{1,0:T(8,128)(2,1)}, bf16[48,1536]{1,0:T(8,128)(2,1)S(1)}, u32[]{:S(2)}, u32[]{:S(2)}) %collective-permute-start.8) | collective-permute-done | bytes 147488 | tf_op jit(solution)/shard_map/ppermute | solution.py:1030
  30.1 1.5 collective-permute-start.9
  31.6 3.3 %collective-permute-done.12.refs_5_.refs_11_ = bf16[96,1536]{1,0:T(8,128)(2,1)S(1)} collective-permute-done((bf16[96,1536]{1,0:T(8,128)(2,1)}, bf16[96,1536]{1,0:T(8,128)(2,1)S(1)}, u32[]{:S(2)}, u32[]{:S(2)}) %collective-permute-start.12) | collective-permute-done | bytes 294944 | tf_op jit(solution)/shard_map/ppermute | solution.py:1030
  35.0 1.6 collective-permute-start.13
  36.8 3.3 %attn_fwd.2 = (bf16[256,384]{1,0:T(8,128)(2,1)S(1)}, bf16[256,1152]{1,0:T(8,128)(2,1)S(1)}, bf16[1536,256]{1,0:T(8,128)(2,1)S(1)}, bf16[256,384]{1,0:T(8,128)(2,...) custom-call(s32[6]{0:T(128)S(1)} %copy-done.1, bf16[256,384]{1,0:T(8,128)(2,1)S(1)} %bitcast.16, ...), custom_call_target="tpu_custom_call" | custom-call | flops 10000000000 | tf_op jit(solution)/shard_map/attn_fwd/pallas_call | solution.py:374
  40.7 3.7 %collective-permute-done.13.refs_6_.refs_12_ = bf16[96,1536]{1,0:T(8,128)(2,1)S(1)} collective-permute-done((bf16[96,1536]{1,0:T(8,128)(2,1)S(1)}, bf16[96,1536]{1,0:T(8,128)(2,1)S(1)}, u32[]{:S(2)}, u32[]{:S(2)}) %collective-permute-start.13) | collective-permute-done | bytes 294944 | tf_op jit(solution)/shard_map/ppermute | solution.py:1033
  44.4 4.1 %mlp_fwd.2 = (f32[256,384]{1,0:T(8,128)S(1)}, bf16[256,384]{1,0:T(8,128)(2,1)S(1)}, bf16[256,1536]{1,0:T(8,128)(2,1)S(1)}, bf16[256,1536]{1,0:T(8,128)(2,1)S(1)}, f32[256,384]{1,0:T(8,128)S(1)}) custom-call(s32[6]{0:T(128)S(1)} %copy-done.1, f32[256,384]{1,0:T(8,128)S(1)} %get-tuple-element.113.refs_1_.refs_3_, f32[16,384]{1,0:T(8,128)S(1)} %get-tuple-element.205.refs_2_, ...), custom_call_target="tpu_custom_call" | custom-call | flops 10000000000 | tf_op jit(solution)/shard_map/mlp_fwd/pallas_call | solution.py:436
  48.5 3.4 %attn_fwd.3 = (bf16[256,384]{1,0:T(8,128)(2,1)S(1)}, bf16[256,1152]{1,0:T(8,128)(2,1)S(1)}, bf16[1536,256]{1,0:T(8,128)(2,1)S(1)}, bf16[256,384]{1,0:T(8,128)(2,...) custom-call(s32[6]{0:T(128)S(1)} %copy-done.1, f32[256,384]{1,0:T(8,128)S(1)} %get-tuple-element.114.refs_1_.refs_3_, ...), custom_call_target="tpu_custom_call" | custom-call | flops 10000000000 | tf_op jit(solution)/shard_map/attn_fwd/pallas_call | solution.py:374
  52.0 4.8 %mlp_fwd.3 = (bf16[256,384]{1,0:T(8,128)(2,1)}, bf16[256,384]{1,0:T(8,128)(2,1)S(1)}, bf16[256,1536]{1,0:T(8,128)(2,1)S(1)}, bf16[256,1536]{1,0:T(8,128)(2,1)S(1)}, f32[256,384]{1,0:T(8,128)S(1)}) custom-call(s32[6]{0:T(128)S(1)} %copy-done.1, f32[256,384]{1,0:T(8,128)S(1)} %get-tuple-element.116.refs_1_.refs_3_, f32[16,384]{1,0:T(8,128)S(1)} %get-tuple-element.204.refs_2_, ...), custom_call_target="tpu_custom_call" | custom-call | flops 10000000000 | tf_op jit(solution)/shard_map/mlp_fwd/pallas_call | solution.py:436
  56.7 6.6 %mlp_bwd.2 = (bf16[1536,384]{1,0:T(8,128)(2,1)S(1)}, bf16[1536,384]{1,0:T(8,128)(2,1)S(1)}, f32[256,384]{1,0:T(8,128)S(1)}, f32[16,384]{1,0:T(8,128)S(1)}) custom-call(s32[6]{0:T(128)S(1)} %copy-done.1, bf16[256,384]{1,0:T(8,128)(2,1)S(1)} %bitcast.15, f32[16,384]{1,0:T(8,128)S(1)} %get-tuple-element.204.refs_2_, ...), custom_call_target="tpu_custom_call" | custom-call | flops 10000000000 | tf_op jit(solution)/shard_map/mlp_bwd/pallas_call | solution.py:527
  63.9 4.9 %attn_bwd.2 = (bf16[768,384]{1,0:T(8,128)(2,1)S(1)}, bf16[784,384]{1,0:T(8,128)(2,1)S(1)}, f32[256,384]{1,0:T(8,128)S(1)}, bf16[16,384]{1,0:T(8,128)(2,1)S(1)}) custom-call(s32[6]{0:T(128)S(1)} %copy-done.1, f32[256,384]{1,0:T(8,128)S(1)} %get-tuple-element.123.refs_1_, f32[16,384]{1,0:T(8,128)S(1)} %get-tuple-element.204.refs_2_, ...), custom_call_target="tpu_custom_call" | custom-call | flops 10000000000 | tf_op jit(solution)/shard_map/attn_bwd/pallas_call | solution.py:646
  68.9 0.8 first_split.4
  70.2 6.4 %mlp_bwd.3 = (bf16[1536,384]{1,0:T(8,128)(2,1)S(1)}, bf16[1536,384]{1,0:T(8,128)(2,1)S(1)}, f32[256,384]{1,0:T(8,128)S(1)}, f32[16,384]{1,0:T(8,128)S(1)}) custom-call(s32[6]{0:T(128)S(1)} %copy-done.1, f32[256,384]{1,0:T(8,128)S(1)} %get-tuple-element.130.refs_1_, f32[16,384]{1,0:T(8,128)S(1)} %get-tuple-element.205.refs_2_, ...), custom_call_target="tpu_custom_call" | custom-call | flops 10000000000 | tf_op jit(solution)/shard_map/mlp_bwd/pallas_call | solution.py:527
  76.6 0.8 first_split.5
  77.4 1.7 %collective-permute-start.18 = (bf16[400,384]{1,0:T(8,128)(2,1)S(1)}, bf16[400,384]{1,0:T(8,128)(2,1)S(1)}, u32[]{:S(2)}, u32[]{:S(2)}) collective-permute-start(bf16[400,384]{1,0:T(8,128)(2,1)S(1)} %get-tuple-element.148.refs_10_.refs_2_), channel_id=1, source_target_pairs={{0,1},{1,0},{2,3},{3,2},{4,5},{5,4},{6,7},{7,6},{8,9},{9,8},{10,11... | collective-permute-start | bytes 921608 | tf_op jit(solution)/shard_map/ppermute | solution.py:1030
  79.1 5.7 %attn_bwd.3 = (bf16[768,384]{1,0:T(8,128)(2,1)S(1)}, bf16[784,384]{1,0:T(8,128)(2,1)S(1)}, f32[256,384]{1,0:T(8,128)}, bf16[16,384]{1,0:T(8,128)(2,1)S(1)}) custom-call(s32[6]{0:T(128)S(1)} %copy-done.1, f32[256,384]{1,0:T(8,128)S(1)} %get-tuple-element.139.refs_1_, f32[16,384]{1,0:T(8,128)S(1)} %get-tuple-element.205.refs_2_, ...), custom_call_target="tpu_custom_call" | custom-call | flops 10000000000 | tf_op jit(solution)/shard_map/attn_bwd/pallas_call | solution.py:646
  85.9 0.7 next_split.6
  86.6 1.6 collective-permute-start.22
  88.2 0.8 first_split.6
  89.7 2.9 %collective-permute-done.18.refs_3_ = bf16[400,384]{1,0:T(8,128)(2,1)S(1)} collective-permute-done((bf16[400,384]{1,0:T(8,128)(2,1)S(1)}, bf16[400,384]{1,0:T(8,128)(2,1)S(1)}, u32[]{:S(2)}, u32[]{:S(2)}) %collective-permute-start.18) | collective-permute-done | bytes 307232 | tf_op jit(solution)/shard_map/ppermute | solution.py:1030
  93.2 1.6 collective-permute-start.21
  94.7 0.8 first_split.7
  96.8 1.6 collective-permute-start.26
  98.9 1.6 collective-permute-start.24
  100.5 3.0 %collective-permute-done.26.refs_2_ = bf16[192,384]{1,0:T(8,128)(2,1)S(1)} collective-permute-done((bf16[192,384]{1,0:T(8,128)(2,1)S(1)}, bf16[192,384]{1,0:T(8,128)(2,1)S(1)}, u32[]{:S(2)}, u32[]{:S(2)}) %collective-permute-start.26) | collective-permute-done | bytes 147488 | tf_op jit(solution)/shard_map/ppermute | solution.py:1033
  103.5 2.6 %collective-permute-start.29 = (bf16[192,384]{1,0:T(8,128)(2,1)S(1)}, bf16[192,384]{1,0:T(8,128)(2,1)S(1)}, u32[]{:S(2)}, u32[]{:S(2)}) collective-permute-start(bf16[192,384]{1,0:T(8,128)(2,1)S(1)} %add_join.11.refs_4_.refs_0_.refs_1_), channel_id=1, source_target_pairs={{0,16},{2,18},{4,20},{6,22},{8,24},{10,26},{12,28},{14,30},{16,0},... | collective-permute-start | bytes 442376 | tf_op jit(solution)/shard_map/ppermute | solution.py:1033
  106.2 0.7 next_split.9
  107.5 2.7 %collective-permute-start.27 = (bf16[320,384]{1,0:T(8,128)(2,1)S(1)}, bf16[320,384]{1,0:T(8,128)(2,1)S(1)}, u32[]{:S(2)}, u32[]{:S(2)}) collective-permute-start(bf16[320,384]{1,0:T(8,128)(2,1)S(1)} %add_join.12.refs_4_.refs_0_.refs_1_), channel_id=1, source_target_pairs={{0,16},{2,18},{4,20},{6,22},{8,24},{10,26},{12,28},{14,30},{16,0},... | collective-permute-start | bytes 737288 | tf_op jit(solution)/shard_map/ppermute | solution.py:1033
  110.1 1.2 collective-permute-done.30.refs_3_
  111.9 1.6 collective-permute-start.33
  113.5 4.1 %collective-permute-done.29.refs_2_ = bf16[192,384]{1,0:T(8,128)(2,1)S(1)} collective-permute-done((bf16[192,384]{1,0:T(8,128)(2,1)S(1)}, bf16[192,384]{1,0:T(8,128)(2,1)S(1)}, u32[]{:S(2)}, u32[]{:S(2)}) %collective-permute-start.29) | collective-permute-done | bytes 147488 | tf_op jit(solution)/shard_map/ppermute | solution.py:1033
  117.6 0.7 collective-permute-start.32
  119.0 1.4 collective-permute-start.31
  120.5 0.7 collective-permute-start.35
  121.2 4.3 %collective-permute-done.32.refs_2_ = bf16[192,384]{1,0:T(8,128)(2,1)S(1)} collective-permute-done((bf16[192,384]{1,0:T(8,128)(2,1)S(1)}, bf16[192,384]{1,0:T(8,128)(2,1)S(1)}, u32[]{:S(2)}, u32[]{:S(2)}) %collective-permute-start.32) | collective-permute-done | bytes 147488 | tf_op jit(solution)/shard_map/ppermute | solution.py:1033
  126.1 0.8 collective-permute-start.40
  126.9 1.7 %collective-permute-done.31.refs_2_ = bf16[192,384]{1,0:T(8,128)(2,1)S(1)} collective-permute-done((bf16[192,384]{1,0:T(8,128)(2,1)S(1)}, bf16[192,384]{1,0:T(8,128)(2,1)S(1)}, u32[]{:S(2)}, u32[]{:S(2)}) %collective-permute-start.31) | collective-permute-done | bytes 147488 | tf_op jit(solution)/shard_map/ppermute | solution.py:1033
  128.7 1.1 collective-permute-start.43
  129.9 3.6 %collective-permute-done.35.refs_2_ = bf16[256,384]{1,0:T(8,128)(2,1)S(1)} collective-permute-done((bf16[256,384]{1,0:T(8,128)(2,1)S(1)}, bf16[256,384]{1,0:T(8,128)(2,1)S(1)}, u32[]{:S(2)}, u32[]{:S(2)}) %collective-permute-start.35) | collective-permute-done | bytes 196640 | tf_op jit(solution)/shard_map/ppermute | solution.py:1033
  133.7 1.3 copy-done
  135.1 2.9 %ada_result.2 = (f32[2,192,2304]{2,1,0:T(8,128)}, f32[32,192]{1,0:T(8,128)S(1)}, f32[32,192]{1,0:T(8,128)S(1)}, f32[16,384]{1,0:T(8,128)S(1)}) custom-call(s32[6]{0:T(128)S(1)} %copy-done.1, bf16[256,384]{1,0:T(8,128)(2,1)S(1)} %get-tuple-element.173.refs_3_.rides, bf16[256,384]{1,0:T(8,128)(2,1)S(1)} %collective-permute-done.34.far, ...), custom_call_target="tpu_custom_call" | custom-call | flops 100000000 | tf_op jit(solution)/shard_map/ada_result/pallas_call | solution.py:913
  138.0 0.7 collective-permute-done.37.refs_2_
  138.7 0.7 collective-permute-start.36
  140.0 2.7 %collective-permute-start.45 = (bf16[192,384]{1,0:T(8,128)(2,1)S(1)}, bf16[192,384]{1,0:T(8,128)(2,1)S(1)}, u32[]{:S(2)}, u32[]{:S(2)}) collective-permute-start(bf16[192,384]{1,0:T(8,128)(2,1)S(1)} %add_join.18.refs_5_.refs_1_), channel_id=1, source_target_pairs={{0,8},{2,10},{4,12},{6,14},{8,0},{10,2},{12,4},{14,6},{16,24},{18,... | collective-permute-start | bytes 442376 | tf_op jit(solution)/shard_map/ppermute | solution.py:1033
  142.8 2.1 %mlp_result.2 = (f32[2,192,1536]{2,1,0:T(8,128)}, f32[2,768,384]{2,1,0:T(8,128)}, f32[8,128]{1,0:T(8,128)S(1)}) custom-call(s32[6]{0:T(128)S(1)} %copy-done.1, bf16[384,384]{1,0:T(8,128)(2,1)S(1)} %join.2.refs_3_.refs_1_, bf16[384,384]{1,0:T(8,128)(2,1)S(1)} %collective-permute-done.40.refs_2_, bf16[384,384]{1,0:T(8,128)(2,1)S(1)} %collective-permute-done.41.refs_3_, ...), custom_call_target="tpu_custom_call" | custom-call | flops 100000000 | tf_op jit(solution)/shard_map/mlp_result/pallas_call | solution.py:838
  144.9 1.7 attn_result.2
  146.6 4.7 %collective-permute-done.36.refs_2_ = bf16[320,384]{1,0:T(8,128)(2,1)S(1)} collective-permute-done((bf16[320,384]{1,0:T(8,128)(2,1)S(1)}, bf16[320,384]{1,0:T(8,128)(2,1)S(1)}, u32[]{:S(2)}, u32[]{:S(2)}) %collective-permute-start.36) | collective-permute-done | bytes 245792 | tf_op jit(solution)/shard_map/ppermute | solution.py:1033
  151.5 1.6 collective-permute-start.47
  154.2 3.1 %ada_result.3 = (f32[2,192,2304]{2,1,0:T(8,128)}, f32[32,192]{1,0:T(8,128)S(1)}, f32[32,192]{1,0:T(8,128)S(1)}, f32[16,384]{1,0:T(8,128)S(1)}) custom-call(s32[6]{0:T(128)S(1)} %copy-done.1, bf16[256,384]{1,0:T(8,128)(2,1)S(1)} %get-tuple-element.179.refs_3_.rides, ...), custom_call_target="tpu_custom_call", output_to_operand_aliasing={{0}: (5, {})} | custom-call | flops 100000000 | tf_op jit(solution)/shard_map/ada_result/pallas_call | solution.py:913
  157.4 2.3 %condition_result.1 = (f32[192,1001]{1,0:T(8,128)}, f32[1,192]{1,0:T(1,128)S(1)}, f32[1,192]{1,0:T(1,128)S(1)}, f32[2,1152]{1,0:T(2,128)}, f32[2,384]{1,0:T(2,12...) custom-call(s32[6]{0:T(128)S(1)} %copy-done.1, f32[32,192]{1,0:T(8,128)S(1)} %get-tuple-element.174.refs_0_.refs_1_, ...), custom_call_target="tpu_custom_call" | custom-call | flops 10000000000 | tf_op jit(solution)/shard_map/condition_result/pallas_call | solution.py:144
  160.3 3.8 %collective-permute-done.50.refs_2_ = bf16[384,384]{1,0:T(8,128)(2,1)S(1)} collective-permute-done((bf16[384,384]{1,0:T(8,128)(2,1)S(1)}, bf16[384,384]{1,0:T(8,128)(2,1)S(1)}, u32[]{:S(2)}, u32[]{:S(2)}) %collective-permute-start.50) | collective-permute-done | bytes 294944 | tf_op jit(solution)/shard_map/ppermute | solution.py:1033
  164.1 1.2 both_halves.1
  165.3 1.7 attn_result.3
  167.0 2.7 %mlp_result.3 = (f32[2,192,1536]{2,1,0:T(8,128)}, f32[2,768,384]{2,1,0:T(8,128)}, f32[8,128]{1,0:T(8,128)}) custom-call(s32[6]{0:T(128)S(1)} %copy-done.1, bf16[384,384]{1,0:T(8,128)(2,1)S(1)} %join.3.refs_2_.refs_1_, bf16[384,384]{1,0:T(8,128)(2,1)S(1)} %collective-permute-done.50.refs_2_, ...), custom_call_target="tpu_custom_call", output_to_operand_aliasing={{0}: (5, {}), {1}: (6, {})} | custom-call | flops 100000000 | tf_op jit(solution)/shard_map/mlp_result/pallas_call | solution.py:838
  (113 shorter events, 13.0 us)
Async XLA Ops:
  2.7 9.0 %collective-permute-start = (f32[8,1536]{1,0:T(8,128)}, f32[8,1536]{1,0:T(8,128)S(1)}, u32[]{:S(2)}, u32[]{:S(2)}) collective-permute-start(f32[8,1536]{1,0:T(8,128)} %first_message.1.refs_1_), channel_id=1, source_target_pairs={{0,1},{1,0},{2,3},{3,2},{4,5},{5,4},{6,7},{7,6},{8,9},{9,8},{10,11... | collective-permute-start | bytes 147464 | tf_op jit(solution)/shard_map/ppermute | solution.py:1030
  9.6 11.1 %collective-permute-start.2 = (bf16[96,1536]{1,0:T(8,128)(2,1)}, bf16[96,1536]{1,0:T(8,128)(2,1)S(1)}, u32[]{:S(2)}, u32[]{:S(2)}) collective-permute-start(bf16[96,1536]{1,0:T(8,128)(2,1)} %get-tuple-element.112), channel_id=1, source_target_pairs={{0,1},{1,0},{2,3},{3,2},{4,5},{5,4},{6,7},{7,6},{8,9},{9,8},{10,11... | collective-permute-start | bytes 884744 | tf_op jit(solution)/shard_map/ppermute | solution.py:1030
  9.7 16.4 %collective-permute-start.4 = (bf16[96,1536]{1,0:T(8,128)(2,1)}, bf16[96,1536]{1,0:T(8,128)(2,1)S(1)}, u32[]{:S(2)}, u32[]{:S(2)}) collective-permute-start(bf16[96,1536]{1,0:T(8,128)(2,1)} %get-tuple-element.109.refs_5_), channel_id=1, source_target_pairs={{0,1},{1,0},{2,3},{3,2},{4,5},{5,4},{6,7},{7,6},{8,9},{9,8},{10,11... | collective-permute-start | bytes 884744 | tf_op jit(solution)/shard_map/ppermute | solution.py:1030
  15.9 11.8 %copy-start.1 = (s32[6]{0:T(128)S(1)}, s32[6]{0:T(128)}, u32[]{:S(2)}) copy-start(s32[6]{0:T(128)} %stack.24.refs_0_.meta) | copy-start | bytes 76
  15.9 11.8 %copy-start.9 = (f32[8,1536]{1,0:T(8,128)S(1)}, f32[8,1536]{1,0:T(8,128)}, u32[]{:S(2)}) copy-start(f32[8,1536]{1,0:T(8,128)} %first_message.1.refs_1_) | copy-start | bytes 147460
  15.9 11.8 %copy-start.11 = (f32[8,1536]{1,0:T(8,128)S(1)}, f32[8,1536]{1,0:T(8,128)}, u32[]{:S(2)}) copy-start(f32[8,1536]{1,0:T(8,128)} %copy-done.10) | copy-start | bytes 147460
  15.9 11.8 %copy-start.12 = (f32[3,2304]{1,0:T(4,128)S(1)}, f32[3,2304]{1,0:T(4,128)}, u32[]{:S(2)}) copy-start(f32[3,2304]{1,0:T(4,128)} %get-tuple-element.110.refs_3_) | copy-start | bytes 82948
  15.9 11.7 %collective-permute-start.1 = (f32[3,2304]{1,0:T(4,128)}, f32[3,2304]{1,0:T(4,128)S(1)}, u32[]{:S(2)}, u32[]{:S(2)}) collective-permute-start(f32[3,2304]{1,0:T(4,128)} %get-tuple-element.111.refs_5_), channel_id=1, source_target_pairs={{0,1},{1,0},{2,3},{3,2},{4,5},{5,4},{6,7},{7,6},{8,9},{9,8},{10,11... | collective-permute-start | bytes 82952 | tf_op jit(solution)/shard_map/ppermute | solution.py:1030
  18.6 11.5 %collective-permute-start.8 = (bf16[48,1536]{1,0:T(8,128)(2,1)}, bf16[48,1536]{1,0:T(8,128)(2,1)S(1)}, u32[]{:S(2)}, u32[]{:S(2)}) collective-permute-start(bf16[48,1536]{1,0:T(8,128)(2,1)} %get-tuple-element.115), channel_id=1, source_target_pairs={{0,1},{1,0},{2,3},{3,2},{4,5},{5,4},{6,7},{7,6},{8,9},{9,8},{10,11... | collective-permute-start | bytes 442376 | tf_op jit(solution)/shard_map/ppermute | solution.py:1030
  20.6 14.4 %collective-permute-start.12 = (bf16[96,1536]{1,0:T(8,128)(2,1)}, bf16[96,1536]{1,0:T(8,128)(2,1)S(1)}, u32[]{:S(2)}, u32[]{:S(2)}) collective-permute-start(bf16[96,1536]{1,0:T(8,128)(2,1)} %get-tuple-element.117), channel_id=1, source_target_pairs={{0,1},{1,0},{2,3},{3,2},{4,5},{5,4},{6,7},{7,6},{8,9},{9,8},{10,11... | collective-permute-start | bytes 884744 | tf_op jit(solution)/shard_map/ppermute | solution.py:1030
  20.7 14.3 %collective-permute-start.3 = (bf16[96,1536]{1,0:T(8,128)(2,1)S(1)}, bf16[96,1536]{1,0:T(8,128)(2,1)S(1)}, u32[]{:S(2)}, u32[]{:S(2)}) collective-permute-start(bf16[96,1536]{1,0:T(8,128)(2,1)S(1)} %collective-permute-done.2.refs_5_.refs_13_), channel_id=1, source_target_pairs={{0,2},{2,0},{4,6},{6,4},{8,10},{10,8},{12,14},{14,12},{16,18},{18,... | collective-permute-start | bytes 884744 | tf_op jit(solution)/shard_map/ppermute | solution.py:1033
  26.1 10.4 %collective-permute-start.5 = (bf16[96,1536]{1,0:T(8,128)(2,1)S(1)}, bf16[96,1536]{1,0:T(8,128)(2,1)S(1)}, u32[]{:S(2)}, u32[]{:S(2)}) collective-permute-start(bf16[96,1536]{1,0:T(8,128)(2,1)S(1)} %collective-permute-done.4.refs_5_.refs_11_), channel_id=1, source_target_pairs={{0,4},{2,6},{4,0},{6,2},{8,12},{10,14},{12,8},{14,10},{16,20},{18,... | collective-permute-start | bytes 884744 | tf_op jit(solution)/shard_map/ppermute | solution.py:1033
  27.7 9.1 %copy-start.5 = (bf16[2,192,1152]{2,1,0:T(8,128)(2,1)S(1)}, bf16[2,192,1152]{2,1,0:T(8,128)(2,1)}, u32[]{:S(2)}) copy-start(bf16[2,192,1152]{2,1,0:T(8,128)(2,1)} %refs_11_.3) | copy-start | bytes 2654212
  27.7 9.1 %copy-start.6 = (bf16[2,192,384]{2,1,0:T(8,128)(2,1)S(1)}, bf16[2,192,384]{2,1,0:T(8,128)(2,1)}, u32[]{:S(2)}) copy-start(bf16[2,192,384]{2,1,0:T(8,128)(2,1)} %refs_12_.1) | copy-start | bytes 884740
  27.7 9.1 %copy-start.8 = (bf16[1,256,384]{2,1,0:T(8,128)(2,1)S(1)}, bf16[1,256,384]{2,1,0:T(8,128)(2,1)}, u32[]{:S(2)}) copy-start(bf16[1,256,384]{2,1,0:T(8,128)(2,1)} %param.16) | copy-start | bytes 589828
  30.1 10.0 %collective-permute-start.9 = (bf16[48,1536]{1,0:T(8,128)(2,1)S(1)}, bf16[48,1536]{1,0:T(8,128)(2,1)S(1)}, u32[]{:S(2)}, u32[]{:S(2)}) collective-permute-start(bf16[48,1536]{1,0:T(8,128)(2,1)S(1)} %collective-permute-done.8.refs_5_.refs_12_), channel_id=1, source_target_pairs={{0,4},{2,6},{4,0},{6,2},{8,12},{10,14},{12,8},{14,10},{16,20},{18,... | collective-permute-start | bytes 442376 | tf_op jit(solution)/shard_map/ppermute | solution.py:1033
  31.6 16.9 %collective-permute-start.10 = (bf16[48,1536]{1,0:T(8,128)(2,1)S(1)}, bf16[48,1536]{1,0:T(8,128)(2,1)S(1)}, u32[]{:S(2)}, u32[]{:S(2)}) collective-permute-start(bf16[48,1536]{1,0:T(8,128)(2,1)S(1)} %collective-permute-done.8.refs_5_.refs_12_), channel_id=1, source_target_pairs={{0,2},{2,0},{4,6},{6,4},{8,10},{10,8},{12,14},{14,12},{16,18},{18,... | collective-permute-start | bytes 442376 | tf_op jit(solution)/shard_map/ppermute | solution.py:1033
  35.0 5.5 %collective-permute-start.6 = (bf16[96,1536]{1,0:T(8,128)(2,1)S(1)}, bf16[96,1536]{1,0:T(8,128)(2,1)S(1)}, u32[]{:S(2)}, u32[]{:S(2)}) collective-permute-start(bf16[96,1536]{1,0:T(8,128)(2,1)S(1)} %collective-permute-done.4.refs_5_.refs_11_), channel_id=1, source_target_pairs={{0,2},{2,0},{4,6},{6,4},{8,10},{10,8},{12,14},{14,12},{16,18},{18,... | collective-permute-start | bytes 884744 | tf_op jit(solution)/shard_map/ppermute | solution.py:1033
  35.0 9.4 %collective-permute-start.13 = (bf16[96,1536]{1,0:T(8,128)(2,1)S(1)}, bf16[96,1536]{1,0:T(8,128)(2,1)S(1)}, u32[]{:S(2)}, u32[]{:S(2)}) collective-permute-start(bf16[96,1536]{1,0:T(8,128)(2,1)S(1)} %collective-permute-done.12.refs_5_.refs_11_), channel_id=1, source_target_pairs={{0,8},{2,10},{4,12},{6,14},{8,0},{10,2},{12,4},{14,6},{16,24},{18,... | collective-permute-start | bytes 884744 | tf_op jit(solution)/shard_map/ppermute | solution.py:1033
  36.5 7.8 %collective-permute-start.7 = (bf16[96,1536]{1,0:T(8,128)(2,1)S(1)}, bf16[96,1536]{1,0:T(8,128)(2,1)S(1)}, u32[]{:S(2)}, u32[]{:S(2)}) collective-permute-start(bf16[96,1536]{1,0:T(8,128)(2,1)S(1)} %collective-permute-done.5.refs_6_.refs_12_), channel_id=1, source_target_pairs={{0,2},{2,0},{4,6},{6,4},{8,10},{10,8},{12,14},{14,12},{16,18},{18,... | collective-permute-start | bytes 884744 | tf_op jit(solution)/shard_map/ppermute | solution.py:1033
  36.8 7.6 %copy-start.3 = (bf16[2,192,1536]{2,1,0:T(8,128)(2,1)S(1)}, bf16[2,192,1536]{2,1,0:T(8,128)(2,1)}, u32[]{:S(2)}) copy-start(bf16[2,192,1536]{2,1,0:T(8,128)(2,1)} %refs_9_.3) | copy-start | bytes 3538948
  36.8 7.6 %copy-start.4 = (bf16[2,768,384]{2,1,0:T(8,128)(2,1)S(1)}, bf16[2,768,384]{2,1,0:T(8,128)(2,1)}, u32[]{:S(2)}) copy-start(bf16[2,768,384]{2,1,0:T(8,128)(2,1)} %refs_10_.5) | copy-start | bytes 3538948
  40.1 11.8 %collective-permute-start.14 = (bf16[96,1536]{1,0:T(8,128)(2,1)S(1)}, bf16[96,1536]{1,0:T(8,128)(2,1)S(1)}, u32[]{:S(2)}, u32[]{:S(2)}) collective-permute-start(bf16[96,1536]{1,0:T(8,128)(2,1)S(1)} %collective-permute-done.12.refs_5_.refs_11_), channel_id=1, source_target_pairs={{0,2},{2,0},{4,6},{6,4},{8,10},{10,8},{12,14},{14,12},{16,18},{18,... | collective-permute-start | bytes 884744 | tf_op jit(solution)/shard_map/ppermute | solution.py:1033
  40.5 8.0 %collective-permute-start.11 = (bf16[48,1536]{1,0:T(8,128)(2,1)S(1)}, bf16[48,1536]{1,0:T(8,128)(2,1)S(1)}, u32[]{:S(2)}, u32[]{:S(2)}) collective-permute-start(bf16[48,1536]{1,0:T(8,128)(2,1)S(1)} %collective-permute-done.9.refs_6_.refs_13_), channel_id=1, source_target_pairs={{0,2},{2,0},{4,6},{6,4},{8,10},{10,8},{12,14},{14,12},{16,18},{18,... | collective-permute-start | bytes 442376 | tf_op jit(solution)/shard_map/ppermute | solution.py:1033
  44.4 7.6 %collective-permute-start.15 = (bf16[96,1536]{1,0:T(8,128)(2,1)S(1)}, bf16[96,1536]{1,0:T(8,128)(2,1)S(1)}, u32[]{:S(2)}, u32[]{:S(2)}) collective-permute-start(bf16[96,1536]{1,0:T(8,128)(2,1)S(1)} %collective-permute-done.13.refs_6_.refs_12_), channel_id=1, source_target_pairs={{0,2},{2,0},{4,6},{6,4},{8,10},{10,8},{12,14},{14,12},{16,18},{18,... | collective-permute-start | bytes 884744 | tf_op jit(solution)/shard_map/ppermute | solution.py:1033
  52.0 4.8 %copy-start.7 = (bf16[1,256,384]{2,1,0:T(8,128)(2,1)S(1)}, bf16[1,256,384]{2,1,0:T(8,128)(2,1)}, u32[]{:S(2)}) copy-start(bf16[1,256,384]{2,1,0:T(8,128)(2,1)} %param.31) | copy-start | bytes 589828
  63.3 5.6 %collective-permute-start.16 = (bf16[1536,384]{1,0:T(8,128)(2,1)S(1)}, bf16[1536,384]{1,0:T(8,128)(2,1)S(1)}, u32[]{:S(2)}, u32[]{:S(2)}) collective-permute-start(bf16[1536,384]{1,0:T(8,128)(2,1)S(1)} %get-tuple-element.136), channel_id=1, source_target_pairs={{0,2},{2,0},{4,6},{6,4},{8,10},{10,8},{12,14},{14,12},{16,18},{18,... | collective-permute-start | bytes 3538952 | tf_op jit(solution)/shard_map/ppermute | solution.py:1033
  68.8 7.8 %collective-permute-start.17 = (bf16[784,384]{1,0:T(8,128)(2,1)S(1)}, bf16[784,384]{1,0:T(8,128)(2,1)S(1)}, u32[]{:S(2)}, u32[]{:S(2)}) collective-permute-start(bf16[784,384]{1,0:T(8,128)(2,1)S(1)} %get-tuple-element.147), channel_id=1, source_target_pairs={{0,2},{2,0},{4,6},{6,4},{8,10},{10,8},{12,14},{14,12},{16,18},{18,... | collective-permute-start | bytes 1806344 | tf_op jit(solution)/shard_map/ppermute | solution.py:1033
  69.7 16.2 %collective-permute-start.20 = (bf16[768,384]{1,0:T(8,128)(2,1)S(1)}, bf16[768,384]{1,0:T(8,128)(2,1)S(1)}, u32[]{:S(2)}, u32[]{:S(2)}) collective-permute-start(bf16[768,384]{1,0:T(8,128)(2,1)S(1)} %get-tuple-element.138.refs_8_.refs_2_), channel_id=1, source_target_pairs={{0,1},{1,0},{2,3},{3,2},{4,5},{5,4},{6,7},{7,6},{8,9},{9,8},{10,11... | collective-permute-start | bytes 1769480 | tf_op jit(solution)/shard_map/ppermute | solution.py:1030
  77.4 15.1 %collective-permute-start.18 = (bf16[400,384]{1,0:T(8,128)(2,1)S(1)}, bf16[400,384]{1,0:T(8,128)(2,1)S(1)}, u32[]{:S(2)}, u32[]{:S(2)}) collective-permute-start(bf16[400,384]{1,0:T(8,128)(2,1)S(1)} %get-tuple-element.148.refs_10_.refs_2_), channel_id=1, source_target_pairs={{0,1},{1,0},{2,3},{3,2},{4,5},{5,4},{6,7},{7,6},{8,9},{9,8},{10,11... | collective-permute-start | bytes 921608 | tf_op jit(solution)/shard_map/ppermute | solution.py:1030
  79.1 9.1 %collective-permute-start.19 = (bf16[1536,384]{1,0:T(8,128)(2,1)S(1)}, bf16[1536,384]{1,0:T(8,128)(2,1)S(1)}, u32[]{:S(2)}, u32[]{:S(2)}) collective-permute-start(bf16[1536,384]{1,0:T(8,128)(2,1)S(1)} %get-tuple-element.152), channel_id=1, source_target_pairs={{0,2},{2,0},{4,6},{6,4},{8,10},{10,8},{12,14},{14,12},{16,18},{18,... | collective-permute-start | bytes 3538952 | tf_op jit(solution)/shard_map/ppermute | solution.py:1033
  84.8 9.9 %collective-permute-start.23 = (bf16[784,384]{1,0:T(8,128)(2,1)S(1)}, bf16[784,384]{1,0:T(8,128)(2,1)S(1)}, u32[]{:S(2)}, u32[]{:S(2)}) collective-permute-start(bf16[784,384]{1,0:T(8,128)(2,1)S(1)} %get-tuple-element.161), channel_id=1, source_target_pairs={{0,2},{2,0},{4,6},{6,4},{8,10},{10,8},{12,14},{14,12},{16,18},{18,... | collective-permute-start | bytes 1806344 | tf_op jit(solution)/shard_map/ppermute | solution.py:1033
  86.6 9.5 %collective-permute-start.22 = (bf16[384,384]{1,0:T(8,128)(2,1)S(1)}, bf16[384,384]{1,0:T(8,128)(2,1)S(1)}, u32[]{:S(2)}, u32[]{:S(2)}) collective-permute-start(bf16[384,384]{1,0:T(8,128)(2,1)S(1)} %get-tuple-element.155.refs_3_.refs_2_), channel_id=1, source_target_pairs={{0,4},{2,6},{4,0},{6,2},{8,12},{10,14},{12,8},{14,10},{16,20},{18,... | collective-permute-start | bytes 884744 | tf_op jit(solution)/shard_map/ppermute | solution.py:1033
  89.1 17.1 %collective-permute-start.25 = (bf16[768,384]{1,0:T(8,128)(2,1)S(1)}, bf16[768,384]{1,0:T(8,128)(2,1)S(1)}, u32[]{:S(2)}, u32[]{:S(2)}) collective-permute-start(bf16[768,384]{1,0:T(8,128)(2,1)S(1)} %get-tuple-element.156.refs_4_.refs_2_), channel_id=1, source_target_pairs={{0,1},{1,0},{2,3},{3,2},{4,5},{5,4},{6,7},{7,6},{8,9},{9,8},{10,11... | collective-permute-start | bytes 1769480 | tf_op jit(solution)/shard_map/ppermute | solution.py:1030
  93.2 5.7 %collective-permute-start.21 = (bf16[224,384]{1,0:T(8,128)(2,1)S(1)}, bf16[224,384]{1,0:T(8,128)(2,1)S(1)}, u32[]{:S(2)}, u32[]{:S(2)}) collective-permute-start(bf16[224,384]{1,0:T(8,128)(2,1)S(1)} %get-tuple-element.158.refs_4_.refs_1_), channel_id=1, source_target_pairs={{0,4},{2,6},{4,0},{6,2},{8,12},{10,14},{12,8},{14,10},{16,20},{18,... | collective-permute-start | bytes 516104 | tf_op jit(solution)/shard_map/ppermute | solution.py:1033
  95.5 15.8 %collective-permute-start.30 = (bf16[400,384]{1,0:T(8,128)(2,1)S(1)}, bf16[400,384]{1,0:T(8,128)(2,1)S(1)}, u32[]{:S(2)}, u32[]{:S(2)}) collective-permute-start(bf16[400,384]{1,0:T(8,128)(2,1)S(1)} %get-tuple-element.162.refs_4_.refs_2_), channel_id=1, source_target_pairs={{0,1},{1,0},{2,3},{3,2},{4,5},{5,4},{6,7},{7,6},{8,9},{9,8},{10,11... | collective-permute-start | bytes 921608 | tf_op jit(solution)/shard_map/ppermute | solution.py:1030
  96.8 6.7 %collective-permute-start.26 = (bf16[192,384]{1,0:T(8,128)(2,1)S(1)}, bf16[192,384]{1,0:T(8,128)(2,1)S(1)}, u32[]{:S(2)}, u32[]{:S(2)}) collective-permute-start(bf16[192,384]{1,0:T(8,128)(2,1)S(1)} %get-tuple-element.163.refs_3_.refs_1_), channel_id=1, source_target_pairs={{0,8},{2,10},{4,12},{6,14},{8,0},{10,2},{12,4},{14,6},{16,24},{18,... | collective-permute-start | bytes 442376 | tf_op jit(solution)/shard_map/ppermute | solution.py:1033
  98.9 8.6 %collective-permute-start.24 = (bf16[256,384]{1,0:T(8,128)(2,1)S(1)}, bf16[256,384]{1,0:T(8,128)(2,1)S(1)}, u32[]{:S(2)}, u32[]{:S(2)}) collective-permute-start(bf16[256,384]{1,0:T(8,128)(2,1)S(1)} %add_join.10.refs_3_.refs_0_.refs_1_), channel_id=1, source_target_pairs={{0,8},{2,10},{4,12},{6,14},{8,0},{10,2},{12,4},{14,6},{16,24},{18,... | collective-permute-start | bytes 589832 | tf_op jit(solution)/shard_map/ppermute | solution.py:1033
  103.5 14.1 %collective-permute-start.29 = (bf16[192,384]{1,0:T(8,128)(2,1)S(1)}, bf16[192,384]{1,0:T(8,128)(2,1)S(1)}, u32[]{:S(2)}, u32[]{:S(2)}) collective-permute-start(bf16[192,384]{1,0:T(8,128)(2,1)S(1)} %add_join.11.refs_4_.refs_0_.refs_1_), channel_id=1, source_target_pairs={{0,16},{2,18},{4,20},{6,22},{8,24},{10,26},{12,28},{14,30},{16,0},... | collective-permute-start | bytes 442376 | tf_op jit(solution)/shard_map/ppermute | solution.py:1033
  106.9 11.5 %collective-permute-start.28 = (bf16[384,384]{1,0:T(8,128)(2,1)S(1)}, bf16[384,384]{1,0:T(8,128)(2,1)S(1)}, u32[]{:S(2)}, u32[]{:S(2)}) collective-permute-start(bf16[384,384]{1,0:T(8,128)(2,1)S(1)} %get-tuple-element.166.refs_3_.refs_2_), channel_id=1, source_target_pairs={{0,4},{2,6},{4,0},{6,2},{8,12},{10,14},{12,8},{14,10},{16,20},{18,... | collective-permute-start | bytes 884744 | tf_op jit(solution)/shard_map/ppermute | solution.py:1033
  107.5 22.3 %collective-permute-start.27 = (bf16[320,384]{1,0:T(8,128)(2,1)S(1)}, bf16[320,384]{1,0:T(8,128)(2,1)S(1)}, u32[]{:S(2)}, u32[]{:S(2)}) collective-permute-start(bf16[320,384]{1,0:T(8,128)(2,1)S(1)} %add_join.12.refs_4_.refs_0_.refs_1_), channel_id=1, source_target_pairs={{0,16},{2,18},{4,20},{6,22},{8,24},{10,26},{12,28},{14,30},{16,0},... | collective-permute-start | bytes 737288 | tf_op jit(solution)/shard_map/ppermute | solution.py:1033
  111.9 8.5 %collective-permute-start.33 = (bf16[224,384]{1,0:T(8,128)(2,1)S(1)}, bf16[224,384]{1,0:T(8,128)(2,1)S(1)}, u32[]{:S(2)}, u32[]{:S(2)}) collective-permute-start(bf16[224,384]{1,0:T(8,128)(2,1)S(1)} %get-tuple-element.169.refs_3_.refs_1_), channel_id=1, source_target_pairs={{0,4},{2,6},{4,0},{6,2},{8,12},{10,14},{12,8},{14,10},{16,20},{18,... | collective-permute-start | bytes 516104 | tf_op jit(solution)/shard_map/ppermute | solution.py:1033
  117.6 7.9 %collective-permute-start.32 = (bf16[192,384]{1,0:T(8,128)(2,1)S(1)}, bf16[192,384]{1,0:T(8,128)(2,1)S(1)}, u32[]{:S(2)}, u32[]{:S(2)}) collective-permute-start(bf16[192,384]{1,0:T(8,128)(2,1)S(1)} %add_join.13.refs_4_.refs_1_), channel_id=1, source_target_pairs={{0,8},{2,10},{4,12},{6,14},{8,0},{10,2},{12,4},{14,6},{16,24},{18,... | collective-permute-start | bytes 442376 | tf_op jit(solution)/shard_map/ppermute | solution.py:1033
  119.0 9.6 %collective-permute-start.31 = (bf16[192,384]{1,0:T(8,128)(2,1)S(1)}, bf16[192,384]{1,0:T(8,128)(2,1)S(1)}, u32[]{:S(2)}, u32[]{:S(2)}) collective-permute-start(bf16[192,384]{1,0:T(8,128)(2,1)S(1)} %get-tuple-element.171.refs_3_.refs_1_), channel_id=1, source_target_pairs={{0,8},{2,10},{4,12},{6,14},{8,0},{10,2},{12,4},{14,6},{16,24},{18,... | collective-permute-start | bytes 442376 | tf_op jit(solution)/shard_map/ppermute | solution.py:1033
  120.5 13.1 %collective-permute-start.35 = (bf16[256,384]{1,0:T(8,128)(2,1)S(1)}, bf16[256,384]{1,0:T(8,128)(2,1)S(1)}, u32[]{:S(2)}, u32[]{:S(2)}) collective-permute-start(bf16[256,384]{1,0:T(8,128)(2,1)S(1)} %add_join.14.refs_3_.refs_0_.refs_1_), channel_id=1, source_target_pairs={{0,8},{2,10},{4,12},{6,14},{8,0},{10,2},{12,4},{14,6},{16,24},{18,... | collective-permute-start | bytes 589832 | tf_op jit(solution)/shard_map/ppermute | solution.py:1033
  126.1 13.4 %collective-permute-start.40 = (bf16[384,384]{1,0:T(8,128)(2,1)S(1)}, bf16[384,384]{1,0:T(8,128)(2,1)S(1)}, u32[]{:S(2)}, u32[]{:S(2)}) collective-permute-start(bf16[384,384]{1,0:T(8,128)(2,1)S(1)} %join.2.refs_3_.refs_1_), channel_id=1, source_target_pairs={{0,4},{2,6},{4,0},{6,2},{8,12},{10,14},{12,8},{14,10},{16,20},{18,... | collective-permute-start | bytes 884744 | tf_op jit(solution)/shard_map/ppermute | solution.py:1033
  126.9 13.1 %collective-permute-start.41 = (bf16[384,384]{1,0:T(8,128)(2,1)S(1)}, bf16[384,384]{1,0:T(8,128)(2,1)S(1)}, u32[]{:S(2)}, u32[]{:S(2)}) collective-permute-start(bf16[384,384]{1,0:T(8,128)(2,1)S(1)} %join.2.refs_3_.refs_1_), channel_id=1, source_target_pairs={{0,2},{2,0},{4,6},{6,4},{8,10},{10,8},{12,14},{14,12},{16,18},{18,... | collective-permute-start | bytes 884744 | tf_op jit(solution)/shard_map/ppermute | solution.py:1033
  128.7 10.8 %collective-permute-start.43 = (bf16[192,384]{1,0:T(8,128)(2,1)S(1)}, bf16[192,384]{1,0:T(8,128)(2,1)S(1)}, u32[]{:S(2)}, u32[]{:S(2)}) collective-permute-start(bf16[192,384]{1,0:T(8,128)(2,1)S(1)} %add_join.15.refs_3_.refs_0_.refs_1_), channel_id=1, source_target_pairs={{0,16},{2,18},{4,20},{6,22},{8,24},{10,26},{12,28},{14,30},{16,0},... | collective-permute-start | bytes 442376 | tf_op jit(solution)/shard_map/ppermute | solution.py:1033
  129.9 3.8 %collective-permute-start.34 = (bf16[256,384]{1,0:T(8,128)(2,1)S(1)}, bf16[256,384]{1,0:T(8,128)(2,1)S(1)}, u32[]{:S(2)}, u32[]{:S(2)}) collective-permute-start(bf16[256,384]{1,0:T(8,128)(2,1)S(1)} %get-tuple-element.173.refs_3_.rides), channel_id=1, source_target_pairs={{0,2},{2,0},{4,6},{6,4},{8,10},{10,8},{12,14},{14,12},{16,18},{18,... | collective-permute-start | bytes 589832 | tf_op jit(solution)/shard_map/ppermute | solution.py:1033
  133.6 1.5 copy-start
  133.6 5.1 %collective-permute-start.37 = (bf16[192,384]{1,0:T(8,128)(2,1)S(1)}, bf16[192,384]{1,0:T(8,128)(2,1)S(1)}, u32[]{:S(2)}, u32[]{:S(2)}) collective-permute-start(bf16[192,384]{1,0:T(8,128)(2,1)S(1)} %get-tuple-element.175.refs_1_), channel_id=1, source_target_pairs={{0,4},{2,6},{4,0},{6,2},{8,12},{10,14},{12,8},{14,10},{16,20},{18,... | collective-permute-start | bytes 442376 | tf_op jit(solution)/shard_map/ppermute | solution.py:1033
  133.6 11.3 %collective-permute-start.38 = (bf16[192,384]{1,0:T(8,128)(2,1)S(1)}, bf16[192,384]{1,0:T(8,128)(2,1)S(1)}, u32[]{:S(2)}, u32[]{:S(2)}) collective-permute-start(bf16[192,384]{1,0:T(8,128)(2,1)S(1)} %get-tuple-element.175.refs_1_), channel_id=1, source_target_pairs={{0,2},{2,0},{4,6},{6,4},{8,10},{10,8},{12,14},{14,12},{16,18},{18,... | collective-permute-start | bytes 442376 | tf_op jit(solution)/shard_map/ppermute | solution.py:1033
  138.7 12.7 %collective-permute-start.36 = (bf16[320,384]{1,0:T(8,128)(2,1)S(1)}, bf16[320,384]{1,0:T(8,128)(2,1)S(1)}, u32[]{:S(2)}, u32[]{:S(2)}) collective-permute-start(bf16[320,384]{1,0:T(8,128)(2,1)S(1)} %add_join.17.refs_0_.refs_1_), channel_id=1, source_target_pairs={{0,16},{2,18},{4,20},{6,22},{8,24},{10,26},{12,28},{14,30},{16,0},... | collective-permute-start | bytes 737288 | tf_op jit(solution)/shard_map/ppermute | solution.py:1033
  139.5 5.5 %collective-permute-start.39 = (bf16[192,384]{1,0:T(8,128)(2,1)S(1)}, bf16[192,384]{1,0:T(8,128)(2,1)S(1)}, u32[]{:S(2)}, u32[]{:S(2)}) collective-permute-start(bf16[192,384]{1,0:T(8,128)(2,1)S(1)} %collective-permute-done.37.refs_2_), channel_id=1, source_target_pairs={{0,2},{2,0},{4,6},{6,4},{8,10},{10,8},{12,14},{14,12},{16,18},{18,... | collective-permute-start | bytes 442376 | tf_op jit(solution)/shard_map/ppermute | solution.py:1033
  139.5 3.3 %collective-permute-start.42 = (bf16[384,384]{1,0:T(8,128)(2,1)S(1)}, bf16[384,384]{1,0:T(8,128)(2,1)S(1)}, u32[]{:S(2)}, u32[]{:S(2)}) collective-permute-start(bf16[384,384]{1,0:T(8,128)(2,1)S(1)} %collective-permute-done.40.refs_2_), channel_id=1, source_target_pairs={{0,2},{2,0},{4,6},{6,4},{8,10},{10,8},{12,14},{14,12},{16,18},{18,... | collective-permute-start | bytes 884744 | tf_op jit(solution)/shard_map/ppermute | solution.py:1033
  140.0 13.0 %collective-permute-start.45 = (bf16[192,384]{1,0:T(8,128)(2,1)S(1)}, bf16[192,384]{1,0:T(8,128)(2,1)S(1)}, u32[]{:S(2)}, u32[]{:S(2)}) collective-permute-start(bf16[192,384]{1,0:T(8,128)(2,1)S(1)} %add_join.18.refs_5_.refs_1_), channel_id=1, source_target_pairs={{0,8},{2,10},{4,12},{6,14},{8,0},{10,2},{12,4},{14,6},{16,24},{18,... | collective-permute-start | bytes 442376 | tf_op jit(solution)/shard_map/ppermute | solution.py:1033
  151.4 2.8 %collective-permute-start.44 = (bf16[256,384]{1,0:T(8,128)(2,1)S(1)}, bf16[256,384]{1,0:T(8,128)(2,1)S(1)}, u32[]{:S(2)}, u32[]{:S(2)}) collective-permute-start(bf16[256,384]{1,0:T(8,128)(2,1)S(1)} %get-tuple-element.179.refs_3_.rides), channel_id=1, source_target_pairs={{0,2},{2,0},{4,6},{6,4},{8,10},{10,8},{12,14},{14,12},{16,18},{18,... | collective-permute-start | bytes 589832 | tf_op jit(solution)/shard_map/ppermute | solution.py:1033
  151.5 8.7 %collective-permute-start.47 = (bf16[192,384]{1,0:T(8,128)(2,1)S(1)}, bf16[192,384]{1,0:T(8,128)(2,1)S(1)}, u32[]{:S(2)}, u32[]{:S(2)}) collective-permute-start(bf16[192,384]{1,0:T(8,128)(2,1)S(1)} %get-tuple-element.190.refs_1_), channel_id=1, source_target_pairs={{0,4},{2,6},{4,0},{6,2},{8,12},{10,14},{12,8},{14,10},{16,20},{18,... | collective-permute-start | bytes 442376 | tf_op jit(solution)/shard_map/ppermute | solution.py:1033
  153.6 10.4 %collective-permute-start.50 = (bf16[384,384]{1,0:T(8,128)(2,1)S(1)}, bf16[384,384]{1,0:T(8,128)(2,1)S(1)}, u32[]{:S(2)}, u32[]{:S(2)}) collective-permute-start(bf16[384,384]{1,0:T(8,128)(2,1)S(1)} %join.3.refs_2_.refs_1_), channel_id=1, source_target_pairs={{0,4},{2,6},{4,0},{6,2},{8,12},{10,14},{12,8},{14,10},{16,20},{18,... | collective-permute-start | bytes 884744 | tf_op jit(solution)/shard_map/ppermute | solution.py:1033
  159.6 4.5 %collective-permute-start.46 = (f32[1,192]{1,0:T(1,128)S(1)}, f32[1,192]{1,0:T(1,128)S(1)}, u32[]{:S(2)}, u32[]{:S(2)}) collective-permute-start(f32[1,192]{1,0:T(1,128)S(1)} %get-tuple-element.186), channel_id=1, source_target_pairs={{0,1},{1,0},{2,3},{3,2},{4,5},{5,4},{6,7},{7,6},{8,9},{9,8},{10,11... | collective-permute-start | bytes 2312 | tf_op jit(solution)/shard_map/ppermute | solution.py:1030
  159.6 5.6 %collective-permute-start.48 = (bf16[192,384]{1,0:T(8,128)(2,1)S(1)}, bf16[192,384]{1,0:T(8,128)(2,1)S(1)}, u32[]{:S(2)}, u32[]{:S(2)}) collective-permute-start(bf16[192,384]{1,0:T(8,128)(2,1)S(1)} %get-tuple-element.190.refs_1_), channel_id=1, source_target_pairs={{0,2},{2,0},{4,6},{6,4},{8,10},{10,8},{12,14},{14,12},{16,18},{18,... | collective-permute-start | bytes 442376 | tf_op jit(solution)/shard_map/ppermute | solution.py:1033
  159.7 7.3 %collective-permute-start.51 = (bf16[384,384]{1,0:T(8,128)(2,1)S(1)}, bf16[384,384]{1,0:T(8,128)(2,1)S(1)}, u32[]{:S(2)}, u32[]{:S(2)}) collective-permute-start(bf16[384,384]{1,0:T(8,128)(2,1)S(1)} %join.3.refs_2_.refs_1_), channel_id=1, source_target_pairs={{0,2},{2,0},{4,6},{6,4},{8,10},{10,8},{12,14},{14,12},{16,18},{18,... | collective-permute-start | bytes 884744 | tf_op jit(solution)/shard_map/ppermute | solution.py:1033
  160.2 5.1 %collective-permute-start.49 = (bf16[192,384]{1,0:T(8,128)(2,1)S(1)}, bf16[192,384]{1,0:T(8,128)(2,1)S(1)}, u32[]{:S(2)}, u32[]{:S(2)}) collective-permute-start(bf16[192,384]{1,0:T(8,128)(2,1)S(1)} %collective-permute-done.47.refs_2_), channel_id=1, source_target_pairs={{0,2},{2,0},{4,6},{6,4},{8,10},{10,8},{12,14},{14,12},{16,18},{18,... | collective-permute-start | bytes 442376 | tf_op jit(solution)/shard_map/ppermute | solution.py:1033
  164.1 2.9 %collective-permute-start.52 = (bf16[384,384]{1,0:T(8,128)(2,1)S(1)}, bf16[384,384]{1,0:T(8,128)(2,1)S(1)}, u32[]{:S(2)}, u32[]{:S(2)}) collective-permute-start(bf16[384,384]{1,0:T(8,128)(2,1)S(1)} %collective-permute-done.50.refs_2_), channel_id=1, source_target_pairs={{0,2},{2,0},{4,6},{6,4},{8,10},{10,8},{12,14},{14,12},{16,18},{18,... | collective-permute-start | bytes 884744 | tf_op jit(solution)/shard_map/ppermute | solution.py:1033
  (2 other events, 1.8 us)

commit v4 on v3

--- a/solution.py
+++ b/solution.py
@@ -107,18 +107,14 @@
         (up_hbm.at[layer], w_up.at[rows_of(x * half, half), :]),
         (down_hbm.at[layer], w_down.at[rows_of(x * tall, tall), :]),
     ]
-    for piece, offset in zip(pieces, offsets):
-        size = piece.shape[0] // 2
+    count = len(pieces) // 2
+    for up_piece, down_piece, offset in zip(pieces[:count], pieces[count:], offsets):
+        size = up_piece.shape[0]
         start = (1 - x) * half + offset * size
-        copies.append((piece.at[pl.ds(0, size), :], w_up.at[rows_of(start, size), :]))
+        copies.append((up_piece, w_up.at[rows_of(start, size), :]))
         for b in range(blocks):
             start = (1 - x) * tall + offset * (blocks * size) + b * size
-            copies.append(
-                (
-                    piece.at[pl.ds(size, size), pl.ds(b * D, D)],
-                    w_down.at[rows_of(start, size), :],
-                )
-            )
+            copies.append((down_piece.at[:, pl.ds(b * D, D)], w_down.at[rows_of(start, size), :]))
     return [pltpu.make_async_copy(s, d, sems.at[i]) for i, (s, d) in enumerate(copies)]
 
 
@@ -163,13 +159,13 @@
     ]
 
 
-def pack_mlp_copies(send, layer, offset, up, down):
+def pack_mlp_copies(send_up, send_down, layer, offset, up, down):
     size = up.shape[1] // 4
     blocks = down.shape[1] // up.shape[1]
-    copies = [(up.at[layer, rows_of(offset * size, size), :], send.at[pl.ds(0, size), :])]
+    copies = [(up.at[layer, rows_of(offset * size, size), :], send_up)]
     for b in range(blocks):
         rows = rows_of(offset * (blocks * size) + b * size, size)
-        copies.append((down.at[layer, rows, :], send.at[pl.ds(size, size), pl.ds(b * D, D)]))
+        copies.append((down.at[layer, rows, :], send_down.at[:, pl.ds(b * D, D)]))
     return copies
 
 
@@ -177,9 +173,9 @@
     half = qkv.shape[1]
     size = half // 4
 
-    def body(meta, qkv, out, up, down, send_attn, send_mlp, sems):
+    def body(meta, qkv, out, up, down, send_attn, send_up, send_down, sems):
         copies = pack_attn_copies(send_attn, layer, parts, piece_offsets(meta, parts, False)[0], qkv, out)
-        copies += pack_mlp_copies(send_mlp, layer, piece_offsets(meta, 4, far)[0], up, down)
+        copies += pack_mlp_copies(send_up, send_down, layer, piece_offsets(meta, 4, far)[0], up, down)
         copies = [pltpu.make_async_copy(s, d, sems.at[i]) for i, (s, d) in enumerate(copies)]
         for copy in copies:
             copy.start()
@@ -190,8 +186,8 @@
         body,
         (meta, qkv, out, up, down),
         [SMEM] + [HBM] * 4,
-        (sds((half // parts, 4 * D), BF16), sds((2 * size, 4 * D), BF16)),
-        (VMEM, VMEM),
+        (sds((half // parts, 4 * D), BF16),) + (sds((size, 4 * D), BF16),) * 2,
+        (VMEM,) * 3,
         name,
         scratch=[pltpu.SemaphoreType.DMA((8,))],
         deps=deps,
@@ -199,44 +195,51 @@
     )
 
 
-def first_message(timestep, labels, ada_bias, qv_bias, out_bias, up_bias, down_bias):
-    ins = (timestep, ada_bias, qv_bias, out_bias, up_bias, down_bias)
-
-    def body(labels, *refs):
-        send, held, sems = refs[6], refs[7:13], refs[13]
-        copies = [pltpu.make_async_copy(refs[i], held[i], sems.at[i]) for i in range(6)]
+def first_messages(meta, timestep, labels, biases, qkv, out, up, down):
+    ins = (timestep,) + biases
+    half = qkv.shape[1]
+
+    def body(meta, labels, *refs):
+        small, weights, outs, held, sems = refs[:6], refs[6:10], refs[10:14], refs[14:20], refs[20]
+        send, send_attn, send_up, send_down = outs
+        pairs = list(zip(small, held))
+        pairs += pack_attn_copies(send_attn, 0, 2, piece_offsets(meta, 2, False)[0], *weights[:2])
+        pairs += pack_mlp_copies(
+            send_up, send_down, 0, piece_offsets(meta, 4, False)[0], *weights[2:]
+        )
+        copies = [pltpu.make_async_copy(s, d, sems.at[i]) for i, (s, d) in enumerate(pairs)]
         for copy in copies:
             copy.start()
         send[...] = jnp.zeros_like(send)
         send[4:5, D : D + 128] = jnp.full((1, 128), labels[0], jnp.int32).astype(F32)
-        for copy in copies:
+        for copy in copies[:6]:
             copy.wait()
-        time, ada, qv, out, up, down = held
+        time, ada, qv, out_b, up_b, down_b = held
         send[0:2, 0 : 3 * D] = ada[...].astype(F32)
         send[0:2, 3 * D : 4 * D] = qv[...].astype(F32)
-        send[2:4, 0 : 2 * D] = up[...].astype(F32)
-        send[2:4, 2 * D : 2 * D + D // 2] = out[...].astype(F32)
-        send[2:4, 1024 : 1024 + D // 2] = down[...].astype(F32)
+        send[2:4, 0 : 2 * D] = up_b[...].astype(F32)
+        send[2:4, 2 * D : 2 * D + D // 2] = out_b[...].astype(F32)
+        send[2:4, 1024 : 1024 + D // 2] = down_b[...].astype(F32)
         send[4:5, 0:D] = time[...]
+        for copy in copies[6:]:
+            copy.wait()
 
     return call(
         body,
-        (labels,) + ins,
-        [SMEM] + [HBM] * 6,
-        sds((8, 4 * D), F32),
-        VMEM,
-        "first_message",
+        (meta, labels) + ins + (qkv, out, up, down),
+        [SMEM, SMEM] + [HBM] * 10,
+        (sds((8, 4 * D), F32), sds((half // 2, 4 * D), BF16)) + (sds((half // 4, 4 * D), BF16),) * 2,
+        (VMEM,) * 4,
+        "first_messages",
         scratch=[pltpu.VMEM(member.shape, member.dtype) for member in ins]
-        + [pltpu.SemaphoreType.DMA((6,))],
+        + [pltpu.SemaphoreType.DMA((16,))],
         limit=WIDE,
     )
 
 
-def condition_kernel(meta, own, got, table_ref, ada_ref, mine_out, send_out, table, ada, sems):
+def condition_kernel(meta, own, got, table_ref, ada, mine_out, send_out, table):
     half = D // 2
     x = meta[0]
-    copy = pltpu.make_async_copy(ada_ref, ada, sems.at[0])
-    copy.start()
     classes = table_ref.shape[1]
     aligned = classes // 128 * 128
     table[:, aligned:] = jnp.zeros((half, table.shape[1] - aligned), BF16)
@@ -252,7 +255,6 @@
     for ref, index in ((mine_out, 0), (send_out, 1)):
         ref[2:3, 0:half] = condition[index : index + 1, :]
         ref[2:3, half:] = jnp.zeros((1, 6 * D - half), F32)
-    copy.wait()
     for layer in range(LAYERS):
         part = dot(act, ada[layer])
         mine_out[layer : layer + 1, :] = part[0:1, :]
@@ -263,17 +265,12 @@
     return call(
         condition_kernel,
         (meta, own, got, table.T, ada),
-        [SMEM] + [VMEM] * 3 + [HBM],
+        [SMEM] + [VMEM] * 4,
         (sds((LAYERS + 1, 6 * D), F32),) * 2,
         (VMEM,) * 2,
         "condition",
-        scratch=[
-            pltpu.VMEM((D // 2, -(-table.shape[0] // 128) * 128), BF16),
-            pltpu.VMEM(ada.shape, BF16),
-            pltpu.SemaphoreType.DMA((1,)),
-        ],
+        scratch=[pltpu.VMEM((D // 2, -(-table.shape[0] // 128) * 128), BF16)],
         deps=deps,
-        limit=WIDE,
     )
 
 
@@ -323,8 +320,10 @@
 def attn_fwd_kernel(layer, far, count, *refs):
     meta, x_ref, vecs, qkv_hbm, out_hbm = refs[:5]
     pieces = refs[5 : 5 + count]
-    modulated_out, qkv_out, prob_out, att_out, branch_out, middle_out = refs[5 + count : 11 + count]
-    w_qkv, w_out, sems = refs[11 + count :]
+    modulated_out, qkv_out, prob_out, att_out, branch_out, w_qkv, w_out, middle_out = refs[
+        5 + count : 13 + count
+    ]
+    sems = refs[13 + count]
     copies = attn_weight_copies(
         meta, layer, qkv_hbm, out_hbm, pieces, piece_offsets(meta, count, far), w_qkv, w_out, sems
     )
@@ -379,13 +378,13 @@
             sds((heads * tokens, tokens), BF16),
             sds((tokens, D), BF16),
             sds((tokens, D), F32),
+            sds((D, 3 * D), BF16),
+            sds((D, D), BF16),
             sds((tokens, D), F32),
         ),
         in_specs=[SMEM, VMEM, VMEM] + [HBM] * 2 + [ANY] * count,
-        out_specs=(VMEM,) * 6,
+        out_specs=(VMEM,) * 8,
         scratch_shapes=[
-            pltpu.VMEM((D, 3 * D), BF16),
-            pltpu.VMEM((D, D), BF16),
             pltpu.SemaphoreType.DMA((2 + 2 * count,)),
         ],
         compiler_params=pltpu.CompilerParams(vmem_limit_bytes=LIMIT),
@@ -398,10 +397,9 @@
     refs = refs[:3] + refs[3 + late :]
     meta, middle_ref, vecs, up_hbm, down_hbm = refs[:5]
     pieces = refs[5 : 5 + count]
-    x_out, mod_out, act_out, slope_out, branch_out = refs[5 + count : 10 + count]
-    w_up, w_down, sems = refs[10 + count :]
+    x_out, mod_out, act_out, slope_out, branch_out, w_up, w_down, sems = refs[5 + count :]
     copies = mlp_weight_copies(
-        meta, layer, up_hbm, down_hbm, pieces, piece_offsets(meta, count, far), w_up, w_down, sems
+        meta, layer, up_hbm, down_hbm, pieces, piece_offsets(meta, count // 2, far), w_up, w_down, sems
     )
     for copy in copies:
         copy.start()
@@ -441,12 +439,12 @@
             sds((tokens, 4 * D), BF16),
             sds((tokens, 4 * D), BF16),
             sds((tokens, D), F32),
+            sds((D, 4 * D), BF16),
+            sds((4 * D, D), BF16),
         ),
         in_specs=[SMEM, VMEM, VMEM] + [ANY] * len(deps) + [HBM] * 2 + [ANY] * count,
-        out_specs=(VMEM,) * 5,
+        out_specs=(VMEM,) * 7,
         scratch_shapes=[
-            pltpu.VMEM((D, 4 * D), BF16),
-            pltpu.VMEM((4 * D, D), BF16),
             pltpu.SemaphoreType.DMA((2 + 5 * count,)),
         ],
         compiler_params=pltpu.CompilerParams(vmem_limit_bytes=LIMIT),
@@ -465,18 +463,9 @@
         send[rows, :] = value
 
 
-def mlp_bwd_kernel(layer, far, count, masked, late, *refs):
-    meta, grad_ref, vecs, middle_ref, branch_ref, act_ref, slope_ref, mod_ref = refs[:8]
-    refs = refs[8 + late :]
-    up_hbm, down_hbm = refs[:2]
-    pieces = refs[2 : 2 + count]
-    keep, send, grad_out, sums_out = refs[2 + count : 6 + count]
-    w_up, w_down, pre_bf, sems = refs[6 + count :]
-    copies = mlp_weight_copies(
-        meta, layer, up_hbm, down_hbm, pieces, piece_offsets(meta, count, far), w_up, w_down, sems
-    )
-    for copy in copies:
-        copy.start()
+def mlp_bwd_kernel(masked, late, *refs):
+    meta, grad_ref, vecs, middle_ref, branch_ref, act_ref, slope_ref, mod_ref, w_up, w_down = refs[:10]
+    keep, send, grad_out, sums_out = refs[10 + late :]
     core = meta[1]
     grad = grad_ref[...].astype(F32)
     if masked:
@@ -491,8 +480,6 @@
         value = dot_tn(act_ref[:, part * D : (part + 1) * D], branch_bf).astype(BF16)
         base = (part // 2) * 4 * half + 2 * half
         split_store(core, value, part % 2, keep, send, slice(base, base + D))
-    for copy in copies:
-        copy.wait()
     mod_two = mod_ref[...]
     grad_mod = None
     for part in range(4):
@@ -519,45 +506,30 @@
     grad_out[...] = grad + norm_back(grad_mod * (1.0 + vecs[4:5, :]), normed, inv_dev)
 
 
-def mlp_bwd(layer, far, masked, meta, grad, vecs, kept, up, down, pieces, deps=()):
-    middle, mod_two, act, slope, branch = kept
+def mlp_bwd(masked, meta, grad, vecs, kept, deps=()):
+    middle, mod_two, act, slope, branch, w_up, w_down = kept
     tokens = middle.shape[0]
-    count = len(pieces)
     late = len(deps)
     return pl.pallas_call(
-        functools.partial(mlp_bwd_kernel, layer, far, count, masked, late),
+        functools.partial(mlp_bwd_kernel, masked, late),
         out_shape=(
             sds((4 * D, D), BF16),
             sds((4 * D, D), BF16),
             sds((tokens, D), F32),
             sds((16, D), F32),
         ),
-        in_specs=[SMEM] + [VMEM] * 7 + [ANY] * late + [HBM] * 2 + [ANY] * count,
+        in_specs=[SMEM] + [VMEM] * 9 + [ANY] * late,
         out_specs=(VMEM,) * 4,
-        scratch_shapes=[
-            pltpu.VMEM((D, 4 * D), BF16),
-            pltpu.VMEM((4 * D, D), BF16),
-            pltpu.VMEM((16, D), BF16),
-            pltpu.SemaphoreType.DMA((2 + 5 * count,)),
-        ],
         compiler_params=pltpu.CompilerParams(vmem_limit_bytes=LIMIT),
         cost_estimate=pl.CostEstimate(flops=10000000000, bytes_accessed=0, transcendentals=0),
         name="mlp_bwd",
-    )(meta, grad, vecs, middle, branch, act, slope, mod_two, *deps, up, down, *pieces)
-
-
-def attn_bwd_kernel(layer, far, count, extra, late, *refs):
-    meta, grad_ref, vecs, x_ref, modulated_ref, qkv_ref, prob_ref, att_ref, branch_ref, part_sums = refs[:10]
-    refs = refs[:10] + refs[10 + late :]
-    qkv_hbm, out_hbm = refs[10:12]
-    pieces = refs[12 : 12 + count]
-    keep, send, grad_out, sums_out = refs[12 + count : 16 + count]
-    w_qkv, w_out, ga_ref, proj_ref, sems = refs[16 + count :]
-    copies = attn_weight_copies(
-        meta, layer, qkv_hbm, out_hbm, pieces, piece_offsets(meta, count, far), w_qkv, w_out, sems
-    )
-    for copy in copies:
-        copy.start()
+    )(meta, grad, vecs, middle, branch, act, slope, mod_two, w_up, w_down, *deps)
+
+
+def attn_bwd_kernel(layer, extra, late, *refs):
+    meta, grad_ref, vecs, x_ref, modulated_ref, qkv_ref, prob_ref, att_ref, branch_ref = refs[:9]
+    w_qkv, w_out, part_sums = refs[9:12]
+    keep, send, grad_out, sums_out, ga_ref, proj_ref = refs[12 + late :]
     core = meta[1]
     half = D // 2
     tokens = grad_ref.shape[0]
@@ -581,8 +553,6 @@
             )
 
     store(dot_tn(att_ref[...], battn_bf).astype(BF16), 3)
-    for copy in copies:
-        copy.wait()
     ga_ref[...] = dot_nt(battn_bf, w_out[...]).astype(BF16)
     masks = head_masks()
     grad_q_sums, grad_v_sums = [], []
@@ -639,31 +609,25 @@
         send[4 * half : 4 * half + 16, :] = total
 
 
-def attn_bwd(layer, far, extra, meta, grad, vecs, x, kept, part_sums, qkv, out, pieces, deps=()):
-    modulated, qkv_val, prob, att, branch = kept
+def attn_bwd(layer, extra, meta, grad, vecs, x, kept, part_sums, deps=()):
+    modulated, qkv_val, prob, att, branch, w_qkv, w_out = kept
     tokens = x.shape[0]
-    count = len(pieces)
+    late = len(deps)
     return pl.pallas_call(
-        functools.partial(attn_bwd_kernel, layer, far, count, extra, len(deps)),
+        functools.partial(attn_bwd_kernel, layer, extra, late),
         out_shape=(
             sds((2 * D, D), BF16),
             sds((2 * D + extra, D), BF16),
             sds((tokens, D), F32),
             sds((16, D), BF16),
         ),
-        in_specs=[SMEM] + [VMEM] * 9 + [ANY] * len(deps) + [HBM] * 2 + [ANY] * count,
+        in_specs=[SMEM] + [VMEM] * 11 + [ANY] * late,
         out_specs=(VMEM,) * 4,
-        scratch_shapes=[
-            pltpu.VMEM((D, 3 * D), BF16),
-            pltpu.VMEM((D, D), BF16),
-            pltpu.VMEM((tokens, D), BF16),
-            pltpu.VMEM((tokens, 3 * D), BF16),
-            pltpu.SemaphoreType.DMA((2 + 2 * count,)),
-        ],
+        scratch_shapes=[pltpu.VMEM((tokens, D), BF16), pltpu.VMEM((tokens, 3 * D), BF16)],
         compiler_params=pltpu.CompilerParams(vmem_limit_bytes=LIMIT),
         cost_estimate=pl.CostEstimate(flops=10000000000, bytes_accessed=0, transcendentals=0),
         name="attn_bwd",
-    )(meta, grad, vecs, x, modulated, qkv_val, prob, att, branch, part_sums, *deps, qkv, out, *pieces)
+    )(meta, grad, vecs, x, modulated, qkv_val, prob, att, branch, w_qkv, w_out, part_sums, *deps)
 
 
 def add_rows(a, a_rows, b, b_rows):
@@ -1034,31 +998,41 @@
 
     CORE, Y, Z = 1, 2, 4
 
-    first = first_message(timestep_embed, labels, ada_bias, qv_bias, out_bias, up_bias, down_bias)
+    first, send_a0, send_u0, send_d0 = first_messages(
+        meta,
+        timestep_embed,
+        labels,
+        (ada_bias, qv_bias, out_bias, up_bias, down_bias),
+        qkv_weight,
+        out_weight,
+        up_weight,
+        down_weight,
+    )
     got_first = over_x(first)
-    send_a0, send_m0 = pack(
-        0, False, 2, meta, qkv_weight, out_weight, up_weight, down_weight, (), "pack_first"
-    )
     classes = class_table.shape[0]
     mine_part, send_part = condition_step(
-        meta, first, got_first, class_table, ada_weight, (send_m0,)
-    )
-    send_a1, send_m1 = pack(
+        meta, first, got_first, class_table, ada_weight, (send_d0,)
+    )
+    send_a1, send_u1, send_d1 = pack(
         1, True, 4, meta, qkv_weight, out_weight, up_weight, down_weight, (send_part,), "pack_rest"
     )
 
-    def fetch(send, distance):
-        got = over_x(send)
+    def relay(got, distance):
         if distance is None:
             return [got, over_rep(got, CORE)]
         next_got = over_rep(got, distance)
         return [got, next_got, over_rep(got, CORE), over_rep(next_got, CORE)]
 
-    pieces_a0 = fetch(send_a0, None)
-    vecs_all = vectors_step(meta, first, got_first, mine_part, over_x(send_part))
-    pieces_m0 = fetch(send_m0, Y)
-    pieces_a1 = fetch(send_a1, Y)
-    pieces_m1 = fetch(send_m1, Z)
+    got_a0, got_u0, got_d0 = over_x(send_a0), over_x(send_u0), over_x(send_d0)
+    got_a1, got_u1, got_d1 = over_x(send_a1), over_x(send_u1), over_x(send_d1)
+    pieces_a0 = relay(got_a0, None)
+    far_u0, far_d0 = over_rep(got_u0, Y), over_rep(got_d0, Y)
+    got_part = over_x(send_part)
+    got_part, far_u0, far_d0 = lax.optimization_barrier((got_part, far_u0, far_d0))
+    vecs_all = vectors_step(meta, first, got_first, mine_part, got_part)
+    pieces_m0 = []
+    for near, far in ((got_u0, far_u0), (got_d0, far_d0)):
+        pieces_m0 += [near, far, over_rep(near, CORE), over_rep(far, CORE)]
     vecs = [vecs_all[layer] for layer in range(LAYERS)]
 
     distances = [Z]
@@ -1069,6 +1043,9 @@
     attn_weights = (qkv_weight, out_weight)
     mlp_weights = (up_weight, down_weight)
     *kept_a0, middle0 = attn_fwd(0, False, meta, stream, vecs[0], *attn_weights, pieces_a0)
+    got_a1, got_u1, got_d1, middle0 = lax.optimization_barrier((got_a1, got_u1, got_d1, middle0))
+    pieces_a1 = relay(got_a1, Y)
+    pieces_m1 = relay(got_u1, Z) + relay(got_d1, Z)
     stream1, *kept_m0 = mlp_fwd(
         0, False, False, meta, middle0, vecs[0], *mlp_weights, pieces_m0
     )
@@ -1125,41 +1102,24 @@
     more = len(distances) - 1
 
     keep, sent, grad, part_sums = mlp_bwd(
-        1, True, True, meta, cotangent[0], vecs[1], (middle1, *kept_m1), *mlp_weights, pieces_m1, deps()
+        True, meta, cotangent[0], vecs[1], (middle1, *kept_m1), deps()
     )
     m1 = reduce_chunk(keep, sent, None)
     advance(m1)
     keep, sent, grad, sums1 = ran(
-        attn_bwd(
-            1, False, 16, meta, grad, vecs[1], stream1, kept_a1, part_sums, *attn_weights, pieces_a1
-        )
+        attn_bwd(1, 16, meta, grad, vecs[1], stream1, kept_a1, part_sums)
     )
     a1 = reduce_chunk(keep, sent, sums1)
     advance(a1)
     advance(m1)
     keep, sent, grad, part_sums = ran(
-        mlp_bwd(
-            0, False, False, meta, grad, vecs[0], (middle0, *kept_m0), *mlp_weights, pieces_m0, deps()
-        )
+        mlp_bwd(False, meta, grad, vecs[0], (middle0, *kept_m0), deps())
     )
     m0 = reduce_chunk(keep, sent, None)
     advance(m0)
     advance(a1)
     keep, sent, grad_stream, sums0 = ran(
-        attn_bwd(
-            0,
-            False,
-            16,
-            meta,
-            grad,
-            vecs[0],
-            stream,
-            kept_a0,
-            part_sums,
-            *attn_weights,
-            pieces_a0,
-            deps(),
-        )
+        attn_bwd(0, 16, meta, grad, vecs[0], stream, kept_a0, part_sums, deps())
     )
     a0 = reduce_chunk(keep, sent, sums0)
     advance(a0)

time: 170 us -> 166 us (0.976)
  Pallas kernels: 76.2 us -> 69.3 us
  starting transfers between devices: 43.2 us -> 48.4 us
  waiting for transfers between devices: 45.2 us -> 43.3 us
    ppermute x11 -> x13, waiting for transfers between devices: 15.1 us -> 9.11 us  [over_x(): return lax.ppermute(value, 'shard', [(0, 1), (1, 0)])]
    ppermute x11 -> x13, starting transfers between devices: 10.7 us -> 15.2 us  [over_x(): return lax.ppermute(value, 'shard', [(0, 1), (1, 0)])]
    ppermute x42 -> x48, waiting for transfers between devices: 30.1 us -> 34.2 us  [over_rep(): return lax.ppermute(value, 'rep', [(r, r ^ distance) for r in range(reps)])]
    pallas_call x4, Pallas kernels: 23.6 us -> 19.5 us  [the longest x2 10.2 us: mlp_bwd(): pl.pallas_call(functools.partial(mlp_bwd_kernel, masked, late), out_shape...]
    pallas_call x29 -> x28, Pallas kernels: 22.8 us -> 19.3 us  [call(): pl.pallas_call(kernel, out_shape=out_shape, in_specs=list(in_specs) + [AN...]
    ppermute x42 -> x48, starting transfers between devices: 32.5 us -> 33.2 us  [over_rep(): return lax.ppermute(value, 'rep', [(r, r ^ distance) for r in range(reps)])]
  transfers between devices with their start and end apart: 53 -> 61, of which waited for: 16 -> 19; matrix products, arithmetic and copies ran while one was open for 0% -> 0% of each run, Pallas kernels for 36% -> 32%
where the time goes in v4:
time: 166 us
  Pallas kernels  69.3 us (42%)
  starting transfers between devices  48.4 us (29%)
  waiting for transfers between devices  43.3 us (26%)
  between operations  2.64 us (2%)
  local copies, waits for them, and re-layouts  2.37 us (1%)
    ppermute x48, waiting for transfers between devices, over_rep(): return lax.ppermute(value, 'rep', [(r, r ^ distance) for r in range(reps)])  34.2 us
    ppermute x48, starting transfers between devices, over_rep(): return lax.ppermute(value, 'rep', [(r, r ^ distance) for r in range(reps)])  33.2 us
    pallas_call x28, Pallas kernels, call(): pl.pallas_call(kernel, out_shape=out_shape, in_specs=list(in_specs) + [AN...  19.3 us
    ppermute x13, starting transfers between devices, over_x(): return lax.ppermute(value, 'shard', [(0, 1), (1, 0)])  15.2 us
    pallas_call x2, Pallas kernels, mlp_bwd(): pl.pallas_call(functools.partial(mlp_bwd_kernel, masked, late), out_shape...  10.2 us
    pallas_call x2, Pallas kernels, mlp_fwd(): pl.pallas_call(functools.partial(mlp_fwd_kernel, layer, far, count, last,...  9.5 us
    pallas_call x2, Pallas kernels, attn_bwd(): pl.pallas_call(functools.partial(attn_bwd_kernel, layer, extra, late), ou...  9.27 us
    ppermute x13, waiting for transfers between devices, over_x(): return lax.ppermute(value, 'shard', [(0, 1), (1, 0)])  9.11 us
  transfers between devices with their start and end apart: 61, of which 19 were waited for; matrix products, arithmetic and copies ran while one was open for 0% of the time, Pallas kernels for 32%

profile of v4, /device:TPU:0, one launch (start us, length us, event | category | flops | bytes accessed | tf_op | source)
XLA Modules:
  0.0 166.0 jit_solution(12857456967229157877)
XLA Ops:
  2.6 2.9 %first_messages.1 = (f32[8,1536]{1,0:T(8,128)}, bf16[96,1536]{1,0:T(8,128)(2,1)}, bf16[48,1536]{1,0:T(8,128)(2,1)}, bf16[48,1536]{1,0:T(8,128)(2,1)}) custom-call(s32[6]{0:T(128)} %stack.24.refs_0_.meta, s32[1]{0:T(128)S(6)} %copy.40.refs_1_, f32[1,384]{1,0:T(1,128)} %refs_2_.2, bf16[2,1152]{1,0:T(2,128)(2,1)} %refs_3_.6, bf16[2,384]{1,0:T(2,128)(2,1)} %refs_4_.7, ...), custom_call_target="tpu_custom_call" | custom-call | flops 10000000000 | tf_op jit(solution)/shard_map/first_messages/pallas_call | solution.py:140
  5.5 3.0 %collective-permute-start = (f32[8,1536]{1,0:T(8,128)}, f32[8,1536]{1,0:T(8,128)S(1)}, u32[]{:S(2)}, u32[]{:S(2)}) collective-permute-start(f32[8,1536]{1,0:T(8,128)} %get-tuple-element.127.refs_1_), channel_id=1, source_target_pairs={{0,1},{1,0},{2,3},{3,2},{4,5},{5,4},{6,7},{7,6},{8,9},{9,8},{10,11... | collective-permute-start | bytes 147464 | tf_op jit(solution)/shard_map/ppermute | solution.py:994
  8.6 1.9 %collective-permute-start.7 = (bf16[48,1536]{1,0:T(8,128)(2,1)}, bf16[48,1536]{1,0:T(8,128)(2,1)S(1)}, u32[]{:S(2)}, u32[]{:S(2)}) collective-permute-start(bf16[48,1536]{1,0:T(8,128)(2,1)} %get-tuple-element.128.refs_5_), channel_id=1, source_target_pairs={{0,1},{1,0},{2,3},{3,2},{4,5},{5,4},{6,7},{7,6},{8,9},{9,8},{10,11... | collective-permute-start | bytes 442376 | tf_op jit(solution)/shard_map/ppermute | solution.py:994
  11.0 0.9 copy-done.11
  11.9 0.8 copy-done.12
  12.7 1.1 condition.1
  13.8 2.4 %collective-permute-start.4 = (f32[3,2304]{1,0:T(4,128)S(1)}, f32[3,2304]{1,0:T(4,128)S(1)}, u32[]{:S(2)}, u32[]{:S(2)}) collective-permute-start(f32[3,2304]{1,0:T(4,128)S(1)} %get-tuple-element.129.refs_5_), channel_id=1, source_target_pairs={{0,1},{1,0},{2,3},{3,2},{4,5},{5,4},{6,7},{7,6},{8,9},{9,8},{10,11... | collective-permute-start | bytes 82952 | tf_op jit(solution)/shard_map/ppermute | solution.py:994
  16.3 1.5 collective-permute-start.6
  17.8 0.8 collective-permute-done.7.refs_9_
  18.6 1.5 collective-permute-start.8
  20.1 2.5 %pack_rest.1 = (bf16[48,1536]{1,0:T(8,128)(2,1)}, bf16[48,1536]{1,0:T(8,128)(2,1)}, bf16[48,1536]{1,0:T(8,128)(2,1)}) custom-call(s32[6]{0:T(128)} %stack.24.refs_0_.meta, bf16[2,192,1152]{2,1,0:T(8,128)(2,1)} %refs_3_.10, bf16[2,192,384]{2,1,0:T(8,128)(2,1)} %refs_4_.12, bf16[2,192,1536]{2,1,0:T(8,128)(2,1)} %refs_3_.11, bf16[2,768,384]{2,1,0:T(8,128)(2,1)} %refs_4_.13, ...), custom_call_target="tpu_custom_call" | custom-call | flops 10000000000 | tf_op jit(solution)/shard_map/pack_rest/pallas_call | solution.py:140
  22.6 1.1 collective-permute-start.1
  23.7 1.4 collective-permute-done.4.refs_4_
  25.2 1.6 collective-permute-start.2
  29.3 3.3 %attn_fwd.2 = (bf16[256,384]{1,0:T(8,128)(2,1)S(1)}, bf16[256,1152]{1,0:T(8,128)(2,1)S(1)}, bf16[1536,256]{1,0:T(8,128)(2,1)S(1)}, bf16[256,384]{1,0:T(8,128)(2,...) custom-call(s32[6]{0:T(128)S(1)} %copy-done.2, ...), custom_call_target="tpu_custom_call" | custom-call | flops 10000000000 | tf_op jit(solution)/shard_map/attn_fwd/pallas_call | solution.py:373
  33.7 2.0 %collective-permute-start.15 = (bf16[48,1536]{1,0:T(8,128)(2,1)S(1)}, bf16[48,1536]{1,0:T(8,128)(2,1)S(1)}, u32[]{:S(2)}, u32[]{:S(2)}) collective-permute-start(bf16[48,1536]{1,0:T(8,128)(2,1)S(1)} %collective-permute-done.1.refs_5_), channel_id=1, source_target_pairs={{0,4},{2,6},{4,0},{6,2},{8,12},{10,14},{12,8},{14,10},{16,20},{18,... | collective-permute-start | bytes 442376 | tf_op jit(solution)/shard_map/ppermute | solution.py:997
  36.2 1.6 collective-permute-start.18
  38.3 1.3 collective-permute-done.15.refs_6_
  39.6 4.4 %mlp_fwd.2 = (f32[256,384]{1,0:T(8,128)S(1)}, bf16[256,384]{1,0:T(8,128)(2,1)S(1)}, bf16[256,1536]{1,0:T(8,128)(2,1)S(1)}, bf16[256,1536]{1,0:T(8,128)(2,1)S(1)}...) custom-call(s32[6]{0:T(128)S(1)} %copy-done.2, ...), custom_call_target="tpu_custom_call" | custom-call | flops 10000000000 | tf_op jit(solution)/shard_map/mlp_fwd/pallas_call | solution.py:434
  45.2 3.4 %attn_fwd.3 = (bf16[256,384]{1,0:T(8,128)(2,1)S(1)}, bf16[256,1152]{1,0:T(8,128)(2,1)S(1)}, bf16[1536,256]{1,0:T(8,128)(2,1)S(1)}, bf16[256,384]{1,0:T(8,128)(2,...) custom-call(s32[6]{0:T(128)S(1)} %copy-done.2, ...), custom_call_target="tpu_custom_call" | custom-call | flops 10000000000 | tf_op jit(solution)/shard_map/attn_fwd/pallas_call | solution.py:373
  48.7 5.1 %mlp_fwd.3 = (bf16[256,384]{1,0:T(8,128)(2,1)}, bf16[256,384]{1,0:T(8,128)(2,1)S(1)}, bf16[256,1536]{1,0:T(8,128)(2,1)S(1)}, bf16[256,1536]{1,0:T(8,128)(2,1)S(1...) custom-call(s32[6]{0:T(128)S(1)} %copy-done.2, ...), custom_call_target="tpu_custom_call" | custom-call | flops 10000000000 | tf_op jit(solution)/shard_map/mlp_fwd/pallas_call | solution.py:434
  53.8 5.2 %mlp_bwd.2 = (bf16[1536,384]{1,0:T(8,128)(2,1)S(1)}, bf16[1536,384]{1,0:T(8,128)(2,1)S(1)}, f32[256,384]{1,0:T(8,128)S(1)}, f32[16,384]{1,0:T(8,128)S(1)}) custom-call(s32[6]{0:T(128)S(1)} %copy-done.2, bf16[256,384]{1,0:T(8,128)(2,1)S(1)} %bitcast.16, f32[16,384]{1,0:T(8,128)S(1)} %get-tuple-element.240.refs_2_, ...), custom_call_target="tpu_custom_call" | custom-call | flops 10000000000 | tf_op jit(solution)/shard_map/mlp_bwd/pallas_call | solution.py:513
  59.6 4.2 %attn_bwd.2 = (bf16[768,384]{1,0:T(8,128)(2,1)S(1)}, bf16[784,384]{1,0:T(8,128)(2,1)S(1)}, f32[256,384]{1,0:T(8,128)S(1)}, bf16[16,384]{1,0:T(8,128)(2,1)S(1)}) custom-call(s32[6]{0:T(128)S(1)} %copy-done.2, f32[256,384]{1,0:T(8,128)S(1)} %get-tuple-element.153.refs_1_, f32[16,384]{1,0:T(8,128)S(1)} %get-tuple-element.240.refs_2_, ...), custom_call_target="tpu_custom_call" | custom-call | flops 10000000000 | tf_op jit(solution)/shard_map/attn_bwd/pallas_call | solution.py:616
  63.9 0.8 first_split.4
  64.7 1.1 collective-permute-start.28
  65.8 5.0 %mlp_bwd.3 = (bf16[1536,384]{1,0:T(8,128)(2,1)S(1)}, bf16[1536,384]{1,0:T(8,128)(2,1)S(1)}, f32[256,384]{1,0:T(8,128)S(1)}, f32[16,384]{1,0:T(8,128)S(1)}) custom-call(s32[6]{0:T(128)S(1)} %copy-done.2, f32[256,384]{1,0:T(8,128)S(1)} %get-tuple-element.162.refs_1_, f32[16,384]{1,0:T(8,128)S(1)} %get-tuple-element.241.refs_2_, ...), custom_call_target="tpu_custom_call" | custom-call | flops 10000000000 | tf_op jit(solution)/shard_map/mlp_bwd/pallas_call | solution.py:513
  70.9 0.8 first_split.5
  71.7 1.0 collective-permute-start.26
  72.7 5.1 %attn_bwd.3 = (bf16[768,384]{1,0:T(8,128)(2,1)S(1)}, bf16[784,384]{1,0:T(8,128)(2,1)S(1)}, f32[256,384]{1,0:T(8,128)}, bf16[16,384]{1,0:T(8,128)(2,1)S(1)}) custom-call(s32[6]{0:T(128)S(1)} %copy-done.2, f32[256,384]{1,0:T(8,128)S(1)} %get-tuple-element.173.refs_1_, f32[16,384]{1,0:T(8,128)S(1)} %get-tuple-element.241.refs_2_, ...), custom_call_target="tpu_custom_call" | custom-call | flops 10000000000 | tf_op jit(solution)/shard_map/attn_bwd/pallas_call | solution.py:616
  78.3 2.6 %collective-permute-done.28.refs_3_ = bf16[768,384]{1,0:T(8,128)(2,1)S(1)} collective-permute-done((bf16[768,384]{1,0:T(8,128)(2,1)S(1)}, bf16[768,384]{1,0:T(8,128)(2,1)S(1)}, u32[]{:S(2)}, u32[]{:S(2)}) %collective-permute-start.28) | collective-permute-done | bytes 589856 | tf_op jit(solution)/shard_map/ppermute | solution.py:994
  81.6 1.7 %collective-permute-start.30 = (bf16[384,384]{1,0:T(8,128)(2,1)S(1)}, bf16[384,384]{1,0:T(8,128)(2,1)S(1)}, u32[]{:S(2)}, u32[]{:S(2)}) collective-permute-start(bf16[384,384]{1,0:T(8,128)(2,1)S(1)} %get-tuple-element.191.refs_3_.refs_2_), channel_id=1, source_target_pairs={{0,4},{2,6},{4,0},{6,2},{8,12},{10,14},{12,8},{14,10},{16,20},{18,... | collective-permute-start | bytes 884744 | tf_op jit(solution)/shard_map/ppermute | solution.py:997
  83.3 0.9 first_split.6
  84.1 1.1 collective-permute-start.33
  85.2 2.3 %collective-permute-done.26.refs_3_ = bf16[400,384]{1,0:T(8,128)(2,1)S(1)} collective-permute-done((bf16[400,384]{1,0:T(8,128)(2,1)S(1)}, bf16[400,384]{1,0:T(8,128)(2,1)S(1)}, u32[]{:S(2)}, u32[]{:S(2)}) %collective-permute-start.26) | collective-permute-done | bytes 307232 | tf_op jit(solution)/shard_map/ppermute | solution.py:994
  88.1 1.7 %collective-permute-start.29 = (bf16[224,384]{1,0:T(8,128)(2,1)S(1)}, bf16[224,384]{1,0:T(8,128)(2,1)S(1)}, u32[]{:S(2)}, u32[]{:S(2)}) collective-permute-start(bf16[224,384]{1,0:T(8,128)(2,1)S(1)} %get-tuple-element.194.refs_4_.refs_1_), channel_id=1, source_target_pairs={{0,4},{2,6},{4,0},{6,2},{8,12},{10,14},{12,8},{14,10},{16,20},{18,... | collective-permute-start | bytes 516104 | tf_op jit(solution)/shard_map/ppermute | solution.py:997
  90.6 1.1 collective-permute-start.38
  92.3 1.6 collective-permute-start.34
  94.0 1.4 collective-permute-start.32
  95.4 4.7 %collective-permute-done.34.refs_2_ = bf16[192,384]{1,0:T(8,128)(2,1)S(1)} collective-permute-done((bf16[192,384]{1,0:T(8,128)(2,1)S(1)}, bf16[192,384]{1,0:T(8,128)(2,1)S(1)}, u32[]{:S(2)}, u32[]{:S(2)}) %collective-permute-start.34) | collective-permute-done | bytes 147488 | tf_op jit(solution)/shard_map/ppermute | solution.py:997
  100.2 1.6 collective-permute-start.37
  103.1 2.1 %collective-permute-start.35 = (bf16[320,384]{1,0:T(8,128)(2,1)S(1)}, bf16[320,384]{1,0:T(8,128)(2,1)S(1)}, u32[]{:S(2)}, u32[]{:S(2)}) collective-permute-start(bf16[320,384]{1,0:T(8,128)(2,1)S(1)} %add_join.12.refs_4_.refs_0_.refs_1_), channel_id=1, source_target_pairs={{0,16},{2,18},{4,20},{6,22},{8,24},{10,26},{12,28},{14,30},{16,0},... | collective-permute-start | bytes 737288 | tf_op jit(solution)/shard_map/ppermute | solution.py:997
  105.2 1.1 collective-permute-done.38.refs_3_
  106.9 1.2 collective-permute-start.41
  108.2 6.1 %collective-permute-done.37.refs_2_ = bf16[192,384]{1,0:T(8,128)(2,1)S(1)} collective-permute-done((bf16[192,384]{1,0:T(8,128)(2,1)S(1)}, bf16[192,384]{1,0:T(8,128)(2,1)S(1)}, u32[]{:S(2)}, u32[]{:S(2)}) %collective-permute-start.37) | collective-permute-done | bytes 147488 | tf_op jit(solution)/shard_map/ppermute | solution.py:997
  115.0 2.1 %collective-permute-start.39 = (bf16[192,384]{1,0:T(8,128)(2,1)S(1)}, bf16[192,384]{1,0:T(8,128)(2,1)S(1)}, u32[]{:S(2)}, u32[]{:S(2)}) collective-permute-start(bf16[192,384]{1,0:T(8,128)(2,1)S(1)} %get-tuple-element.207.refs_3_.refs_1_), channel_id=1, source_target_pairs={{0,8},{2,10},{4,12},{6,14},{8,0},{10,2},{12,4},{14,6},{16,24},{18,... | collective-permute-start | bytes 442376 | tf_op jit(solution)/shard_map/ppermute | solution.py:997
  117.2 3.9 %collective-permute-done.40.refs_2_ = bf16[192,384]{1,0:T(8,128)(2,1)S(1)} collective-permute-done((bf16[192,384]{1,0:T(8,128)(2,1)S(1)}, bf16[192,384]{1,0:T(8,128)(2,1)S(1)}, u32[]{:S(2)}, u32[]{:S(2)}) %collective-permute-start.40) | collective-permute-done | bytes 147488 | tf_op jit(solution)/shard_map/ppermute | solution.py:997
  121.9 2.4 %collective-permute-done.39.refs_2_ = bf16[192,384]{1,0:T(8,128)(2,1)S(1)} collective-permute-done((bf16[192,384]{1,0:T(8,128)(2,1)S(1)}, bf16[192,384]{1,0:T(8,128)(2,1)S(1)}, u32[]{:S(2)}, u32[]{:S(2)}) %collective-permute-start.39) | collective-permute-done | bytes 147488 | tf_op jit(solution)/shard_map/ppermute | solution.py:997
  124.4 0.9 collective-permute-start.51
  125.8 1.9 %collective-permute-done.43.refs_2_ = bf16[256,384]{1,0:T(8,128)(2,1)S(1)} collective-permute-done((bf16[256,384]{1,0:T(8,128)(2,1)S(1)}, bf16[256,384]{1,0:T(8,128)(2,1)S(1)}, u32[]{:S(2)}, u32[]{:S(2)}) %collective-permute-start.43) | collective-permute-done | bytes 196640 | tf_op jit(solution)/shard_map/ppermute | solution.py:997
  127.8 1.4 collective-permute-done.42.far
  129.3 2.9 %ada_result.2 = (f32[2,192,2304]{2,1,0:T(8,128)}, f32[32,192]{1,0:T(8,128)S(1)}, f32[32,192]{1,0:T(8,128)S(1)}, f32[16,384]{1,0:T(8,128)S(1)}) custom-call(s32[6]{0:T(128)S(1)} %copy-done.2, bf16[256,384]{1,0:T(8,128)(2,1)S(1)} %get-tuple-element.209.refs_3_.rides, bf16[256,384]{1,0:T(8,128)(2,1)S(1)} %collective-permute-done.42.far, ...), custom_call_target="tpu_custom_call" | custom-call | flops 100000000 | tf_op jit(solution)/shard_map/ada_result/pallas_call | solution.py:877
  132.2 2.2 %collective-permute-done.45.refs_2_ = bf16[192,384]{1,0:T(8,128)(2,1)S(1)} collective-permute-done((bf16[192,384]{1,0:T(8,128)(2,1)S(1)}, bf16[192,384]{1,0:T(8,128)(2,1)S(1)}, u32[]{:S(2)}, u32[]{:S(2)}) %collective-permute-start.45) | collective-permute-done | bytes 147488 | tf_op jit(solution)/shard_map/ppermute | solution.py:997
  134.4 0.8 collective-permute-start.44
  135.8 2.5 %collective-permute-start.53 = (bf16[192,384]{1,0:T(8,128)(2,1)S(1)}, bf16[192,384]{1,0:T(8,128)(2,1)S(1)}, u32[]{:S(2)}, u32[]{:S(2)}) collective-permute-start(bf16[192,384]{1,0:T(8,128)(2,1)S(1)} %add_join.18.refs_5_.refs_1_), channel_id=1, source_target_pairs={{0,8},{2,10},{4,12},{6,14},{8,0},{10,2},{12,4},{14,6},{16,24},{18,... | collective-permute-start | bytes 442376 | tf_op jit(solution)/shard_map/ppermute | solution.py:997
  138.3 2.1 %mlp_result.2 = (f32[2,192,1536]{2,1,0:T(8,128)}, f32[2,768,384]{2,1,0:T(8,128)}, f32[8,128]{1,0:T(8,128)S(1)}) custom-call(s32[6]{0:T(128)S(1)} %copy-done.2, bf16[384,384]{1,0:T(8,128)(2,1)S(1)} %join.2.refs_3_.refs_1_, bf16[384,384]{1,0:T(8,128)(2,1)S(1)} %collective-permute-done.48.refs_2_, bf16[384,384]{1,0:T(8,128)(2,1)S(1)} %collective-permute-done.49.refs_3_, ...), custom_call_target="tpu_custom_call" | custom-call | flops 100000000 | tf_op jit(solution)/shard_map/mlp_result/pallas_call | solution.py:802
  140.5 1.7 %attn_result.2 = (f32[2,192,1152]{2,1,0:T(8,128)}, f32[2,192,384]{2,1,0:T(8,128)}, f32[8,128]{1,0:T(8,128)S(1)}) custom-call(s32[6]{0:T(128)S(1)} %copy-done.2, bf16[192,384]{1,0:T(8,128)(2,1)S(1)} %get-tuple-element.211.refs_1_, bf16[192,384]{1,0:T(8,128)(2,1)S(1)} %collective-permute-done.45.refs_2_, bf16[192,384]{1,0:T(8,128)(2,1)S(1)} %collective-permute-done.46.refs_3_, ...), custom_call_target="tpu_custom_call" | custom-call | flops 100000000 | tf_op jit(solution)/shard_map/attn_result/pallas_call | solution.py:802
  142.2 5.9 %collective-permute-done.44.refs_2_ = bf16[320,384]{1,0:T(8,128)(2,1)S(1)} collective-permute-done((bf16[320,384]{1,0:T(8,128)(2,1)S(1)}, bf16[320,384]{1,0:T(8,128)(2,1)S(1)}, u32[]{:S(2)}, u32[]{:S(2)}) %collective-permute-start.44) | collective-permute-done | bytes 245792 | tf_op jit(solution)/shard_map/ppermute | solution.py:997
  149.2 1.6 collective-permute-start.58
  150.9 3.1 %ada_result.3 = (f32[2,192,2304]{2,1,0:T(8,128)}, f32[32,192]{1,0:T(8,128)S(1)}, f32[32,192]{1,0:T(8,128)S(1)}, f32[16,384]{1,0:T(8,128)S(1)}) custom-call(s32[6]{0:T(128)S(1)} %copy-done.2, bf16[256,384]{1,0:T(8,128)(2,1)S(1)} %get-tuple-element.215.refs_3_.rides, ...), custom_call_target="tpu_custom_call", output_to_operand_aliasing={{0}: (5, {})} | custom-call | flops 100000000 | tf_op jit(solution)/shard_map/ada_result/pallas_call | solution.py:877
  154.0 2.3 %condition_result.1 = (f32[192,1001]{1,0:T(8,128)}, f32[1,192]{1,0:T(1,128)S(1)}, f32[1,192]{1,0:T(1,128)S(1)}, f32[2,1152]{1,0:T(2,128)}, f32[2,384]{1,0:T(2,12...) custom-call(s32[6]{0:T(128)S(1)} %copy-done.2, f32[32,192]{1,0:T(8,128)S(1)} %get-tuple-element.210.refs_0_.refs_1_, ...), custom_call_target="tpu_custom_call" | custom-call | flops 10000000000 | tf_op jit(solution)/shard_map/condition_result/pallas_call | solution.py:140
  157.1 3.1 %collective-permute-done.58.refs_2_ = bf16[384,384]{1,0:T(8,128)(2,1)S(1)} collective-permute-done((bf16[384,384]{1,0:T(8,128)(2,1)S(1)}, bf16[384,384]{1,0:T(8,128)(2,1)S(1)}, u32[]{:S(2)}, u32[]{:S(2)}) %collective-permute-start.58) | collective-permute-done | bytes 294944 | tf_op jit(solution)/shard_map/ppermute | solution.py:997
  160.2 1.2 both_halves.1
  161.4 1.7 %attn_result.3 = (f32[2,192,1152]{2,1,0:T(8,128)}, f32[2,192,384]{2,1,0:T(8,128)}, f32[8,128]{1,0:T(8,128)S(1)}) custom-call(s32[6]{0:T(128)S(1)} %copy-done.2, bf16[192,384]{1,0:T(8,128)(2,1)S(1)} %get-tuple-element.226.refs_1_, bf16[192,384]{1,0:T(8,128)(2,1)S(1)} %collective-permute-done.55.refs_2_, ...), custom_call_target="tpu_custom_call", output_to_operand_aliasing={{0}: (5, {}), {1}: (6, {})} | custom-call | flops 100000000 | tf_op jit(solution)/shard_map/attn_result/pallas_call | solution.py:802
  163.1 2.7 %mlp_result.3 = (f32[2,192,1536]{2,1,0:T(8,128)}, f32[2,768,384]{2,1,0:T(8,128)}, f32[8,128]{1,0:T(8,128)}) custom-call(s32[6]{0:T(128)S(1)} %copy-done.2, bf16[384,384]{1,0:T(8,128)(2,1)S(1)} %join.3.refs_2_.refs_1_, bf16[384,384]{1,0:T(8,128)(2,1)S(1)} %collective-permute-done.58.refs_2_, ...), custom_call_target="tpu_custom_call", output_to_operand_aliasing={{0}: (5, {}), {1}: (6, {})} | custom-call | flops 100000000 | tf_op jit(solution)/shard_map/mlp_result/pallas_call | solution.py:802
  (132 shorter events, 17.7 us)
Async XLA Ops:
  5.5 5.5 %collective-permute-start = (f32[8,1536]{1,0:T(8,128)}, f32[8,1536]{1,0:T(8,128)S(1)}, u32[]{:S(2)}, u32[]{:S(2)}) collective-permute-start(f32[8,1536]{1,0:T(8,128)} %get-tuple-element.127.refs_1_), channel_id=1, source_target_pairs={{0,1},{1,0},{2,3},{3,2},{4,5},{5,4},{6,7},{7,6},{8,9},{9,8},{10,11... | collective-permute-start | bytes 147464 | tf_op jit(solution)/shard_map/ppermute | solution.py:994
  8.5 7.8 %collective-permute-start.5 = (bf16[48,1536]{1,0:T(8,128)(2,1)}, bf16[48,1536]{1,0:T(8,128)(2,1)S(1)}, u32[]{:S(2)}, u32[]{:S(2)}) collective-permute-start(bf16[48,1536]{1,0:T(8,128)(2,1)} %get-tuple-element.134), channel_id=1, source_target_pairs={{0,1},{1,0},{2,3},{3,2},{4,5},{5,4},{6,7},{7,6},{8,9},{9,8},{10,11... | collective-permute-start | bytes 442376 | tf_op jit(solution)/shard_map/ppermute | solution.py:994
  8.6 10.1 %collective-permute-start.7 = (bf16[48,1536]{1,0:T(8,128)(2,1)}, bf16[48,1536]{1,0:T(8,128)(2,1)S(1)}, u32[]{:S(2)}, u32[]{:S(2)}) collective-permute-start(bf16[48,1536]{1,0:T(8,128)(2,1)} %get-tuple-element.128.refs_5_), channel_id=1, source_target_pairs={{0,1},{1,0},{2,3},{3,2},{4,5},{5,4},{6,7},{7,6},{8,9},{9,8},{10,11... | collective-permute-start | bytes 442376 | tf_op jit(solution)/shard_map/ppermute | solution.py:994
  10.5 16.7 %collective-permute-start.9 = (bf16[96,1536]{1,0:T(8,128)(2,1)}, bf16[96,1536]{1,0:T(8,128)(2,1)S(1)}, u32[]{:S(2)}, u32[]{:S(2)}) collective-permute-start(bf16[96,1536]{1,0:T(8,128)(2,1)} %get-tuple-element.136), channel_id=1, source_target_pairs={{0,1},{1,0},{2,3},{3,2},{4,5},{5,4},{6,7},{7,6},{8,9},{9,8},{10,11... | collective-permute-start | bytes 884744 | tf_op jit(solution)/shard_map/ppermute | solution.py:994
  13.8 13.9 %copy-start.2 = (s32[6]{0:T(128)S(1)}, s32[6]{0:T(128)}, u32[]{:S(2)}) copy-start(s32[6]{0:T(128)} %stack.24.refs_0_.meta) | copy-start | bytes 76
  13.8 13.9 %copy-start.13 = (f32[8,1536]{1,0:T(8,128)S(1)}, f32[8,1536]{1,0:T(8,128)}, u32[]{:S(2)}) copy-start(f32[8,1536]{1,0:T(8,128)} %get-tuple-element.127.refs_1_) | copy-start | bytes 147460
  13.8 11.4 %collective-permute-start.4 = (f32[3,2304]{1,0:T(4,128)S(1)}, f32[3,2304]{1,0:T(4,128)S(1)}, u32[]{:S(2)}, u32[]{:S(2)}) collective-permute-start(f32[3,2304]{1,0:T(4,128)S(1)} %get-tuple-element.129.refs_5_), channel_id=1, source_target_pairs={{0,1},{1,0},{2,3},{3,2},{4,5},{5,4},{6,7},{7,6},{8,9},{9,8},{10,11... | collective-permute-start | bytes 82952 | tf_op jit(solution)/shard_map/ppermute | solution.py:994
  16.3 10.5 %collective-permute-start.6 = (bf16[48,1536]{1,0:T(8,128)(2,1)S(1)}, bf16[48,1536]{1,0:T(8,128)(2,1)S(1)}, u32[]{:S(2)}, u32[]{:S(2)}) collective-permute-start(bf16[48,1536]{1,0:T(8,128)(2,1)S(1)} %collective-permute-done.5.refs_5_), channel_id=1, source_target_pairs={{0,4},{2,6},{4,0},{6,2},{8,12},{10,14},{12,8},{14,10},{16,20},{18,... | collective-permute-start | bytes 442376 | tf_op jit(solution)/shard_map/ppermute | solution.py:997
  18.6 8.6 %collective-permute-start.8 = (bf16[48,1536]{1,0:T(8,128)(2,1)S(1)}, bf16[48,1536]{1,0:T(8,128)(2,1)S(1)}, u32[]{:S(2)}, u32[]{:S(2)}) collective-permute-start(bf16[48,1536]{1,0:T(8,128)(2,1)S(1)} %collective-permute-done.7.refs_9_), channel_id=1, source_target_pairs={{0,4},{2,6},{4,0},{6,2},{8,12},{10,14},{12,8},{14,10},{16,20},{18,... | collective-permute-start | bytes 442376 | tf_op jit(solution)/shard_map/ppermute | solution.py:997
  22.6 10.0 %collective-permute-start.1 = (bf16[48,1536]{1,0:T(8,128)(2,1)}, bf16[48,1536]{1,0:T(8,128)(2,1)S(1)}, u32[]{:S(2)}, u32[]{:S(2)}) collective-permute-start(bf16[48,1536]{1,0:T(8,128)(2,1)} %get-tuple-element.130), channel_id=1, source_target_pairs={{0,1},{1,0},{2,3},{3,2},{4,5},{5,4},{6,7},{7,6},{8,9},{9,8},{10,11... | collective-permute-start | bytes 442376 | tf_op jit(solution)/shard_map/ppermute | solution.py:994
  25.2 7.8 %collective-permute-start.2 = (bf16[48,1536]{1,0:T(8,128)(2,1)}, bf16[48,1536]{1,0:T(8,128)(2,1)S(1)}, u32[]{:S(2)}, u32[]{:S(2)}) collective-permute-start(bf16[48,1536]{1,0:T(8,128)(2,1)} %get-tuple-element.131), channel_id=1, source_target_pairs={{0,1},{1,0},{2,3},{3,2},{4,5},{5,4},{6,7},{7,6},{8,9},{9,8},{10,11... | collective-permute-start | bytes 442376 | tf_op jit(solution)/shard_map/ppermute | solution.py:994
  26.7 7.0 %collective-permute-start.3 = (bf16[48,1536]{1,0:T(8,128)(2,1)}, bf16[48,1536]{1,0:T(8,128)(2,1)S(1)}, u32[]{:S(2)}, u32[]{:S(2)}) collective-permute-start(bf16[48,1536]{1,0:T(8,128)(2,1)} %get-tuple-element.132), channel_id=1, source_target_pairs={{0,1},{1,0},{2,3},{3,2},{4,5},{5,4},{6,7},{7,6},{8,9},{9,8},{10,11... | collective-permute-start | bytes 442376 | tf_op jit(solution)/shard_map/ppermute | solution.py:994
  27.2 8.5 %collective-permute-start.11 = (bf16[48,1536]{1,0:T(8,128)(2,1)S(1)}, bf16[48,1536]{1,0:T(8,128)(2,1)S(1)}, u32[]{:S(2)}, u32[]{:S(2)}) collective-permute-start(bf16[48,1536]{1,0:T(8,128)(2,1)S(1)} %collective-permute-done.5.refs_5_), channel_id=1, source_target_pairs={{0,2},{2,0},{4,6},{6,4},{8,10},{10,8},{12,14},{14,12},{16,18},{18,... | collective-permute-start | bytes 442376 | tf_op jit(solution)/shard_map/ppermute | solution.py:997
  27.2 1.8 %collective-permute-start.10 = (bf16[96,1536]{1,0:T(8,128)(2,1)S(1)}, bf16[96,1536]{1,0:T(8,128)(2,1)S(1)}, u32[]{:S(2)}, u32[]{:S(2)}) collective-permute-start(bf16[96,1536]{1,0:T(8,128)(2,1)S(1)} %collective-permute-done.9.refs_5_), channel_id=1, source_target_pairs={{0,2},{2,0},{4,6},{6,4},{8,10},{10,8},{12,14},{14,12},{16,18},{18,... | collective-permute-start | bytes 884744 | tf_op jit(solution)/shard_map/ppermute | solution.py:997
  29.0 6.7 %collective-permute-start.13 = (bf16[48,1536]{1,0:T(8,128)(2,1)S(1)}, bf16[48,1536]{1,0:T(8,128)(2,1)S(1)}, u32[]{:S(2)}, u32[]{:S(2)}) collective-permute-start(bf16[48,1536]{1,0:T(8,128)(2,1)S(1)} %collective-permute-done.7.refs_9_), channel_id=1, source_target_pairs={{0,2},{2,0},{4,6},{6,4},{8,10},{10,8},{12,14},{14,12},{16,18},{18,... | collective-permute-start | bytes 442376 | tf_op jit(solution)/shard_map/ppermute | solution.py:997
  29.3 10.3 %copy-start.4 = (bf16[2,192,1536]{2,1,0:T(8,128)(2,1)S(1)}, bf16[2,192,1536]{2,1,0:T(8,128)(2,1)}, u32[]{:S(2)}) copy-start(bf16[2,192,1536]{2,1,0:T(8,128)(2,1)} %refs_3_.11) | copy-start | bytes 3538948
  32.7 3.6 %collective-permute-start.12 = (bf16[48,1536]{1,0:T(8,128)(2,1)S(1)}, bf16[48,1536]{1,0:T(8,128)(2,1)S(1)}, u32[]{:S(2)}, u32[]{:S(2)}) collective-permute-start(bf16[48,1536]{1,0:T(8,128)(2,1)S(1)} %collective-permute-done.6.refs_6_), channel_id=1, source_target_pairs={{0,2},{2,0},{4,6},{6,4},{8,10},{10,8},{12,14},{14,12},{16,18},{18,... | collective-permute-start | bytes 442376 | tf_op jit(solution)/shard_map/ppermute | solution.py:997
  32.9 4.9 %collective-permute-start.14 = (bf16[48,1536]{1,0:T(8,128)(2,1)S(1)}, bf16[48,1536]{1,0:T(8,128)(2,1)S(1)}, u32[]{:S(2)}, u32[]{:S(2)}) collective-permute-start(bf16[48,1536]{1,0:T(8,128)(2,1)S(1)} %collective-permute-done.8.refs_10_), channel_id=1, source_target_pairs={{0,2},{2,0},{4,6},{6,4},{8,10},{10,8},{12,14},{14,12},{16,18},{18,... | collective-permute-start | bytes 442376 | tf_op jit(solution)/shard_map/ppermute | solution.py:997
  33.7 5.8 %collective-permute-start.15 = (bf16[48,1536]{1,0:T(8,128)(2,1)S(1)}, bf16[48,1536]{1,0:T(8,128)(2,1)S(1)}, u32[]{:S(2)}, u32[]{:S(2)}) collective-permute-start(bf16[48,1536]{1,0:T(8,128)(2,1)S(1)} %collective-permute-done.1.refs_5_), channel_id=1, source_target_pairs={{0,4},{2,6},{4,0},{6,2},{8,12},{10,14},{12,8},{14,10},{16,20},{18,... | collective-permute-start | bytes 442376 | tf_op jit(solution)/shard_map/ppermute | solution.py:997
  35.7 8.3 %collective-permute-start.16 = (bf16[48,1536]{1,0:T(8,128)(2,1)S(1)}, bf16[48,1536]{1,0:T(8,128)(2,1)S(1)}, u32[]{:S(2)}, u32[]{:S(2)}) collective-permute-start(bf16[48,1536]{1,0:T(8,128)(2,1)S(1)} %collective-permute-done.1.refs_5_), channel_id=1, source_target_pairs={{0,2},{2,0},{4,6},{6,4},{8,10},{10,8},{12,14},{14,12},{16,18},{18,... | collective-permute-start | bytes 442376 | tf_op jit(solution)/shard_map/ppermute | solution.py:997
  35.7 12.9 %collective-permute-start.19 = (bf16[48,1536]{1,0:T(8,128)(2,1)S(1)}, bf16[48,1536]{1,0:T(8,128)(2,1)S(1)}, u32[]{:S(2)}, u32[]{:S(2)}) collective-permute-start(bf16[48,1536]{1,0:T(8,128)(2,1)S(1)} %collective-permute-done.2.refs_5_), channel_id=1, source_target_pairs={{0,2},{2,0},{4,6},{6,4},{8,10},{10,8},{12,14},{14,12},{16,18},{18,... | collective-permute-start | bytes 442376 | tf_op jit(solution)/shard_map/ppermute | solution.py:997
  36.2 8.3 %collective-permute-start.18 = (bf16[48,1536]{1,0:T(8,128)(2,1)S(1)}, bf16[48,1536]{1,0:T(8,128)(2,1)S(1)}, u32[]{:S(2)}, u32[]{:S(2)}) collective-permute-start(bf16[48,1536]{1,0:T(8,128)(2,1)S(1)} %collective-permute-done.2.refs_5_), channel_id=1, source_target_pairs={{0,8},{2,10},{4,12},{6,14},{8,0},{10,2},{12,4},{14,6},{16,24},{18,... | collective-permute-start | bytes 442376 | tf_op jit(solution)/shard_map/ppermute | solution.py:997
  37.8 7.4 %collective-permute-start.21 = (bf16[48,1536]{1,0:T(8,128)(2,1)S(1)}, bf16[48,1536]{1,0:T(8,128)(2,1)S(1)}, u32[]{:S(2)}, u32[]{:S(2)}) collective-permute-start(bf16[48,1536]{1,0:T(8,128)(2,1)S(1)} %collective-permute-done.3.refs_9_), channel_id=1, source_target_pairs={{0,8},{2,10},{4,12},{6,14},{8,0},{10,2},{12,4},{14,6},{16,24},{18,... | collective-permute-start | bytes 442376 | tf_op jit(solution)/shard_map/ppermute | solution.py:997
  39.6 5.7 %collective-permute-start.17 = (bf16[48,1536]{1,0:T(8,128)(2,1)S(1)}, bf16[48,1536]{1,0:T(8,128)(2,1)S(1)}, u32[]{:S(2)}, u32[]{:S(2)}) collective-permute-start(bf16[48,1536]{1,0:T(8,128)(2,1)S(1)} %collective-permute-done.15.refs_6_), channel_id=1, source_target_pairs={{0,2},{2,0},{4,6},{6,4},{8,10},{10,8},{12,14},{14,12},{16,18},{18,... | collective-permute-start | bytes 442376 | tf_op jit(solution)/shard_map/ppermute | solution.py:997
  44.0 4.7 %collective-permute-start.22 = (bf16[48,1536]{1,0:T(8,128)(2,1)S(1)}, bf16[48,1536]{1,0:T(8,128)(2,1)S(1)}, u32[]{:S(2)}, u32[]{:S(2)}) collective-permute-start(bf16[48,1536]{1,0:T(8,128)(2,1)S(1)} %collective-permute-done.3.refs_9_), channel_id=1, source_target_pairs={{0,2},{2,0},{4,6},{6,4},{8,10},{10,8},{12,14},{14,12},{16,18},{18,... | collective-permute-start | bytes 442376 | tf_op jit(solution)/shard_map/ppermute | solution.py:997
  44.6 4.1 %collective-permute-start.20 = (bf16[48,1536]{1,0:T(8,128)(2,1)S(1)}, bf16[48,1536]{1,0:T(8,128)(2,1)S(1)}, u32[]{:S(2)}, u32[]{:S(2)}) collective-permute-start(bf16[48,1536]{1,0:T(8,128)(2,1)S(1)} %collective-permute-done.18.refs_6_), channel_id=1, source_target_pairs={{0,2},{2,0},{4,6},{6,4},{8,10},{10,8},{12,14},{14,12},{16,18},{18,... | collective-permute-start | bytes 442376 | tf_op jit(solution)/shard_map/ppermute | solution.py:997
  45.2 3.5 %collective-permute-start.23 = (bf16[48,1536]{1,0:T(8,128)(2,1)S(1)}, bf16[48,1536]{1,0:T(8,128)(2,1)S(1)}, u32[]{:S(2)}, u32[]{:S(2)}) collective-permute-start(bf16[48,1536]{1,0:T(8,128)(2,1)S(1)} %collective-permute-done.21.refs_10_), channel_id=1, source_target_pairs={{0,2},{2,0},{4,6},{6,4},{8,10},{10,8},{12,14},{14,12},{16,18},{18,... | collective-permute-start | bytes 442376 | tf_op jit(solution)/shard_map/ppermute | solution.py:997
  59.1 4.8 %collective-permute-start.24 = (bf16[1536,384]{1,0:T(8,128)(2,1)S(1)}, bf16[1536,384]{1,0:T(8,128)(2,1)S(1)}, u32[]{:S(2)}, u32[]{:S(2)}) collective-permute-start(bf16[1536,384]{1,0:T(8,128)(2,1)S(1)} %get-tuple-element.170), channel_id=1, source_target_pairs={{0,2},{2,0},{4,6},{6,4},{8,10},{10,8},{12,14},{14,12},{16,18},{18,... | collective-permute-start | bytes 3538952 | tf_op jit(solution)/shard_map/ppermute | solution.py:997
  63.8 7.1 %collective-permute-start.25 = (bf16[784,384]{1,0:T(8,128)(2,1)S(1)}, bf16[784,384]{1,0:T(8,128)(2,1)S(1)}, u32[]{:S(2)}, u32[]{:S(2)}) collective-permute-start(bf16[784,384]{1,0:T(8,128)(2,1)S(1)} %get-tuple-element.183), channel_id=1, source_target_pairs={{0,2},{2,0},{4,6},{6,4},{8,10},{10,8},{12,14},{14,12},{16,18},{18,... | collective-permute-start | bytes 1806344 | tf_op jit(solution)/shard_map/ppermute | solution.py:997
  64.7 16.2 %collective-permute-start.28 = (bf16[768,384]{1,0:T(8,128)(2,1)S(1)}, bf16[768,384]{1,0:T(8,128)(2,1)S(1)}, u32[]{:S(2)}, u32[]{:S(2)}) collective-permute-start(bf16[768,384]{1,0:T(8,128)(2,1)S(1)} %get-tuple-element.172.refs_10_.refs_2_), channel_id=1, source_target_pairs={{0,1},{1,0},{2,3},{3,2},{4,5},{5,4},{6,7},{7,6},{8,9},{9,8},{10,11... | collective-permute-start | bytes 1769480 | tf_op jit(solution)/shard_map/ppermute | solution.py:994
  71.7 15.8 %collective-permute-start.26 = (bf16[400,384]{1,0:T(8,128)(2,1)S(1)}, bf16[400,384]{1,0:T(8,128)(2,1)S(1)}, u32[]{:S(2)}, u32[]{:S(2)}) collective-permute-start(bf16[400,384]{1,0:T(8,128)(2,1)S(1)} %get-tuple-element.184.refs_12_.refs_2_), channel_id=1, source_target_pairs={{0,1},{1,0},{2,3},{3,2},{4,5},{5,4},{6,7},{7,6},{8,9},{9,8},{10,11... | collective-permute-start | bytes 921608 | tf_op jit(solution)/shard_map/ppermute | solution.py:994
  72.7 10.6 %collective-permute-start.27 = (bf16[1536,384]{1,0:T(8,128)(2,1)S(1)}, bf16[1536,384]{1,0:T(8,128)(2,1)S(1)}, u32[]{:S(2)}, u32[]{:S(2)}) collective-permute-start(bf16[1536,384]{1,0:T(8,128)(2,1)S(1)} %get-tuple-element.188), channel_id=1, source_target_pairs={{0,2},{2,0},{4,6},{6,4},{8,10},{10,8},{12,14},{14,12},{16,18},{18,... | collective-permute-start | bytes 3538952 | tf_op jit(solution)/shard_map/ppermute | solution.py:997
  77.8 12.0 %collective-permute-start.31 = (bf16[784,384]{1,0:T(8,128)(2,1)S(1)}, bf16[784,384]{1,0:T(8,128)(2,1)S(1)}, u32[]{:S(2)}, u32[]{:S(2)}) collective-permute-start(bf16[784,384]{1,0:T(8,128)(2,1)S(1)} %get-tuple-element.197), channel_id=1, source_target_pairs={{0,2},{2,0},{4,6},{6,4},{8,10},{10,8},{12,14},{14,12},{16,18},{18,... | collective-permute-start | bytes 1806344 | tf_op jit(solution)/shard_map/ppermute | solution.py:997
  81.6 10.1 %collective-permute-start.30 = (bf16[384,384]{1,0:T(8,128)(2,1)S(1)}, bf16[384,384]{1,0:T(8,128)(2,1)S(1)}, u32[]{:S(2)}, u32[]{:S(2)}) collective-permute-start(bf16[384,384]{1,0:T(8,128)(2,1)S(1)} %get-tuple-element.191.refs_3_.refs_2_), channel_id=1, source_target_pairs={{0,4},{2,6},{4,0},{6,2},{8,12},{10,14},{12,8},{14,10},{16,20},{18,... | collective-permute-start | bytes 884744 | tf_op jit(solution)/shard_map/ppermute | solution.py:997
  84.1 17.7 %collective-permute-start.33 = (bf16[768,384]{1,0:T(8,128)(2,1)S(1)}, bf16[768,384]{1,0:T(8,128)(2,1)S(1)}, u32[]{:S(2)}, u32[]{:S(2)}) collective-permute-start(bf16[768,384]{1,0:T(8,128)(2,1)S(1)} %get-tuple-element.192.refs_4_.refs_2_), channel_id=1, source_target_pairs={{0,1},{1,0},{2,3},{3,2},{4,5},{5,4},{6,7},{7,6},{8,9},{9,8},{10,11... | collective-permute-start | bytes 1769480 | tf_op jit(solution)/shard_map/ppermute | solution.py:994
  88.1 5.8 %collective-permute-start.29 = (bf16[224,384]{1,0:T(8,128)(2,1)S(1)}, bf16[224,384]{1,0:T(8,128)(2,1)S(1)}, u32[]{:S(2)}, u32[]{:S(2)}) collective-permute-start(bf16[224,384]{1,0:T(8,128)(2,1)S(1)} %get-tuple-element.194.refs_4_.refs_1_), channel_id=1, source_target_pairs={{0,4},{2,6},{4,0},{6,2},{8,12},{10,14},{12,8},{14,10},{16,20},{18,... | collective-permute-start | bytes 516104 | tf_op jit(solution)/shard_map/ppermute | solution.py:997
  90.6 15.7 %collective-permute-start.38 = (bf16[400,384]{1,0:T(8,128)(2,1)S(1)}, bf16[400,384]{1,0:T(8,128)(2,1)S(1)}, u32[]{:S(2)}, u32[]{:S(2)}) collective-permute-start(bf16[400,384]{1,0:T(8,128)(2,1)S(1)} %get-tuple-element.198.refs_4_.refs_2_), channel_id=1, source_target_pairs={{0,1},{1,0},{2,3},{3,2},{4,5},{5,4},{6,7},{7,6},{8,9},{9,8},{10,11... | collective-permute-start | bytes 921608 | tf_op jit(solution)/shard_map/ppermute | solution.py:994
  92.3 7.8 %collective-permute-start.34 = (bf16[192,384]{1,0:T(8,128)(2,1)S(1)}, bf16[192,384]{1,0:T(8,128)(2,1)S(1)}, u32[]{:S(2)}, u32[]{:S(2)}) collective-permute-start(bf16[192,384]{1,0:T(8,128)(2,1)S(1)} %get-tuple-element.199.refs_3_.refs_1_), channel_id=1, source_target_pairs={{0,8},{2,10},{4,12},{6,14},{8,0},{10,2},{12,4},{14,6},{16,24},{18,... | collective-permute-start | bytes 442376 | tf_op jit(solution)/shard_map/ppermute | solution.py:997
  94.0 9.0 %collective-permute-start.32 = (bf16[256,384]{1,0:T(8,128)(2,1)S(1)}, bf16[256,384]{1,0:T(8,128)(2,1)S(1)}, u32[]{:S(2)}, u32[]{:S(2)}) collective-permute-start(bf16[256,384]{1,0:T(8,128)(2,1)S(1)} %add_join.10.refs_3_.refs_0_.refs_1_), channel_id=1, source_target_pairs={{0,8},{2,10},{4,12},{6,14},{8,0},{10,2},{12,4},{14,6},{16,24},{18,... | collective-permute-start | bytes 589832 | tf_op jit(solution)/shard_map/ppermute | solution.py:997
  100.2 14.1 %collective-permute-start.37 = (bf16[192,384]{1,0:T(8,128)(2,1)S(1)}, bf16[192,384]{1,0:T(8,128)(2,1)S(1)}, u32[]{:S(2)}, u32[]{:S(2)}) collective-permute-start(bf16[192,384]{1,0:T(8,128)(2,1)S(1)} %add_join.11.refs_4_.refs_0_.refs_1_), channel_id=1, source_target_pairs={{0,16},{2,18},{4,20},{6,22},{8,24},{10,26},{12,28},{14,30},{16,0},... | collective-permute-start | bytes 442376 | tf_op jit(solution)/shard_map/ppermute | solution.py:997
  102.5 11.9 %collective-permute-start.36 = (bf16[384,384]{1,0:T(8,128)(2,1)S(1)}, bf16[384,384]{1,0:T(8,128)(2,1)S(1)}, u32[]{:S(2)}, u32[]{:S(2)}) collective-permute-start(bf16[384,384]{1,0:T(8,128)(2,1)S(1)} %get-tuple-element.202.refs_3_.refs_2_), channel_id=1, source_target_pairs={{0,4},{2,6},{4,0},{6,2},{8,12},{10,14},{12,8},{14,10},{16,20},{18,... | collective-permute-start | bytes 884744 | tf_op jit(solution)/shard_map/ppermute | solution.py:997
  103.1 22.2 %collective-permute-start.35 = (bf16[320,384]{1,0:T(8,128)(2,1)S(1)}, bf16[320,384]{1,0:T(8,128)(2,1)S(1)}, u32[]{:S(2)}, u32[]{:S(2)}) collective-permute-start(bf16[320,384]{1,0:T(8,128)(2,1)S(1)} %add_join.12.refs_4_.refs_0_.refs_1_), channel_id=1, source_target_pairs={{0,16},{2,18},{4,20},{6,22},{8,24},{10,26},{12,28},{14,30},{16,0},... | collective-permute-start | bytes 737288 | tf_op jit(solution)/shard_map/ppermute | solution.py:997
  106.9 10.2 %collective-permute-start.41 = (bf16[224,384]{1,0:T(8,128)(2,1)S(1)}, bf16[224,384]{1,0:T(8,128)(2,1)S(1)}, u32[]{:S(2)}, u32[]{:S(2)}) collective-permute-start(bf16[224,384]{1,0:T(8,128)(2,1)S(1)} %get-tuple-element.205.refs_3_.refs_1_), channel_id=1, source_target_pairs={{0,4},{2,6},{4,0},{6,2},{8,12},{10,14},{12,8},{14,10},{16,20},{18,... | collective-permute-start | bytes 516104 | tf_op jit(solution)/shard_map/ppermute | solution.py:997
  114.3 6.9 %collective-permute-start.40 = (bf16[192,384]{1,0:T(8,128)(2,1)S(1)}, bf16[192,384]{1,0:T(8,128)(2,1)S(1)}, u32[]{:S(2)}, u32[]{:S(2)}) collective-permute-start(bf16[192,384]{1,0:T(8,128)(2,1)S(1)} %add_join.13.refs_4_.refs_1_), channel_id=1, source_target_pairs={{0,8},{2,10},{4,12},{6,14},{8,0},{10,2},{12,4},{14,6},{16,24},{18,... | collective-permute-start | bytes 442376 | tf_op jit(solution)/shard_map/ppermute | solution.py:997
  115.0 9.3 %collective-permute-start.39 = (bf16[192,384]{1,0:T(8,128)(2,1)S(1)}, bf16[192,384]{1,0:T(8,128)(2,1)S(1)}, u32[]{:S(2)}, u32[]{:S(2)}) collective-permute-start(bf16[192,384]{1,0:T(8,128)(2,1)S(1)} %get-tuple-element.207.refs_3_.refs_1_), channel_id=1, source_target_pairs={{0,8},{2,10},{4,12},{6,14},{8,0},{10,2},{12,4},{14,6},{16,24},{18,... | collective-permute-start | bytes 442376 | tf_op jit(solution)/shard_map/ppermute | solution.py:997
  117.1 10.6 %collective-permute-start.43 = (bf16[256,384]{1,0:T(8,128)(2,1)S(1)}, bf16[256,384]{1,0:T(8,128)(2,1)S(1)}, u32[]{:S(2)}, u32[]{:S(2)}) collective-permute-start(bf16[256,384]{1,0:T(8,128)(2,1)S(1)} %add_join.14.refs_3_.refs_0_.refs_1_), channel_id=1, source_target_pairs={{0,8},{2,10},{4,12},{6,14},{8,0},{10,2},{12,4},{14,6},{16,24},{18,... | collective-permute-start | bytes 589832 | tf_op jit(solution)/shard_map/ppermute | solution.py:997
  121.7 14.0 %collective-permute-start.49 = (bf16[384,384]{1,0:T(8,128)(2,1)S(1)}, bf16[384,384]{1,0:T(8,128)(2,1)S(1)}, u32[]{:S(2)}, u32[]{:S(2)}) collective-permute-start(bf16[384,384]{1,0:T(8,128)(2,1)S(1)} %join.2.refs_3_.refs_1_), channel_id=1, source_target_pairs={{0,2},{2,0},{4,6},{6,4},{8,10},{10,8},{12,14},{14,12},{16,18},{18,... | collective-permute-start | bytes 884744 | tf_op jit(solution)/shard_map/ppermute | solution.py:997
  121.8 13.4 %collective-permute-start.48 = (bf16[384,384]{1,0:T(8,128)(2,1)S(1)}, bf16[384,384]{1,0:T(8,128)(2,1)S(1)}, u32[]{:S(2)}, u32[]{:S(2)}) collective-permute-start(bf16[384,384]{1,0:T(8,128)(2,1)S(1)} %join.2.refs_3_.refs_1_), channel_id=1, source_target_pairs={{0,4},{2,6},{4,0},{6,2},{8,12},{10,14},{12,8},{14,10},{16,20},{18,... | collective-permute-start | bytes 884744 | tf_op jit(solution)/shard_map/ppermute | solution.py:997
  124.4 10.8 %collective-permute-start.51 = (bf16[192,384]{1,0:T(8,128)(2,1)S(1)}, bf16[192,384]{1,0:T(8,128)(2,1)S(1)}, u32[]{:S(2)}, u32[]{:S(2)}) collective-permute-start(bf16[192,384]{1,0:T(8,128)(2,1)S(1)} %add_join.15.refs_3_.refs_0_.refs_1_), channel_id=1, source_target_pairs={{0,16},{2,18},{4,20},{6,22},{8,24},{10,26},{12,28},{14,30},{16,0},... | collective-permute-start | bytes 442376 | tf_op jit(solution)/shard_map/ppermute | solution.py:997
  125.3 9.1 %collective-permute-start.45 = (bf16[192,384]{1,0:T(8,128)(2,1)S(1)}, bf16[192,384]{1,0:T(8,128)(2,1)S(1)}, u32[]{:S(2)}, u32[]{:S(2)}) collective-permute-start(bf16[192,384]{1,0:T(8,128)(2,1)S(1)} %get-tuple-element.211.refs_1_), channel_id=1, source_target_pairs={{0,4},{2,6},{4,0},{6,2},{8,12},{10,14},{12,8},{14,10},{16,20},{18,... | collective-permute-start | bytes 442376 | tf_op jit(solution)/shard_map/ppermute | solution.py:997
  127.7 1.4 collective-permute-start.42
  129.2 11.3 %collective-permute-start.46 = (bf16[192,384]{1,0:T(8,128)(2,1)S(1)}, bf16[192,384]{1,0:T(8,128)(2,1)S(1)}, u32[]{:S(2)}, u32[]{:S(2)}) collective-permute-start(bf16[192,384]{1,0:T(8,128)(2,1)S(1)} %get-tuple-element.211.refs_1_), channel_id=1, source_target_pairs={{0,2},{2,0},{4,6},{6,4},{8,10},{10,8},{12,14},{14,12},{16,18},{18,... | collective-permute-start | bytes 442376 | tf_op jit(solution)/shard_map/ppermute | solution.py:997
  134.4 13.7 %collective-permute-start.44 = (bf16[320,384]{1,0:T(8,128)(2,1)S(1)}, bf16[320,384]{1,0:T(8,128)(2,1)S(1)}, u32[]{:S(2)}, u32[]{:S(2)}) collective-permute-start(bf16[320,384]{1,0:T(8,128)(2,1)S(1)} %add_join.17.refs_0_.refs_1_), channel_id=1, source_target_pairs={{0,16},{2,18},{4,20},{6,22},{8,24},{10,26},{12,28},{14,30},{16,0},... | collective-permute-start | bytes 737288 | tf_op jit(solution)/shard_map/ppermute | solution.py:997
  135.2 5.3 %collective-permute-start.47 = (bf16[192,384]{1,0:T(8,128)(2,1)S(1)}, bf16[192,384]{1,0:T(8,128)(2,1)S(1)}, u32[]{:S(2)}, u32[]{:S(2)}) collective-permute-start(bf16[192,384]{1,0:T(8,128)(2,1)S(1)} %collective-permute-done.45.refs_2_), channel_id=1, source_target_pairs={{0,2},{2,0},{4,6},{6,4},{8,10},{10,8},{12,14},{14,12},{16,18},{18,... | collective-permute-start | bytes 442376 | tf_op jit(solution)/shard_map/ppermute | solution.py:997
  135.2 3.1 %collective-permute-start.50 = (bf16[384,384]{1,0:T(8,128)(2,1)S(1)}, bf16[384,384]{1,0:T(8,128)(2,1)S(1)}, u32[]{:S(2)}, u32[]{:S(2)}) collective-permute-start(bf16[384,384]{1,0:T(8,128)(2,1)S(1)} %collective-permute-done.48.refs_2_), channel_id=1, source_target_pairs={{0,2},{2,0},{4,6},{6,4},{8,10},{10,8},{12,14},{14,12},{16,18},{18,... | collective-permute-start | bytes 884744 | tf_op jit(solution)/shard_map/ppermute | solution.py:997
  135.8 12.9 %collective-permute-start.53 = (bf16[192,384]{1,0:T(8,128)(2,1)S(1)}, bf16[192,384]{1,0:T(8,128)(2,1)S(1)}, u32[]{:S(2)}, u32[]{:S(2)}) collective-permute-start(bf16[192,384]{1,0:T(8,128)(2,1)S(1)} %add_join.18.refs_5_.refs_1_), channel_id=1, source_target_pairs={{0,8},{2,10},{4,12},{6,14},{8,0},{10,2},{12,4},{14,6},{16,24},{18,... | collective-permute-start | bytes 442376 | tf_op jit(solution)/shard_map/ppermute | solution.py:997
  148.1 8.9 %collective-permute-start.55 = (bf16[192,384]{1,0:T(8,128)(2,1)S(1)}, bf16[192,384]{1,0:T(8,128)(2,1)S(1)}, u32[]{:S(2)}, u32[]{:S(2)}) collective-permute-start(bf16[192,384]{1,0:T(8,128)(2,1)S(1)} %get-tuple-element.226.refs_1_), channel_id=1, source_target_pairs={{0,4},{2,6},{4,0},{6,2},{8,12},{10,14},{12,8},{14,10},{16,20},{18,... | collective-permute-start | bytes 442376 | tf_op jit(solution)/shard_map/ppermute | solution.py:997
  148.7 2.2 %collective-permute-start.52 = (bf16[256,384]{1,0:T(8,128)(2,1)S(1)}, bf16[256,384]{1,0:T(8,128)(2,1)S(1)}, u32[]{:S(2)}, u32[]{:S(2)}) collective-permute-start(bf16[256,384]{1,0:T(8,128)(2,1)S(1)} %get-tuple-element.215.refs_3_.rides), channel_id=1, source_target_pairs={{0,2},{2,0},{4,6},{6,4},{8,10},{10,8},{12,14},{14,12},{16,18},{18,... | collective-permute-start | bytes 589832 | tf_op jit(solution)/shard_map/ppermute | solution.py:997
  149.2 11.0 %collective-permute-start.58 = (bf16[384,384]{1,0:T(8,128)(2,1)S(1)}, bf16[384,384]{1,0:T(8,128)(2,1)S(1)}, u32[]{:S(2)}, u32[]{:S(2)}) collective-permute-start(bf16[384,384]{1,0:T(8,128)(2,1)S(1)} %join.3.refs_2_.refs_1_), channel_id=1, source_target_pairs={{0,4},{2,6},{4,0},{6,2},{8,12},{10,14},{12,8},{14,10},{16,20},{18,... | collective-permute-start | bytes 884744 | tf_op jit(solution)/shard_map/ppermute | solution.py:997
  156.3 3.9 %collective-permute-start.54 = (f32[1,192]{1,0:T(1,128)S(1)}, f32[1,192]{1,0:T(1,128)S(1)}, u32[]{:S(2)}, u32[]{:S(2)}) collective-permute-start(f32[1,192]{1,0:T(1,128)S(1)} %get-tuple-element.222), channel_id=1, source_target_pairs={{0,1},{1,0},{2,3},{3,2},{4,5},{5,4},{6,7},{7,6},{8,9},{9,8},{10,11... | collective-permute-start | bytes 2312 | tf_op jit(solution)/shard_map/ppermute | solution.py:994
  156.5 4.9 %collective-permute-start.56 = (bf16[192,384]{1,0:T(8,128)(2,1)S(1)}, bf16[192,384]{1,0:T(8,128)(2,1)S(1)}, u32[]{:S(2)}, u32[]{:S(2)}) collective-permute-start(bf16[192,384]{1,0:T(8,128)(2,1)S(1)} %get-tuple-element.226.refs_1_), channel_id=1, source_target_pairs={{0,2},{2,0},{4,6},{6,4},{8,10},{10,8},{12,14},{14,12},{16,18},{18,... | collective-permute-start | bytes 442376 | tf_op jit(solution)/shard_map/ppermute | solution.py:997
  156.6 6.5 %collective-permute-start.59 = (bf16[384,384]{1,0:T(8,128)(2,1)S(1)}, bf16[384,384]{1,0:T(8,128)(2,1)S(1)}, u32[]{:S(2)}, u32[]{:S(2)}) collective-permute-start(bf16[384,384]{1,0:T(8,128)(2,1)S(1)} %join.3.refs_2_.refs_1_), channel_id=1, source_target_pairs={{0,2},{2,0},{4,6},{6,4},{8,10},{10,8},{12,14},{14,12},{16,18},{18,... | collective-permute-start | bytes 884744 | tf_op jit(solution)/shard_map/ppermute | solution.py:997
  157.0 4.4 %collective-permute-start.57 = (bf16[192,384]{1,0:T(8,128)(2,1)S(1)}, bf16[192,384]{1,0:T(8,128)(2,1)S(1)}, u32[]{:S(2)}, u32[]{:S(2)}) collective-permute-start(bf16[192,384]{1,0:T(8,128)(2,1)S(1)} %collective-permute-done.55.refs_2_), channel_id=1, source_target_pairs={{0,2},{2,0},{4,6},{6,4},{8,10},{10,8},{12,14},{14,12},{16,18},{18,... | collective-permute-start | bytes 442376 | tf_op jit(solution)/shard_map/ppermute | solution.py:997
  160.2 2.9 %collective-permute-start.60 = (bf16[384,384]{1,0:T(8,128)(2,1)S(1)}, bf16[384,384]{1,0:T(8,128)(2,1)S(1)}, u32[]{:S(2)}, u32[]{:S(2)}) collective-permute-start(bf16[384,384]{1,0:T(8,128)(2,1)S(1)} %collective-permute-done.58.refs_2_), channel_id=1, source_target_pairs={{0,2},{2,0},{4,6},{6,4},{8,10},{10,8},{12,14},{14,12},{16,18},{18,... | collective-permute-start | bytes 884744 | tf_op jit(solution)/shard_map/ppermute | solution.py:997
  (12 other events, 54.6 us)

commit v5 on v4

--- a/solution.py
+++ b/solution.py
@@ -409,16 +409,13 @@
     mod_out[...] = mod_two
     for copy in copies:
         copy.wait()
-    branch = None
     for part in range(4):
         cols = slice(part * D, (part + 1) * D)
         pre_act = dot(mod_two, w_up[:, cols]) + vecs[10 + part : 11 + part, :]
         value, slope = gelu_parts(pre_act)
-        value = value.astype(BF16)
-        act_out[:, cols] = value
+        act_out[:, cols] = value.astype(BF16)
         slope_out[:, cols] = slope.astype(BF16)
-        term = dot(value, w_down[cols, :])
-        branch = term if branch is None else branch + term
+    branch = dot(act_out[...], w_down[...])
     branch = branch + vecs[9:10, :]
     branch_out[...] = branch
     result = middle + vecs[5:6, :] * branch
@@ -1011,7 +1008,7 @@
     got_first = over_x(first)
     classes = class_table.shape[0]
     mine_part, send_part = condition_step(
-        meta, first, got_first, class_table, ada_weight, (send_d0,)
+        meta, first, got_first, class_table, ada_weight, (send_a0,)
     )
     send_a1, send_u1, send_d1 = pack(
         1, True, 4, meta, qkv_weight, out_weight, up_weight, down_weight, (send_part,), "pack_rest"
@@ -1023,12 +1020,14 @@
         next_got = over_rep(got, distance)
         return [got, next_got, over_rep(got, CORE), over_rep(next_got, CORE)]
 
-    got_a0, got_u0, got_d0 = over_x(send_a0), over_x(send_u0), over_x(send_d0)
+    send_u0, send_d0, send_part = lax.optimization_barrier((send_u0, send_d0, send_part))
+    got_a0 = over_x(send_a0)
+    got_part = over_x(send_part)
+    got_u0, got_d0 = over_x(send_u0), over_x(send_d0)
     got_a1, got_u1, got_d1 = over_x(send_a1), over_x(send_u1), over_x(send_d1)
     pieces_a0 = relay(got_a0, None)
     far_u0, far_d0 = over_rep(got_u0, Y), over_rep(got_d0, Y)
-    got_part = over_x(send_part)
-    got_part, far_u0, far_d0 = lax.optimization_barrier((got_part, far_u0, far_d0))
+    got_part, got_u0 = lax.optimization_barrier((got_part, got_u0))
     vecs_all = vectors_step(meta, first, got_first, mine_part, got_part)
     pieces_m0 = []
     for near, far in ((got_u0, far_u0), (got_d0, far_d0)):
@@ -1061,7 +1060,7 @@
         last[0] = result[-1] if isinstance(result, (tuple, list)) else result
         return result
 
-    def reduce_chunk(keep, sent, sums):
+    def reduce_chunk(keep, sent, sums, halve):
         got = over_rep(sent, CORE)
         yield
         keep, sent = ran(first_split(meta, keep, got, sums, deps()))
@@ -1071,27 +1070,26 @@
         got = over_rep(sent, Y)
         yield
         steps = distances
-        if sums is None:
+        if halve:
             keep, sent = ran(next_split(5, meta, keep, sent, got, deps()))
             got = over_rep(sent, Z)
             steps = distances[1:]
             yield
         rows = keep.shape[0]
         for distance in steps:
-            (sent,) = ran(add_join(keep, sent, got, rows, False, deps()))
-            keep = sent
+            (joined,) = ran(add_join(keep, sent, got, rows, False, deps()))
+            keep = sent = joined
             got = over_rep(sent, distance)
             yield
         mine, *rides = ran(add_join(keep, sent, got, rows, True, deps()))
-        if sums is None:
+        if rides:
+            rides = (rides[0], over_rep(rides[0], CORE))
+        if halve:
             got = over_rep(mine, Z)
-            yield
+            yield rides
             mine = ran(join(meta, mine, got, deps()))
         next_mine = over_rep(mine, Y)
-        result = (mine, next_mine, over_rep(mine, CORE), over_rep(next_mine, CORE))
-        if rides:
-            rides = (rides[0], over_rep(rides[0], CORE))
-        yield result, rides
+        yield (mine, next_mine, over_rep(mine, CORE), over_rep(next_mine, CORE)), rides
 
     def advance(chunk, times=1):
         result = None
@@ -1104,27 +1102,31 @@
     keep, sent, grad, part_sums = mlp_bwd(
         True, meta, cotangent[0], vecs[1], (middle1, *kept_m1), deps()
     )
-    m1 = reduce_chunk(keep, sent, None)
+    m1 = reduce_chunk(keep, sent, None, True)
     advance(m1)
     keep, sent, grad, sums1 = ran(
         attn_bwd(1, 16, meta, grad, vecs[1], stream1, kept_a1, part_sums)
     )
-    a1 = reduce_chunk(keep, sent, sums1)
+    a1 = reduce_chunk(keep, sent, sums1, True)
     advance(a1)
     advance(m1)
     keep, sent, grad, part_sums = ran(
         mlp_bwd(False, meta, grad, vecs[0], (middle0, *kept_m0), deps())
     )
-    m0 = reduce_chunk(keep, sent, None)
+    m0 = reduce_chunk(keep, sent, None, True)
     advance(m0)
     advance(a1)
     keep, sent, grad_stream, sums0 = ran(
         attn_bwd(0, 16, meta, grad, vecs[0], stream, kept_a0, part_sums, deps())
     )
-    a0 = reduce_chunk(keep, sent, sums0)
+    a0 = reduce_chunk(keep, sent, sums0, True)
     advance(a0)
-    for chunk in (m1, m0, a1, a0, m1, a1):
-        advance(chunk)
+    advance(m1)
+    advance(m0)
+    advance(a1)
+    advance(m1)
+    advance(a0)
+    advance(a1)
     advance(m1, more)
     advance(m0)
     advance(a1, more)
@@ -1134,17 +1136,19 @@
     advance(a0)
     result_m1, _ = advance(m1)
     advance(m0, more)
+    rides1 = advance(a1)
+    advance(a0, more)
     result_a1, rides1 = advance(a1)
-    advance(a0, more)
     ada_grad, cond1, condition, sums1 = ran(ada_result(1, meta, None, *rides1, ada_weight, (), deps()))
     advance(m0)
     *mlp_grads, _ = ran(mlp_result(1, meta, result_m1, (), deps()))
     *attn_grads, _ = ran(attn_result(1, meta, result_a1, (), deps()))
-    result_a0, rides0 = advance(a0)
+    rides0 = advance(a0)
     result_m0, _ = advance(m0)
     ada_grad, cond0, labels_all, sums0 = ran(
         ada_result(0, meta, condition, *rides0, ada_weight, (ada_grad,), deps())
     )
+    result_a0, rides0 = advance(a0)
     table_grad, mine_cond, send_cond, *bias_grads = ran(
         condition_result(
             meta, condition, labels_all, (cond0, cond1), (sums0, sums1), classes, deps()

time: 166 us -> 160 us (0.964)
  waiting for transfers between devices: 43.3 us -> 27.7 us
  starting transfers between devices: 48.4 us -> 55.5 us
    ppermute x48 -> x50, waiting for transfers between devices: 34.2 us -> 15.6 us  [over_rep(): return lax.ppermute(value, 'rep', [(r, r ^ distance) for r in range(reps)])]
    ppermute x48 -> x50, starting transfers between devices: 33.2 us -> 38.8 us  [over_rep(): return lax.ppermute(value, 'rep', [(r, r ^ distance) for r in range(reps)])]
    ppermute x13, waiting for transfers between devices: 9.11 us -> 12.1 us  [over_x(): return lax.ppermute(value, 'shard', [(0, 1), (1, 0)])]
    pallas_call x28 -> x30, Pallas kernels: 19.3 us -> 21.4 us  [call(): pl.pallas_call(kernel, out_shape=out_shape, in_specs=list(in_specs) + [AN...]
  transfers between devices with their start and end apart: 61 -> 63, of which waited for: 19 -> 23; matrix products, arithmetic and copies ran while one was open for 0% -> 0% of each run, Pallas kernels for 32% -> 35%
where the time goes in v5:
time: 160 us; the launch traced here: 159 us
  Pallas kernels  70.9 us (44%)
  starting transfers between devices  55.5 us (35%)
  waiting for transfers between devices  27.7 us (17%)
  between operations  2.68 us (2%)
  local copies, waits for them, and re-layouts  2.44 us (2%)
    ppermute x50, starting transfers between devices, over_rep(): return lax.ppermute(value, 'rep', [(r, r ^ distance) for r in range(reps)])  38.8 us
    pallas_call x30, Pallas kernels, call(): pl.pallas_call(kernel, out_shape=out_shape, in_specs=list(in_specs) + [AN...  21.4 us
    ppermute x13, starting transfers between devices, over_x(): return lax.ppermute(value, 'shard', [(0, 1), (1, 0)])  16.7 us
    ppermute x50, waiting for transfers between devices, over_rep(): return lax.ppermute(value, 'rep', [(r, r ^ distance) for r in range(reps)])  15.6 us
    ppermute x13, waiting for transfers between devices, over_x(): return lax.ppermute(value, 'shard', [(0, 1), (1, 0)])  12.1 us
    pallas_call x2, Pallas kernels, mlp_bwd(): pl.pallas_call(functools.partial(mlp_bwd_kernel, masked, late), out_shape...  10.2 us
    pallas_call x2, Pallas kernels, attn_bwd(): pl.pallas_call(functools.partial(attn_bwd_kernel, layer, extra, late), ou...  9.27 us
    pallas_call x2, Pallas kernels, mlp_fwd(): pl.pallas_call(functools.partial(mlp_fwd_kernel, layer, far, count, last,...  8.98 us
  transfers between devices with their start and end apart: 63, of which 23 were waited for; matrix products, arithmetic and copies ran while one was open for 0% of the time, Pallas kernels for 35%

profile of v5, /device:TPU:0, one launch (start us, length us, event | category | flops | bytes accessed | tf_op | source)
XLA Modules:
  0.0 159.2 jit_solution(3377538189685726211)
XLA Ops:
  2.6 2.9 %first_messages.1 = (f32[8,1536]{1,0:T(8,128)}, bf16[96,1536]{1,0:T(8,128)(2,1)}, bf16[48,1536]{1,0:T(8,128)(2,1)}, bf16[48,1536]{1,0:T(8,128)(2,1)}) custom-call(s32[6]{0:T(128)} %stack.24.refs_0_.meta, s32[1]{0:T(128)S(6)} %copy.40.refs_1_, f32[1,384]{1,0:T(1,128)} %refs_2_.2, bf16[2,1152]{1,0:T(2,128)(2,1)} %refs_3_.6, bf16[2,384]{1,0:T(2,128)(2,1)} %refs_4_.7, ...), custom_call_target="tpu_custom_call" | custom-call | flops 10000000000 | tf_op jit(solution)/shard_map/first_messages/pallas_call | solution.py:140
  5.5 3.0 %collective-permute-start = (f32[8,1536]{1,0:T(8,128)}, f32[8,1536]{1,0:T(8,128)S(1)}, u32[]{:S(2)}, u32[]{:S(2)}) collective-permute-start(f32[8,1536]{1,0:T(8,128)} %get-tuple-element.133.refs_1_), channel_id=1, source_target_pairs={{0,1},{1,0},{2,3},{3,2},{4,5},{5,4},{6,7},{7,6},{8,9},{9,8},{10,11... | collective-permute-start | bytes 147464 | tf_op jit(solution)/shard_map/ppermute | solution.py:991
  8.6 2.4 %collective-permute-done.refs_2_ = f32[8,1536]{1,0:T(8,128)S(1)} collective-permute-done((f32[8,1536]{1,0:T(8,128)}, f32[8,1536]{1,0:T(8,128)S(1)}, u32[]{:S(2)}, u32[]{:S(2)}) %collective-permute-start) | collective-permute-done | bytes 49184 | tf_op jit(solution)/shard_map/ppermute | solution.py:991
  11.0 1.0 copy-done.9
  11.9 0.8 copy-done.12
  12.7 1.1 condition.1
  13.9 2.4 %collective-permute-start.4 = (f32[3,2304]{1,0:T(4,128)S(1)}, f32[3,2304]{1,0:T(4,128)S(1)}, u32[]{:S(2)}, u32[]{:S(2)}) collective-permute-start(f32[3,2304]{1,0:T(4,128)S(1)} %get-tuple-element.142.refs_5_), channel_id=1, source_target_pairs={{0,1},{1,0},{2,3},{3,2},{4,5},{5,4},{6,7},{7,6},{8,9},{9,8},{10,11... | collective-permute-start | bytes 82952 | tf_op jit(solution)/shard_map/ppermute | solution.py:991
  16.4 2.5 %pack_rest.1 = (bf16[48,1536]{1,0:T(8,128)(2,1)}, bf16[48,1536]{1,0:T(8,128)(2,1)}, bf16[48,1536]{1,0:T(8,128)(2,1)}) custom-call(s32[6]{0:T(128)} %stack.24.refs_0_.meta, bf16[2,192,1152]{2,1,0:T(8,128)(2,1)} %refs_3_.10, bf16[2,192,384]{2,1,0:T(8,128)(2,1)} %refs_4_.12, bf16[2,192,1536]{2,1,0:T(8,128)(2,1)} %refs_3_.11, bf16[2,768,384]{2,1,0:T(8,128)(2,1)} %refs_4_.13, ...), custom_call_target="tpu_custom_call" | custom-call | flops 10000000000 | tf_op jit(solution)/shard_map/pack_rest/pallas_call | solution.py:140
  18.9 2.0 %collective-permute-start.11 = (bf16[48,1536]{1,0:T(8,128)(2,1)S(1)}, bf16[48,1536]{1,0:T(8,128)(2,1)S(1)}, u32[]{:S(2)}, u32[]{:S(2)}) collective-permute-start(bf16[48,1536]{1,0:T(8,128)(2,1)S(1)} %copy-done.15), channel_id=1, source_target_pairs={{0,1},{1,0},{2,3},{3,2},{4,5},{5,4},{6,7},{7,6},{8,9},{9,8},{10,11... | collective-permute-start | bytes 442376 | tf_op jit(solution)/shard_map/ppermute | solution.py:991
  21.0 1.9 %collective-permute-start.2 = (bf16[48,1536]{1,0:T(8,128)(2,1)}, bf16[48,1536]{1,0:T(8,128)(2,1)S(1)}, u32[]{:S(2)}, u32[]{:S(2)}) collective-permute-start(bf16[48,1536]{1,0:T(8,128)(2,1)} %get-tuple-element.137), channel_id=1, source_target_pairs={{0,1},{1,0},{2,3},{3,2},{4,5},{5,4},{6,7},{7,6},{8,9},{9,8},{10,11... | collective-permute-start | bytes 442376 | tf_op jit(solution)/shard_map/ppermute | solution.py:991
  24.5 1.8 %collective-permute-done.11.refs_9_ = bf16[48,1536]{1,0:T(8,128)(2,1)S(1)} collective-permute-done((bf16[48,1536]{1,0:T(8,128)(2,1)S(1)}, bf16[48,1536]{1,0:T(8,128)(2,1)S(1)}, u32[]{:S(2)}, u32[]{:S(2)}) %collective-permute-start.11) | collective-permute-done | bytes 147488 | tf_op jit(solution)/shard_map/ppermute | solution.py:991
  26.3 1.5 collective-permute-start.8
  28.3 3.3 %attn_fwd.2 = (bf16[256,384]{1,0:T(8,128)(2,1)S(1)}, bf16[256,1152]{1,0:T(8,128)(2,1)S(1)}, bf16[1536,256]{1,0:T(8,128)(2,1)S(1)}, bf16[256,384]{1,0:T(8,128)(2,...) custom-call(s32[6]{0:T(128)S(1)} %copy-done.2, ...), custom_call_target="tpu_custom_call" | custom-call | flops 10000000000 | tf_op jit(solution)/shard_map/attn_fwd/pallas_call | solution.py:373
  32.7 1.2 collective-permute-done.12.refs_10_
  33.9 1.8 %collective-permute-start.15 = (bf16[48,1536]{1,0:T(8,128)(2,1)S(1)}, bf16[48,1536]{1,0:T(8,128)(2,1)S(1)}, u32[]{:S(2)}, u32[]{:S(2)}) collective-permute-start(bf16[48,1536]{1,0:T(8,128)(2,1)S(1)} %collective-permute-done.1.refs_5_), channel_id=1, source_target_pairs={{0,4},{2,6},{4,0},{6,2},{8,12},{10,14},{12,8},{14,10},{16,20},{18,... | collective-permute-start | bytes 442376 | tf_op jit(solution)/shard_map/ppermute | solution.py:994
  36.2 1.6 collective-permute-start.18
  38.3 1.9 %collective-permute-done.15.refs_6_ = bf16[48,1536]{1,0:T(8,128)(2,1)S(1)} collective-permute-done((bf16[48,1536]{1,0:T(8,128)(2,1)S(1)}, bf16[48,1536]{1,0:T(8,128)(2,1)S(1)}, u32[]{:S(2)}, u32[]{:S(2)}) %collective-permute-start.15) | collective-permute-done | bytes 147488 | tf_op jit(solution)/shard_map/ppermute | solution.py:994
  40.2 4.1 %mlp_fwd.2 = (f32[256,384]{1,0:T(8,128)S(1)}, bf16[256,384]{1,0:T(8,128)(2,1)S(1)}, bf16[256,1536]{1,0:T(8,128)(2,1)S(1)}, bf16[256,1536]{1,0:T(8,128)(2,1)S(1)}...) custom-call(s32[6]{0:T(128)S(1)} %copy-done.2, ...), custom_call_target="tpu_custom_call" | custom-call | flops 10000000000 | tf_op jit(solution)/shard_map/mlp_fwd/pallas_call | solution.py:431
  45.4 3.4 %attn_fwd.3 = (bf16[256,384]{1,0:T(8,128)(2,1)S(1)}, bf16[256,1152]{1,0:T(8,128)(2,1)S(1)}, bf16[1536,256]{1,0:T(8,128)(2,1)S(1)}, bf16[256,384]{1,0:T(8,128)(2,...) custom-call(s32[6]{0:T(128)S(1)} %copy-done.2, ...), custom_call_target="tpu_custom_call" | custom-call | flops 10000000000 | tf_op jit(solution)/shard_map/attn_fwd/pallas_call | solution.py:373
  48.9 4.8 %mlp_fwd.3 = (bf16[256,384]{1,0:T(8,128)(2,1)}, bf16[256,384]{1,0:T(8,128)(2,1)S(1)}, bf16[256,1536]{1,0:T(8,128)(2,1)S(1)}, bf16[256,1536]{1,0:T(8,128)(2,1)S(1...) custom-call(s32[6]{0:T(128)S(1)} %copy-done.2, ...), custom_call_target="tpu_custom_call" | custom-call | flops 10000000000 | tf_op jit(solution)/shard_map/mlp_fwd/pallas_call | solution.py:431
  53.8 5.2 %mlp_bwd.2 = (bf16[1536,384]{1,0:T(8,128)(2,1)S(1)}, bf16[1536,384]{1,0:T(8,128)(2,1)S(1)}, f32[256,384]{1,0:T(8,128)S(1)}, f32[16,384]{1,0:T(8,128)S(1)}) custom-call(s32[6]{0:T(128)S(1)} %copy-done.2, bf16[256,384]{1,0:T(8,128)(2,1)S(1)} %bitcast.16, f32[16,384]{1,0:T(8,128)S(1)} %get-tuple-element.252.refs_2_, ...), custom_call_target="tpu_custom_call" | custom-call | flops 10000000000 | tf_op jit(solution)/shard_map/mlp_bwd/pallas_call | solution.py:510
  59.4 4.2 %attn_bwd.2 = (bf16[768,384]{1,0:T(8,128)(2,1)S(1)}, bf16[784,384]{1,0:T(8,128)(2,1)S(1)}, f32[256,384]{1,0:T(8,128)S(1)}, bf16[16,384]{1,0:T(8,128)(2,1)S(1)}) custom-call(s32[6]{0:T(128)S(1)} %copy-done.2, f32[256,384]{1,0:T(8,128)S(1)} %get-tuple-element.161.refs_1_, f32[16,384]{1,0:T(8,128)S(1)} %get-tuple-element.252.refs_2_, ...), custom_call_target="tpu_custom_call" | custom-call | flops 10000000000 | tf_op jit(solution)/shard_map/attn_bwd/pallas_call | solution.py:613
  63.8 0.8 first_split.4
  64.6 1.4 collective-permute-start.28
  66.1 5.0 %mlp_bwd.3 = (bf16[1536,384]{1,0:T(8,128)(2,1)S(1)}, bf16[1536,384]{1,0:T(8,128)(2,1)S(1)}, f32[256,384]{1,0:T(8,128)S(1)}, f32[16,384]{1,0:T(8,128)S(1)}) custom-call(s32[6]{0:T(128)S(1)} %copy-done.2, f32[256,384]{1,0:T(8,128)S(1)} %get-tuple-element.170.refs_1_, f32[16,384]{1,0:T(8,128)S(1)} %get-tuple-element.253.refs_2_, ...), custom_call_target="tpu_custom_call" | custom-call | flops 10000000000 | tf_op jit(solution)/shard_map/mlp_bwd/pallas_call | solution.py:510
  72.6 5.1 %attn_bwd.3 = (bf16[768,384]{1,0:T(8,128)(2,1)S(1)}, bf16[784,384]{1,0:T(8,128)(2,1)S(1)}, f32[256,384]{1,0:T(8,128)}, bf16[16,384]{1,0:T(8,128)(2,1)S(1)}) custom-call(s32[6]{0:T(128)S(1)} %copy-done.2, f32[256,384]{1,0:T(8,128)S(1)} %get-tuple-element.181.refs_1_, f32[16,384]{1,0:T(8,128)S(1)} %get-tuple-element.253.refs_2_, ...), custom_call_target="tpu_custom_call" | custom-call | flops 10000000000 | tf_op jit(solution)/shard_map/attn_bwd/pallas_call | solution.py:613
  78.2 2.6 %collective-permute-done.28.refs_3_ = bf16[768,384]{1,0:T(8,128)(2,1)S(1)} collective-permute-done((bf16[768,384]{1,0:T(8,128)(2,1)S(1)}, bf16[768,384]{1,0:T(8,128)(2,1)S(1)}, u32[]{:S(2)}, u32[]{:S(2)}) %collective-permute-start.28) | collective-permute-done | bytes 589856 | tf_op jit(solution)/shard_map/ppermute | solution.py:991
  81.6 1.6 %collective-permute-start.31 = (bf16[384,384]{1,0:T(8,128)(2,1)S(1)}, bf16[384,384]{1,0:T(8,128)(2,1)S(1)}, u32[]{:S(2)}, u32[]{:S(2)}) collective-permute-start(bf16[384,384]{1,0:T(8,128)(2,1)S(1)} %get-tuple-element.199.refs_3_.refs_2_), channel_id=1, source_target_pairs={{0,4},{2,6},{4,0},{6,2},{8,12},{10,14},{12,8},{14,10},{16,20},{18,... | collective-permute-start | bytes 884744 | tf_op jit(solution)/shard_map/ppermute | solution.py:994
  83.2 0.9 first_split.6
  84.0 1.4 collective-permute-start.33
  85.5 2.0 %collective-permute-done.26.refs_3_ = bf16[400,384]{1,0:T(8,128)(2,1)S(1)} collective-permute-done((bf16[400,384]{1,0:T(8,128)(2,1)S(1)}, bf16[400,384]{1,0:T(8,128)(2,1)S(1)}, u32[]{:S(2)}, u32[]{:S(2)}) %collective-permute-start.26) | collective-permute-done | bytes 307232 | tf_op jit(solution)/shard_map/ppermute | solution.py:991
  88.1 1.6 %collective-permute-start.29 = (bf16[224,384]{1,0:T(8,128)(2,1)S(1)}, bf16[224,384]{1,0:T(8,128)(2,1)S(1)}, u32[]{:S(2)}, u32[]{:S(2)}) collective-permute-start(bf16[224,384]{1,0:T(8,128)(2,1)S(1)} %get-tuple-element.202.refs_4_.refs_2_), channel_id=1, source_target_pairs={{0,4},{2,6},{4,0},{6,2},{8,12},{10,14},{12,8},{14,10},{16,20},{18,... | collective-permute-start | bytes 516104 | tf_op jit(solution)/shard_map/ppermute | solution.py:994
  90.3 1.6 %collective-permute-start.34 = (bf16[192,384]{1,0:T(8,128)(2,1)S(1)}, bf16[192,384]{1,0:T(8,128)(2,1)S(1)}, u32[]{:S(2)}, u32[]{:S(2)}) collective-permute-start(bf16[192,384]{1,0:T(8,128)(2,1)S(1)} %get-tuple-element.206.refs_4_.refs_1_), channel_id=1, source_target_pairs={{0,8},{2,10},{4,12},{6,14},{8,0},{10,2},{12,4},{14,6},{16,24},{18,... | collective-permute-start | bytes 442376 | tf_op jit(solution)/shard_map/ppermute | solution.py:994
  92.8 1.4 collective-permute-start.38
  94.8 1.0 collective-permute-start.32
  96.1 2.6 %collective-permute-start.37 = (bf16[192,384]{1,0:T(8,128)(2,1)S(1)}, bf16[192,384]{1,0:T(8,128)(2,1)S(1)}, u32[]{:S(2)}, u32[]{:S(2)}) collective-permute-start(bf16[192,384]{1,0:T(8,128)(2,1)S(1)} %add_join.8.refs_4_.refs_0_.refs_1_), channel_id=1, source_target_pairs={{0,16},{2,18},{4,20},{6,22},{8,24},{10,26},{12,28},{14,30},{16,0},... | collective-permute-start | bytes 442376 | tf_op jit(solution)/shard_map/ppermute | solution.py:994
  98.7 1.6 %collective-permute-done.33.refs_3_ = bf16[768,384]{1,0:T(8,128)(2,1)S(1)} collective-permute-done((bf16[768,384]{1,0:T(8,128)(2,1)S(1)}, bf16[768,384]{1,0:T(8,128)(2,1)S(1)}, u32[]{:S(2)}, u32[]{:S(2)}) %collective-permute-start.33) | collective-permute-done | bytes 589856 | tf_op jit(solution)/shard_map/ppermute | solution.py:991
  101.1 1.3 collective-permute-start.36
  102.4 2.7 %collective-permute-start.35 = (bf16[224,384]{1,0:T(8,128)(2,1)S(1)}, bf16[224,384]{1,0:T(8,128)(2,1)S(1)}, u32[]{:S(2)}, u32[]{:S(2)}) collective-permute-start(bf16[224,384]{1,0:T(8,128)(2,1)S(1)} %add_join.9.refs_4_.refs_0_.refs_1_), channel_id=1, source_target_pairs={{0,16},{2,18},{4,20},{6,22},{8,24},{10,26},{12,28},{14,30},{16,0},... | collective-permute-start | bytes 516104 | tf_op jit(solution)/shard_map/ppermute | solution.py:994
  105.1 1.0 collective-permute-done.38.refs_3_
  106.7 1.4 collective-permute-start.41
  108.1 1.6 %collective-permute-start.40 = (bf16[192,384]{1,0:T(8,128)(2,1)S(1)}, bf16[192,384]{1,0:T(8,128)(2,1)S(1)}, u32[]{:S(2)}, u32[]{:S(2)}) collective-permute-start(bf16[192,384]{1,0:T(8,128)(2,1)S(1)} %add_join.10.refs_4_.refs_1_), channel_id=1, source_target_pairs={{0,8},{2,10},{4,12},{6,14},{8,0},{10,2},{12,4},{14,6},{16,24},{18,... | collective-permute-start | bytes 442376 | tf_op jit(solution)/shard_map/ppermute | solution.py:994
  110.9 1.3 collective-permute-done.41.refs_3_
  112.8 1.6 %collective-permute-start.44 = (bf16[160,384]{1,0:T(8,128)(2,1)S(1)}, bf16[160,384]{1,0:T(8,128)(2,1)S(1)}, u32[]{:S(2)}, u32[]{:S(2)}) collective-permute-start(bf16[160,384]{1,0:T(8,128)(2,1)S(1)} %get-tuple-element.219.refs_3_.refs_1_), channel_id=1, source_target_pairs={{0,8},{2,10},{4,12},{6,14},{8,0},{10,2},{12,4},{14,6},{16,24},{18,... | collective-permute-start | bytes 368648 | tf_op jit(solution)/shard_map/ppermute | solution.py:994
  115.5 0.9 collective-permute-start.49
  116.4 1.7 %collective-permute-done.39.refs_2_ = bf16[192,384]{1,0:T(8,128)(2,1)S(1)} collective-permute-done((bf16[192,384]{1,0:T(8,128)(2,1)S(1)}, bf16[192,384]{1,0:T(8,128)(2,1)S(1)}, u32[]{:S(2)}, u32[]{:S(2)}) %collective-permute-start.39) | collective-permute-done | bytes 147488 | tf_op jit(solution)/shard_map/ppermute | solution.py:994
  118.1 2.3 %collective-permute-start.52 = (bf16[192,384]{1,0:T(8,128)(2,1)S(1)}, bf16[192,384]{1,0:T(8,128)(2,1)S(1)}, u32[]{:S(2)}, u32[]{:S(2)}) collective-permute-start(bf16[192,384]{1,0:T(8,128)(2,1)S(1)} %add_join.11.refs_3_.refs_0_.refs_1_), channel_id=1, source_target_pairs={{0,16},{2,18},{4,20},{6,22},{8,24},{10,26},{12,28},{14,30},{16,0},... | collective-permute-start | bytes 442376 | tf_op jit(solution)/shard_map/ppermute | solution.py:994
  120.5 2.0 %collective-permute-start.43 = (bf16[96,384]{1,0:T(8,128)(2,1)S(1)}, bf16[96,384]{1,0:T(8,128)(2,1)S(1)}, u32[]{:S(2)}, u32[]{:S(2)}) collective-permute-start(bf16[96,384]{1,0:T(8,128)(2,1)S(1)} %get-tuple-element.221.refs_1_), channel_id=1, source_target_pairs={{0,8},{2,10},{4,12},{6,14},{8,0},{10,2},{12,4},{14,6},{16,24},{18,... | collective-permute-start | bytes 221192 | tf_op jit(solution)/shard_map/ppermute | solution.py:994
  122.5 2.9 %collective-permute-done.43.refs_2_ = bf16[96,384]{1,0:T(8,128)(2,1)S(1)} collective-permute-done((bf16[96,384]{1,0:T(8,128)(2,1)S(1)}, bf16[96,384]{1,0:T(8,128)(2,1)S(1)}, u32[]{:S(2)}, u32[]{:S(2)}) %collective-permute-start.43) | collective-permute-done | bytes 73760 | tf_op jit(solution)/shard_map/ppermute | solution.py:994
  126.7 1.8 %collective-permute-start.45 = (bf16[224,384]{1,0:T(8,128)(2,1)S(1)}, bf16[224,384]{1,0:T(8,128)(2,1)S(1)}, u32[]{:S(2)}, u32[]{:S(2)}) collective-permute-start(bf16[224,384]{1,0:T(8,128)(2,1)S(1)} %add_join.13.refs_3_.refs_0_.refs_1_), channel_id=1, source_target_pairs={{0,16},{2,18},{4,20},{6,22},{8,24},{10,26},{12,28},{14,30},{16,0},... | collective-permute-start | bytes 516104 | tf_op jit(solution)/shard_map/ppermute | solution.py:994
  128.5 2.9 %ada_result.2 = (f32[2,192,2304]{2,1,0:T(8,128)}, f32[32,192]{1,0:T(8,128)S(1)}, f32[32,192]{1,0:T(8,128)S(1)}, f32[16,384]{1,0:T(8,128)S(1)}) custom-call(s32[6]{0:T(128)S(1)} %copy-done.2, bf16[256,384]{1,0:T(8,128)(2,1)S(1)} %get-tuple-element.220.refs_3_.rides, bf16[256,384]{1,0:T(8,128)(2,1)S(1)} %collective-permute-done.42.far, ...), custom_call_target="tpu_custom_call" | custom-call | flops 100000000 | tf_op jit(solution)/shard_map/ada_result/pallas_call | solution.py:874
  132.3 0.9 collective-permute-start.54
  133.3 2.1 %mlp_result.2 = (f32[2,192,1536]{2,1,0:T(8,128)}, f32[2,768,384]{2,1,0:T(8,128)}, f32[8,128]{1,0:T(8,128)S(1)}) custom-call(s32[6]{0:T(128)S(1)} %copy-done.2, bf16[384,384]{1,0:T(8,128)(2,1)S(1)} %join.4.refs_3_.refs_1_, bf16[384,384]{1,0:T(8,128)(2,1)S(1)} %collective-permute-done.49.refs_2_, bf16[384,384]{1,0:T(8,128)(2,1)S(1)} %collective-permute-done.50.refs_3_, ...), custom_call_target="tpu_custom_call" | custom-call | flops 100000000 | tf_op jit(solution)/shard_map/mlp_result/pallas_call | solution.py:799
  135.5 1.7 %attn_result.2 = (f32[2,192,1152]{2,1,0:T(8,128)}, f32[2,192,384]{2,1,0:T(8,128)}, f32[8,128]{1,0:T(8,128)S(1)}) custom-call(s32[6]{0:T(128)S(1)} %copy-done.2, bf16[192,384]{1,0:T(8,128)(2,1)S(1)} %join.5.refs_0_.refs_1_, bf16[192,384]{1,0:T(8,128)(2,1)S(1)} %collective-permute-done.46.refs_2_, bf16[192,384]{1,0:T(8,128)(2,1)S(1)} %collective-permute-done.47.refs_3_, ...), custom_call_target="tpu_custom_call" | custom-call | flops 100000000 | tf_op jit(solution)/shard_map/attn_result/pallas_call | solution.py:799
  137.2 1.0 collective-permute-done.45.refs_2_
  138.4 2.7 %collective-permute-done.54.refs_2_ = bf16[192,384]{1,0:T(8,128)(2,1)S(1)} collective-permute-done((bf16[192,384]{1,0:T(8,128)(2,1)S(1)}, bf16[192,384]{1,0:T(8,128)(2,1)S(1)}, u32[]{:S(2)}, u32[]{:S(2)}) %collective-permute-start.54) | collective-permute-done | bytes 147488 | tf_op jit(solution)/shard_map/ppermute | solution.py:994
  141.6 1.5 collective-permute-start.60
  143.1 3.1 %ada_result.3 = (f32[2,192,2304]{2,1,0:T(8,128)}, f32[32,192]{1,0:T(8,128)S(1)}, f32[32,192]{1,0:T(8,128)S(1)}, f32[16,384]{1,0:T(8,128)S(1)}) custom-call(s32[6]{0:T(128)S(1)} %copy-done.2, bf16[256,384]{1,0:T(8,128)(2,1)S(1)} %get-tuple-element.227.refs_3_.rides, ...), custom_call_target="tpu_custom_call", output_to_operand_aliasing={{0}: (5, {})} | custom-call | flops 100000000 | tf_op jit(solution)/shard_map/ada_result/pallas_call | solution.py:874
  147.5 2.3 %condition_result.1 = (f32[192,1001]{1,0:T(8,128)}, f32[1,192]{1,0:T(1,128)S(1)}, f32[1,192]{1,0:T(1,128)S(1)}, f32[2,1152]{1,0:T(2,128)}, f32[2,384]{1,0:T(2,12...) custom-call(s32[6]{0:T(128)S(1)} %copy-done.2, f32[32,192]{1,0:T(8,128)S(1)} %get-tuple-element.223.refs_0_.refs_1_, ...), custom_call_target="tpu_custom_call" | custom-call | flops 10000000000 | tf_op jit(solution)/shard_map/condition_result/pallas_call | solution.py:140
  149.8 1.4 collective-permute-start.56
  151.7 1.6 collective-permute-done.57.refs_2_
  153.3 1.2 both_halves.1
  154.6 1.7 %attn_result.3 = (f32[2,192,1152]{2,1,0:T(8,128)}, f32[2,192,384]{2,1,0:T(8,128)}, f32[8,128]{1,0:T(8,128)S(1)}) custom-call(s32[6]{0:T(128)S(1)} %copy-done.2, bf16[192,384]{1,0:T(8,128)(2,1)S(1)} %join.7.refs_7_.refs_1_, bf16[192,384]{1,0:T(8,128)(2,1)S(1)} %collective-permute-done.57.refs_2_, ...), custom_call_target="tpu_custom_call", output_to_operand_aliasing={{0}: (5, {}), {1}: (6, {})} | custom-call | flops 100000000 | tf_op jit(solution)/shard_map/attn_result/pallas_call | solution.py:799
  156.3 2.7 %mlp_result.3 = (f32[2,192,1536]{2,1,0:T(8,128)}, f32[2,768,384]{2,1,0:T(8,128)}, f32[8,128]{1,0:T(8,128)}) custom-call(s32[6]{0:T(128)S(1)} %copy-done.2, bf16[384,384]{1,0:T(8,128)(2,1)S(1)} %join.6.refs_2_.refs_1_, bf16[384,384]{1,0:T(8,128)(2,1)S(1)} %collective-permute-done.60.refs_2_, ...), custom_call_target="tpu_custom_call", output_to_operand_aliasing={{0}: (5, {}), {1}: (6, {})} | custom-call | flops 100000000 | tf_op jit(solution)/shard_map/mlp_result/pallas_call | solution.py:799
  (142 shorter events, 21.5 us)
Async XLA Ops:
  5.5 5.5 %collective-permute-start = (f32[8,1536]{1,0:T(8,128)}, f32[8,1536]{1,0:T(8,128)S(1)}, u32[]{:S(2)}, u32[]{:S(2)}) collective-permute-start(f32[8,1536]{1,0:T(8,128)} %get-tuple-element.133.refs_1_), channel_id=1, source_target_pairs={{0,1},{1,0},{2,3},{3,2},{4,5},{5,4},{6,7},{7,6},{8,9},{9,8},{10,11... | collective-permute-start | bytes 147464 | tf_op jit(solution)/shard_map/ppermute | solution.py:991
  8.5 15.3 %collective-permute-start.6 = (bf16[96,1536]{1,0:T(8,128)(2,1)}, bf16[96,1536]{1,0:T(8,128)(2,1)S(1)}, u32[]{:S(2)}, u32[]{:S(2)}) collective-permute-start(bf16[96,1536]{1,0:T(8,128)(2,1)} %get-tuple-element.134.refs_5_), channel_id=1, source_target_pairs={{0,1},{1,0},{2,3},{3,2},{4,5},{5,4},{6,7},{7,6},{8,9},{9,8},{10,11... | collective-permute-start | bytes 884744 | tf_op jit(solution)/shard_map/ppermute | solution.py:991
  13.9 7.1 %collective-permute-start.4 = (f32[3,2304]{1,0:T(4,128)S(1)}, f32[3,2304]{1,0:T(4,128)S(1)}, u32[]{:S(2)}, u32[]{:S(2)}) collective-permute-start(f32[3,2304]{1,0:T(4,128)S(1)} %get-tuple-element.142.refs_5_), channel_id=1, source_target_pairs={{0,1},{1,0},{2,3},{3,2},{4,5},{5,4},{6,7},{7,6},{8,9},{9,8},{10,11... | collective-permute-start | bytes 82952 | tf_op jit(solution)/shard_map/ppermute | solution.py:991
  16.3 6.8 %collective-permute-start.5 = (bf16[48,1536]{1,0:T(8,128)(2,1)S(1)}, bf16[48,1536]{1,0:T(8,128)(2,1)S(1)}, u32[]{:S(2)}, u32[]{:S(2)}) collective-permute-start(bf16[48,1536]{1,0:T(8,128)(2,1)S(1)} %copy-done.16), channel_id=1, source_target_pairs={{0,1},{1,0},{2,3},{3,2},{4,5},{5,4},{6,7},{7,6},{8,9},{9,8},{10,11... | collective-permute-start | bytes 442376 | tf_op jit(solution)/shard_map/ppermute | solution.py:991
  18.9 7.3 %collective-permute-start.11 = (bf16[48,1536]{1,0:T(8,128)(2,1)S(1)}, bf16[48,1536]{1,0:T(8,128)(2,1)S(1)}, u32[]{:S(2)}, u32[]{:S(2)}) collective-permute-start(bf16[48,1536]{1,0:T(8,128)(2,1)S(1)} %copy-done.15), channel_id=1, source_target_pairs={{0,1},{1,0},{2,3},{3,2},{4,5},{5,4},{6,7},{7,6},{8,9},{9,8},{10,11... | collective-permute-start | bytes 442376 | tf_op jit(solution)/shard_map/ppermute | solution.py:991
  20.9 10.7 %collective-permute-start.1 = (bf16[48,1536]{1,0:T(8,128)(2,1)}, bf16[48,1536]{1,0:T(8,128)(2,1)S(1)}, u32[]{:S(2)}, u32[]{:S(2)}) collective-permute-start(bf16[48,1536]{1,0:T(8,128)(2,1)} %get-tuple-element.136), channel_id=1, source_target_pairs={{0,1},{1,0},{2,3},{3,2},{4,5},{5,4},{6,7},{7,6},{8,9},{9,8},{10,11... | collective-permute-start | bytes 442376 | tf_op jit(solution)/shard_map/ppermute | solution.py:991
  21.0 11.2 %collective-permute-start.2 = (bf16[48,1536]{1,0:T(8,128)(2,1)}, bf16[48,1536]{1,0:T(8,128)(2,1)S(1)}, u32[]{:S(2)}, u32[]{:S(2)}) collective-permute-start(bf16[48,1536]{1,0:T(8,128)(2,1)} %get-tuple-element.137), channel_id=1, source_target_pairs={{0,1},{1,0},{2,3},{3,2},{4,5},{5,4},{6,7},{7,6},{8,9},{9,8},{10,11... | collective-permute-start | bytes 442376 | tf_op jit(solution)/shard_map/ppermute | solution.py:991
  23.1 10.8 %collective-permute-start.3 = (bf16[48,1536]{1,0:T(8,128)(2,1)}, bf16[48,1536]{1,0:T(8,128)(2,1)S(1)}, u32[]{:S(2)}, u32[]{:S(2)}) collective-permute-start(bf16[48,1536]{1,0:T(8,128)(2,1)} %get-tuple-element.138), channel_id=1, source_target_pairs={{0,1},{1,0},{2,3},{3,2},{4,5},{5,4},{6,7},{7,6},{8,9},{9,8},{10,11... | collective-permute-start | bytes 442376 | tf_op jit(solution)/shard_map/ppermute | solution.py:991
  23.7 4.0 %collective-permute-start.7 = (bf16[96,1536]{1,0:T(8,128)(2,1)S(1)}, bf16[96,1536]{1,0:T(8,128)(2,1)S(1)}, u32[]{:S(2)}, u32[]{:S(2)}) collective-permute-start(bf16[96,1536]{1,0:T(8,128)(2,1)S(1)} %collective-permute-done.6.refs_5_), channel_id=1, source_target_pairs={{0,2},{2,0},{4,6},{6,4},{8,10},{10,8},{12,14},{14,12},{16,18},{18,... | collective-permute-start | bytes 884744 | tf_op jit(solution)/shard_map/ppermute | solution.py:994
  26.3 6.1 %collective-permute-start.8 = (bf16[48,1536]{1,0:T(8,128)(2,1)S(1)}, bf16[48,1536]{1,0:T(8,128)(2,1)S(1)}, u32[]{:S(2)}, u32[]{:S(2)}) collective-permute-start(bf16[48,1536]{1,0:T(8,128)(2,1)S(1)} %collective-permute-done.5.refs_5_), channel_id=1, source_target_pairs={{0,4},{2,6},{4,0},{6,2},{8,12},{10,14},{12,8},{14,10},{16,20},{18,... | collective-permute-start | bytes 442376 | tf_op jit(solution)/shard_map/ppermute | solution.py:994
  27.8 6.1 %collective-permute-start.12 = (bf16[48,1536]{1,0:T(8,128)(2,1)S(1)}, bf16[48,1536]{1,0:T(8,128)(2,1)S(1)}, u32[]{:S(2)}, u32[]{:S(2)}) collective-permute-start(bf16[48,1536]{1,0:T(8,128)(2,1)S(1)} %collective-permute-done.11.refs_9_), channel_id=1, source_target_pairs={{0,4},{2,6},{4,0},{6,2},{8,12},{10,14},{12,8},{14,10},{16,20},{18,... | collective-permute-start | bytes 442376 | tf_op jit(solution)/shard_map/ppermute | solution.py:994
  28.3 11.9 %copy-start.4 = (bf16[2,192,1536]{2,1,0:T(8,128)(2,1)S(1)}, bf16[2,192,1536]{2,1,0:T(8,128)(2,1)}, u32[]{:S(2)}) copy-start(bf16[2,192,1536]{2,1,0:T(8,128)(2,1)} %refs_3_.11) | copy-start | bytes 3538948
  31.7 4.0 %collective-permute-start.9 = (bf16[48,1536]{1,0:T(8,128)(2,1)S(1)}, bf16[48,1536]{1,0:T(8,128)(2,1)S(1)}, u32[]{:S(2)}, u32[]{:S(2)}) collective-permute-start(bf16[48,1536]{1,0:T(8,128)(2,1)S(1)} %collective-permute-done.5.refs_5_), channel_id=1, source_target_pairs={{0,2},{2,0},{4,6},{6,4},{8,10},{10,8},{12,14},{14,12},{16,18},{18,... | collective-permute-start | bytes 442376 | tf_op jit(solution)/shard_map/ppermute | solution.py:994
  32.2 3.6 %collective-permute-start.13 = (bf16[48,1536]{1,0:T(8,128)(2,1)S(1)}, bf16[48,1536]{1,0:T(8,128)(2,1)S(1)}, u32[]{:S(2)}, u32[]{:S(2)}) collective-permute-start(bf16[48,1536]{1,0:T(8,128)(2,1)S(1)} %collective-permute-done.11.refs_9_), channel_id=1, source_target_pairs={{0,2},{2,0},{4,6},{6,4},{8,10},{10,8},{12,14},{14,12},{16,18},{18,... | collective-permute-start | bytes 442376 | tf_op jit(solution)/shard_map/ppermute | solution.py:994
  32.3 3.9 %collective-permute-start.10 = (bf16[48,1536]{1,0:T(8,128)(2,1)S(1)}, bf16[48,1536]{1,0:T(8,128)(2,1)S(1)}, u32[]{:S(2)}, u32[]{:S(2)}) collective-permute-start(bf16[48,1536]{1,0:T(8,128)(2,1)S(1)} %collective-permute-done.8.refs_6_), channel_id=1, source_target_pairs={{0,2},{2,0},{4,6},{6,4},{8,10},{10,8},{12,14},{14,12},{16,18},{18,... | collective-permute-start | bytes 442376 | tf_op jit(solution)/shard_map/ppermute | solution.py:994
  33.9 3.9 %collective-permute-start.14 = (bf16[48,1536]{1,0:T(8,128)(2,1)S(1)}, bf16[48,1536]{1,0:T(8,128)(2,1)S(1)}, u32[]{:S(2)}, u32[]{:S(2)}) collective-permute-start(bf16[48,1536]{1,0:T(8,128)(2,1)S(1)} %collective-permute-done.12.refs_10_), channel_id=1, source_target_pairs={{0,2},{2,0},{4,6},{6,4},{8,10},{10,8},{12,14},{14,12},{16,18},{18,... | collective-permute-start | bytes 442376 | tf_op jit(solution)/shard_map/ppermute | solution.py:994
  33.9 6.3 %collective-permute-start.15 = (bf16[48,1536]{1,0:T(8,128)(2,1)S(1)}, bf16[48,1536]{1,0:T(8,128)(2,1)S(1)}, u32[]{:S(2)}, u32[]{:S(2)}) collective-permute-start(bf16[48,1536]{1,0:T(8,128)(2,1)S(1)} %collective-permute-done.1.refs_5_), channel_id=1, source_target_pairs={{0,4},{2,6},{4,0},{6,2},{8,12},{10,14},{12,8},{14,10},{16,20},{18,... | collective-permute-start | bytes 442376 | tf_op jit(solution)/shard_map/ppermute | solution.py:994
  35.7 8.6 %collective-permute-start.16 = (bf16[48,1536]{1,0:T(8,128)(2,1)S(1)}, bf16[48,1536]{1,0:T(8,128)(2,1)S(1)}, u32[]{:S(2)}, u32[]{:S(2)}) collective-permute-start(bf16[48,1536]{1,0:T(8,128)(2,1)S(1)} %collective-permute-done.1.refs_5_), channel_id=1, source_target_pairs={{0,2},{2,0},{4,6},{6,4},{8,10},{10,8},{12,14},{14,12},{16,18},{18,... | collective-permute-start | bytes 442376 | tf_op jit(solution)/shard_map/ppermute | solution.py:994
  35.7 13.2 %collective-permute-start.19 = (bf16[48,1536]{1,0:T(8,128)(2,1)S(1)}, bf16[48,1536]{1,0:T(8,128)(2,1)S(1)}, u32[]{:S(2)}, u32[]{:S(2)}) collective-permute-start(bf16[48,1536]{1,0:T(8,128)(2,1)S(1)} %collective-permute-done.2.refs_5_), channel_id=1, source_target_pairs={{0,2},{2,0},{4,6},{6,4},{8,10},{10,8},{12,14},{14,12},{16,18},{18,... | collective-permute-start | bytes 442376 | tf_op jit(solution)/shard_map/ppermute | solution.py:994
  36.2 8.7 %collective-permute-start.18 = (bf16[48,1536]{1,0:T(8,128)(2,1)S(1)}, bf16[48,1536]{1,0:T(8,128)(2,1)S(1)}, u32[]{:S(2)}, u32[]{:S(2)}) collective-permute-start(bf16[48,1536]{1,0:T(8,128)(2,1)S(1)} %collective-permute-done.2.refs_5_), channel_id=1, source_target_pairs={{0,8},{2,10},{4,12},{6,14},{8,0},{10,2},{12,4},{14,6},{16,24},{18,... | collective-permute-start | bytes 442376 | tf_op jit(solution)/shard_map/ppermute | solution.py:994
  37.8 7.4 %collective-permute-start.21 = (bf16[48,1536]{1,0:T(8,128)(2,1)S(1)}, bf16[48,1536]{1,0:T(8,128)(2,1)S(1)}, u32[]{:S(2)}, u32[]{:S(2)}) collective-permute-start(bf16[48,1536]{1,0:T(8,128)(2,1)S(1)} %collective-permute-done.3.refs_9_), channel_id=1, source_target_pairs={{0,8},{2,10},{4,12},{6,14},{8,0},{10,2},{12,4},{14,6},{16,24},{18,... | collective-permute-start | bytes 442376 | tf_op jit(solution)/shard_map/ppermute | solution.py:994
  40.2 5.2 %collective-permute-start.17 = (bf16[48,1536]{1,0:T(8,128)(2,1)S(1)}, bf16[48,1536]{1,0:T(8,128)(2,1)S(1)}, u32[]{:S(2)}, u32[]{:S(2)}) collective-permute-start(bf16[48,1536]{1,0:T(8,128)(2,1)S(1)} %collective-permute-done.15.refs_6_), channel_id=1, source_target_pairs={{0,2},{2,0},{4,6},{6,4},{8,10},{10,8},{12,14},{14,12},{16,18},{18,... | collective-permute-start | bytes 442376 | tf_op jit(solution)/shard_map/ppermute | solution.py:994
  44.4 4.5 %collective-permute-start.22 = (bf16[48,1536]{1,0:T(8,128)(2,1)S(1)}, bf16[48,1536]{1,0:T(8,128)(2,1)S(1)}, u32[]{:S(2)}, u32[]{:S(2)}) collective-permute-start(bf16[48,1536]{1,0:T(8,128)(2,1)S(1)} %collective-permute-done.3.refs_9_), channel_id=1, source_target_pairs={{0,2},{2,0},{4,6},{6,4},{8,10},{10,8},{12,14},{14,12},{16,18},{18,... | collective-permute-start | bytes 442376 | tf_op jit(solution)/shard_map/ppermute | solution.py:994
  44.9 4.0 %collective-permute-start.20 = (bf16[48,1536]{1,0:T(8,128)(2,1)S(1)}, bf16[48,1536]{1,0:T(8,128)(2,1)S(1)}, u32[]{:S(2)}, u32[]{:S(2)}) collective-permute-start(bf16[48,1536]{1,0:T(8,128)(2,1)S(1)} %collective-permute-done.18.refs_6_), channel_id=1, source_target_pairs={{0,2},{2,0},{4,6},{6,4},{8,10},{10,8},{12,14},{14,12},{16,18},{18,... | collective-permute-start | bytes 442376 | tf_op jit(solution)/shard_map/ppermute | solution.py:994
  45.2 3.7 %collective-permute-start.23 = (bf16[48,1536]{1,0:T(8,128)(2,1)S(1)}, bf16[48,1536]{1,0:T(8,128)(2,1)S(1)}, u32[]{:S(2)}, u32[]{:S(2)}) collective-permute-start(bf16[48,1536]{1,0:T(8,128)(2,1)S(1)} %collective-permute-done.21.refs_10_), channel_id=1, source_target_pairs={{0,2},{2,0},{4,6},{6,4},{8,10},{10,8},{12,14},{14,12},{16,18},{18,... | collective-permute-start | bytes 442376 | tf_op jit(solution)/shard_map/ppermute | solution.py:994
  59.0 4.8 %collective-permute-start.24 = (bf16[1536,384]{1,0:T(8,128)(2,1)S(1)}, bf16[1536,384]{1,0:T(8,128)(2,1)S(1)}, u32[]{:S(2)}, u32[]{:S(2)}) collective-permute-start(bf16[1536,384]{1,0:T(8,128)(2,1)S(1)} %get-tuple-element.178), channel_id=1, source_target_pairs={{0,2},{2,0},{4,6},{6,4},{8,10},{10,8},{12,14},{14,12},{16,18},{18,... | collective-permute-start | bytes 3538952 | tf_op jit(solution)/shard_map/ppermute | solution.py:994
  63.5 7.6 %collective-permute-start.25 = (bf16[784,384]{1,0:T(8,128)(2,1)S(1)}, bf16[784,384]{1,0:T(8,128)(2,1)S(1)}, u32[]{:S(2)}, u32[]{:S(2)}) collective-permute-start(bf16[784,384]{1,0:T(8,128)(2,1)S(1)} %get-tuple-element.191), channel_id=1, source_target_pairs={{0,2},{2,0},{4,6},{6,4},{8,10},{10,8},{12,14},{14,12},{16,18},{18,... | collective-permute-start | bytes 1806344 | tf_op jit(solution)/shard_map/ppermute | solution.py:994
  64.6 16.2 %collective-permute-start.28 = (bf16[768,384]{1,0:T(8,128)(2,1)S(1)}, bf16[768,384]{1,0:T(8,128)(2,1)S(1)}, u32[]{:S(2)}, u32[]{:S(2)}) collective-permute-start(bf16[768,384]{1,0:T(8,128)(2,1)S(1)} %get-tuple-element.180.refs_10_.refs_2_), channel_id=1, source_target_pairs={{0,1},{1,0},{2,3},{3,2},{4,5},{5,4},{6,7},{7,6},{8,9},{9,8},{10,11... | collective-permute-start | bytes 1769480 | tf_op jit(solution)/shard_map/ppermute | solution.py:991
  71.9 15.5 %collective-permute-start.26 = (bf16[400,384]{1,0:T(8,128)(2,1)S(1)}, bf16[400,384]{1,0:T(8,128)(2,1)S(1)}, u32[]{:S(2)}, u32[]{:S(2)}) collective-permute-start(bf16[400,384]{1,0:T(8,128)(2,1)S(1)} %get-tuple-element.192.refs_12_.refs_2_), channel_id=1, source_target_pairs={{0,1},{1,0},{2,3},{3,2},{4,5},{5,4},{6,7},{7,6},{8,9},{9,8},{10,11... | collective-permute-start | bytes 921608 | tf_op jit(solution)/shard_map/ppermute | solution.py:991
  72.6 10.6 %collective-permute-start.27 = (bf16[1536,384]{1,0:T(8,128)(2,1)S(1)}, bf16[1536,384]{1,0:T(8,128)(2,1)S(1)}, u32[]{:S(2)}, u32[]{:S(2)}) collective-permute-start(bf16[1536,384]{1,0:T(8,128)(2,1)S(1)} %get-tuple-element.196), channel_id=1, source_target_pairs={{0,2},{2,0},{4,6},{6,4},{8,10},{10,8},{12,14},{14,12},{16,18},{18,... | collective-permute-start | bytes 3538952 | tf_op jit(solution)/shard_map/ppermute | solution.py:994
  77.7 14.2 %collective-permute-start.30 = (bf16[784,384]{1,0:T(8,128)(2,1)S(1)}, bf16[784,384]{1,0:T(8,128)(2,1)S(1)}, u32[]{:S(2)}, u32[]{:S(2)}) collective-permute-start(bf16[784,384]{1,0:T(8,128)(2,1)S(1)} %get-tuple-element.204), channel_id=1, source_target_pairs={{0,2},{2,0},{4,6},{6,4},{8,10},{10,8},{12,14},{14,12},{16,18},{18,... | collective-permute-start | bytes 1806344 | tf_op jit(solution)/shard_map/ppermute | solution.py:994
  81.6 8.1 %collective-permute-start.31 = (bf16[384,384]{1,0:T(8,128)(2,1)S(1)}, bf16[384,384]{1,0:T(8,128)(2,1)S(1)}, u32[]{:S(2)}, u32[]{:S(2)}) collective-permute-start(bf16[384,384]{1,0:T(8,128)(2,1)S(1)} %get-tuple-element.199.refs_3_.refs_2_), channel_id=1, source_target_pairs={{0,4},{2,6},{4,0},{6,2},{8,12},{10,14},{12,8},{14,10},{16,20},{18,... | collective-permute-start | bytes 884744 | tf_op jit(solution)/shard_map/ppermute | solution.py:994
  84.0 16.3 %collective-permute-start.33 = (bf16[768,384]{1,0:T(8,128)(2,1)S(1)}, bf16[768,384]{1,0:T(8,128)(2,1)S(1)}, u32[]{:S(2)}, u32[]{:S(2)}) collective-permute-start(bf16[768,384]{1,0:T(8,128)(2,1)S(1)} %get-tuple-element.200.refs_4_.refs_2_), channel_id=1, source_target_pairs={{0,1},{1,0},{2,3},{3,2},{4,5},{5,4},{6,7},{7,6},{8,9},{9,8},{10,11... | collective-permute-start | bytes 1769480 | tf_op jit(solution)/shard_map/ppermute | solution.py:991
  88.1 6.1 %collective-permute-start.29 = (bf16[224,384]{1,0:T(8,128)(2,1)S(1)}, bf16[224,384]{1,0:T(8,128)(2,1)S(1)}, u32[]{:S(2)}, u32[]{:S(2)}) collective-permute-start(bf16[224,384]{1,0:T(8,128)(2,1)S(1)} %get-tuple-element.202.refs_4_.refs_2_), channel_id=1, source_target_pairs={{0,4},{2,6},{4,0},{6,2},{8,12},{10,14},{12,8},{14,10},{16,20},{18,... | collective-permute-start | bytes 516104 | tf_op jit(solution)/shard_map/ppermute | solution.py:994
  90.3 5.7 %collective-permute-start.34 = (bf16[192,384]{1,0:T(8,128)(2,1)S(1)}, bf16[192,384]{1,0:T(8,128)(2,1)S(1)}, u32[]{:S(2)}, u32[]{:S(2)}) collective-permute-start(bf16[192,384]{1,0:T(8,128)(2,1)S(1)} %get-tuple-element.206.refs_4_.refs_1_), channel_id=1, source_target_pairs={{0,8},{2,10},{4,12},{6,14},{8,0},{10,2},{12,4},{14,6},{16,24},{18,... | collective-permute-start | bytes 442376 | tf_op jit(solution)/shard_map/ppermute | solution.py:994
  92.8 13.3 %collective-permute-start.38 = (bf16[400,384]{1,0:T(8,128)(2,1)S(1)}, bf16[400,384]{1,0:T(8,128)(2,1)S(1)}, u32[]{:S(2)}, u32[]{:S(2)}) collective-permute-start(bf16[400,384]{1,0:T(8,128)(2,1)S(1)} %get-tuple-element.207.refs_4_.refs_2_), channel_id=1, source_target_pairs={{0,1},{1,0},{2,3},{3,2},{4,5},{5,4},{6,7},{7,6},{8,9},{9,8},{10,11... | collective-permute-start | bytes 921608 | tf_op jit(solution)/shard_map/ppermute | solution.py:991
  94.8 7.6 %collective-permute-start.32 = (bf16[160,384]{1,0:T(8,128)(2,1)S(1)}, bf16[160,384]{1,0:T(8,128)(2,1)S(1)}, u32[]{:S(2)}, u32[]{:S(2)}) collective-permute-start(bf16[160,384]{1,0:T(8,128)(2,1)S(1)} %get-tuple-element.209.refs_3_.refs_1_), channel_id=1, source_target_pairs={{0,8},{2,10},{4,12},{6,14},{8,0},{10,2},{12,4},{14,6},{16,24},{18,... | collective-permute-start | bytes 368648 | tf_op jit(solution)/shard_map/ppermute | solution.py:994
  96.1 11.9 %collective-permute-start.37 = (bf16[192,384]{1,0:T(8,128)(2,1)S(1)}, bf16[192,384]{1,0:T(8,128)(2,1)S(1)}, u32[]{:S(2)}, u32[]{:S(2)}) collective-permute-start(bf16[192,384]{1,0:T(8,128)(2,1)S(1)} %add_join.8.refs_4_.refs_0_.refs_1_), channel_id=1, source_target_pairs={{0,16},{2,18},{4,20},{6,22},{8,24},{10,26},{12,28},{14,30},{16,0},... | collective-permute-start | bytes 442376 | tf_op jit(solution)/shard_map/ppermute | solution.py:994
  101.1 8.7 %collective-permute-start.36 = (bf16[384,384]{1,0:T(8,128)(2,1)S(1)}, bf16[384,384]{1,0:T(8,128)(2,1)S(1)}, u32[]{:S(2)}, u32[]{:S(2)}) collective-permute-start(bf16[384,384]{1,0:T(8,128)(2,1)S(1)} %get-tuple-element.212.refs_3_.refs_2_), channel_id=1, source_target_pairs={{0,4},{2,6},{4,0},{6,2},{8,12},{10,14},{12,8},{14,10},{16,20},{18,... | collective-permute-start | bytes 884744 | tf_op jit(solution)/shard_map/ppermute | solution.py:994
  102.4 18.0 %collective-permute-start.35 = (bf16[224,384]{1,0:T(8,128)(2,1)S(1)}, bf16[224,384]{1,0:T(8,128)(2,1)S(1)}, u32[]{:S(2)}, u32[]{:S(2)}) collective-permute-start(bf16[224,384]{1,0:T(8,128)(2,1)S(1)} %add_join.9.refs_4_.refs_0_.refs_1_), channel_id=1, source_target_pairs={{0,16},{2,18},{4,20},{6,22},{8,24},{10,26},{12,28},{14,30},{16,0},... | collective-permute-start | bytes 516104 | tf_op jit(solution)/shard_map/ppermute | solution.py:994
  106.7 5.5 %collective-permute-start.41 = (bf16[224,384]{1,0:T(8,128)(2,1)S(1)}, bf16[224,384]{1,0:T(8,128)(2,1)S(1)}, u32[]{:S(2)}, u32[]{:S(2)}) collective-permute-start(bf16[224,384]{1,0:T(8,128)(2,1)S(1)} %get-tuple-element.215.refs_3_.refs_2_), channel_id=1, source_target_pairs={{0,4},{2,6},{4,0},{6,2},{8,12},{10,14},{12,8},{14,10},{16,20},{18,... | collective-permute-start | bytes 516104 | tf_op jit(solution)/shard_map/ppermute | solution.py:994
  108.1 6.8 %collective-permute-start.40 = (bf16[192,384]{1,0:T(8,128)(2,1)S(1)}, bf16[192,384]{1,0:T(8,128)(2,1)S(1)}, u32[]{:S(2)}, u32[]{:S(2)}) collective-permute-start(bf16[192,384]{1,0:T(8,128)(2,1)S(1)} %add_join.10.refs_4_.refs_1_), channel_id=1, source_target_pairs={{0,8},{2,10},{4,12},{6,14},{8,0},{10,2},{12,4},{14,6},{16,24},{18,... | collective-permute-start | bytes 442376 | tf_op jit(solution)/shard_map/ppermute | solution.py:994
  110.4 7.7 %collective-permute-start.39 = (bf16[192,384]{1,0:T(8,128)(2,1)S(1)}, bf16[192,384]{1,0:T(8,128)(2,1)S(1)}, u32[]{:S(2)}, u32[]{:S(2)}) collective-permute-start(bf16[192,384]{1,0:T(8,128)(2,1)S(1)} %get-tuple-element.217.refs_4_.refs_1_), channel_id=1, source_target_pairs={{0,8},{2,10},{4,12},{6,14},{8,0},{10,2},{12,4},{14,6},{16,24},{18,... | collective-permute-start | bytes 442376 | tf_op jit(solution)/shard_map/ppermute | solution.py:994
  112.8 9.7 %collective-permute-start.44 = (bf16[160,384]{1,0:T(8,128)(2,1)S(1)}, bf16[160,384]{1,0:T(8,128)(2,1)S(1)}, u32[]{:S(2)}, u32[]{:S(2)}) collective-permute-start(bf16[160,384]{1,0:T(8,128)(2,1)S(1)} %get-tuple-element.219.refs_3_.refs_1_), channel_id=1, source_target_pairs={{0,8},{2,10},{4,12},{6,14},{8,0},{10,2},{12,4},{14,6},{16,24},{18,... | collective-permute-start | bytes 368648 | tf_op jit(solution)/shard_map/ppermute | solution.py:994
  115.5 16.2 %collective-permute-start.49 = (bf16[384,384]{1,0:T(8,128)(2,1)S(1)}, bf16[384,384]{1,0:T(8,128)(2,1)S(1)}, u32[]{:S(2)}, u32[]{:S(2)}) collective-permute-start(bf16[384,384]{1,0:T(8,128)(2,1)S(1)} %join.4.refs_3_.refs_1_), channel_id=1, source_target_pairs={{0,4},{2,6},{4,0},{6,2},{8,12},{10,14},{12,8},{14,10},{16,20},{18,... | collective-permute-start | bytes 884744 | tf_op jit(solution)/shard_map/ppermute | solution.py:994
  118.1 13.3 %collective-permute-start.52 = (bf16[192,384]{1,0:T(8,128)(2,1)S(1)}, bf16[192,384]{1,0:T(8,128)(2,1)S(1)}, u32[]{:S(2)}, u32[]{:S(2)}) collective-permute-start(bf16[192,384]{1,0:T(8,128)(2,1)S(1)} %add_join.11.refs_3_.refs_0_.refs_1_), channel_id=1, source_target_pairs={{0,16},{2,18},{4,20},{6,22},{8,24},{10,26},{12,28},{14,30},{16,0},... | collective-permute-start | bytes 442376 | tf_op jit(solution)/shard_map/ppermute | solution.py:994
  120.5 4.9 %collective-permute-start.43 = (bf16[96,384]{1,0:T(8,128)(2,1)S(1)}, bf16[96,384]{1,0:T(8,128)(2,1)S(1)}, u32[]{:S(2)}, u32[]{:S(2)}) collective-permute-start(bf16[96,384]{1,0:T(8,128)(2,1)S(1)} %get-tuple-element.221.refs_1_), channel_id=1, source_target_pairs={{0,8},{2,10},{4,12},{6,14},{8,0},{10,2},{12,4},{14,6},{16,24},{18,... | collective-permute-start | bytes 221192 | tf_op jit(solution)/shard_map/ppermute | solution.py:994
  122.5 4.2 %collective-permute-start.42 = (bf16[256,384]{1,0:T(8,128)(2,1)S(1)}, bf16[256,384]{1,0:T(8,128)(2,1)S(1)}, u32[]{:S(2)}, u32[]{:S(2)}) collective-permute-start(bf16[256,384]{1,0:T(8,128)(2,1)S(1)} %get-tuple-element.220.refs_3_.rides), channel_id=1, source_target_pairs={{0,2},{2,0},{4,6},{6,4},{8,10},{10,8},{12,14},{14,12},{16,18},{18,... | collective-permute-start | bytes 589832 | tf_op jit(solution)/shard_map/ppermute | solution.py:994
  126.0 6.0 %collective-permute-start.46 = (bf16[192,384]{1,0:T(8,128)(2,1)S(1)}, bf16[192,384]{1,0:T(8,128)(2,1)S(1)}, u32[]{:S(2)}, u32[]{:S(2)}) collective-permute-start(bf16[192,384]{1,0:T(8,128)(2,1)S(1)} %join.5.refs_0_.refs_1_), channel_id=1, source_target_pairs={{0,4},{2,6},{4,0},{6,2},{8,12},{10,14},{12,8},{14,10},{16,20},{18,... | collective-permute-start | bytes 442376 | tf_op jit(solution)/shard_map/ppermute | solution.py:994
  126.7 5.6 %collective-permute-start.50 = (bf16[384,384]{1,0:T(8,128)(2,1)S(1)}, bf16[384,384]{1,0:T(8,128)(2,1)S(1)}, u32[]{:S(2)}, u32[]{:S(2)}) collective-permute-start(bf16[384,384]{1,0:T(8,128)(2,1)S(1)} %join.4.refs_3_.refs_1_), channel_id=1, source_target_pairs={{0,2},{2,0},{4,6},{6,4},{8,10},{10,8},{12,14},{14,12},{16,18},{18,... | collective-permute-start | bytes 884744 | tf_op jit(solution)/shard_map/ppermute | solution.py:994
  126.7 11.5 %collective-permute-start.45 = (bf16[224,384]{1,0:T(8,128)(2,1)S(1)}, bf16[224,384]{1,0:T(8,128)(2,1)S(1)}, u32[]{:S(2)}, u32[]{:S(2)}) collective-permute-start(bf16[224,384]{1,0:T(8,128)(2,1)S(1)} %add_join.13.refs_3_.refs_0_.refs_1_), channel_id=1, source_target_pairs={{0,16},{2,18},{4,20},{6,22},{8,24},{10,26},{12,28},{14,30},{16,0},... | collective-permute-start | bytes 516104 | tf_op jit(solution)/shard_map/ppermute | solution.py:994
  131.5 4.0 %collective-permute-start.47 = (bf16[192,384]{1,0:T(8,128)(2,1)S(1)}, bf16[192,384]{1,0:T(8,128)(2,1)S(1)}, u32[]{:S(2)}, u32[]{:S(2)}) collective-permute-start(bf16[192,384]{1,0:T(8,128)(2,1)S(1)} %join.5.refs_0_.refs_1_), channel_id=1, source_target_pairs={{0,2},{2,0},{4,6},{6,4},{8,10},{10,8},{12,14},{14,12},{16,18},{18,... | collective-permute-start | bytes 442376 | tf_op jit(solution)/shard_map/ppermute | solution.py:994
  131.8 1.6 collective-permute-start.51
  132.0 3.5 %collective-permute-start.48 = (bf16[192,384]{1,0:T(8,128)(2,1)S(1)}, bf16[192,384]{1,0:T(8,128)(2,1)S(1)}, u32[]{:S(2)}, u32[]{:S(2)}) collective-permute-start(bf16[192,384]{1,0:T(8,128)(2,1)S(1)} %collective-permute-done.46.refs_2_), channel_id=1, source_target_pairs={{0,2},{2,0},{4,6},{6,4},{8,10},{10,8},{12,14},{14,12},{16,18},{18,... | collective-permute-start | bytes 442376 | tf_op jit(solution)/shard_map/ppermute | solution.py:994
  132.3 8.7 %collective-permute-start.54 = (bf16[192,384]{1,0:T(8,128)(2,1)S(1)}, bf16[192,384]{1,0:T(8,128)(2,1)S(1)}, u32[]{:S(2)}, u32[]{:S(2)}) collective-permute-start(bf16[192,384]{1,0:T(8,128)(2,1)S(1)} %add_join.14.refs_5_.refs_1_), channel_id=1, source_target_pairs={{0,8},{2,10},{4,12},{6,14},{8,0},{10,2},{12,4},{14,6},{16,24},{18,... | collective-permute-start | bytes 442376 | tf_op jit(solution)/shard_map/ppermute | solution.py:994
  138.2 8.0 %collective-permute-start.55 = (bf16[96,384]{1,0:T(8,128)(2,1)S(1)}, bf16[96,384]{1,0:T(8,128)(2,1)S(1)}, u32[]{:S(2)}, u32[]{:S(2)}) collective-permute-start(bf16[96,384]{1,0:T(8,128)(2,1)S(1)} %get-tuple-element.233.refs_1_), channel_id=1, source_target_pairs={{0,8},{2,10},{4,12},{6,14},{8,0},{10,2},{12,4},{14,6},{16,24},{18,... | collective-permute-start | bytes 221192 | tf_op jit(solution)/shard_map/ppermute | solution.py:994
  138.4 4.7 %collective-permute-start.53 = (bf16[256,384]{1,0:T(8,128)(2,1)S(1)}, bf16[256,384]{1,0:T(8,128)(2,1)S(1)}, u32[]{:S(2)}, u32[]{:S(2)}) collective-permute-start(bf16[256,384]{1,0:T(8,128)(2,1)S(1)} %get-tuple-element.227.refs_3_.rides), channel_id=1, source_target_pairs={{0,2},{2,0},{4,6},{6,4},{8,10},{10,8},{12,14},{14,12},{16,18},{18,... | collective-permute-start | bytes 589832 | tf_op jit(solution)/shard_map/ppermute | solution.py:994
  141.6 10.0 %collective-permute-start.60 = (bf16[384,384]{1,0:T(8,128)(2,1)S(1)}, bf16[384,384]{1,0:T(8,128)(2,1)S(1)}, u32[]{:S(2)}, u32[]{:S(2)}) collective-permute-start(bf16[384,384]{1,0:T(8,128)(2,1)S(1)} %join.6.refs_2_.refs_1_), channel_id=1, source_target_pairs={{0,4},{2,6},{4,0},{6,2},{8,12},{10,14},{12,8},{14,10},{16,20},{18,... | collective-permute-start | bytes 884744 | tf_op jit(solution)/shard_map/ppermute | solution.py:994
  146.8 6.4 %collective-permute-start.57 = (bf16[192,384]{1,0:T(8,128)(2,1)S(1)}, bf16[192,384]{1,0:T(8,128)(2,1)S(1)}, u32[]{:S(2)}, u32[]{:S(2)}) collective-permute-start(bf16[192,384]{1,0:T(8,128)(2,1)S(1)} %join.7.refs_7_.refs_1_), channel_id=1, source_target_pairs={{0,4},{2,6},{4,0},{6,2},{8,12},{10,14},{12,8},{14,10},{16,20},{18,... | collective-permute-start | bytes 442376 | tf_op jit(solution)/shard_map/ppermute | solution.py:994
  149.8 3.6 %collective-permute-start.56 = (f32[1,192]{1,0:T(1,128)S(1)}, f32[1,192]{1,0:T(1,128)S(1)}, u32[]{:S(2)}, u32[]{:S(2)}) collective-permute-start(f32[1,192]{1,0:T(1,128)S(1)} %get-tuple-element.235), channel_id=1, source_target_pairs={{0,1},{1,0},{2,3},{3,2},{4,5},{5,4},{6,7},{7,6},{8,9},{9,8},{10,11... | collective-permute-start | bytes 2312 | tf_op jit(solution)/shard_map/ppermute | solution.py:991
  151.1 5.1 %collective-permute-start.61 = (bf16[384,384]{1,0:T(8,128)(2,1)S(1)}, bf16[384,384]{1,0:T(8,128)(2,1)S(1)}, u32[]{:S(2)}, u32[]{:S(2)}) collective-permute-start(bf16[384,384]{1,0:T(8,128)(2,1)S(1)} %join.6.refs_2_.refs_1_), channel_id=1, source_target_pairs={{0,2},{2,0},{4,6},{6,4},{8,10},{10,8},{12,14},{14,12},{16,18},{18,... | collective-permute-start | bytes 884744 | tf_op jit(solution)/shard_map/ppermute | solution.py:994
  151.1 3.4 %collective-permute-start.58 = (bf16[192,384]{1,0:T(8,128)(2,1)S(1)}, bf16[192,384]{1,0:T(8,128)(2,1)S(1)}, u32[]{:S(2)}, u32[]{:S(2)}) collective-permute-start(bf16[192,384]{1,0:T(8,128)(2,1)S(1)} %join.7.refs_7_.refs_1_), channel_id=1, source_target_pairs={{0,2},{2,0},{4,6},{6,4},{8,10},{10,8},{12,14},{14,12},{16,18},{18,... | collective-permute-start | bytes 442376 | tf_op jit(solution)/shard_map/ppermute | solution.py:994
  151.6 4.6 %collective-permute-start.62 = (bf16[384,384]{1,0:T(8,128)(2,1)S(1)}, bf16[384,384]{1,0:T(8,128)(2,1)S(1)}, u32[]{:S(2)}, u32[]{:S(2)}) collective-permute-start(bf16[384,384]{1,0:T(8,128)(2,1)S(1)} %collective-permute-done.60.refs_2_), channel_id=1, source_target_pairs={{0,2},{2,0},{4,6},{6,4},{8,10},{10,8},{12,14},{14,12},{16,18},{18,... | collective-permute-start | bytes 884744 | tf_op jit(solution)/shard_map/ppermute | solution.py:994
  153.2 1.4 collective-permute-start.59
  (16 other events, 89.6 us)
